TPU v7x, 32 devices: a whole 2x2x4 slice. The times are simulated.
32 devices in a mesh: dp: 4 (over z), seq: 4 (over y, x), tensor: 2 (over core).
Axes of the slice: x: 2, y: 2, z: 4, core: 2. Of those that a mesh axis runs over, the one named last changes fastest.
Arguments:
- inputs: bfloat16 [2, 8, 1024, 1536], P(None, 'dp', 'seq', 'tensor'), may hold values from -6 to 6
- segments: int32 [2, 8, 1024], P(None, 'dp'), may hold values from 0 to 5, as said below
- cotangent: bfloat16 [2, 8, 1024, 1536], P(None, 'dp', 'seq', 'tensor'), may hold values from -6 to 6
- prenorm: float32 [1536], replicated, may hold values from 0.5 to 1.5
- inproj: bfloat16 [2, 1536, 3072], P(None, 'dp', 'tensor'), may hold values from -0.15625 to 0.15625
- statproj: bfloat16 [1536, 256], P('dp'), may hold values from -0.15625 to 0.15625
- stepproj: bfloat16 [1536, 48], P('dp', 'tensor'), may hold values from -0.15625 to 0.15625
- outproj: bfloat16 [3072, 1536], P('tensor', 'dp'), may hold values from -0.109375 to 0.109375
- convinner: float32 [5, 3072], P(None, 'tensor'), may hold values from -0.5 to 0.5
- convstate: float32 [5, 256], replicated, may hold values from -0.5 to 0.5
- headparam: float32 [3, 48], P(None, 'tensor'), may hold values from -9 to 5, as said below
- gatenorm: float32 [3072], P('tensor'), may hold values from 0.5 to 1.5
- prenorm_moment: float32 [1536], P('tensor'), may hold values from -1.5 to 1.5
- inproj_moment: float32 [2, 1536, 3072], P(None, ('dp', 'seq'), 'tensor'), may hold values from -1.5 to 1.5
- statproj_moment: float32 [1536, 256], P(('dp', 'seq'), 'tensor'), may hold values from -1.5 to 1.5
- stepproj_moment: float32 [1536, 48], P(('dp', 'seq'), 'tensor'), may hold values from -1.5 to 1.5
- outproj_moment: float32 [3072, 1536], P('tensor', ('dp', 'seq')), may hold values from -1.5 to 1.5
- convinner_moment: float32 [5, 3072], P(None, 'tensor'), may hold values from -1.5 to 1.5
- convstate_moment: float32 [5, 256], P(None, 'tensor'), may hold values from -1.5 to 1.5
- headparam_moment: float32 [3, 48], P(None, 'tensor'), may hold values from -1.5 to 1.5
- gatenorm_moment: float32 [3072], P('tensor'), may hold values from -1.5 to 1.5
Outputs:
- layer_out: bfloat16 [2, 8, 1024, 1536], P(None, 'dp', 'seq', 'tensor')
- input_grad: bfloat16 [2, 8, 1024, 1536], P(None, 'dp', 'seq', 'tensor')
- grad_norm: float32 [], replicated
- prenorm_newmoment: float32 [1536], P('tensor')
- inproj_newmoment: float32 [2, 1536, 3072], P(None, ('dp', 'seq'), 'tensor')
- statproj_newmoment: float32 [1536, 256], P(('dp', 'seq'), 'tensor')
- stepproj_newmoment: float32 [1536, 48], P(('dp', 'seq'), 'tensor')
- outproj_newmoment: float32 [3072, 1536], P('tensor', ('dp', 'seq'))
- convinner_newmoment: float32 [5, 3072], P(None, 'tensor')
- convstate_newmoment: float32 [5, 256], P(None, 'tensor')
- headparam_newmoment: float32 [3, 48], P(None, 'tensor')
- gatenorm_newmoment: float32 [3072], P('tensor')
- inproj_new: bfloat16 [2, 1536, 3072], P(None, ('dp', 'seq'), 'tensor')
- statproj_new: bfloat16 [1536, 256], P(('dp', 'seq'), 'tensor')
- stepproj_new: bfloat16 [1536, 48], P(('dp', 'seq'), 'tensor')
- outproj_new: bfloat16 [3072, 1536], P('tensor', ('dp', 'seq'))
- convinner_new: float32 [5, 3072], P(None, 'tensor')
- convstate_new: float32 [5, 256], P(None, 'tensor')
Inputs may be any that keep to these rules, and one draw needn't show every extreme that they name: `segments`: along each sequence the document numbers start at 0 and never fall; a document has 200 tokens or more, except the last one of a sequence. `headparam`: row 0 is added to a head's step before the softplus, row 1 is the logarithm of its decay rate, row 2 the weight of its skip term.
All inputs are finite; a program needn't handle non-finite values.
Results may differ from a plain program's by a relative error of at most 0.0093.
Values may be sent and summed in bfloat16 or wider, within the bound.
No kernel may reach another device: no remote copies, remote signals or barrier semaphores. Data moves between devices by JAX's collectives and lax.ppermute only.
A program may use at most 256 MiB of HBM per device.

v0:
```python
import math

import jax
import jax.numpy as jnp
from jax import lax
from jax.sharding import PartitionSpec as P

D = 1536
INNER = 3072
HEADDIM = 64
STATE = 128
CONV = 4
MB = 2


EPS = 1e-05
LEARN = 0.05
CLIP_RMS = 0.25
HIGH = lax.Precision.HIGHEST


def shifted(block, axis, distance):
    devices = range(lax.axis_size(axis))
    route = [(i - distance, i) for i in devices if i - distance in devices]
    return lax.ppermute(block, axis, route)


def prefix(array, axis, combine, identity):
    size, position = (lax.axis_size(axis), lax.axis_index(axis))
    everything = jax.tree.map(
        lambda part, kind: lax.all_gather(part.astype(kind), axis),
        array,
        (jnp.bfloat16, jnp.bfloat16),
    )
    start = jax.tree.map(
        lambda part, zero: jnp.broadcast_to(jnp.asarray(zero, part.dtype), part.shape),
        array,
        identity,
    )

    def prefix_step(k, before):
        reached = k < position
        new = combine(
            before, jax.tree.map(lambda part, own: part[k].astype(own.dtype), everything, array)
        )
        return jax.tree.map(lambda a, b: jnp.where(reached, a, b), new, before)

    return lax.fori_loop(0, size, prefix_step, start)


def entering_2(array, axis, combine, identity):
    size, position = (lax.axis_size(axis), lax.axis_index(axis))
    everything = jax.tree.map(lambda part: lax.all_gather(part, axis), array)
    start = jax.tree.map(
        lambda part, zero: jnp.broadcast_to(jnp.asarray(zero, part.dtype), part.shape),
        array,
        identity,
    )

    def entering_step(k, before):
        at = size - 1 - k
        reached = at > position
        new = combine(before, jax.tree.map(lambda part: part[at], everything))
        return jax.tree.map(lambda a, b: jnp.where(reached, a, b), new, before)

    return lax.fori_loop(0, size, entering_step, start)


def rms_scale(values, weight):
    return values * lax.rsqrt(jnp.mean(values * values, axis=-1, keepdims=True) + EPS) * weight


def conv_block(padded, seg_pad, kernel):
    length = padded.shape[0] - (CONV - 1)
    own_seg = seg_pad[CONV - 1 :]
    summed = jnp.broadcast_to(kernel[CONV], (length, kernel.shape[1]))
    for offset in range(CONV):
        window = padded[offset : offset + length]
        same_doc = (seg_pad[offset : offset + length] == own_seg)[:, None]
        summed = summed + kernel[offset] * jnp.where(same_doc, window, 0.0)
    return jax.nn.silu(summed)


def decay_table(cumulative, segids):
    row_count = segids.shape[0]
    places = jnp.arange(row_count)
    allowed = (segids[:, None] == segids[None, :]) & (places[:, None] >= places[None, :])
    allowed = allowed[:, :, None]
    gap_values = cumulative[:, None, :] - cumulative[None, :, :]
    return jnp.where(allowed, jnp.exp(jnp.where(allowed, gap_values, -60.0)), 0.0)


def head_rates(raw_step, params):
    step_sizes = jax.nn.softplus(raw_step + params[0])
    return (step_sizes, jnp.cumsum(-step_sizes * jnp.exp(params[1]), axis=0))


def mix_out(values, b_proj, c_proj, raw_step, params, segids, before, carry_in):
    step_sizes, cumulative = head_rates(raw_step, params)
    scores = jnp.dot(c_proj, b_proj.T, precision=HIGH)
    weights = scores[:, :, None] * decay_table(cumulative, segids) * step_sizes[None, :, :]
    result = jnp.einsum("tsh,shp->thp", weights, values, precision=HIGH)
    entering = jnp.where((segids == before)[:, None], jnp.exp(cumulative), 0.0)
    carried = jnp.einsum("tn,hpn->thp", c_proj, carry_in, precision=HIGH)
    return result + entering[:, :, None] * carried + params[2][None, :, None] * values


def mix_state(values, b_proj, raw_step, params, segids, before):
    step_sizes, cumulative = head_rates(raw_step, params)
    tail_weight = (
        jnp.where(
            (segids == segids[-1])[:, None], jnp.exp(cumulative[-1][None, :] - cumulative), 0.0
        )
        * step_sizes
    )
    summary = jnp.einsum("sh,shp,sn->hpn", tail_weight, values, b_proj, precision=HIGH)
    passing = jnp.where(segids[-1] == before, jnp.exp(cumulative[-1]), 0.0)
    return (summary, passing)


def chain(earlier, later):
    return (earlier[0] * later[0], later[0][..., None, None] * earlier[1] + later[1])


def add_tree(totals, terms):
    if totals is None:
        return terms
    return jax.tree.map(jnp.add, totals, terms)


def project(left_rows, matrix):
    return jnp.einsum("bld,dk->blk", left_rows, matrix, preferred_element_type=jnp.float32)


def weight_grad(left_rows, right_rows):
    return jnp.einsum("bld,blk->dk", left_rows, right_rows, preferred_element_type=jnp.float32)


def back_project(grad_rows, matrix):
    return jnp.einsum("blk,dk->bld", grad_rows, matrix, preferred_element_type=jnp.float32)


def body(
    inputs,
    segments,
    cotangent,
    prenorm,
    inproj,
    statproj,
    stepproj,
    outproj,
    convinner,
    convstate,
    headparam,
    gatenorm,
    prenorm_moment,
    inproj_moment,
    statproj_moment,
    stepproj_moment,
    outproj_moment,
    convinner_moment,
    convstate_moment,
    headparam_moment,
    gatenorm_moment,
):
    tensor_at = lax.axis_index("tensor")
    seq_at = lax.axis_index("seq")
    data_at = lax.axis_index("dp")
    tensor_count = lax.axis_size("tensor")
    batch_count = inputs.shape[1]
    span_len = inputs.shape[2]
    inner_local = convinner.shape[1]
    heads_local = headparam.shape[1]
    state_half = 2 * STATE // tensor_count
    model_half = D // tensor_count
    rows_full, grads_full = (
        lax.all_gather(inputs, "tensor", axis=3, tiled=True),
        lax.all_gather(cotangent, "tensor", axis=3, tiled=True),
    )
    seg_padded = jnp.pad(segments, ((0, 0), (0, 0), (CONV - 1, 0)), constant_values=-1)
    seg_local = lax.dynamic_slice_in_dim(seg_padded, seq_at * span_len, span_len + CONV - 1, 2)
    kernel = jnp.concatenate([convinner, convstate], axis=1)
    shares = None
    smalls = None
    outputs = []
    input_grads = []
    for batch in range(MB):
        inproj_all, statproj_all, stepproj_all, outproj_all = (
            lax.all_gather(inproj, "dp", axis=1, tiled=True),
            lax.all_gather(statproj, "dp", axis=0, tiled=True),
            lax.all_gather(stepproj, "dp", axis=0, tiled=True),
            lax.all_gather(outproj, "dp", axis=1, tiled=True),
        )
        rows = rows_full[batch].astype(jnp.float32)
        normed, norm_back = jax.vjp(rms_scale, rows, prenorm)
        normed_low = normed.astype(jnp.bfloat16)
        gate_pre = project(normed_low, inproj_all[0])
        inner_pre = project(normed_low, inproj_all[1])
        state_pre = project(normed_low, statproj_all)
        raw_step = project(normed_low, stepproj_all)
        mixed = jnp.concatenate([inner_pre, state_pre], axis=2).astype(jnp.bfloat16)
        edge_in = shifted(mixed[:, span_len - (CONV - 1) :, :], "seq", 1)
        padded = jnp.concatenate([edge_in, mixed], axis=1).astype(jnp.float32)
        seg_now = seg_local[batch]
        own_seg = seg_now[:, CONV - 1 :]
        before = seg_now[:, CONV - 2]
        conv_out, conv_back = jax.vjp(
            lambda pad_vals, kernel_in: jax.vmap(conv_block, in_axes=(0, 0, None))(
                pad_vals, seg_now, kernel_in
            ),
            padded,
            kernel,
        )
        values = conv_out[..., :inner_local].reshape(batch_count, span_len, heads_local, HEADDIM)
        b_proj = conv_out[..., inner_local : inner_local + STATE]
        c_proj = conv_out[..., inner_local + STATE :]
        (summary, passing), state_back = jax.vjp(
            lambda value_in, b_part, raw_part, param_in: jax.vmap(
                mix_state, in_axes=(0, 0, 0, None, 0, 0)
            )(value_in, b_part, raw_part, param_in, own_seg, before),
            values,
            b_proj,
            raw_step,
            headparam,
        )
        identity = (jnp.ones_like(passing), jnp.zeros_like(summary))
        _, carry_in = prefix((passing, summary), "seq", chain, identity)
        mixer, out_back = jax.vjp(
            lambda value_in, b_part, c_part, raw_part, param_in, state_in: jax.vmap(
                mix_out, in_axes=(0, 0, 0, 0, None, 0, 0, 0)
            )(value_in, b_part, c_part, raw_part, param_in, own_seg, before, state_in),
            values,
            b_proj,
            c_proj,
            raw_step,
            headparam,
            carry_in,
        )
        flat_mixer = mixer.reshape(batch_count, span_len, inner_local)
        gate_act = jax.nn.silu(gate_pre)
        gated_in = flat_mixer * gate_act
        total_sq = lax.psum(jnp.sum(gated_in * gated_in, axis=-1), "tensor")
        scale = lax.rsqrt(total_sq / INNER + EPS)[..., None]
        gated_low = (gated_in * scale * gatenorm).astype(jnp.bfloat16)
        branch_part = project(gated_low, outproj_all)
        branch_own = lax.psum_scatter(branch_part, "tensor", scatter_dimension=2, tiled=True)
        outputs.append((inputs[batch].astype(jnp.float32) + branch_own).astype(jnp.bfloat16))
        grad_rows = grads_full[batch]
        d_gated = back_project(grad_rows, outproj_all)
        g_outproj = jnp.einsum(
            "blk,bld->kd", gated_low, grad_rows, preferred_element_type=jnp.float32
        )
        g_gatenorm = jnp.sum(d_gated * gated_in * scale, axis=(0, 1))
        weighted = d_gated * gatenorm
        cross = lax.psum(jnp.sum(weighted * gated_in, axis=-1), "tensor")
        d_in = weighted * scale - gated_in * scale**3 * (cross / INNER)[..., None]
        d_mixer = d_in * gate_act
        sigma = jax.nn.sigmoid(gate_pre)
        d_gate = d_in * flat_mixer * sigma * (1.0 + gate_pre * (1.0 - sigma))
        d_values, d_bproj, d_cproj, d_raw, d_param, d_carry = out_back(
            d_mixer.reshape(batch_count, span_len, heads_local, HEADDIM)
        )
        _, d_after = entering_2((passing, d_carry), "seq", chain, identity)
        d_passing = jnp.sum(d_after * carry_in, axis=(2, 3))
        d_values_tail, d_bproj_tail, d_raw_tail, d_param_tail = state_back((d_after, d_passing))
        d_state = lax.psum(jnp.concatenate([d_bproj + d_bproj_tail, d_cproj], axis=2), "tensor")
        d_conv = jnp.concatenate(
            [(d_values + d_values_tail).reshape(batch_count, span_len, inner_local), d_state],
            axis=2,
        )
        d_padded, d_kernel = conv_back(d_conv)
        edge_back = shifted(d_padded[:, : CONV - 1, :].astype(jnp.bfloat16), "seq", -1).astype(
            jnp.float32
        )
        d_mixed = d_padded[:, CONV - 1 :, :] + jnp.pad(
            edge_back, ((0, 0), (span_len - (CONV - 1), 0), (0, 0))
        )
        d_mixed_low = d_mixed.astype(jnp.bfloat16)
        d_gate_low = d_gate.astype(jnp.bfloat16)
        d_raw_low = (d_raw + d_raw_tail).astype(jnp.bfloat16)
        d_inner_low = d_mixed_low[..., :inner_local]
        d_state_low = lax.dynamic_slice_in_dim(
            d_mixed_low[..., inner_local:], tensor_at * state_half, state_half, 2
        )
        statproj_own = lax.dynamic_slice_in_dim(statproj_all, tensor_at * state_half, state_half, 1)
        g_inproj = jnp.stack(
            [weight_grad(normed_low, d_gate_low), weight_grad(normed_low, d_inner_low)]
        )
        g_statproj = weight_grad(normed_low, d_state_low)
        g_stepproj = weight_grad(normed_low, d_raw_low)
        d_normed_part = (
            back_project(d_gate_low, inproj_all[0])
            + back_project(d_inner_low, inproj_all[1])
            + back_project(d_state_low, statproj_own)
            + back_project(d_raw_low, stepproj_all)
        )
        d_normed = lax.psum(d_normed_part, "tensor")
        d_rows, d_prenorm = norm_back(d_normed)
        own_rows = lax.dynamic_slice_in_dim(d_rows, tensor_at * model_half, model_half, 2)
        input_grads.append((own_rows + cotangent[batch].astype(jnp.float32)).astype(jnp.bfloat16))
        big_terms = (g_inproj, g_outproj, g_statproj, g_stepproj)
        small_terms = (
            lax.dynamic_slice_in_dim(d_prenorm, tensor_at * model_half, model_half, 0),
            d_kernel[:, :inner_local],
            lax.dynamic_slice_in_dim(
                d_kernel[:, inner_local:], tensor_at * state_half, state_half, 1
            ),
            d_param + d_param_tail,
            g_gatenorm,
        )
        shares = add_tree(
            shares,
            (
                lax.psum_scatter(big_terms[0], ("dp", "seq"), scatter_dimension=1, tiled=True),
                lax.psum_scatter(big_terms[1], ("dp", "seq"), scatter_dimension=1, tiled=True),
                lax.psum_scatter(big_terms[2], ("dp", "seq"), scatter_dimension=0, tiled=True),
                lax.psum_scatter(big_terms[3], ("dp", "seq"), scatter_dimension=0, tiled=True),
            ),
        )
        smalls = add_tree(
            smalls,
            lax.psum(
                (small_terms[0], small_terms[1], small_terms[2], small_terms[3], small_terms[4]),
                ("dp", "seq"),
            ),
        )
    big_sq = jnp.sum(jnp.stack([jnp.sum(term * term) for term in shares]))
    small_sq = jnp.sum(jnp.stack([jnp.sum(term * term) for term in smalls]))
    first_owner = jnp.where((data_at == 0) & (seq_at == 0), 1.0, 0.0)
    norm_sq = lax.psum(big_sq + first_owner * small_sq, ("dp", "seq", "tensor"))
    grad_norm = jnp.sqrt(norm_sq)
    heads_all = INNER // HEADDIM
    entries = (
        2 * D * INNER
        + 2 * D * STATE
        + D * heads_all
        + INNER * D
        + (CONV + 1) * (INNER + 2 * STATE)
        + 3 * heads_all
        + INNER
        + D
    )
    limit = CLIP_RMS * math.sqrt(entries)
    factor = limit / jnp.maximum(grad_norm, limit)
    shard_rows = shares[0].shape[1]
    row_start = seq_at * shard_rows
    big_current = (
        lax.dynamic_slice_in_dim(inproj, row_start, shard_rows, 1),
        lax.dynamic_slice_in_dim(outproj, row_start, shard_rows, 1),
        lax.dynamic_slice_in_dim(
            lax.dynamic_slice_in_dim(statproj, row_start, shard_rows, 0),
            tensor_at * state_half,
            state_half,
            1,
        ),
        lax.dynamic_slice_in_dim(stepproj, row_start, shard_rows, 0),
    )
    conv_current = (
        convinner,
        lax.dynamic_slice_in_dim(convstate, tensor_at * state_half, state_half, 1),
    )
    big_moments = (inproj_moment, outproj_moment, statproj_moment, stepproj_moment)
    small_moments = (
        prenorm_moment,
        convinner_moment,
        convstate_moment,
        headparam_moment,
        gatenorm_moment,
    )
    big_new_moments = [
        0.5 * moment_item + 0.5 * factor * grad_item
        for moment_item, grad_item in zip(big_moments, shares)
    ]
    small_new_moments = [
        0.5 * moment_item + 0.5 * factor * grad_item
        for moment_item, grad_item in zip(small_moments, smalls)
    ]
    big_new = [
        (weight_item.astype(jnp.float32) - LEARN * moment_item).astype(weight_item.dtype)
        for weight_item, moment_item in zip(big_current, big_new_moments)
    ]
    conv_new = [
        (weight_item - LEARN * moment_item).astype(weight_item.dtype)
        for weight_item, moment_item in zip(conv_current, small_new_moments[1:3])
    ]
    return (
        jnp.stack(outputs),
        jnp.stack(input_grads),
        grad_norm,
        small_new_moments[0],
        big_new_moments[0],
        big_new_moments[2],
        big_new_moments[3],
        big_new_moments[1],
        small_new_moments[1],
        small_new_moments[2],
        small_new_moments[3],
        small_new_moments[4],
        big_new[0],
        big_new[2],
        big_new[3],
        big_new[1],
        conv_new[0],
        conv_new[1],
    )


def solution(mesh):
    return jax.shard_map(
        body,
        mesh=mesh,
        in_specs=(
            P(None, "dp", "seq", "tensor"),
            P(None, "dp", None),
            P(None, "dp", "seq", "tensor"),
            P(),
            P(None, "dp", "tensor"),
            P("dp", None),
            P("dp", "tensor"),
            P("tensor", "dp"),
            P(None, "tensor"),
            P(),
            P(None, "tensor"),
            P("tensor"),
            P("tensor"),
            P(None, ("dp", "seq"), "tensor"),
            P(("dp", "seq"), "tensor"),
            P(("dp", "seq"), "tensor"),
            P("tensor", ("dp", "seq")),
            P(None, "tensor"),
            P(None, "tensor"),
            P(None, "tensor"),
            P("tensor"),
        ),
        out_specs=(
            P(None, "dp", "seq", "tensor"),
            P(None, "dp", "seq", "tensor"),
            P(),
            P("tensor"),
            P(None, ("dp", "seq"), "tensor"),
            P(("dp", "seq"), "tensor"),
            P(("dp", "seq"), "tensor"),
            P("tensor", ("dp", "seq")),
            P(None, "tensor"),
            P(None, "tensor"),
            P(None, "tensor"),
            P("tensor"),
            P(None, ("dp", "seq"), "tensor"),
            P(("dp", "seq"), "tensor"),
            P(("dp", "seq"), "tensor"),
            P("tensor", ("dp", "seq")),
            P(None, "tensor"),
            P(None, "tensor"),
        ),
        check_vma=False,
    )
```

profile of v0, /device:TPU:0, one launch (start us, length us, event | category | flops | bytes accessed | tf_op | source)
XLA Modules:
  0.0 1598.8 jit_solution(3247117643734960114)
XLA Ops:
  10.3 21.8 %all_gather.64 = bf16[1536,256]{0,1:T(8,128)(2,1)} all-gather(bf16[384,256]{0,1:T(8,128)(2,1)S(1)} %copy.205), channel_id=1, replica_groups=mesh['dp'=4,'seq'=4,'tensor'=2] {'dp'}, dimensions={0}, use_global_device_ids=true | all-gather | bytes 983040 | tf_op jit(solution)/shard_map/all_gather | solution.py:190
  33.4 13.6 all_gather.65
  61.8 132.6 %all-gather.15.cloned.1.call-done = bf16[2,1536,1536]{2,1,0:T(8,128)(2,1)} async-done(((bf16[2,384,1536]{2,1,0:T(8,128)(2,1)}), bf16[2,1536,1536]{2,1,0:T(8,128)(2,1)}) %all-gather.15.cloned.1.call-update) | async-done | bytes 9437200 | tf_op jit(solution)/shard_map/all_gather | solution.py:189
  247.2 9.6 all_gather.70
  263.5 35.0 %all-gather.17.cloned.1.call-done = bf16[1536,1536]{1,0:T(8,128)(2,1)} async-done(((bf16[1536,384]{1,0:T(8,128)(2,1)}), bf16[1536,1536]{1,0:T(8,128)(2,1)}) %all-gather.17.cloned.1.call-update) | async-done | bytes 4718608 | tf_op jit(solution)/shard_map/all_gather | solution.py:192
  310.5 32.8 %all-gather.23.cloned.1.call-done = bf16[8,24,64,128]{3,2,1,0:T(8,128)(2,1)} async-done(((bf16[2,24,64,128]{3,2,1,0:T(8,128)(2,1)}), bf16[8,24,64,128]{3,2,1,0:T(8,128)(2,1)}) %all-gather.23.cloned.1.call-update) | async-done | bytes 3145744 | tf_op jit(solution)/shard_map/all_gather | solution.py:31
  353.4 15.9 fusion.74
  373.4 16.1 %all-gather.21.cloned.1.call-done = bf16[8,24,64,128]{3,2,1,0:T(8,128)(2,1)} async-done(((bf16[2,24,64,128]{3,2,1,0:T(8,128)(2,1)}), bf16[8,24,64,128]{3,2,1,0:T(8,128)(2,1)}) %all-gather.21.cloned.1.call-update) | async-done | bytes 3145744 | tf_op jit(solution)/shard_map/all_gather | solution.py:31
  399.6 16.3 %fusion.75 = f32[2,256,24,64]{1,3,2,0:T(8,128)} fusion(f32[2,256,24,64]{1,3,2,0:T(8,128)S(1)} %bitcast.653, f32[2,256,24,64]{1,3,2,0:T(8,128)S(1)} %fusion.180, f32[2,256,24]{1,2,0:T(8,128)S(1)} %copy-done.118, f32[2,256,24]{1,2,0:T(8,128)S(1)} %bitcast_bitcast_fusion.5, f32[2,256,256]{2,1,0:T(8,128)S(1)} %copy-done.57, ...), kind=kOutput, calls=%fused_computation.143 | convolution fusion | flops 2434793472 | bytes 10240096 | tf_op jit(solution)/shard_map/jvp(vmap(tsh,shp->thp))/dot_general | solution.py:102
  419.6 9.4 multiply_reduce_fusion.24
  429.1 8.1 multiply_reduce_fusion.26
  439.7 11.1 multiply_reduce_fusion.13
  453.2 17.2 %multiply_reduce_fusion.15 = (f32[1536]{0:T(1024)}, f32[2,256,1536]{2,1,0:T(8,128)}, bf16[2,256,1536]{2,1,0:T(8,128)(2,1)}, bf16[2,256,1536]{2,1,0:T(8,128)(2,1)}, f32[1536]{0:T(1024)}, /*index=5*/f32[2,256,1536]{2,1,0:T(8,128)}) fusion(f32[2,256,1792]{2,1,0:T(8,128)} %get-tuple-element.692, f32[2,256,1536]{2,1,0:T(8,128)} %get-tuple-element.770, ...), kind=kLoop, calls=%fused_computation.149 | loop fusion | flops 29881344 | bytes 40925184 | tf_op jit(solution)/shard_map/transpose(jvp(vmap()))/reduce_sum | solution.py:105
  489.5 8.6 all_gather.74
  513.0 23.4 %fusion.21 = (f32[2,256,24]{1,2,0:T(8,128)}, f32[2,256,24]{1,2,0:T(8,128)}, f32[2,256,24]{1,2,0:T(8,128)}, f32[2,256,256]{2,1,0:T(8,128)S(1)}) fusion(f32[2,256,24]{1,2,0:T(8,128)S(1)} %copy-done.118, f32[2,256,24]{1,2,0:T(8,128)S(1)} %bitcast_bitcast_fusion.5, f32[2,256,256]{2,1,0:T(8,128)S(1)} %copy-done.58, pred[2,256,256]{2,1,0:T(8,128)(4,1)} %get-tuple-element.724, ...), kind=kOutput, calls=%fused_computation.41 | convolution fusion | flops 2462937088 | bytes 7716864 | tf_op jit(solution)/shard_map/transpose(jvp(vmap(tsh,shp->thp)))/dot_general | solution.py:102
  543.4 20.6 %fusion.23 = (f32[2,256,24]{1,2,0:T(8,128)}, f32[2,256,24]{1,2,0:T(8,128)}, f32[2,256,24]{1,2,0:T(8,128)}, f32[2,256,256]{2,1,0:T(8,128)S(1)}) fusion(f32[2,256,24]{1,2,0:T(8,128)S(1)} %copy-done.117, f32[2,256,24]{1,2,0:T(8,128)S(1)} %copy-done.77, f32[2,256,256]{2,1,0:T(8,128)S(1)} %copy-done.56, pred[2,256,256]{2,1,0:T(8,128)(4,1)S(1)} %copy-done.88, ...), kind=kOutput, calls=%fused_computation.43 | convolution fusion | flops 2462937088 | bytes 7716864 | tf_op jit(solution)/shard_map/transpose(jvp(vmap(tsh,shp->thp)))/dot_general | solution.py:102
  567.1 17.6 %while.62 = (s32[]{:T(128)}, f32[2,24,64,128]{3,2,1,0:T(8,128)}, s32[]{:T(128)}, f32[4,2,24]{2,1,0:T(2,128)}, f32[4,2,24,64,128]{4,3,2,1,0:T(8,128)}, /*index=5*/s32[]{:T(128)}, s32[]{:T(128)}, s32[]{:T(128)}, s32[]{:T(128)}) while((s32[]{:T(128)}, f32[2,24,64,128]{3,2,1,0:T(8,128)}, s32[]{:T(128)}, f32[4,2,24]{2,1,0:T(2,128)}, ...), condition=%wide.region_19.21_spmd.clone, body=%wide.region_18.20_spmd.clone.sunk | while | flops 1572872 | bytes 4719335 | solution.py:66
  584.7 37.6 %all-gather.27.cloned.1.call-done = f32[8,24,64,128]{3,2,1,0:T(8,128)} async-done(((f32[2,24,64,128]{3,2,1,0:T(8,128)}), f32[8,24,64,128]{3,2,1,0:T(8,128)}) %all-gather.27.cloned.1.call-update) | async-done | bytes 6291472 | tf_op jit(solution)/shard_map/all_gather | solution.py:53
  622.3 17.8 %while.63 = (s32[]{:T(128)}, f32[2,24,64,128]{3,2,1,0:T(8,128)}, s32[]{:T(128)}, f32[4,2,24]{2,1,0:T(2,128)}, f32[4,2,24,64,128]{4,3,2,1,0:T(8,128)}, /*index=5*/s32[]{:T(128)}, s32[]{:T(128)}, s32[]{:T(128)}, s32[]{:T(128)}) while((s32[]{:T(128)}, f32[2,24,64,128]{3,2,1,0:T(8,128)}, s32[]{:T(128)}, f32[4,2,24]{2,1,0:T(2,128)}, ...), condition=%wide.region_37.39_spmd.clone, body=%wide.region_36.38_spmd.clone.sunk | while | flops 1572872 | bytes 4719335 | solution.py:66
  686.5 8.8 fusion.58
  737.5 14.4 fusion.73
  755.6 14.1 fusion.72
  780.4 10.8 multiply_reduce_fusion.9
  795.9 8.8 broadcast_multiply_fusion
  871.8 11.8 maximum_add_fusion
  894.9 8.4 reduce-scatter.19.cloned.1.call-done
  905.2 125.4 %reduce-scatter.17.cloned.1.call-done = f32[96,128]{1,0:T(8,128)} async-done(((f32[1536,128]{1,0:T(8,128)}), f32[96,128]{1,0:T(8,128)}) %reduce-scatter.17.cloned.1.call-update) | async-done | bytes 49168 | tf_op jit(solution)/shard_map/reduce_scatter | solution.py:316
  1032.0 32.3 %all-reduce.43.cloned.1.call-done = (f32[2,256,1536]{2,1,0:T(8,128)}, f32[2,256,1536]{2,1,0:T(8,128)}) async-done(((f32[2,256,1536]{2,1,0:T(8,128)}, f32[2,256,1536]{2,1,0:T(8,128)}), (f32[2,256,1536]{2,1,0:T(8,128)}, f32[2,256,1536]{2,1,0:T(8,128)})) %all-reduce.43.cloned.1.call-update) | async-done | bytes 6291472 | tf_op jit(solution)/shard_map/psum | solution.py:297
  1070.1 79.8 %all-reduce.35 = (f32[768]{0:T(1024)S(1)}, f32[5,1536]{1,0:T(8,128)S(1)}, f32[5,128]{1,0:T(8,128)S(1)}, f32[3,24]{1,0:T(4,128)S(1)}, f32[1536]{0:T(1024)S(1)}) all-reduce(f32[768]{0:T(1024)S(1)} %dynamic-slice_add_fusion, f32[5,1536]{1,0:T(8,128)S(1)} %slice_add_fusion.2, ...), channel_id=1, replica_groups=mesh['dp'=4,'seq'=4,'tensor'=2] {'dp','seq'}, use_global_device_ids=true, to_apply=%region_65.67 | all-reduce | flops 10696 | bytes 85568 | tf_op jit(solution)/shard_map/psum | solution.py:322
  1160.5 83.4 %reduce-scatter.15.cloned.1.call-done = f32[1536,96]{0,1:T(8,128)} async-done(((f32[1536,1536]{0,1:T(8,128)}), f32[1536,96]{0,1:T(8,128)}) %reduce-scatter.15.cloned.1.call-update) | async-done | bytes 589840 | tf_op jit(solution)/shard_map/reduce_scatter | solution.py:315
  1245.8 288.9 %reduce-scatter.13.cloned.1.call-done = f32[2,96,1536]{2,1,0:T(8,128)} async-done(((f32[2,1536,1536]{2,1,0:T(8,128)}), f32[2,96,1536]{2,1,0:T(8,128)}) %reduce-scatter.13.cloned.1.call-update) | async-done | bytes 1179664 | tf_op jit(solution)/shard_map/reduce_scatter | solution.py:314
  1540.8 39.3 %psum.151 = f32[]{:T(128)} all-reduce(f32[]{:T(128)S(6)} %add.581), channel_id=1, replica_groups=mesh['dp'=4,'seq'=4,'tensor'=2] {'dp','seq','tensor'}, use_global_device_ids=true, to_apply=%region_105.107 | all-reduce | flops 1 | bytes 8 | tf_op jit(solution)/shard_map/psum | solution.py:330
  (734 shorter events, 430.1 us)
Async XLA Ops:
  7.2 41.8 %all-gather.13.cloned.1.call-start = ((), (), s32[]{:S(2)}) async-start(), calls=%async_computation.6 | async-start | bytes 4718592 | tf_op jit(solution)/shard_map/all_gather | solution.py:177
  8.0 186.5 %all-gather.15.cloned.1.call-start = ((), (), s32[]{:S(2)}) async-start(), calls=%async_computation.7 | async-start | bytes 11796480 | tf_op jit(solution)/shard_map/all_gather | solution.py:189
  8.7 254.7 %all-gather.19.cloned.1.call-start = ((), (), s32[]{:S(2)}) async-start(), calls=%async_computation.11 | async-start | bytes 4718592 | tf_op jit(solution)/shard_map/all_gather | solution.py:178
  9.5 289.0 %all-gather.17.cloned.1.call-start = ((), (), s32[]{:S(2)}) async-start(), calls=%async_computation.8 | async-start | bytes 5898240 | tf_op jit(solution)/shard_map/all_gather | solution.py:192
  10.1 333.2 %all-gather.23.cloned.1.call-start = ((), (), s32[]{:S(2)}) async-start(), calls=%async_computation.13 | async-start | bytes 3932160 | tf_op jit(solution)/shard_map/all_gather | solution.py:31
  53.1 179.1 %copy-start.47 = (f32[2,256,24]{1,2,0:T(8,128)}, f32[2,256,24]{1,2,0:T(8,128)S(1)}, u32[]{:S(2)}) copy-start(f32[2,256,24]{1,2,0:T(8,128)S(1)} %get-tuple-element.768) | copy-start | bytes 147460
  199.7 10.0 collective-permute-start.1
  205.8 4.9 collective-permute-start
  230.2 159.3 %all-gather.21.cloned.1.call-start = ((), (), s32[]{:S(2)}) async-start(), calls=%async_computation.12 | async-start | bytes 3932160 | tf_op jit(solution)/shard_map/all_gather | solution.py:31
  232.0 281.0 %copy-start.80 = (f32[2,256,24]{1,2,0:T(8,128)}, f32[2,256,24]{1,2,0:T(8,128)S(1)}, u32[]{:S(2)}) copy-start(f32[2,256,24]{1,2,0:T(8,128)S(1)} %bitcast_bitcast_fusion.5) | copy-start | bytes 147460
  232.9 407.2 %copy-start.60 = (f32[2,256,24]{1,2,0:T(8,128)}, f32[2,256,24]{1,2,0:T(8,128)S(1)}, u32[]{:S(2)}) copy-start(f32[2,256,24]{1,2,0:T(8,128)S(1)} %get-tuple-element.727) | copy-start | bytes 147460
  246.1 321.0 %all-gather.25.cloned.1.call-start = ((), (), s32[]{:S(2)}) async-start(), calls=%async_computation.14 | async-start | bytes 7864320 | tf_op jit(solution)/shard_map/all_gather | solution.py:53
  479.9 142.4 %all-gather.27.cloned.1.call-start = ((), (), s32[]{:S(2)}) async-start(), calls=%async_computation.15 | async-start | bytes 7864320 | tf_op jit(solution)/shard_map/all_gather | solution.py:53
  489.4 290.9 %all-reduce.45.cloned.1.call-start = ((), (), s32[]{:S(2)}) async-start(), calls=%async_computation.21 | async-start | bytes 2097152 | tf_op jit(solution)/shard_map/psum | solution.py:266
  658.7 231.2 %reduce-scatter.11.cloned.1.call-start = ((), (), s32[]{:S(2)}) async-start(), calls=%async_computation.10 | async-start | bytes 4718592 | tf_op jit(solution)/shard_map/reduce_scatter | solution.py:246
  666.8 223.1 %reduce-scatter.9.cloned.1.call-start = ((), (), s32[]{:S(2)}) async-start(), calls=%async_computation.9 | async-start | bytes 4718592 | tf_op jit(solution)/shard_map/reduce_scatter | solution.py:246
  695.3 208.0 %reduce-scatter.19.cloned.1.call-start = ((), (), s32[]{:S(2)}) async-start(), calls=%async_computation.19 | async-start | bytes 835584
  780.2 250.4 %reduce-scatter.17.cloned.1.call-start = ((), (), s32[]{:S(2)}) async-start(), calls=%async_computation.18 | async-start | bytes 835584 | tf_op jit(solution)/shard_map/reduce_scatter | solution.py:316
  811.1 7.2 collective-permute-start.2
  817.1 6.4 collective-permute-start.3
  826.8 237.6 %all-reduce.43.cloned.1.call-start = ((), (), s32[]{:S(2)}) async-start(), calls=%async_computation.20 | async-start | bytes 12582912 | tf_op jit(solution)/shard_map/psum | solution.py:297
  844.9 399.0 %reduce-scatter.15.cloned.1.call-start = ((), (), s32[]{:S(2)}) async-start(), calls=%async_computation.17 | async-start | bytes 10027008 | tf_op jit(solution)/shard_map/reduce_scatter | solution.py:315
  856.2 678.5 %reduce-scatter.13.cloned.1.call-start = ((), (), s32[]{:S(2)}) async-start(), calls=%async_computation.16 | async-start | bytes 20054016 | tf_op jit(solution)/shard_map/reduce_scatter | solution.py:314
  892.8 171.5 %copy-start.152 = (f32[2,256]{1,0:T(2,128)S(1)}, f32[2,256]{1,0:T(2,128)}, u32[]{:S(2)}) copy-start(f32[2,256]{1,0:T(2,128)} %copy-done.148) | copy-start | bytes 6148
  1160.4 420.5 %copy-start.191 = (f32[1536]{0:T(1024)S(1)}, f32[1536]{0:T(1024)}, u32[]{:S(2)}) copy-start(f32[1536]{0:T(1024)} %param.50) | copy-start | bytes 18436
  1160.4 421.1 %copy-start.210 = (f32[3,24]{1,0:T(4,128)S(1)}, f32[3,24]{1,0:T(4,128)}, u32[]{:S(2)}) copy-start(f32[3,24]{1,0:T(4,128)} %param.49) | copy-start | bytes 868
  1160.4 421.7 %copy-start.147 = (f32[5,256]{1,0:T(8,128)S(1)}, f32[5,256]{1,0:T(8,128)}, u32[]{:S(2)}) copy-start(f32[5,256]{1,0:T(8,128)} %param.39) | copy-start | bytes 15364
  1160.5 421.6 %copy-start.195 = (f32[5,128]{1,0:T(8,128)S(1)}, f32[5,128]{1,0:T(8,128)}, u32[]{:S(2)}) copy-start(f32[5,128]{1,0:T(8,128)} %param.48) | copy-start | bytes 7684
  1160.5 422.2 %copy-start.86 = (f32[5,1536]{1,0:T(8,128)S(1)}, f32[5,1536]{1,0:T(8,128)}, u32[]{:S(2)}) copy-start(f32[5,1536]{1,0:T(8,128)} %param.38) | copy-start | bytes 92164
  1160.5 422.2 %copy-start.115 = (f32[5,1536]{1,0:T(8,128)S(1)}, f32[5,1536]{1,0:T(8,128)}, u32[]{:S(2)}) copy-start(f32[5,1536]{1,0:T(8,128)} %param.47) | copy-start | bytes 92164
  1160.5 422.9 %copy-start.179 = (f32[96,24]{0,1:T(8,128)S(1)}, f32[96,24]{0,1:T(8,128)}, u32[]{:S(2)}) copy-start(f32[96,24]{0,1:T(8,128)} %param.45) | copy-start | bytes 27652
  1160.5 424.2 %copy-start.194 = (f32[768]{0:T(1024)S(1)}, f32[768]{0:T(1024)}, u32[]{:S(2)}) copy-start(f32[768]{0:T(1024)} %param.42) | copy-start | bytes 9220
  (212 other events, 2251.0 us)
Sparse Core Ops, SparseCore 0:
  9.6 14.8 all-gather.12
  26.0 168.3 all-gather.14
  196.0 10.4 all-gather.18
  207.9 90.5 all-gather.16
  300.7 42.4 all-gather.22
  345.5 43.9 all-gather.20
  480.0 70.1 all-gather.24
  552.1 70.1 all-gather.26
  658.8 19.6 all-reduce.44
  680.7 12.0 reduce-scatter.10
  695.4 11.7 reduce-scatter.8
  780.3 122.9 reduce-scatter.18
  909.3 121.2 reduce-scatter.16
  1033.2 31.1 all-reduce.42
  1069.9 174.0 reduce-scatter.14
  1250.5 284.0 reduce-scatter.12
where the time goes:
time: 1610 us; the launch traced here: 1600 us
  waiting for transfers between devices  801 us (50%)
  matrix products  313 us (19%)
  other arithmetic  195 us (12%)
  blocking collectives  192 us (12%)
  local copies, waits for them, and re-layouts  61.5 us (4%)
  between operations  24.9 us (2%)
    reduce_scatter x1, waiting for transfers between devices, body(): lax.psum_scatter(big_terms[0], ('dp', 'seq'), scatter_dimension=1, tiled=...  289 us
    all_gather x1, waiting for transfers between devices, body(): lax.all_gather(inproj, 'dp', axis=1, tiled=True)  133 us
    reduce_scatter x1, waiting for transfers between devices, body(): lax.psum_scatter(big_terms[2], ('dp', 'seq'), scatter_dimension=0, tiled=...  125 us
    dot_general x6, matrix products, mix_out(): result = jnp.einsum('tsh,shp->thp', weights, values, precision=HIGH)  105 us
    reduce_scatter x1, waiting for transfers between devices, body(): lax.psum_scatter(big_terms[1], ('dp', 'seq'), scatter_dimension=1, tiled=...  83.4 us
    psum x1, blocking collectives, body(): lax.psum((small_terms[0], small_terms[1], small_terms[2], small_terms[3],...  79.8 us
    dot_general x10, matrix products, back_project(): jnp.einsum('blk,dk->bld', grad_rows, matrix, preferred_element_type=jnp.f...  49.4 us
    all_gather x2, waiting for transfers between devices, prefix(): lax.all_gather(part.astype(kind), axis)  48.9 us
  transfers between devices with their start and end apart: 20, of which 12 were waited for; matrix products, arithmetic and copies ran while one was open for 27% of the time, Pallas kernels for 0%

commit v1 on v0

--- a/solution.py
+++ b/solution.py
@@ -3,6 +3,8 @@
 import jax
 import jax.numpy as jnp
 from jax import lax
+from jax.experimental import pallas as pl
+from jax.experimental.pallas import tpu as pltpu
 from jax.sharding import PartitionSpec as P
 
 D = 1536
@@ -140,7 +142,7 @@
     return jnp.einsum("blk,dk->bld", grad_rows, matrix, preferred_element_type=jnp.float32)
 
 
-def body(
+def general_body(
     inputs,
     segments,
     cotangent,
@@ -405,9 +407,824 @@
     )
 
 
+BLOCKS = 4
+SPAN = 256
+QUARTER = 384
+QHEADS = 6
+BF = jnp.bfloat16
+F32 = jnp.float32
+ROUTE_X = [(i, i ^ 1) for i in range(BLOCKS)]
+ROUTE_Y = [(i, i ^ 2) for i in range(BLOCKS)]
+ROUTE_D = [(i, i ^ 3) for i in range(BLOCKS)]
+SWAP = [(0, 1), (1, 0)]
+VMEM_LIMIT = 56 * 1024 * 1024
+
+
+def dot_nn(a, b):
+    return lax.dot_general(a, b, (((1,), (0,)), ((), ())), preferred_element_type=F32)
+
+
+def dot_nt(a, b):
+    return lax.dot_general(a, b, (((1,), (1,)), ((), ())), preferred_element_type=F32)
+
+
+def dot_tn(a, b):
+    return lax.dot_general(a, b, (((0,), (0,)), ((), ())), preferred_element_type=F32)
+
+
+def dot_exact(a, b):
+    return lax.dot_general(
+        a, b, (((1,), (0,)), ((), ())), precision=HIGH, preferred_element_type=F32
+    )
+
+
+def sigmoid(v):
+    return 1.0 / (1.0 + jnp.exp(-v))
+
+
+def pair_cols(table, k, low_half):
+    return jnp.where(low_half, table[:, 2 * k : 2 * k + 1], table[:, 2 * k + 1 : 2 * k + 2])
+
+
+def rates(raw, head):
+    shifted_raw = raw + head[0:1]
+    step = jnp.maximum(shifted_raw, 0.0) + jnp.log1p(jnp.exp(-jnp.abs(shifted_raw)))
+    return shifted_raw, step
+
+
+def block_terms(raw, head, cols):
+    shifted_raw, step = rates(raw, head)
+    rows_at = lax.broadcasted_iota(jnp.int32, (SPAN, SPAN), 0)
+    cols_at = lax.broadcasted_iota(jnp.int32, (SPAN, SPAN), 1)
+    lower = jnp.where(rows_at >= cols_at, 1.0, 0.0)
+    cum = dot_exact(lower, -step * head[1:2])
+    last = cum[SPAN - 1 : SPAN]
+    enter = jnp.exp(cum) * cols[:, 4:5]
+    leave = jnp.exp(last - cum) * cols[:, 5:6]
+    passing = jnp.exp(last) * cols[SPAN - 1 : SPAN, 4:5]
+    return shifted_raw, step, cum, enter, leave, passing, rows_at >= cols_at
+
+
+def fwd_kernel(
+    place_ref, mixed_ref, gate_ref, raw_ref, cols_ref, segr_ref, taps_ref, head_ref, chan_ref,
+    pre_ref, y_ref, hin_ref, gun_ref, sq_ref, buf, state,
+):
+    @pl.when(pl.program_id(1) == 0)
+    def _():
+        buf[0:8] = jnp.zeros((8, buf.shape[1]), F32)
+        state[...] = jnp.zeros_like(state)
+
+    mixed = mixed_ref[0, 0].astype(F32)
+    buf[8 : 8 + SPAN] = mixed
+    cols = cols_ref[0, 0]
+    taps = taps_ref[...]
+    pre = jnp.broadcast_to(taps[CONV : CONV + 1], mixed.shape)
+    for j in range(CONV):
+        window = mixed if j == CONV - 1 else buf[5 + j : 5 + j + SPAN]
+        pre = pre + taps[j : j + 1] * (window * cols[:, j : j + 1])
+    buf[0:8] = mixed[SPAN - 8 :]
+    pre_ref[0, 0] = pre
+    act = pre * sigmoid(pre)
+    values = act[:, :QUARTER]
+    b_low = act[:, QUARTER : QUARTER + STATE].astype(BF)
+    c_low = act[:, QUARTER + STATE :].astype(BF)
+    _, step, cum, enter, leave, passing, lower = block_terms(raw_ref[0, 0], head_ref[...], cols)
+    cum_t = cum.T
+    scores = dot_nt(c_low, b_low)
+    allowed = lower & (cols[:, 6:7] == segr_ref[0, 0, 0:1])
+    block_out = jnp.where(allowed, 0.0, -1e30)
+    low_half = lax.broadcasted_iota(jnp.int32, (SPAN, 128), 1) < HEADDIM
+    held = state[...].astype(BF)
+    hin_ref[0, 0] = held
+    carried = dot_nt(c_low, held)
+    skip = chan_ref[1:2]
+    tails = []
+    outs = []
+    for k in range(QHEADS // 2):
+        at = slice(128 * k, 128 * (k + 1))
+        scaled = (pair_cols(step, k, low_half) * values[:, at]).astype(BF)
+        parts = []
+        for h in (2 * k, 2 * k + 1):
+            decay = jnp.exp(cum[:, h : h + 1] - cum_t[h : h + 1] + block_out)
+            parts.append(dot_nn((scores * decay).astype(BF), scaled))
+        own = jnp.where(low_half, parts[0], parts[1])
+        outs.append(
+            own + pair_cols(enter, k, low_half) * carried[:, at] + skip[:, at] * values[:, at]
+        )
+        tails.append((pair_cols(leave, k, low_half) * scaled.astype(F32)).astype(BF))
+    y = jnp.concatenate(outs, axis=1)
+    y_ref[0, 0] = y
+    added = dot_tn(jnp.concatenate(tails, axis=1), b_low)
+    for h in range(QHEADS):
+        at = slice(HEADDIM * h, HEADDIM * (h + 1))
+        state[at] = passing[:, h : h + 1] * state[at] + added[at]
+    gate = gate_ref[0, 0]
+    gated_in = y * (gate * sigmoid(gate))
+    sq_ref[0, 0] = jnp.sum(gated_in * gated_in, axis=1, keepdims=True)
+    gun_ref[0, 0] = (gated_in * chan_ref[0:1]).astype(BF)
+
+
+def bwd_kernel(
+    place_ref, mixed_ref, pre_ref, raw_ref, y_ref, hin_ref, dy_ref, cols_ref, segr_ref, taps_ref,
+    head_ref, chan_ref, dcat_ref, dbc_ref, slope_ref, gtap_ref, ghead_ref,
+    buf, d_state, bc_edge, slope_edge,
+):
+    @pl.when(pl.program_id(1) == 0)
+    def _():
+        buf[SPAN:] = jnp.zeros((8, QUARTER), F32)
+        d_state[...] = jnp.zeros_like(d_state)
+        bc_edge[...] = jnp.zeros_like(bc_edge)
+        slope_edge[...] = jnp.zeros_like(slope_edge)
+
+    @pl.when((pl.program_id(0) == 0) & (pl.program_id(1) == 0))
+    def _():
+        gtap_ref[...] = jnp.zeros_like(gtap_ref)
+        ghead_ref[...] = jnp.zeros_like(ghead_ref)
+
+    cols = cols_ref[0, 0]
+    head = head_ref[...]
+    taps = taps_ref[...]
+    pre = pre_ref[0, 0]
+    sigma = sigmoid(pre)
+    act = pre * sigma
+    slope = sigma * (1.0 + pre * (1.0 - sigma))
+    values = act[:, :QUARTER]
+    b_low = act[:, QUARTER : QUARTER + STATE].astype(BF)
+    c_low = act[:, QUARTER + STATE :].astype(BF)
+    shifted_raw, step, cum, enter, leave, passing, lower = block_terms(raw_ref[0, 0], head, cols)
+    cum_t = cum.T
+    scores = dot_nt(c_low, b_low)
+    allowed = lower & (cols[:, 6:7] == segr_ref[0, 0, 0:1])
+    block_out = jnp.where(allowed, 0.0, -1e30)
+    low_half = lax.broadcasted_iota(jnp.int32, (SPAN, 128), 1) < HEADDIM
+    held = hin_ref[0, 0]
+    dy_low = dy_ref[0, 0]
+    dy = dy_low.astype(F32)
+    d_after = d_state[...]
+    d_after_low = d_after.astype(BF)
+    from_after = dot_nt(b_low, d_after_low)
+    skip = chan_ref[1:2]
+    zero_low = jnp.zeros((SPAN, 128), BF)
+    d_scores = jnp.zeros((SPAN, SPAN), F32)
+    d_values = []
+    d_scaled_all = []
+    scaled_all = []
+    tail_terms = []
+    tails = []
+    entering = []
+    for k in range(QHEADS // 2):
+        at = slice(128 * k, 128 * (k + 1))
+        step_k = pair_cols(step, k, low_half)
+        scaled = (step_k * values[:, at]).astype(BF)
+        scaled_f = scaled.astype(F32)
+        dy_k = dy_low[:, at]
+        parts = []
+        for h in (2 * k, 2 * k + 1):
+            decay = jnp.exp(cum[:, h : h + 1] - cum_t[h : h + 1] + block_out)
+            weights = (scores * decay).astype(BF)
+            parts.append(dot_tn(weights, dy_k))
+            mine = low_half if h % 2 == 0 else jnp.logical_not(low_half)
+            d_weights = dot_nt(jnp.where(mine, dy_k, zero_low), scaled)
+            d_scores = d_scores + d_weights * decay
+        leave_k = pair_cols(leave, k, low_half)
+        tail_part = leave_k * from_after[:, at]
+        d_scaled = jnp.where(low_half, parts[0], parts[1]) + tail_part
+        d_scaled_all.append(d_scaled)
+        scaled_all.append(scaled_f)
+        tail_terms.append(scaled_f * tail_part)
+        tails.append((leave_k * scaled_f).astype(BF))
+        entering.append((pair_cols(enter, k, low_half) * dy[:, at]).astype(BF))
+        d_values.append(step_k * d_scaled + skip[:, at] * dy[:, at])
+    d_scaled = jnp.concatenate(d_scaled_all, axis=1)
+    scaled = jnp.concatenate(scaled_all, axis=1)
+    enter_dy = jnp.concatenate(entering, axis=1)
+    d_scores_low = d_scores.astype(BF)
+    d_c = dot_nn(d_scores_low, b_low) + dot_nn(enter_dy, held)
+    d_b = dot_tn(d_scores_low, c_low) + dot_nn(jnp.concatenate(tails, axis=1), d_after_low)
+    d_bc = jnp.concatenate([d_b, d_c], axis=1)
+    dbc_ref[0, 0, 0:SPAN] = d_bc.astype(BF)
+    dbc_ref[0, 0, SPAN : SPAN + 16] = bc_edge[...].astype(BF)
+    bc_edge[...] = d_bc[0:16]
+    slope_ref[0, 0, 0:SPAN] = slope[:, QUARTER:]
+    slope_ref[0, 0, SPAN : SPAN + 16] = slope_edge[...]
+    slope_edge[...] = slope[0:16, QUARTER:]
+    chan_at = lax.broadcasted_iota(jnp.int32, (QUARTER, 128), 0)
+    head_at = lax.broadcasted_iota(jnp.int32, (QUARTER, 128), 1)
+    gather = jnp.where(
+        (chan_at >= head_at * HEADDIM) & (chan_at < (head_at + 1) * HEADDIM), 1.0, 0.0
+    )
+    by_values = dot_exact(values * d_scaled, gather)
+    by_skip = dot_exact(values * dy, gather)
+    tail_sum = dot_exact(jnp.concatenate(tail_terms, axis=1), gather)
+    d_cum = dot_exact(dy * (y_ref[0, 0] - skip * values) - scaled * d_scaled, gather)
+    state_dot = jnp.sum(d_after * held.astype(F32), axis=1, keepdims=True)
+    state_terms = jnp.sum(state_dot * gather, axis=0, keepdims=True)
+    at_last = jnp.sum(tail_sum, axis=0, keepdims=True) + passing * state_terms
+    rows_at = lax.broadcasted_iota(jnp.int32, (SPAN, SPAN), 0)
+    cols_at = lax.broadcasted_iota(jnp.int32, (SPAN, SPAN), 1)
+    upper = jnp.where(rows_at <= cols_at, 1.0, 0.0)
+    d_rate = dot_exact(upper, d_cum) + at_last
+    d_step = by_values - head[1:2] * d_rate
+    d_raw = d_step * sigmoid(shifted_raw)
+    ghead_ref[0:1] += jnp.sum(d_raw, axis=0, keepdims=True)
+    ghead_ref[1:2] += jnp.sum(-step * head[1:2] * d_rate, axis=0, keepdims=True)
+    ghead_ref[2:3] += jnp.sum(by_skip, axis=0, keepdims=True)
+    dcat_ref[0, 0, :, QUARTER:] = d_raw.astype(BF)
+    new_state = dot_tn(enter_dy, c_low)
+    for h in range(QHEADS):
+        at = slice(HEADDIM * h, HEADDIM * (h + 1))
+        d_state[at] = passing[:, h : h + 1] * d_after[at] + new_state[at]
+    d_pre = jnp.concatenate(d_values, axis=1) * slope[:, :QUARTER]
+    buf[0:SPAN] = d_pre
+    mixed = mixed_ref[0, 0, :, :QUARTER].astype(F32)
+    d_mixed = jnp.zeros((SPAN, QUARTER), F32)
+    for j in range(CONV):
+        ahead = CONV - 1 - j
+        window = (d_pre if ahead == 0 else buf[ahead : ahead + SPAN]) * cols[:, 8 + j : 9 + j]
+        d_mixed = d_mixed + taps[j : j + 1, :QUARTER] * window
+        gtap_ref[j : j + 1] += jnp.sum(mixed * window, axis=0, keepdims=True)
+    gtap_ref[CONV : CONV + 1] += jnp.sum(d_pre, axis=0, keepdims=True)
+    buf[SPAN:] = d_pre[0:8]
+    dcat_ref[0, 0, :, :QUARTER] = d_mixed.astype(BF)
+
+
+def slot_spec(rows, width, order):
+    return pl.BlockSpec((1, 1, rows, width), lambda q, j, place: (q, order(j) ^ place[0], 0, 0))
+
+
+def place_spec(rows, width, order):
+    return pl.BlockSpec((1, 1, rows, width), lambda q, j, place: (q, order(j), 0, 0))
+
+
+def fixed_spec(rows, width):
+    return pl.BlockSpec((rows, width), lambda q, j, place: (0, 0))
+
+
+def run_fwd(place, mixed, gate, raw, cols, segr, taps, head, chan):
+    width = mixed.shape[-1]
+
+    def order(j):
+        return j
+
+    def out(rows, cols_of, kind):
+        return jax.ShapeDtypeStruct((2, BLOCKS, rows, cols_of), kind)
+
+    return pl.pallas_call(
+        fwd_kernel,
+        grid_spec=pltpu.PrefetchScalarGridSpec(
+            num_scalar_prefetch=1,
+            grid=(2, BLOCKS),
+            in_specs=[
+                slot_spec(SPAN, width, order),
+                slot_spec(SPAN, QUARTER, order),
+                slot_spec(SPAN, 128, order),
+                place_spec(SPAN, 128, order),
+                place_spec(8, SPAN, order),
+                fixed_spec(8, width),
+                fixed_spec(8, 128),
+                fixed_spec(8, QUARTER),
+            ],
+            out_specs=[
+                slot_spec(SPAN, width, order),
+                slot_spec(SPAN, QUARTER, order),
+                slot_spec(QUARTER, STATE, order),
+                slot_spec(SPAN, QUARTER, order),
+                slot_spec(SPAN, 1, order),
+            ],
+            scratch_shapes=[
+                pltpu.VMEM((SPAN + 8, width), F32),
+                pltpu.VMEM((QUARTER, STATE), F32),
+            ],
+        ),
+        out_shape=[
+            out(SPAN, width, F32),
+            out(SPAN, QUARTER, F32),
+            out(QUARTER, STATE, BF),
+            out(SPAN, QUARTER, BF),
+            out(SPAN, 1, F32),
+        ],
+        compiler_params=pltpu.CompilerParams(vmem_limit_bytes=VMEM_LIMIT),
+        name="mix_forward",
+    )(place, mixed, gate, raw, cols, segr, taps, head, chan)
+
+
+def run_bwd(place, mixed, pre, raw, y, hin, dy, cols, segr, taps, head, chan):
+    width = mixed.shape[-1]
+    states = 2 * STATE
+
+    def order(j):
+        return BLOCKS - 1 - j
+
+    def out(rows, cols_of, kind):
+        return jax.ShapeDtypeStruct((2, BLOCKS, rows, cols_of), kind)
+
+    return pl.pallas_call(
+        bwd_kernel,
+        grid_spec=pltpu.PrefetchScalarGridSpec(
+            num_scalar_prefetch=1,
+            grid=(2, BLOCKS),
+            in_specs=[
+                slot_spec(SPAN, width, order),
+                slot_spec(SPAN, width, order),
+                slot_spec(SPAN, 128, order),
+                slot_spec(SPAN, QUARTER, order),
+                slot_spec(QUARTER, STATE, order),
+                slot_spec(SPAN, QUARTER, order),
+                place_spec(SPAN, 128, order),
+                place_spec(8, SPAN, order),
+                fixed_spec(8, width),
+                fixed_spec(8, 128),
+                fixed_spec(8, QUARTER),
+            ],
+            out_specs=[
+                slot_spec(SPAN, QUARTER + 128, order),
+                slot_spec(SPAN + 16, states, order),
+                slot_spec(SPAN + 16, states, order),
+                fixed_spec(8, QUARTER),
+                fixed_spec(8, 128),
+            ],
+            scratch_shapes=[
+                pltpu.VMEM((SPAN + 8, QUARTER), F32),
+                pltpu.VMEM((QUARTER, STATE), F32),
+                pltpu.VMEM((16, states), F32),
+                pltpu.VMEM((16, states), F32),
+            ],
+        ),
+        out_shape=[
+            out(SPAN, QUARTER + 128, BF),
+            out(SPAN + 16, states, BF),
+            out(SPAN + 16, states, F32),
+            jax.ShapeDtypeStruct((8, QUARTER), F32),
+            jax.ShapeDtypeStruct((8, 128), F32),
+        ],
+        compiler_params=pltpu.CompilerParams(vmem_limit_bytes=VMEM_LIMIT),
+        name="mix_backward",
+    )(place, mixed, pre, raw, y, hin, dy, cols, segr, taps, head, chan)
+
+
+def swap_cores(block):
+    return lax.ppermute(block, "tensor", SWAP)
+
+
+def over_x(block):
+    return lax.ppermute(block, "seq", ROUTE_X)
+
+
+def over_y(block):
+    return lax.ppermute(block, "seq", ROUTE_Y)
+
+
+def over_d(block):
+    return lax.ppermute(block, "seq", ROUTE_D)
+
+
+def gather_plane(piece):
+    half = piece.shape[0] // 2
+    by_x = over_x(piece)
+    by_y = over_y(piece)
+    far_a = over_x(by_y[:half])
+    far_b = over_y(by_x[half:])
+    return piece, by_x, by_y, far_a, far_b
+
+
+def gather_tokens(piece):
+    own, by_x, by_y, far_a, far_b = gather_plane(piece)
+    others = [swap_cores(part) for part in (own, by_x, by_y, far_a, far_b)]
+    rows = jnp.concatenate([own, by_x, by_y, far_a, far_b] + others, axis=0)
+    return rows.reshape(2, BLOCKS, SPAN, D)
+
+
+def add_low(a, b):
+    return (a.astype(F32) + b.astype(F32)).astype(BF)
+
+
+def scatter_plane(slots):
+    half = slots[0].shape[0] // 2
+    far_a = over_x(slots[3][:half])
+    far_b = over_y(slots[3][half:])
+    first_x = over_x(slots[1][:half])
+    first_y = over_y(slots[2][half:])
+    second_x = over_x(add_low(slots[1][half:], far_b))
+    second_y = over_y(add_low(slots[2][:half], far_a))
+    lower = slots[0][:half].astype(F32) + first_x.astype(F32) + second_y.astype(F32)
+    upper = slots[0][half:].astype(F32) + second_x.astype(F32) + first_y.astype(F32)
+    return jnp.concatenate([lower, upper], axis=0)
+
+
+def sum_plane_slots(table):
+    table = table + swap_cores(table)[:, ::-1]
+    shape = table.shape
+    pairs = table.reshape(shape[:2] + (2, 2) + shape[3:])
+    pairs = pairs + over_x(pairs)[:, :, :, ::-1]
+    pairs = pairs + over_y(pairs)[:, :, ::-1]
+    return pairs.reshape(shape)
+
+
+def fast_body(
+    inputs,
+    segments,
+    cotangent,
+    prenorm,
+    inproj,
+    statproj,
+    stepproj,
+    outproj,
+    convinner,
+    convstate,
+    headparam,
+    gatenorm,
+    prenorm_moment,
+    inproj_moment,
+    statproj_moment,
+    stepproj_moment,
+    outproj_moment,
+    convinner_moment,
+    convstate_moment,
+    headparam_moment,
+    gatenorm_moment,
+):
+    core = lax.axis_index("tensor")
+    chip = lax.axis_index("seq")
+    data_at = lax.axis_index("dp")
+    dp_count = lax.axis_size("dp")
+    heads_local = headparam.shape[1]
+    rows_local = inproj.shape[1]
+    shard = rows_local // BLOCKS
+    half_d = D // 2
+    place = chip.astype(jnp.int32).reshape(1)
+
+    def by_core(first, second):
+        return jnp.where(core == 0, first, second)
+
+    def quarter(array, axis, width):
+        return lax.dynamic_slice_in_dim(array, chip * width, width, axis)
+
+    step_flat = stepproj.reshape(-1, 512)
+    pad_rows = -step_flat.shape[0] % 16
+    first_block = jnp.concatenate(
+        [
+            jnp.concatenate(
+                [
+                    quarter(inproj[1], 1, QUARTER),
+                    lax.dynamic_slice_in_dim(statproj, core * STATE, STATE, 1),
+                ],
+                axis=1,
+            ),
+            step_flat,
+            jnp.zeros((pad_rows, 512), BF),
+        ],
+        axis=0,
+    )
+    first_all = lax.all_gather(first_block, "dp", axis=0)
+    second_block = jnp.concatenate(
+        [quarter(inproj[0], 1, QUARTER), quarter(outproj, 0, QUARTER).T], axis=1
+    )
+    second_all = lax.all_gather(second_block, "dp", axis=0, tiled=True)
+
+    def whole_rows(array):
+        mine = lax.dynamic_index_in_dim(array, core, 1, keepdims=False)
+        theirs = lax.dynamic_index_in_dim(array, 1 - core, 1, keepdims=False)
+        got = swap_cores(theirs)
+        return by_core(
+            jnp.concatenate([mine, got], axis=2), jnp.concatenate([got, mine], axis=2)
+        )
+
+    rows_whole = whole_rows(inputs)
+    normed_own = rms_scale(rows_whole.astype(F32), prenorm).astype(BF)
+    normed = [gather_tokens(normed_own[m]) for m in range(MB)]
+    cot_own = whole_rows(cotangent)
+    cots = [gather_tokens(cot_own[m]) for m in range(MB)]
+
+    w_first = first_all[:, :rows_local].reshape(D, 512)
+    state_got = swap_cores(w_first[:, QUARTER:])
+    w_state = by_core(
+        jnp.concatenate([w_first[:, QUARTER:], state_got], axis=1),
+        jnp.concatenate([state_got, w_first[:, QUARTER:]], axis=1),
+    )
+    w_inner = w_first[:, :QUARTER]
+    w_mixed = jnp.concatenate([w_inner, w_state], axis=1)
+    w_step_all = first_all[:, rows_local : rows_local + step_flat.shape[0]].reshape(D, heads_local)
+    w_step = jnp.pad(quarter(w_step_all, 1, QHEADS), ((0, 0), (0, 128 - QHEADS)))
+    w_gate = second_all[:, :QUARTER]
+    w_out = second_all[:, QUARTER:]
+
+    seg_mine = jnp.concatenate(
+        [
+            lax.dynamic_index_in_dim(segments, core, 1),
+            lax.dynamic_index_in_dim(segments, 1 - core, 1),
+        ],
+        axis=1,
+    )
+    length = segments.shape[2]
+    seg_pad = jnp.pad(seg_mine, ((0, 0), (0, 0), (8, 8)), constant_values=-1)
+
+    def seen(offset):
+        return lax.slice_in_dim(seg_pad, 8 + offset, 8 + offset + length, axis=2)
+
+    blocked = seg_mine.reshape(MB, 2, BLOCKS, SPAN)
+    before = jnp.concatenate(
+        [jnp.full((MB, 2, 1), -1, jnp.int32), blocked[:, :, :-1, -1]], axis=2
+    )[..., None]
+    flags = [(seen(j - (CONV - 1)) == seg_mine).reshape(blocked.shape) for j in range(CONV)]
+    flags.append(blocked == before)
+    flags.append(blocked == blocked[..., -1:])
+    flags.append(blocked)
+    flags.append(jnp.zeros_like(blocked))
+    for j in range(CONV):
+        flags.append((seen(CONV - 1 - j) == seg_mine).reshape(blocked.shape))
+    cols = jnp.stack([flag.astype(F32) for flag in flags], axis=-1)
+    cols = jnp.pad(cols, ((0, 0),) * 4 + ((0, 128 - len(flags)),))
+    segr = jnp.broadcast_to(
+        blocked.astype(F32)[:, :, :, None, :], (MB, 2, BLOCKS, 8, SPAN)
+    )
+
+    taps_inner = quarter(convinner, 1, QUARTER)
+    taps = jnp.pad(jnp.concatenate([taps_inner, convstate], axis=1), ((0, 3), (0, 0)))
+    head_own = quarter(headparam, 1, QHEADS)
+    head = jnp.pad(
+        jnp.stack([head_own[0], jnp.exp(head_own[1]), head_own[2]]),
+        ((0, 5), (0, 128 - QHEADS)),
+    )
+    gain = quarter(gatenorm, 0, QUARTER)
+    chan = jnp.pad(jnp.stack([gain, jnp.repeat(head_own[2], HEADDIM)]), ((0, 6), (0, 0)))
+
+    def rows_dot(left, right):
+        return lax.dot_general(left, right, (((3,), (0,)), ((), ())), preferred_element_type=F32)
+
+    def rows_dot_t(left, right):
+        return lax.dot_general(left, right, (((3,), (1,)), ((), ())), preferred_element_type=F32)
+
+    def over_tokens(left, right):
+        return lax.dot_general(
+            left, right, (((0, 1, 2), (0, 1, 2)), ((), ())), preferred_element_type=F32
+        )
+
+    def half_rows(matrix, at):
+        return lax.dynamic_slice_in_dim(matrix, at * half_d, half_d, 0)
+
+    def to_owner(mine, theirs):
+        got = swap_cores(theirs)
+        total = [add_low(mine[:, s], got[::-1, s]).reshape(2 * SPAN, -1) for s in range(BLOCKS)]
+        return scatter_plane(total).reshape(2, SPAN, -1)
+
+    kept = []
+    for m in range(MB):
+        mixed = rows_dot(normed[m], w_mixed).astype(BF)
+        raw = rows_dot(normed[m], w_step)
+        gate = rows_dot(normed[m], w_gate)
+        pre, y, hin, gun, sq = run_fwd(
+            place, mixed, gate, raw, cols[m], segr[m], taps, head, chan
+        )
+        kept.append((mixed, raw, gate, pre, y, hin, gun, sq))
+
+    layer_out = []
+    g_out = None
+    g_gate = None
+    g_late = None
+    g_gain = 0.0
+    smalls = None
+    d_tokens = []
+    state_parts = []
+    for m in range(MB):
+        mixed, raw, gate, pre, y, hin, gun, sq = kept[m]
+        d_gated = rows_dot(cots[m], w_out)
+        cross = jnp.sum(d_gated * gun.astype(F32), axis=-1)
+        sums = sum_plane_slots(jnp.stack([sq[..., 0], cross]))
+        scale = lax.rsqrt(sums[0] / INNER + EPS)[..., None]
+        pull = (sums[1] / INNER)[..., None] * scale * scale * scale
+        mine = rows_dot_t(gun, half_rows(w_out, core)).astype(BF)
+        theirs = rows_dot_t(gun, half_rows(w_out, 1 - core)).astype(BF)
+        branch = to_owner(mine, theirs) * scale[:, 0]
+        layer_out.append(branch)
+        sigma = jax.nn.sigmoid(gate)
+        gate_act = gate * sigma
+        gated_in = y * gate_act
+        d_in = d_gated * gain * scale - gated_in * pull
+        dy = (d_in * gate_act).astype(BF)
+        d_gate = (d_in * y * sigma * (1.0 + gate * (1.0 - sigma))).astype(BF)
+        g_gain = g_gain + jnp.sum(d_gated * gated_in * scale, axis=(0, 1, 2))
+        gated = (gun.astype(F32) * scale).astype(BF)
+        g_out = add_tree(g_out, over_tokens(cots[m], gated))
+        g_gate = add_tree(g_gate, over_tokens(normed[m], d_gate))
+        d_late, d_bc, slope, g_taps, g_head = run_bwd(
+            place, mixed, pre, raw, y, hin, dy, cols[m], segr[m], taps, head, chan
+        )
+        g_late = add_tree(g_late, over_tokens(normed[m], d_late))
+        smalls = add_tree(smalls, (g_taps, g_head))
+        w_late = jnp.concatenate([w_inner, w_step], axis=1)
+
+        def back(at):
+            total = rows_dot_t(d_gate, half_rows(w_gate, at))
+            return (total + rows_dot_t(d_late, half_rows(w_late, at))).astype(BF)
+
+        d_tokens.append(to_owner(back(core), back(1 - core)))
+        keep = by_core(d_bc[..., :STATE], d_bc[..., STATE:])
+        give = by_core(d_bc[..., STATE:], d_bc[..., :STATE])
+        total = add_low(keep, swap_cores(give)[::-1])
+        d_conv = (
+            total[:, 0].astype(F32)
+            + over_x(total[:, 1]).astype(F32)
+            + over_y(total[:, 2]).astype(F32)
+            + over_d(total[:, 3]).astype(F32)
+        )
+        d_pre = d_conv * by_core(slope[:, 0, :, :STATE], slope[:, 0, :, STATE:])
+        state_parts.append((d_pre, by_core(
+            mixed[:, 0, :, QUARTER : QUARTER + STATE], mixed[:, 0, :, QUARTER + STATE :]
+        )))
+
+    d_pre = jnp.concatenate([part[0] for part in state_parts], axis=0)
+    mixed_state = jnp.concatenate([part[1] for part in state_parts], axis=0).astype(F32)
+    cols_own = lax.dynamic_index_in_dim(cols, chip, 2, keepdims=False).reshape(
+        2 * MB, SPAN, 128
+    )
+    taps_state = lax.dynamic_slice_in_dim(convstate, core * STATE, STATE, 1)
+    d_mixed_state = 0.0
+    g_state_taps = []
+    for j in range(CONV):
+        ahead = CONV - 1 - j
+        window = d_pre[:, ahead : ahead + SPAN] * cols_own[:, :, 8 + j : 9 + j]
+        d_mixed_state = d_mixed_state + taps_state[j] * window
+        g_state_taps.append(jnp.sum(mixed_state * window, axis=(0, 1)))
+    g_state_taps.append(jnp.sum(d_pre[:, :SPAN], axis=(0, 1)))
+    g_state_taps = jnp.stack(g_state_taps)
+    d_mixed_state = d_mixed_state.astype(BF)
+    normed_block = jnp.concatenate([block[:, 0] for block in normed], axis=0)
+    g_state = lax.dot_general(
+        normed_block, d_mixed_state, (((0, 1), (0, 1)), ((), ())), preferred_element_type=F32
+    )
+    state_other = swap_cores(d_mixed_state.reshape(MB, 2, SPAN, STATE)[:, ::-1])
+    state_mine = d_mixed_state.reshape(MB, 2, SPAN, STATE)
+    d_state_both = by_core(
+        jnp.concatenate([state_mine, state_other], axis=3),
+        jnp.concatenate([state_other, state_mine], axis=3),
+    )
+    from_state = rows_dot_t(d_state_both, half_rows(w_state, core))
+
+    def in_order(block):
+        return by_core(block, block[:, ::-1])
+
+    layer_out = in_order(jnp.stack(layer_out))
+    outputs = (inputs.astype(F32) + layer_out).astype(BF)
+    d_normed = in_order(jnp.stack(d_tokens) + from_state)
+    rows_own = inputs.astype(F32)
+    gain_own = lax.dynamic_slice_in_dim(prenorm, core * half_d, half_d, 0)
+    weighted = d_normed * gain_own
+    pair_sums = jnp.stack(
+        [jnp.sum(rows_own * rows_own, axis=-1), jnp.sum(weighted * rows_own, axis=-1)]
+    )
+    pair_sums = pair_sums + swap_cores(pair_sums)
+    root = lax.rsqrt(pair_sums[0] / D + EPS)[..., None]
+    input_grads = (
+        cotangent.astype(F32)
+        + weighted * root
+        - rows_own * root * root * root * (pair_sums[1] / D)[..., None]
+    ).astype(BF)
+
+    def over_dp(grad):
+        return lax.psum_scatter(grad.astype(BF), "dp", scatter_dimension=0, tiled=True)
+
+    g_mid = over_dp(jnp.concatenate([g_out, g_gate], axis=1))
+    g_end = over_dp(jnp.concatenate([g_late, g_state], axis=1))
+    columns = jnp.concatenate([g_mid, g_end], axis=1).reshape(BLOCKS, shard, -1)
+
+    def for_slot(s):
+        return lax.dynamic_index_in_dim(columns, chip ^ s, 0, keepdims=False)
+
+    got = [for_slot(0), over_x(for_slot(1)), over_y(for_slot(2)), over_d(for_slot(3))]
+
+    def spread(first, width, total):
+        base = jnp.zeros((shard, total), F32)
+        for s in range(BLOCKS):
+            base = lax.dynamic_update_slice_in_dim(
+                base, got[s][:, first : first + width].astype(F32), (chip ^ s) * width, 1
+            )
+        return base
+
+    inner_local = BLOCKS * QUARTER
+    share_out = spread(0, QUARTER, inner_local).T
+    share_in = jnp.stack(
+        [spread(QUARTER, QUARTER, inner_local), spread(2 * QUARTER, QUARTER, inner_local)]
+    )
+    share_step = spread(3 * QUARTER, QHEADS, heads_local)
+    at_state = 3 * QUARTER + 128
+    share_state = sum(part[:, at_state : at_state + STATE].astype(F32) for part in got)
+
+    row_start = chip * shard
+    inproj_own = lax.dynamic_slice_in_dim(inproj, row_start, shard, 1)
+    outproj_own = lax.dynamic_slice_in_dim(outproj, row_start, shard, 1)
+    statproj_own = lax.dynamic_slice_in_dim(
+        lax.dynamic_slice_in_dim(statproj, row_start, shard, 0), core * STATE, STATE, 1
+    )
+    stepproj_own = lax.dynamic_slice_in_dim(stepproj, row_start, shard, 0)
+    gain_part = (
+        jnp.sum(inproj_own.astype(F32) * share_in, axis=(0, 2))
+        + jnp.sum(statproj_own.astype(F32) * share_state, axis=1)
+        + jnp.sum(stepproj_own.astype(F32) * share_step, axis=1)
+    )
+    gain_part = gain_part + swap_cores(gain_part)
+    gain_at = data_at * rows_local + row_start
+    g_prenorm = gain_part / lax.dynamic_slice_in_dim(prenorm, gain_at, shard, 0)
+
+    g_taps, g_head = smalls
+
+    def put(values, width, total):
+        base = jnp.zeros(values.shape[:-1] + (total,), F32)
+        return lax.dynamic_update_slice_in_dim(base, values, chip * width, values.ndim - 1)
+
+    small_parts = [
+        put(g_taps[: CONV + 1], QUARTER, inner_local),
+        put(g_gain, QUARTER, inner_local),
+        put(g_head[:3, :QHEADS], QHEADS, heads_local),
+        g_state_taps,
+    ]
+    sizes = [part.size for part in small_parts]
+    vector = jnp.concatenate([part.reshape(-1) for part in small_parts])
+    vector = jnp.pad(vector, (0, -vector.size % 1024)).reshape(-1, 128)
+
+    def sum_all(value):
+        value = value + over_x(value)
+        value = value + over_y(value)
+        hop = 1
+        while hop < dp_count:
+            value = value + lax.ppermute(value, "dp", [(i, i ^ hop) for i in range(dp_count)])
+            hop *= 2
+        return value
+
+    vector = sum_all(vector).reshape(-1)
+    small_sums = []
+    start = 0
+    for part, size in zip(small_parts, sizes):
+        small_sums.append(vector[start : start + size].reshape(part.shape))
+        start += size
+    s_taps, s_gain, s_head, s_state_taps = small_sums
+
+    big = (share_in, share_out, share_state, share_step)
+    owner_sq = sum(jnp.sum(term * term) for term in big)
+    small_sq = sum(jnp.sum(term * term) for term in small_sums)
+    first_owner = jnp.where((data_at == 0) & (chip == 0), 1.0, 0.0)
+    local_sq = owner_sq + first_owner * small_sq
+    local_sq = local_sq + swap_cores(local_sq) + jnp.sum(g_prenorm * g_prenorm)
+    last = jnp.zeros((D + 128,), F32)
+    last = lax.dynamic_update_slice_in_dim(last, g_prenorm, gain_at, 0)
+    last = last.at[D].set(local_sq)
+    last = sum_all(last)
+    grad_norm = jnp.sqrt(last[D])
+    s_prenorm = lax.dynamic_slice_in_dim(last, core * half_d, half_d, 0)
+
+    entries = (
+        2 * D * INNER
+        + 2 * D * STATE
+        + D * (INNER // HEADDIM)
+        + INNER * D
+        + (CONV + 1) * (INNER + 2 * STATE)
+        + 3 * (INNER // HEADDIM)
+        + INNER
+        + D
+    )
+    limit = CLIP_RMS * math.sqrt(entries)
+    factor = limit / jnp.maximum(grad_norm, limit)
+
+    def moved(moment, grad):
+        return 0.5 * moment + 0.5 * factor * grad
+
+    def stepped(weight, moment):
+        return (weight.astype(F32) - LEARN * moment).astype(weight.dtype)
+
+    new_prenorm = moved(prenorm_moment, s_prenorm)
+    new_in = moved(inproj_moment, share_in)
+    new_state = moved(statproj_moment, share_state)
+    new_step = moved(stepproj_moment, share_step)
+    new_out = moved(outproj_moment, share_out)
+    new_taps = moved(convinner_moment, s_taps)
+    new_state_taps = moved(convstate_moment, s_state_taps)
+    new_head = moved(headparam_moment, s_head)
+    new_gain = moved(gatenorm_moment, s_gain)
+    return (
+        outputs,
+        input_grads,
+        grad_norm,
+        new_prenorm,
+        new_in,
+        new_state,
+        new_step,
+        new_out,
+        new_taps,
+        new_state_taps,
+        new_head,
+        new_gain,
+        stepped(inproj_own, new_in),
+        stepped(statproj_own, new_state),
+        stepped(stepproj_own, new_step),
+        stepped(outproj_own, new_out),
+        stepped(convinner, new_taps),
+        stepped(lax.dynamic_slice_in_dim(convstate, core * STATE, STATE, 1), new_state_taps),
+    )
+
+
 def solution(mesh):
+    fast = mesh.shape["seq"] == BLOCKS and mesh.shape["tensor"] == 2
     return jax.shard_map(
-        body,
+        fast_body if fast else general_body,
         mesh=mesh,
         in_specs=(
             P(None, "dp", "seq", "tensor"),

time: 1610 us -> 792 us (0.49)
  waiting for transfers between devices: 801 us -> 177 us
  blocking collectives: 192 us -> 0 us
  matrix products: 313 us -> 157 us
  Pallas kernels: 0 us -> 126 us
  other arithmetic: 195 us -> 80 us
  local copies, waits for them, and re-layouts: 61.5 us -> 138 us
  starting transfers between devices: 11.5 us -> 79.7 us
    reduce_scatter x5 -> x2, waiting for transfers between devices: 498 us -> 0.04 us  [over_dp(): lax.psum_scatter(grad.astype(BF), 'dp', scatter_dimension=0, tiled=True)]
    all_gather x8 -> x2, waiting for transfers between devices: 254 us -> 0.01 us  [the longest x1 0.01 us: fast_body(): first_all = lax.all_gather(first_block, 'dp', axis=0)]
    ppermute x4 -> x96, waiting for transfers between devices: 5.2 us -> 177 us  [the longest x27 108 us: over_x(): return lax.ppermute(block, 'seq', ROUTE_X)]
    dot_general x54 -> x28, matrix products: 313 us -> 157 us  [the longest x13 59.1 us: rows_dot_t(): lax.dot_general(left, right, (((3,), (1,)), ((), ())), preferred_element_...]
    pallas_call x0 -> x4, Pallas kernels: none -> 126 us  [the longest x2 83.8 us: run_bwd(): pl.pallas_call(bwd_kernel, grid_spec=pltpu.PrefetchScalarGridSpec(num_sca...]
    psum x4 -> x0, blocking collectives: 124 us -> none  [the longest x1 79.8 us: body(): lax.psum((small_terms[0], small_terms[1], small_terms[2], small_terms[3],...]
    ppermute x4 -> x96, starting transfers between devices: 9.88 us -> 79.5 us  [the longest x27 30 us: over_x(): return lax.ppermute(block, 'seq', ROUTE_X)]
    all_gather x6 -> x0, blocking collectives: 68.1 us -> none  [the longest x1 21.8 us: body(): lax.all_gather(statproj, 'dp', axis=0, tiled=True)]
  transfers between devices with their start and end apart: 20 -> 100, of which waited for: 12 -> 36; matrix products, arithmetic and copies ran while one was open for 27% -> 41% of each run, Pallas kernels for 0% -> 13%
where the time goes in v1:
time: 792 us; the launch traced here: 781 us
  waiting for transfers between devices  177 us (22%)
  matrix products  157 us (20%)
  local copies, waits for them, and re-layouts  138 us (17%)
  Pallas kernels  126 us (16%)
  other arithmetic  80 us (10%)
  starting transfers between devices  79.7 us (10%)
  between operations  24.7 us (3%)
    ppermute x27, waiting for transfers between devices, over_x(): return lax.ppermute(block, 'seq', ROUTE_X)  108 us
    pallas_call x2, Pallas kernels, run_bwd(): pl.pallas_call(bwd_kernel, grid_spec=pltpu.PrefetchScalarGridSpec(num_sca...  83.8 us
    dot_general x13, matrix products, rows_dot_t(): lax.dot_general(left, right, (((3,), (1,)), ((), ())), preferred_element_...  59.1 us
    dot_general x8, matrix products, rows_dot(): lax.dot_general(left, right, (((3,), (0,)), ((), ())), preferred_element_...  58.5 us
    ppermute x27, waiting for transfers between devices, over_y(): return lax.ppermute(block, 'seq', ROUTE_Y)  54.8 us
    unnamed x216, local copies, waits for them, and re-layouts  42.6 us
    pallas_call x2, Pallas kernels, run_fwd(): pl.pallas_call(fwd_kernel, grid_spec=pltpu.PrefetchScalarGridSpec(num_sca...  42.5 us
    dot_general x6, matrix products, over_tokens(): lax.dot_general(left, right, (((0, 1, 2), (0, 1, 2)), ((), ())), preferre...  38.5 us
  transfers between devices with their start and end apart: 100, of which 36 were waited for; matrix products, arithmetic and copies ran while one was open for 41% of the time, Pallas kernels for 13%

profile of v1, /device:TPU:0, one launch (start us, length us, event | category | flops | bytes accessed | tf_op | source)
XLA Modules:
  0.0 781.4 jit_solution(10286540802196806459)
XLA Ops:
  54.5 16.5 %stack.114 = f32[2,2,4,256,12]{4,3,2,1,0:T(8,128)S(1)} concatenate(f32[2,2,4,256,1]{4,3,2,1,0:T(8,128)} %reshape.772, f32[2,2,4,256,1]{4,3,2,1,0:T(8,128)} %reshape.773, f32[2,2,4,256,1]{4,3,2,1,0:T(8,128)} %reshape.774, f32[2,2,4,256,1]{4,3,2,1,0:T(8,128)} %reshape.702, f32[2,2,4,256,1]{4,3,2,1,0:T(8,128)} %copy.263, f32[2,2,4,256,1]{4,3,2,1,0:T(8,128)} %copy.264, ...), dimensions={4} | concatenate | bytes 393216 | tf_op jit(solution)/shard_map/stack | solution.py:935
  89.0 11.9 %collective-permute-done.19 = bf16[256,1536]{1,0:T(8,128)(2,1)S(1)} collective-permute-done((bf16[256,1536]{1,0:T(8,128)(2,1)S(1)}, bf16[256,1536]{1,0:T(8,128)(2,1)S(1)}, u32[]{:S(2)}, u32[]{:S(2)}) %collective-permute-start.19) | collective-permute-done | bytes 786464 | tf_op jit(solution)/shard_map/ppermute | solution.py:770
  103.2 14.7 %collective-permute-done.47 = bf16[256,1536]{1,0:T(8,128)(2,1)S(1)} collective-permute-done((bf16[256,1536]{1,0:T(8,128)(2,1)S(1)}, bf16[256,1536]{1,0:T(8,128)(2,1)S(1)}, u32[]{:S(2)}, u32[]{:S(2)}) %collective-permute-start.47) | collective-permute-done | bytes 786464 | tf_op jit(solution)/shard_map/ppermute | solution.py:770
  121.9 12.8 %collective-permute-done.1 = bf16[256,1536]{1,0:T(8,128)(2,1)S(1)} collective-permute-done((bf16[256,1536]{1,0:T(8,128)(2,1)S(1)}, bf16[256,1536]{1,0:T(8,128)(2,1)S(1)}, u32[]{:S(2)}, u32[]{:S(2)}) %collective-permute-start.1) | collective-permute-done | bytes 786464 | tf_op jit(solution)/shard_map/ppermute | solution.py:770
  137.1 13.2 %collective-permute-done.31 = bf16[256,1536]{1,0:T(8,128)(2,1)S(1)} collective-permute-done((bf16[256,1536]{1,0:T(8,128)(2,1)S(1)}, bf16[256,1536]{1,0:T(8,128)(2,1)S(1)}, u32[]{:S(2)}, u32[]{:S(2)}) %collective-permute-start.31) | collective-permute-done | bytes 786464 | tf_op jit(solution)/shard_map/ppermute | solution.py:770
  154.4 5.9 collective-permute-done.21
  162.4 6.8 collective-permute-done.49
  172.1 6.4 collective-permute-done.50
  234.0 7.4 fusion.36
  243.3 7.1 convolution_convert_fusion.4.mixed_ref
  252.6 8.2 %fusion.51.gate_ref = f32[2,4,256,384]{3,2,1,0:T(8,128)} fusion(bf16[2,4,256,1536]{3,2,1,0:T(8,128)(2,1)} %bitcast.45, bf16[1536,768]{1,0:T(8,128)(2,1)} %all-gather.4.cloned.1.call-done), kind=kOutput, calls=%fused_computation.119 | convolution fusion | flops 2415919104 | bytes 10616832 | tf_op jit(solution)/shard_map/dot_general | solution.py:952
  261.4 21.3 %mix_forward.3 = (f32[2,4,256,640]{3,2,1,0:T(8,128)}, f32[2,4,256,384]{3,2,1,0:T(8,128)}, bf16[2,4,384,128]{3,2,1,0:T(8,128)(2,1)}, bf16[2,4,256,384]{3,2,1,0:T(8,128)(2,1)}, f32[2,4,256,1]{3,2,1,0:T(8,128)}) custom-call(s32[1]{0:T(128)} %bitcast.place_ref, bf16[2,4,256,640]{3,2,1,0:T(8,128)(2,1)} %copy-done.7, f32[2,4,256,384]{3,2,1,0:T(8,128)} %fusion.51.gate_ref, ...), custom_call_target="tpu_custom_call" | custom-call | tf_op jit(solution)/shard_map/mix_forward/pallas_call | solution.py:672
  293.1 8.8 %fusion.8 = (f32[2,4,256]{2,1,0:T(4,128)S(1)}, f32[2,4,256,384]{3,2,1,0:T(8,128)}) fusion(bf16[2,4,256,384]{3,2,1,0:T(8,128)(2,1)} %get-tuple-element.52, bf16[2,4,256,1536]{3,2,1,0:T(8,128)(2,1)} %bitcast.62, bf16[1536,768]{1,0:T(8,128)(2,1)} %all-gather.4.cloned.1.call-done), kind=kOutput, calls=%fused_computation.26 | convolution fusion | flops 2418276352 | bytes 12197888 | tf_op jit(solution)/shard_map/dot_general | solution.py:952
  302.2 7.9 %fusion.53.gate_ref = f32[2,4,256,384]{3,2,1,0:T(8,128)} fusion(bf16[2,4,256,1536]{3,2,1,0:T(8,128)(2,1)} %bitcast.4, bf16[1536,768]{1,0:T(8,128)(2,1)S(1)} %copy-done.22), kind=kOutput, calls=%fused_computation.121 | convolution fusion | flops 2415919104 | bytes 10616832 | tf_op jit(solution)/shard_map/dot_general | solution.py:952
  310.8 21.2 %mix_forward.2 = (f32[2,4,256,640]{3,2,1,0:T(8,128)}, f32[2,4,256,384]{3,2,1,0:T(8,128)}, bf16[2,4,384,128]{3,2,1,0:T(8,128)(2,1)}, bf16[2,4,256,384]{3,2,1,0:T(8,128)(2,1)}, f32[2,4,256,1]{3,2,1,0:T(8,128)}) custom-call(s32[1]{0:T(128)} %bitcast.place_ref, bf16[2,4,256,640]{3,2,1,0:T(8,128)(2,1)} %copy.269.mixed_ref, f32[2,4,256,384]{3,2,1,0:T(8,128)} %fusion.53.gate_ref, ...), custom_call_target="tpu_custom_call" | custom-call | tf_op jit(solution)/shard_map/mix_forward/pallas_call | solution.py:672
  338.7 7.9 %fusion.6 = (f32[2,4,256]{2,1,0:T(4,128)S(1)}, f32[2,4,256,384]{3,2,1,0:T(8,128)}) fusion(bf16[2,4,256,384]{3,2,1,0:T(8,128)(2,1)S(1)} %copy-done.79, bf16[2,4,256,1536]{3,2,1,0:T(8,128)(2,1)} %bitcast.488, bf16[1536,768]{1,0:T(8,128)(2,1)S(1)} %copy-done.23), kind=kOutput, calls=%fused_computation.24 | convolution fusion | flops 2418276352 | bytes 12197888 | tf_op jit(solution)/shard_map/dot_general | solution.py:952
  358.6 7.4 convolution_bitcast_fusion.4
  366.2 10.6 %multiply_convert_fusion.3 = (bf16[2,4,256,384]{3,2,1,0:T(8,128)(2,1)S(1)}, bf16[2,4,256,384]{3,2,1,0:T(8,128)(2,1)}, f32[384]{0:T(512)}, f32[384]{0:T(512)}, bf...) fusion(f32[2,4,256,384]{3,2,1,0:T(8,128)} %fusion.53.gate_ref, ...), kind=kLoop, calls=%fused_computation.51 | loop fusion | flops 33029376 | bytes 25203200 | tf_op jit(solution)/shard_map/convert_element_type | solution.py:1004
  376.8 41.9 %mix_backward.2 = (bf16[2,4,256,512]{3,2,1,0:T(8,128)(2,1)}, bf16[2,4,272,256]{3,2,1,0:T(8,128)(2,1)}, f32[2,4,272,256]{3,2,1,0:T(8,128)}, f32[8,384]{1,0:T(8,128)}, f32[8,128]{1,0:T(8,128)}) custom-call(s32[1]{0:T(128)} %bitcast.place_ref, bf16[2,4,256,640]{3,2,1,0:T(8,128)(2,1)} %copy.269.mixed_ref, f32[2,4,256,640]{3,2,1,0:T(8,128)} %get-tuple-element.55.pre_ref, ...), custom_call_target="tpu_custom_call" | custom-call | tf_op jit(solution)/shard_map/mix_backward/pallas_call | solution.py:721
  418.7 6.3 fusion.132
  429.6 41.9 %mix_backward.3 = (bf16[2,4,256,512]{3,2,1,0:T(8,128)(2,1)}, bf16[2,4,272,256]{3,2,1,0:T(8,128)(2,1)}, f32[2,4,272,256]{3,2,1,0:T(8,128)}, f32[8,384]{1,0:T(8,128)}, f32[8,128]{1,0:T(8,128)}) custom-call(s32[1]{0:T(128)} %bitcast.place_ref, bf16[2,4,256,640]{3,2,1,0:T(8,128)(2,1)} %copy-done.7, f32[2,4,256,640]{3,2,1,0:T(8,128)} %get-tuple-element.59.pre_ref, ...), custom_call_target="tpu_custom_call" | custom-call | tf_op jit(solution)/shard_map/mix_backward/pallas_call | solution.py:721
  478.4 6.3 convolution_bitcast_fusion
  484.7 6.5 fusion.25
  491.3 6.7 fusion.28
  538.8 6.2 fusion.126
  545.1 6.7 fusion.29
  552.3 6.3 add_convert_fusion
  560.6 6.4 add_convert_fusion.1
  606.4 6.8 collective-permute-done.42
  660.0 7.3 collective-permute-done.14
  668.8 5.9 collective-permute-done.16
  678.0 6.2 collective-permute-done.62
  (670 shorter events, 399.3 us)
Async XLA Ops:
  7.2 211.4 %all-gather.6.cloned.1.call-start = ((), (), s32[]{:S(2)}) async-start(), calls=%async_computation.3 | async-start | bytes 2129920 | tf_op jit(solution)/shard_map/all_gather | solution.py:878
  12.3 240.3 %all-gather.4.cloned.1.call-start = ((), (), s32[]{:S(2)}) async-start(), calls=%async_computation.2 | async-start | bytes 2949120 | tf_op jit(solution)/shard_map/all_gather | solution.py:882
  15.0 60.6 %collective-permute-start.18 = (bf16[2,256,768]{2,1,0:T(8,128)(2,1)}, bf16[2,256,768]{2,1,0:T(8,128)(2,1)}, u32[]{:S(2)}, u32[]{:S(2)}) collective-permute-start(bf16[2,256,768]{2,1,0:T(8,128)(2,1)} %get-tuple-element.173), channel_id=1, source_target_pairs={{0,1},{1,0},{2,3},{3,2},{4,5},{5,4},{6,7},{7,6},{8,9},{9,8},{10,11... | collective-permute-start | bytes 2359304 | tf_op jit(solution)/shard_map/ppermute | solution.py:766
  16.4 67.2 %collective-permute-start = (bf16[2,256,768]{2,1,0:T(8,128)(2,1)}, bf16[2,256,768]{2,1,0:T(8,128)(2,1)}, u32[]{:S(2)}, u32[]{:S(2)}) collective-permute-start(bf16[2,256,768]{2,1,0:T(8,128)(2,1)} %get-tuple-element.174), channel_id=1, source_target_pairs={{0,1},{1,0},{2,3},{3,2},{4,5},{5,4},{6,7},{7,6},{8,9},{9,8},{10,11... | collective-permute-start | bytes 2359304 | tf_op jit(solution)/shard_map/ppermute | solution.py:766
  18.6 683.4 %reduce-scatter.9.cloned.1.call-start = ((), (), s32[]{:S(2)}) async-start(), calls=%async_computation.5 | async-start | bytes 2457600 | tf_op jit(solution)/shard_map/reduce_scatter | solution.py:1084
  77.5 25.0 %collective-permute-start.20 = (bf16[256,1536]{1,0:T(8,128)(2,1)S(1)}, bf16[256,1536]{1,0:T(8,128)(2,1)S(1)}, u32[]{:S(2)}, u32[]{:S(2)}) collective-permute-start(bf16[256,1536]{1,0:T(8,128)(2,1)S(1)} %get-tuple-element.164), channel_id=1, source_target_pairs={{0,4},{2,6},{4,0},{6,2},{1,5},{3,7},{5,1},{7,3},{8,12},{10,14},{12... | collective-permute-start | bytes 2359304 | tf_op jit(solution)/shard_map/ppermute | solution.py:774
  80.5 20.4 %collective-permute-start.19 = (bf16[256,1536]{1,0:T(8,128)(2,1)S(1)}, bf16[256,1536]{1,0:T(8,128)(2,1)S(1)}, u32[]{:S(2)}, u32[]{:S(2)}) collective-permute-start(bf16[256,1536]{1,0:T(8,128)(2,1)S(1)} %get-tuple-element.164), channel_id=1, source_target_pairs={{0,2},{2,0},{4,6},{6,4},{1,3},{3,1},{5,7},{7,5},{8,10},{10,8},{12,... | collective-permute-start | bytes 2359304 | tf_op jit(solution)/shard_map/ppermute | solution.py:770
  82.0 38.2 %collective-permute-start.48 = (bf16[256,1536]{1,0:T(8,128)(2,1)S(1)}, bf16[256,1536]{1,0:T(8,128)(2,1)S(1)}, u32[]{:S(2)}, u32[]{:S(2)}) collective-permute-start(bf16[256,1536]{1,0:T(8,128)(2,1)S(1)} %get-tuple-element.165), channel_id=1, source_target_pairs={{0,4},{2,6},{4,0},{6,2},{1,5},{3,7},{5,1},{7,3},{8,12},{10,14},{12... | collective-permute-start | bytes 2359304 | tf_op jit(solution)/shard_map/ppermute | solution.py:774
  82.5 35.3 %collective-permute-start.47 = (bf16[256,1536]{1,0:T(8,128)(2,1)S(1)}, bf16[256,1536]{1,0:T(8,128)(2,1)S(1)}, u32[]{:S(2)}, u32[]{:S(2)}) collective-permute-start(bf16[256,1536]{1,0:T(8,128)(2,1)S(1)} %get-tuple-element.165), channel_id=1, source_target_pairs={{0,2},{2,0},{4,6},{6,4},{1,3},{3,1},{5,7},{7,5},{8,10},{10,8},{12,... | collective-permute-start | bytes 2359304 | tf_op jit(solution)/shard_map/ppermute | solution.py:770
  89.0 106.0 %collective-permute-start.5 = (bf16[256,1536]{1,0:T(8,128)(2,1)S(1)}, bf16[256,1536]{1,0:T(8,128)(2,1)S(1)}, u32[]{:S(2)}, u32[]{:S(2)}) collective-permute-start(bf16[256,1536]{1,0:T(8,128)(2,1)S(1)} %get-tuple-element.168), channel_id=1, source_target_pairs={{0,1},{1,0},{2,3},{3,2},{4,5},{5,4},{6,7},{7,6},{8,9},{9,8},{10,11... | collective-permute-start | bytes 2359304 | tf_op jit(solution)/shard_map/ppermute | solution.py:766
  101.0 33.7 %collective-permute-start.1 = (bf16[256,1536]{1,0:T(8,128)(2,1)S(1)}, bf16[256,1536]{1,0:T(8,128)(2,1)S(1)}, u32[]{:S(2)}, u32[]{:S(2)}) collective-permute-start(bf16[256,1536]{1,0:T(8,128)(2,1)S(1)} %get-tuple-element.168), channel_id=1, source_target_pairs={{0,2},{2,0},{4,6},{6,4},{1,3},{3,1},{5,7},{7,5},{8,10},{10,8},{12,... | collective-permute-start | bytes 2359304 | tf_op jit(solution)/shard_map/ppermute | solution.py:770
  102.5 33.1 %collective-permute-start.2 = (bf16[256,1536]{1,0:T(8,128)(2,1)S(1)}, bf16[256,1536]{1,0:T(8,128)(2,1)S(1)}, u32[]{:S(2)}, u32[]{:S(2)}) collective-permute-start(bf16[256,1536]{1,0:T(8,128)(2,1)S(1)} %get-tuple-element.168), channel_id=1, source_target_pairs={{0,4},{2,6},{4,0},{6,2},{1,5},{3,7},{5,1},{7,3},{8,12},{10,14},{12... | collective-permute-start | bytes 2359304 | tf_op jit(solution)/shard_map/ppermute | solution.py:774
  117.8 32.5 %collective-permute-start.31 = (bf16[256,1536]{1,0:T(8,128)(2,1)S(1)}, bf16[256,1536]{1,0:T(8,128)(2,1)S(1)}, u32[]{:S(2)}, u32[]{:S(2)}) collective-permute-start(bf16[256,1536]{1,0:T(8,128)(2,1)S(1)} %get-tuple-element.169), channel_id=1, source_target_pairs={{0,2},{2,0},{4,6},{6,4},{1,3},{3,1},{5,7},{7,5},{8,10},{10,8},{12,... | collective-permute-start | bytes 2359304 | tf_op jit(solution)/shard_map/ppermute | solution.py:770
  120.2 32.5 %collective-permute-start.32 = (bf16[256,1536]{1,0:T(8,128)(2,1)S(1)}, bf16[256,1536]{1,0:T(8,128)(2,1)S(1)}, u32[]{:S(2)}, u32[]{:S(2)}) collective-permute-start(bf16[256,1536]{1,0:T(8,128)(2,1)S(1)} %get-tuple-element.169), channel_id=1, source_target_pairs={{0,4},{2,6},{4,0},{6,2},{1,5},{3,7},{5,1},{7,3},{8,12},{10,14},{12... | collective-permute-start | bytes 2359304 | tf_op jit(solution)/shard_map/ppermute | solution.py:774
  134.7 61.8 %collective-permute-start.35 = (bf16[256,1536]{1,0:T(8,128)(2,1)S(1)}, bf16[256,1536]{1,0:T(8,128)(2,1)S(1)}, u32[]{:S(2)}, u32[]{:S(2)}) collective-permute-start(bf16[256,1536]{1,0:T(8,128)(2,1)S(1)} %get-tuple-element.169), channel_id=1, source_target_pairs={{0,1},{1,0},{2,3},{3,2},{4,5},{5,4},{6,7},{7,6},{8,9},{9,8},{10,11... | collective-permute-start | bytes 2359304 | tf_op jit(solution)/shard_map/ppermute | solution.py:766
  135.6 35.5 %collective-permute-start.23 = (bf16[256,1536]{1,0:T(8,128)(2,1)S(1)}, bf16[256,1536]{1,0:T(8,128)(2,1)S(1)}, u32[]{:S(2)}, u32[]{:S(2)}) collective-permute-start(bf16[256,1536]{1,0:T(8,128)(2,1)S(1)} %get-tuple-element.164), channel_id=1, source_target_pairs={{0,1},{1,0},{2,3},{3,2},{4,5},{5,4},{6,7},{7,6},{8,9},{9,8},{10,11... | collective-permute-start | bytes 2359304 | tf_op jit(solution)/shard_map/ppermute | solution.py:766
  301.9 45.0 %collective-permute-start.56 = (f32[2,2,4,256]{3,2,1,0:T(4,128)S(1)}, f32[2,2,4,256]{3,2,1,0:T(4,128)S(1)}, u32[]{:S(2)}, u32[]{:S(2)}) collective-permute-start(f32[2,2,4,256]{3,2,1,0:T(4,128)S(1)} %pad_maximum_fusion.16), channel_id=1, source_target_pairs={{0,1},{1,0},{2,3},{3,2},{4,5},{5,4},{6,7},{7,6},{8,9},{9,8},{10,11... | collective-permute-start | bytes 49160 | tf_op jit(solution)/shard_map/ppermute | solution.py:766
  357.2 231.7 %collective-permute-start.40 = (bf16[2,4,256,768]{3,2,1,0:T(8,128)(2,1)}, bf16[2,4,256,768]{3,2,1,0:T(8,128)(2,1)}, u32[]{:S(2)}, u32[]{:S(2)}) collective-permute-start(bf16[2,4,256,768]{3,2,1,0:T(8,128)(2,1)} %convolution_convert_fusion), channel_id=1, source_target_pairs={{0,1},{1,0},{2,3},{3,2},{4,5},{5,4},{6,7},{7,6},{8,9},{9,8},{10,11... | collective-permute-start | bytes 9437192 | tf_op jit(solution)/shard_map/ppermute | solution.py:766
  357.2 238.1 %collective-permute-start.11 = (bf16[2,4,256,768]{3,2,1,0:T(8,128)(2,1)}, bf16[2,4,256,768]{3,2,1,0:T(8,128)(2,1)}, u32[]{:S(2)}, u32[]{:S(2)}) collective-permute-start(bf16[2,4,256,768]{3,2,1,0:T(8,128)(2,1)} %convolution_convert_fusion.2), channel_id=1, source_target_pairs={{0,1},{1,0},{2,3},{3,2},{4,5},{5,4},{6,7},{7,6},{8,9},{9,8},{10,11... | collective-permute-start | bytes 9437192 | tf_op jit(solution)/shard_map/ppermute | solution.py:766
  472.9 37.5 %collective-permute-start.77 = (bf16[2,4,272,128]{3,2,0,1:T(8,128)(2,1)S(1)}, bf16[2,4,272,128]{3,2,0,1:T(8,128)(2,1)S(1)}, u32[]{:S(2)}, u32[]{:S(2)}) collective-permute-start(bf16[2,4,272,128]{3,2,0,1:T(8,128)(2,1)S(1)} %broadcast_select_fusion), channel_id=1, source_target_pairs={{0,1},{1,0},{2,3},{3,2},{4,5},{5,4},{6,7},{7,6},{8,9},{9,8},{10,11... | collective-permute-start | bytes 1671176 | tf_op jit(solution)/shard_map/ppermute | solution.py:766
  473.0 40.5 %collective-permute-start.73 = (bf16[2,4,272,128]{3,2,0,1:T(8,128)(2,1)S(1)}, bf16[2,4,272,128]{3,2,0,1:T(8,128)(2,1)S(1)}, u32[]{:S(2)}, u32[]{:S(2)}) collective-permute-start(bf16[2,4,272,128]{3,2,0,1:T(8,128)(2,1)S(1)} %broadcast_select_fusion.1), channel_id=1, source_target_pairs={{0,1},{1,0},{2,3},{3,2},{4,5},{5,4},{6,7},{7,6},{8,9},{9,8},{10,11... | collective-permute-start | bytes 1671176 | tf_op jit(solution)/shard_map/ppermute | solution.py:766
  524.4 75.0 %collective-permute-start.59 = (bf16[2,4,256,768]{3,2,1,0:T(8,128)(2,1)}, bf16[2,4,256,768]{3,2,1,0:T(8,128)(2,1)}, u32[]{:S(2)}, u32[]{:S(2)}) collective-permute-start(bf16[2,4,256,768]{3,2,1,0:T(8,128)(2,1)} %add_convert_fusion.2), channel_id=1, source_target_pairs={{0,1},{1,0},{2,3},{3,2},{4,5},{5,4},{6,7},{7,6},{8,9},{9,8},{10,11... | collective-permute-start | bytes 9437192 | tf_op jit(solution)/shard_map/ppermute | solution.py:766
  538.7 163.3 %reduce-scatter.7.cloned.1.call-start = ((), (), s32[]{:S(2)}) async-start(), calls=%async_computation.4 | async-start | bytes 2949120 | tf_op jit(solution)/shard_map/reduce_scatter | solution.py:1084
  582.1 21.4 %collective-permute-start.66 = (bf16[2,4,256,768]{3,2,1,0:T(8,128)(2,1)}, bf16[2,4,256,768]{3,2,1,0:T(8,128)(2,1)S(1)}, u32[]{:S(2)}, u32[]{:S(2)}) collective-permute-start(bf16[2,4,256,768]{3,2,1,0:T(8,128)(2,1)} %add_convert_fusion), channel_id=1, source_target_pairs={{0,1},{1,0},{2,3},{3,2},{4,5},{5,4},{6,7},{7,6},{8,9},{9,8},{10,11... | collective-permute-start | bytes 9437192 | tf_op jit(solution)/shard_map/ppermute | solution.py:766
  592.7 50.6 %collective-permute-start.41 = (bf16[256,768]{1,0:T(8,128)(2,1)S(1)}, bf16[256,768]{1,0:T(8,128)(2,1)S(1)}, u32[]{:S(2)}, u32[]{:S(2)}) collective-permute-start(bf16[256,768]{1,0:T(8,128)(2,1)S(1)} %slice_bitcast_fusion.28), channel_id=1, source_target_pairs={{0,2},{2,0},{4,6},{6,4},{1,3},{3,1},{5,7},{7,5},{8,10},{10,8},{12,... | collective-permute-start | bytes 1179656 | tf_op jit(solution)/shard_map/ppermute | solution.py:770
  593.8 50.9 %collective-permute-start.46 = (bf16[256,768]{1,0:T(8,128)(2,1)S(1)}, bf16[256,768]{1,0:T(8,128)(2,1)S(1)}, u32[]{:S(2)}, u32[]{:S(2)}) collective-permute-start(bf16[256,768]{1,0:T(8,128)(2,1)S(1)} %slice_bitcast_fusion.22), channel_id=1, source_target_pairs={{0,4},{2,6},{4,0},{6,2},{1,5},{3,7},{5,1},{7,3},{8,12},{10,14},{12... | collective-permute-start | bytes 1179656 | tf_op jit(solution)/shard_map/ppermute | solution.py:774
  644.7 31.2 %collective-permute-start.60 = (bf16[256,768]{1,0:T(8,128)(2,1)S(1)}, bf16[256,768]{1,0:T(8,128)(2,1)S(1)}, u32[]{:S(2)}, u32[]{:S(2)}) collective-permute-start(bf16[256,768]{1,0:T(8,128)(2,1)S(1)} %slice_bitcast_fusion.20), channel_id=1, source_target_pairs={{0,2},{2,0},{4,6},{6,4},{1,3},{3,1},{5,7},{7,5},{8,10},{10,8},{12,... | collective-permute-start | bytes 1179656 | tf_op jit(solution)/shard_map/ppermute | solution.py:770
  652.0 22.8 %collective-permute-start.16 = (bf16[256,768]{1,0:T(8,128)(2,1)S(1)}, bf16[256,768]{1,0:T(8,128)(2,1)S(1)}, u32[]{:S(2)}, u32[]{:S(2)}) collective-permute-start(bf16[256,768]{1,0:T(8,128)(2,1)S(1)} %fusion.73), channel_id=1, source_target_pairs={{0,2},{2,0},{4,6},{6,4},{1,3},{3,1},{5,7},{7,5},{8,10},{10,8},{12,... | collective-permute-start | bytes 1179656 | tf_op jit(solution)/shard_map/ppermute | solution.py:770
  657.9 19.5 %collective-permute-start.65 = (bf16[256,768]{1,0:T(8,128)(2,1)S(1)}, bf16[256,768]{1,0:T(8,128)(2,1)S(1)}, u32[]{:S(2)}, u32[]{:S(2)}) collective-permute-start(bf16[256,768]{1,0:T(8,128)(2,1)S(1)} %slice_bitcast_fusion.14), channel_id=1, source_target_pairs={{0,4},{2,6},{4,0},{6,2},{1,5},{3,7},{5,1},{7,3},{8,12},{10,14},{12... | collective-permute-start | bytes 1179656 | tf_op jit(solution)/shard_map/ppermute | solution.py:774
  659.2 32.6 %collective-permute-start.67 = (bf16[256,768]{1,0:T(8,128)(2,1)S(1)}, bf16[256,768]{1,0:T(8,128)(2,1)S(1)}, u32[]{:S(2)}, u32[]{:S(2)}) collective-permute-start(bf16[256,768]{1,0:T(8,128)(2,1)S(1)} %slice_bitcast_fusion.12), channel_id=1, source_target_pairs={{0,2},{2,0},{4,6},{6,4},{1,3},{3,1},{5,7},{7,5},{8,10},{10,8},{12,... | collective-permute-start | bytes 1179656 | tf_op jit(solution)/shard_map/ppermute | solution.py:770
  677.3 20.8 %collective-permute-start.69 = (bf16[256,768]{1,0:T(8,128)(2,1)S(1)}, bf16[256,768]{1,0:T(8,128)(2,1)S(1)}, u32[]{:S(2)}, u32[]{:S(2)}) collective-permute-start(bf16[256,768]{1,0:T(8,128)(2,1)S(1)} %fusion.63), channel_id=1, source_target_pairs={{0,4},{2,6},{4,0},{6,2},{1,5},{3,7},{5,1},{7,3},{8,12},{10,14},{12... | collective-permute-start | bytes 1179656 | tf_op jit(solution)/shard_map/ppermute | solution.py:774
  701.9 47.8 %collective-permute-start.82 = (f32[2,2,2,256]{3,2,1,0:T(2,128)S(1)}, f32[2,2,2,256]{3,2,1,0:T(2,128)S(1)}, u32[]{:S(2)}, u32[]{:S(2)}) collective-permute-start(f32[2,2,2,256]{3,2,1,0:T(2,128)S(1)} %pad_maximum_fusion.17), channel_id=1, source_target_pairs={{0,1},{1,0},{2,3},{3,2},{4,5},{5,4},{6,7},{7,6},{8,9},{9,8},{10,11... | collective-permute-start | bytes 24584 | tf_op jit(solution)/shard_map/ppermute | solution.py:766
  (155 other events, 1290.5 us)
Sparse Core Ops, SparseCore 0:
  12.4 41.9 all-gather.5
  56.5 49.3 all-gather.3
  538.8 42.5 reduce-scatter.8
  583.5 47.2 reduce-scatter.6

commit v2 on v0

--- a/solution.py
+++ b/solution.py
@@ -3,6 +3,8 @@
 import jax
 import jax.numpy as jnp
 from jax import lax
+from jax.experimental import pallas as pl
+from jax.experimental.pallas import tpu as pltpu
 from jax.sharding import PartitionSpec as P
 
 D = 1536
@@ -140,7 +142,7 @@
     return jnp.einsum("blk,dk->bld", grad_rows, matrix, preferred_element_type=jnp.float32)
 
 
-def body(
+def general_body(
     inputs,
     segments,
     cotangent,
@@ -405,9 +407,1328 @@
     )
 
 
+BLOCKS = 4
+SPAN = 256
+PART = 128
+PARTS = SPAN // PART
+PACKED = 48
+QUARTER = 384
+QHEADS = 6
+BF = jnp.bfloat16
+F32 = jnp.float32
+ROUTE_X = [(i, i ^ 1) for i in range(BLOCKS)]
+ROUTE_Y = [(i, i ^ 2) for i in range(BLOCKS)]
+SWAP = [(0, 1), (1, 0)]
+VMEM_LIMIT = 56 * 1024 * 1024
+
+
+def dot_nn(a, b):
+    return lax.dot_general(a, b, (((1,), (0,)), ((), ())), preferred_element_type=F32)
+
+
+def dot_nt(a, b):
+    return lax.dot_general(a, b, (((1,), (1,)), ((), ())), preferred_element_type=F32)
+
+
+def dot_tn(a, b):
+    return lax.dot_general(a, b, (((0,), (0,)), ((), ())), preferred_element_type=F32)
+
+
+def dot_exact(a, b):
+    return lax.dot_general(
+        a, b, (((1,), (0,)), ((), ())), precision=HIGH, preferred_element_type=F32
+    )
+
+
+def sigmoid(v):
+    return 1.0 / (1.0 + jnp.exp(-v))
+
+
+def pair_cols(table, k, low_half):
+    return jnp.where(low_half, table[:, 2 * k : 2 * k + 1], table[:, 2 * k + 1 : 2 * k + 2])
+
+
+def split_sum(triangle, table):
+    first = table.astype(BF)
+    rest = table - first.astype(F32)
+    second = rest.astype(BF)
+    third = (rest - second.astype(F32)).astype(BF)
+    parts = (
+        first.astype(F32)
+        + pltpu.roll(second.astype(F32), 8, 1)
+        + pltpu.roll(third.astype(F32), 16, 1)
+    )
+    sums = dot_nn(triangle, parts.astype(BF))
+    return sums + pltpu.roll(sums, 120, 1) + pltpu.roll(sums, 112, 1)
+
+
+def head_sums(table, gather):
+    first = table.astype(BF)
+    second = (table - first.astype(F32)).astype(BF)
+    return dot_nn(first, gather) + dot_nn(second, gather)
+
+
+def rates(raw, head):
+    shifted_raw = raw + head[0:1]
+    step = jnp.maximum(shifted_raw, 0.0) + jnp.log1p(jnp.exp(-jnp.abs(shifted_raw)))
+    lanes = lax.broadcasted_iota(jnp.int32, raw.shape, 1)
+    return shifted_raw, jnp.where(lanes < QHEADS, step, 0.0)
+
+
+def triangle(keep):
+    rows_at = lax.broadcasted_iota(jnp.int32, (PART, PART), 0)
+    cols_at = lax.broadcasted_iota(jnp.int32, (PART, PART), 1)
+    return jnp.where(keep(rows_at, cols_at), 1.0, 0.0).astype(BF)
+
+
+def part_terms(step, head, cols, segr):
+    cum = split_sum(triangle(lambda r, c: r >= c), -step * head[1:2])
+    last = cum[PART - 1 : PART]
+    enter = jnp.exp(cum) * cols[:, 4:5]
+    leave = jnp.exp(last - cum) * cols[:, 5:6]
+    passing = jnp.exp(last) * cols[PART - 1 : PART, 4:5]
+    rows_at = lax.broadcasted_iota(jnp.int32, (PART, PART), 0)
+    cols_at = lax.broadcasted_iota(jnp.int32, (PART, PART), 1)
+    allowed = (rows_at >= cols_at) & (cols[:, 6:7] == segr)
+    return cum, enter, leave, passing, jnp.where(allowed, 0.0, -1e30)
+
+
+def segment_flags(seg_ref, block):
+    begin = pl.multiple_of(block * SPAN, 128)
+    around = seg_ref[0, :, pl.ds(begin, SPAN + 256)]
+    here = around[:, 128 : 128 + SPAN]
+    flags = []
+    for shift in (3, 2, 1, 0):
+        flags.append(pltpu.roll(around, shift, 1)[:, 128 : 128 + SPAN] == here)
+    ends = [around[:, PART * k + 127 : PART * k + 128] for k in range(PARTS + 1)]
+    parts = [here[:, PART * k : PART * (k + 1)] for k in range(PARTS)]
+    flags.append(jnp.concatenate([parts[k] == ends[k] for k in range(PARTS)], axis=1))
+    flags.append(jnp.concatenate([parts[k] == ends[k + 1] for k in range(PARTS)], axis=1))
+    for shift in (3, 2, 1, 0):
+        later = pltpu.roll(around, SPAN + 256 - shift, 1) if shift else around
+        flags.append(later[:, 128 : 128 + SPAN] == here)
+    flags = [jnp.where(flag, 1.0, 0.0) for flag in flags]
+    at = lax.broadcasted_iota(jnp.int32, (8, SPAN), 0)
+    first = here
+    for row in range(6):
+        first = jnp.where(at == row, flags[row], first)
+    second = flags[9]
+    for row in range(3):
+        second = jnp.where(at == row, flags[6 + row], second)
+    return jnp.concatenate([first, second], axis=0)
+
+
+def to_columns(rows):
+    filled = jnp.concatenate([rows, jnp.zeros((128 - rows.shape[0], SPAN), F32)], axis=0)
+    return filled.T
+
+
+def current(own_ref, other_ref):
+    return jnp.where(pl.program_id(0) == 0, own_ref[0], other_ref[0])
+
+
+def current_halves(own_refs, other_refs):
+    halves = [current(own, other) for own, other in zip(own_refs, other_refs)]
+    return jnp.concatenate(halves, axis=0)
+
+
+def fwd_kernel(
+    place_ref, own_ref, other_ref, w_ref, seg_ref, taps_ref, head_ref, chan_ref, mixed_ref, raw_ref, pre_ref, y_ref, hin_ref, buf, state,
+):
+    @pl.when(pl.program_id(1) == 0)
+    def _():
+        buf[0:8] = jnp.zeros((8, buf.shape[1]), F32)
+        state[...] = jnp.zeros_like(state)
+
+    width = QUARTER + 2 * STATE
+    projected = dot_nn(current(own_ref, other_ref), w_ref[...])
+    raw = projected[:, width:]
+    raw_ref[0, 0] = raw
+    mixed_low = projected[:, :width].astype(BF)
+    mixed_ref[0, 0] = mixed_low
+    mixed = mixed_low.astype(F32)
+    buf[8 : 8 + SPAN] = mixed
+    rows = segment_flags(seg_ref, pl.program_id(1))
+    cols_all = to_columns(rows)
+    taps = taps_ref[...]
+    head = head_ref[...]
+    pre = jnp.broadcast_to(taps[CONV : CONV + 1], mixed.shape)
+    for j in range(CONV):
+        window = mixed if j == CONV - 1 else buf[5 + j : 5 + j + SPAN]
+        pre = pre + taps[j : j + 1] * (window * cols_all[:, j : j + 1])
+    buf[0:8] = mixed[SPAN - 8 :]
+    pre_ref[0, 0] = pre
+    act = pre * sigmoid(pre)
+    _, step_all = rates(raw, head)
+    skip = chan_ref[1:2]
+    low_half = lax.broadcasted_iota(jnp.int32, (PART, 128), 1) < HEADDIM
+    zero_low = jnp.zeros((PART, 128), BF)
+    for part in range(SPAN // PART):
+        at_rows = slice(part * PART, (part + 1) * PART)
+        cols = cols_all[at_rows]
+        values = act[at_rows, :QUARTER]
+        b_low = act[at_rows, QUARTER : QUARTER + STATE].astype(BF)
+        c_low = act[at_rows, QUARTER + STATE :].astype(BF)
+        step = step_all[at_rows]
+        cum, enter, leave, passing, block_out = part_terms(step, head, cols, rows[6:7, at_rows])
+        cum_t = cum.T
+        scores = dot_nt(c_low, b_low)
+        held_f = state[...]
+        held = held_f.astype(BF)
+        hin_ref[0, 0, QUARTER * part : QUARTER * (part + 1)] = held
+        carried = dot_nt(c_low, held)
+        tails = []
+        for k in range(QHEADS // 2):
+            at = slice(128 * k, 128 * (k + 1))
+            scaled = (pair_cols(step, k, low_half) * values[:, at]).astype(BF)
+            weights = []
+            for h in (2 * k, 2 * k + 1):
+                decay = jnp.exp(cum[:, h : h + 1] - cum_t[h : h + 1] + block_out)
+                weights.append((scores * decay).astype(BF))
+            both = jnp.concatenate(
+                [jnp.where(low_half, scaled, zero_low), jnp.where(low_half, zero_low, scaled)],
+                axis=0,
+            )
+            own = dot_nn(jnp.concatenate(weights, axis=1), both)
+            y_ref[0, 0, at_rows, at] = (
+                own
+                + pair_cols(enter, k, low_half) * carried[:, at]
+                + skip[:, at] * values[:, at]
+            )
+            tails.append((pair_cols(leave, k, low_half) * scaled.astype(F32)).astype(BF))
+        added = dot_tn(jnp.concatenate(tails, axis=1), b_low)
+        for h in range(QHEADS):
+            at = slice(HEADDIM * h, HEADDIM * (h + 1))
+            state[at] = passing[:, h : h + 1] * held_f[at] + added[at]
+
+
+def core_rows(place_ref):
+    half = D // 2
+    core = place_ref[0]
+    own = pl.multiple_of(core * half, half)
+    other = pl.multiple_of((1 - core) * half, half)
+    return pl.ds(own, half), pl.ds(other, half)
+
+
+def gate_kernel(
+    place_ref, own_ref, other_ref, cot_own_0, cot_own_1, cot_other_0, cot_other_1, y_ref,
+    w_gate_ref, w_out_ref, chan_ref,
+    gate_ref, d_gated_ref, mine_ref, theirs_ref, stat_ref,
+):
+    gate = dot_nn(current(own_ref, other_ref), w_gate_ref[...])
+    gate_ref[0, 0] = gate
+    gated_in = y_ref[0, 0] * (gate * sigmoid(gate))
+    weighted = gated_in * chan_ref[0:1]
+    gun = weighted.astype(BF)
+    cot = current_halves((cot_own_0, cot_own_1), (cot_other_0, cot_other_1))
+    d_gated = dot_nn(cot, w_out_ref[...])
+    d_gated_ref[0, 0] = d_gated
+    own, other = core_rows(place_ref)
+    mine_ref[0, 0] = dot_nt(gun, w_out_ref[own]).astype(BF)
+    theirs_ref[0, 0] = dot_nt(gun, w_out_ref[other]).astype(BF)
+    square = jnp.sum(gated_in * gated_in, axis=1, keepdims=True)
+    cross = jnp.sum(d_gated * weighted, axis=1, keepdims=True)
+    lanes = lax.broadcasted_iota(jnp.int32, (SPAN, 128), 1)
+    table = jnp.where(lanes == 0, square, jnp.where(lanes == 1, cross, 0.0))
+    stat_ref[0, 0] = table.T[0:8]
+
+
+def start_sums(total, seed_ref):
+    @pl.when((pl.program_id(0) == 0) & (pl.program_id(1) == 0))
+    def _():
+        total[...] = jnp.zeros_like(total) if seed_ref is None else seed_ref[...]
+
+
+def finish_sums(total, out_ref):
+    @pl.when((pl.program_id(0) == 1) & (pl.program_id(1) == BLOCKS - 1))
+    def _():
+        rows_of = out_ref.shape[2]
+        for z in range(out_ref.shape[0]):
+            out_ref[z] = total[:, z * rows_of : (z + 1) * rows_of].astype(BF)
+
+
+def gate_back_first(*refs):
+    gate_back_step(*refs[:12], None, *refs[12:])
+
+
+def gate_back_last(*refs):
+    gate_back_step(*refs[:13], *refs[13:16], refs[17])
+    finish_sums(refs[17], refs[16])
+
+
+def gate_back_step(
+    place_ref, own_ref, other_ref, cot_own_0, cot_own_1, cot_other_0, cot_other_1, y_ref,
+    gate_ref, d_gated_ref, stat_ref, chan_ref, seed_ref,
+    dy_ref, d_gate_ref, g_gain_ref, g_ref,
+):
+    start_sums(g_ref, seed_ref)
+    start_sums(g_gain_ref, None)
+    stat = to_columns(stat_ref[0, 0])
+    scale = lax.rsqrt(stat[:, 0:1] * (1.0 / INNER) + EPS)
+    pull = stat[:, 1:2] * (1.0 / INNER) * scale * scale * scale
+    gate = gate_ref[0, 0]
+    y = y_ref[0, 0]
+    sigma = sigmoid(gate)
+    gate_act = gate * sigma
+    gated_in = y * gate_act
+    scaled_gain = chan_ref[0:1] * scale
+    d_in = d_gated_ref[0, 0] * scaled_gain - gated_in * pull
+    dy_ref[0, 0] = (d_in * gate_act).astype(BF)
+    d_gate = (d_in * y * (sigma + gate_act * (1.0 - sigma))).astype(BF)
+    d_gate_ref[0, 0] = d_gate
+    gated = (gated_in * scaled_gain).astype(BF)
+    by_gain = d_gated_ref[0, 0] * gated_in * scale
+    g_gain_ref[0:1] += jnp.sum(by_gain, axis=0, keepdims=True)
+    cot = current_halves((cot_own_0, cot_own_1), (cot_other_0, cot_other_1))
+    g_ref[:QUARTER] += dot_tn(gated, cot)
+    g_ref[QUARTER:] += dot_tn(d_gate, current(own_ref, other_ref))
+
+
+def bwd_first(*refs):
+    bwd_step(*refs[:16], None, refs[16], None, None, *refs[17:])
+
+
+def bwd_last(*refs):
+    total = refs[-1]
+    bwd_step(*refs[:17], total, *refs[18:-1])
+    finish_sums(total, refs[17])
+
+
+def bwd_step(
+    place_ref, own_ref, other_ref, mixed_ref, pre_ref, raw_ref, y_ref, hin_ref, dy_ref,
+    d_gate_ref, seg_ref, taps_ref, head_ref, chan_ref, w_ref, w_gate_ref,
+    seed_ref,
+    g_ref, keep_ref, give_ref, slope_ref, gtap_ref, ghead_ref, mine_ref, theirs_ref,
+    buf, d_state, bc_edge, slope_edge, d_late,
+):
+    start_sums(g_ref, seed_ref)
+
+    @pl.when(pl.program_id(1) == 0)
+    def _():
+        buf[SPAN:] = jnp.zeros((8, QUARTER), F32)
+        d_state[...] = jnp.zeros_like(d_state)
+        bc_edge[...] = jnp.zeros_like(bc_edge)
+        slope_edge[...] = jnp.zeros_like(slope_edge)
+
+    @pl.when((pl.program_id(0) == 0) & (pl.program_id(1) == 0))
+    def _():
+        gtap_ref[...] = jnp.zeros_like(gtap_ref)
+        ghead_ref[...] = jnp.zeros_like(ghead_ref)
+
+    rows = segment_flags(seg_ref, BLOCKS - 1 - pl.program_id(1))
+    cols_all = to_columns(rows)
+    head = head_ref[...]
+    taps = taps_ref[...]
+    pre = pre_ref[0, 0]
+    sigma = sigmoid(pre)
+    act = pre * sigma
+    slope = sigma * (1.0 + pre * (1.0 - sigma))
+    first_core = place_ref[0] == 0
+
+    def store(ref, first_row, rows):
+        if keep_ref is not None:
+            ref[0, 0, first_row : first_row + rows.shape[0]] = rows
+            return
+        for at in range(first_row, first_row + rows.shape[0], 16):
+            group = at // PACKED
+            row = SPAN + at % PACKED
+            ref[0, 0, row : row + 16, 128 * group : 128 * (group + 1)] = rows[
+                at - first_row : at - first_row + 16
+            ]
+
+    keep_at = mine_ref if keep_ref is None else keep_ref
+    give_at = theirs_ref if give_ref is None else give_ref
+    slope_half = jnp.where(
+        first_core, slope[:, QUARTER : QUARTER + STATE], slope[:, QUARTER + STATE :]
+    )
+    slope_ref[0, 0, 0:SPAN] = slope_half
+    slope_ref[0, 0, SPAN : SPAN + 16] = slope_edge[...]
+    slope_edge[...] = slope_half[0:16]
+    if keep_ref is None:
+        for ref in (mine_ref, theirs_ref):
+            ref[0, 0, SPAN + 32 :, 640:] = jnp.zeros((16, 128), BF)
+    store(keep_at, SPAN, bc_edge[:, :STATE].astype(BF))
+    store(give_at, SPAN, bc_edge[:, STATE:].astype(BF))
+    shifted_all, step_all = rates(raw_ref[0, 0], head)
+    skip = chan_ref[1:2]
+    low_half = lax.broadcasted_iota(jnp.int32, (PART, 128), 1) < HEADDIM
+    zero_low = jnp.zeros((PART, 128), BF)
+    chan_at = lax.broadcasted_iota(jnp.int32, (QUARTER, 128), 0)
+    head_at = lax.broadcasted_iota(jnp.int32, (QUARTER, 128), 1)
+    gather = jnp.where(
+        (chan_at >= head_at * HEADDIM) & (chan_at < (head_at + 1) * HEADDIM), 1.0, 0.0
+    )
+    gather_low = gather.astype(BF)
+    upper = triangle(lambda r, c: r <= c)
+    for part in reversed(range(SPAN // PART)):
+        at_rows = slice(part * PART, (part + 1) * PART)
+        cols = cols_all[at_rows]
+        values = act[at_rows, :QUARTER]
+        b_low = act[at_rows, QUARTER : QUARTER + STATE].astype(BF)
+        c_low = act[at_rows, QUARTER + STATE :].astype(BF)
+        step = step_all[at_rows]
+        cum, enter, leave, passing, block_out = part_terms(step, head, cols, rows[6:7, at_rows])
+        cum_t = cum.T
+        scores = dot_nt(c_low, b_low)
+        held = hin_ref[0, 0, QUARTER * part : QUARTER * (part + 1)]
+        dy_low = dy_ref[0, 0, at_rows]
+        dy = dy_low.astype(F32)
+        d_after = d_state[...]
+        d_after_low = d_after.astype(BF)
+        from_after = dot_nt(b_low, d_after_low)
+        d_scores = jnp.zeros((PART, PART), F32)
+        d_scaled_all = []
+        scaled_all = []
+        tail_terms = []
+        tails = []
+        entering = []
+        for k in range(QHEADS // 2):
+            at = slice(128 * k, 128 * (k + 1))
+            step_k = pair_cols(step, k, low_half)
+            scaled = (step_k * values[:, at]).astype(BF)
+            scaled_f = scaled.astype(F32)
+            dy_k = dy_low[:, at]
+            dy_both = jnp.concatenate(
+                [jnp.where(low_half, dy_k, zero_low), jnp.where(low_half, zero_low, dy_k)],
+                axis=0,
+            )
+            d_weights = dot_nt(dy_both, scaled)
+            weights = []
+            for at_h, h in enumerate((2 * k, 2 * k + 1)):
+                decay = jnp.exp(cum[:, h : h + 1] - cum_t[h : h + 1] + block_out)
+                weights.append((scores * decay).astype(BF))
+                d_scores = d_scores + d_weights[at_h * PART : (at_h + 1) * PART] * decay
+            leave_k = pair_cols(leave, k, low_half)
+            tail_part = leave_k * from_after[:, at]
+            d_scaled = dot_tn(jnp.concatenate(weights, axis=0), dy_both) + tail_part
+            d_scaled_all.append(d_scaled)
+            scaled_all.append(scaled_f)
+            tail_terms.append(jnp.sum(scaled_f * tail_part, axis=0, keepdims=True))
+            tails.append((leave_k * scaled_f).astype(BF))
+            entering.append((pair_cols(enter, k, low_half) * dy[:, at]).astype(BF))
+            d_values = step_k * d_scaled + skip[:, at] * dy[:, at]
+            buf[at_rows, at] = d_values * slope[at_rows, at]
+        d_scaled = jnp.concatenate(d_scaled_all, axis=1)
+        scaled = jnp.concatenate(scaled_all, axis=1)
+        enter_dy = jnp.concatenate(entering, axis=1)
+        d_scores_low = d_scores.astype(BF)
+        d_c = dot_nn(d_scores_low, b_low) + dot_nn(enter_dy, held)
+        d_b = dot_tn(d_scores_low, c_low) + dot_nn(jnp.concatenate(tails, axis=1), d_after_low)
+        kept_half = jnp.where(first_core, d_b, d_c)
+        given_half = jnp.where(first_core, d_c, d_b)
+        store(keep_at, part * PART, kept_half.astype(BF))
+        store(give_at, part * PART, given_half.astype(BF))
+        if part == 0:
+            bc_edge[:, :STATE] = kept_half[0:16]
+            bc_edge[:, STATE:] = given_half[0:16]
+        by_values = head_sums(values * d_scaled, gather_low)
+        y_part = y_ref[0, 0, at_rows] - skip * values
+        d_cum = head_sums(dy * y_part - scaled * d_scaled, gather_low)
+        tail_row = jnp.concatenate(tail_terms, axis=1)
+        tail_sum = dot_exact(jnp.broadcast_to(tail_row, (8, QUARTER)), gather)[0:1]
+        state_dot = jnp.sum(d_after * held.astype(F32), axis=1, keepdims=True)
+        state_terms = jnp.sum(state_dot * gather, axis=0, keepdims=True)
+        at_last = tail_sum + passing * state_terms
+        d_rate = split_sum(upper, d_cum) + at_last
+        d_step = by_values - head[1:2] * d_rate
+        d_raw = d_step * sigmoid(shifted_all[at_rows])
+        ghead_ref[0:1, :128] += jnp.sum(d_raw, axis=0, keepdims=True)
+        ghead_ref[1:2, :128] += jnp.sum(-step * head[1:2] * d_rate, axis=0, keepdims=True)
+        ghead_ref[2:3] += jnp.sum(values * dy, axis=0, keepdims=True)
+        d_late[at_rows, QUARTER:] = d_raw.astype(BF)
+        new_state = dot_tn(enter_dy, c_low)
+        for h in range(QHEADS):
+            at = slice(HEADDIM * h, HEADDIM * (h + 1))
+            d_state[at] = passing[:, h : h + 1] * d_after[at] + new_state[at]
+    mixed = mixed_ref[0, 0, :, :QUARTER].astype(F32)
+    d_mixed = jnp.zeros((SPAN, QUARTER), F32)
+    for j in range(CONV):
+        ahead = CONV - 1 - j
+        window = buf[ahead : ahead + SPAN] * cols_all[:, 8 + j : 9 + j]
+        d_mixed = d_mixed + taps[j : j + 1, :QUARTER] * window
+        gtap_ref[j : j + 1] += jnp.sum(mixed * window, axis=0, keepdims=True)
+    gtap_ref[CONV : CONV + 1] += jnp.sum(buf[0:SPAN], axis=0, keepdims=True)
+    buf[SPAN:] = buf[0:8]
+    d_late[:, :QUARTER] = d_mixed.astype(BF)
+    late = d_late[...]
+    g_ref[...] += dot_tn(late, current(own_ref, other_ref))[: QUARTER + 16]
+    d_gate = d_gate_ref[0, 0]
+    width = QUARTER + 2 * STATE
+    for rows_at, out_ref in zip(core_rows(place_ref), (mine_ref, theirs_ref)):
+        total = dot_nt(late[:, :QUARTER], w_ref[rows_at, :QUARTER])
+        total = total + dot_nt(late[:, QUARTER:], w_ref[rows_at, width:])
+        out_ref[0, 0, :SPAN] = (total + dot_nt(d_gate, w_gate_ref[rows_at])).astype(BF)
+
+
+def slot_spec(rows, width, order):
+    return pl.BlockSpec((1, 1, rows, width), lambda q, j, place: (q, order(j), 0, 0))
+
+
+def segment_spec():
+    return pl.BlockSpec(
+        (1, 8, BLOCKS * SPAN + 256), lambda q, j, place: (q, 0, 0)
+    )
+
+
+def fixed_spec(rows, width):
+    return pl.BlockSpec((rows, width), lambda q, j, place: (0, 0))
+
+
+def out_shape(rows, cols_of, kind):
+    return jax.ShapeDtypeStruct((2, BLOCKS, rows, cols_of), kind)
+
+
+def upward(j):
+    return j
+
+
+def downward(j):
+    return BLOCKS - 1 - j
+
+
+def own_spec(order, rows=SPAN, at=0):
+    def index(q, j, place):
+        return (jnp.where(q == 0, order(j), order(BLOCKS - 1)), at, 0)
+
+    return pl.BlockSpec((1, rows, D), index)
+
+
+def other_spec(order, rows=SPAN, at=0):
+    def index(q, j, place):
+        return (jnp.where(q == 0, order(0), order(j)), at, 0)
+
+    return pl.BlockSpec((1, rows, D), index)
+
+
+def cot_specs(cots):
+    half = SPAN // 2
+    second = 0 if cots[0].shape[1] == half else 1
+    return [
+        own_spec(upward, half),
+        own_spec(upward, half, second),
+        other_spec(upward, half),
+        other_spec(upward, half, second),
+    ]
+
+
+def call_blocks(kernel, name, place, operands, in_specs, outs, scratch=()):
+    return pl.pallas_call(
+        kernel,
+        grid_spec=pltpu.PrefetchScalarGridSpec(
+            num_scalar_prefetch=1,
+            grid=(2, BLOCKS),
+            in_specs=in_specs,
+            out_specs=[spec for spec, _ in outs],
+            scratch_shapes=list(scratch),
+        ),
+        out_shape=[shape for _, shape in outs],
+        compiler_params=pltpu.CompilerParams(vmem_limit_bytes=VMEM_LIMIT),
+        cost_estimate=pl.CostEstimate(flops=1024, bytes_accessed=1024, transcendentals=0),
+        name=name,
+    )(place, *operands)
+
+
+def slot_out(rows, width, kind, order):
+    return slot_spec(rows, width, order), out_shape(rows, width, kind)
+
+
+def lead_out(rows, width, order, flipped):
+    def index(q, j, place):
+        return (order(j), 1 - q if flipped else q, 0, 0)
+
+    shape = jax.ShapeDtypeStruct((BLOCKS, 2, rows, width), BF)
+    return pl.BlockSpec((1, 1, rows, width), index), shape
+
+
+def fixed_out(rows, width):
+    return fixed_spec(rows, width), jax.ShapeDtypeStruct((rows, width), F32)
+
+
+def run_fwd(place, tokens, w_first, rows, taps, head, chan):
+    width = QUARTER + 2 * STATE
+    return call_blocks(
+        fwd_kernel,
+        "mix_forward",
+        place,
+        (*tokens, w_first, rows, taps, head, chan),
+        [
+            own_spec(upward),
+            other_spec(upward),
+            fixed_spec(D, width + 128),
+            segment_spec(),
+            fixed_spec(8, width),
+            fixed_spec(8, 128),
+            fixed_spec(8, QUARTER),
+        ],
+        [
+            slot_out(SPAN, width, BF, upward),
+            slot_out(SPAN, 128, F32, upward),
+            slot_out(SPAN, width, F32, upward),
+            slot_out(SPAN, QUARTER, F32, upward),
+            slot_out(PARTS * QUARTER, STATE, BF, upward),
+        ],
+        [pltpu.VMEM((SPAN + 8, width), F32), pltpu.VMEM((QUARTER, STATE), F32)],
+    )
+
+
+def run_gate(place, tokens, cots, y, w_gate, w_out, chan):
+    half = D // 2
+    return call_blocks(
+        gate_kernel,
+        "gate_forward",
+        place,
+        (*tokens, *cots, y, w_gate, w_out, chan),
+        [
+            own_spec(upward),
+            other_spec(upward),
+            *cot_specs(cots),
+            slot_spec(SPAN, QUARTER, upward),
+            fixed_spec(D, QUARTER),
+            fixed_spec(D, QUARTER),
+            fixed_spec(8, QUARTER),
+        ],
+        [
+            slot_out(SPAN, QUARTER, F32, upward),
+            slot_out(SPAN, QUARTER, F32, upward),
+            lead_out(SPAN, half, upward, False),
+            lead_out(SPAN, half, upward, True),
+            slot_out(8, SPAN, F32, upward),
+        ],
+    )
+
+
+def sums_out(rows, dp_count, last):
+    if not last:
+        return fixed_out(rows, D), []
+    share = D // dp_count
+    spec = pl.BlockSpec((dp_count, rows, share), lambda q, j, place: (0, 0, 0))
+    out = spec, jax.ShapeDtypeStruct((dp_count, rows, share), BF)
+    return out, [pltpu.VMEM((rows, D), F32)]
+
+
+def run_gate_back(place, tokens, cots, y, gate, d_gated, stat, chan, seed, dp_count):
+    last = seed is not None
+    total, scratch = sums_out(2 * QUARTER, dp_count, last)
+    return call_blocks(
+        gate_back_last if last else gate_back_first,
+        "gate_backward",
+        place,
+        (*tokens, *cots, y, gate, d_gated, stat, chan) + ((seed,) if last else ()),
+        [
+            own_spec(upward),
+            other_spec(upward),
+            *cot_specs(cots),
+            slot_spec(SPAN, QUARTER, upward),
+            slot_spec(SPAN, QUARTER, upward),
+            slot_spec(SPAN, QUARTER, upward),
+            slot_spec(8, SPAN, upward),
+            fixed_spec(8, QUARTER),
+        ]
+        + ([fixed_spec(2 * QUARTER, D)] if last else []),
+        [
+            slot_out(SPAN, QUARTER, BF, upward),
+            slot_out(SPAN, QUARTER, BF, upward),
+            fixed_out(8, QUARTER),
+            total,
+        ],
+        scratch,
+    )
+
+
+def run_bwd(place, tokens, kept, dy, d_gate, rows, taps, head, chan, weights, seed, dp_count):
+    mixed, raw, pre, y, hin = kept
+    width = mixed.shape[-1]
+    states = 2 * STATE
+    half = D // 2
+    last = seed is not None
+    total, scratch = sums_out(QUARTER + 16, dp_count, last)
+    rows_out = SPAN if last else SPAN + PACKED
+    maps_out = [lead_out(SPAN + 16, STATE, downward, flip) for flip in (False, True)] if last else []
+    return call_blocks(
+        bwd_last if last else bwd_first,
+        "mix_backward",
+        place,
+        (*tokens, mixed, pre, raw, y, hin, dy, d_gate, rows, taps, head, chan, *weights)
+        + ((seed,) if last else ()),
+        [
+            own_spec(downward),
+            other_spec(downward),
+            slot_spec(SPAN, width, downward),
+            slot_spec(SPAN, width, downward),
+            slot_spec(SPAN, 128, downward),
+            slot_spec(SPAN, QUARTER, downward),
+            slot_spec(PARTS * QUARTER, STATE, downward),
+            slot_spec(SPAN, QUARTER, downward),
+            slot_spec(SPAN, QUARTER, downward),
+            segment_spec(),
+            fixed_spec(8, width),
+            fixed_spec(8, 128),
+            fixed_spec(8, QUARTER),
+            fixed_spec(D, width + 128),
+            fixed_spec(D, QUARTER),
+        ]
+        + ([fixed_spec(QUARTER + 16, D)] if last else []),
+        [
+            total,
+            *maps_out,
+            slot_out(SPAN + 16, STATE, F32, downward),
+            fixed_out(8, QUARTER),
+            fixed_out(8, QUARTER),
+            lead_out(rows_out, half, downward, False),
+            lead_out(rows_out, half, downward, True),
+        ],
+        [
+            pltpu.VMEM((SPAN + 8, QUARTER), F32),
+            pltpu.VMEM((QUARTER, STATE), F32),
+            pltpu.VMEM((16, states), F32),
+            pltpu.VMEM((16, STATE), F32),
+            pltpu.VMEM((SPAN, QUARTER + 128), BF),
+        ]
+        + scratch,
+    )
+
+
+def maps_kernel(
+    place_ref, packed_ref, maps_ref, slope_0, slope_1, mixed_0, mixed_1, seg_0, seg_1,
+    own_0, other_0, own_1, other_1, taps_ref,
+    d_maps_ref, g_ref, g_taps_ref, buf,
+):
+    chip = place_ref[1]
+    taps = taps_ref[...]
+    buf[SPAN + 16 :] = jnp.zeros((8, STATE), F32)
+    sums = [jnp.zeros((1, STATE), F32) for _ in range(CONV + 1)]
+    g_maps = jnp.zeros((STATE, D), F32)
+    slopes, mixes, segs = (slope_0, slope_1), (mixed_0, mixed_1), (seg_0, seg_1)
+    tokens = ((own_0, other_0), (own_1, other_1))
+    for m in range(MB):
+        for q in range(2):
+            if m == 0:
+                total = packed_ref[0, q].astype(F32)
+                for src in range(1, BLOCKS):
+                    total = total + packed_ref[src, q].astype(F32)
+                groups = [total[:, 128 * k : 128 * (k + 1)] for k in range(6)]
+                d_conv = jnp.concatenate(groups, axis=0)[: SPAN + 16]
+            else:
+                d_conv = maps_ref[0, q].astype(F32)
+                for src in range(1, BLOCKS):
+                    d_conv = d_conv + maps_ref[src, q].astype(F32)
+            d_pre = d_conv * slopes[m][q, 0]
+            buf[0 : SPAN + 16] = d_pre
+            cols = to_columns(segment_flags(segs[m].at[q : q + 1], chip))
+            mixed = mixes[m][q, 0].astype(F32)
+            d_mixed = jnp.zeros((SPAN, STATE), F32)
+            for j in range(CONV):
+                ahead = CONV - 1 - j
+                window = buf[ahead : ahead + SPAN] * cols[:, 8 + j : 9 + j]
+                d_mixed = d_mixed + taps[j : j + 1] * window
+                sums[j] = sums[j] + jnp.sum(mixed * window, axis=0, keepdims=True)
+            sums[CONV] = sums[CONV] + jnp.sum(d_pre[:SPAN], axis=0, keepdims=True)
+            low = d_mixed.astype(BF)
+            d_maps_ref[m, q] = low
+            g_maps = g_maps + dot_tn(low, tokens[m][q][0])
+    g_taps_ref[...] = jnp.concatenate(sums + [jnp.zeros((3, STATE), F32)], axis=0)
+    rows_of = g_ref.shape[2]
+    for z in range(g_ref.shape[0]):
+        g_ref[z] = g_maps[:, z * rows_of : (z + 1) * rows_of].astype(BF)
+
+
+def run_maps(place, packed, maps, slopes, mixes, segs, tokens, taps, dp_count):
+    def whole(shape):
+        return pl.BlockSpec(shape, lambda i, place: (0,) * len(shape))
+
+    def slope_spec():
+        return pl.BlockSpec((2, 1, SPAN + 16, STATE), lambda i, place: (0, place[1], 0, 0))
+
+    def mixed_spec():
+        first = QUARTER // STATE
+        return pl.BlockSpec(
+            (2, 1, SPAN, STATE), lambda i, place: (0, place[1], 0, first + place[0])
+        )
+
+    def token_spec():
+        return pl.BlockSpec((1, SPAN, D), lambda i, place: (place[1], 0, 0))
+
+    share = D // dp_count
+    return pl.pallas_call(
+        maps_kernel,
+        grid_spec=pltpu.PrefetchScalarGridSpec(
+            num_scalar_prefetch=1,
+            grid=(1,),
+            in_specs=[
+                whole(packed.shape),
+                whole(maps.shape),
+                slope_spec(),
+                slope_spec(),
+                mixed_spec(),
+                mixed_spec(),
+                whole(segs[0].shape),
+                whole(segs[1].shape),
+                token_spec(),
+                token_spec(),
+                token_spec(),
+                token_spec(),
+                whole(taps.shape),
+            ],
+            out_specs=[
+                whole((MB, 2, SPAN, STATE)),
+                whole((dp_count, STATE, share)),
+                whole((8, STATE)),
+            ],
+            scratch_shapes=[pltpu.VMEM((SPAN + 24, STATE), F32)],
+        ),
+        out_shape=[
+            jax.ShapeDtypeStruct((MB, 2, SPAN, STATE), BF),
+            jax.ShapeDtypeStruct((dp_count, STATE, share), BF),
+            jax.ShapeDtypeStruct((8, STATE), F32),
+        ],
+        compiler_params=pltpu.CompilerParams(vmem_limit_bytes=VMEM_LIMIT),
+        cost_estimate=pl.CostEstimate(flops=1024, bytes_accessed=1024, transcendentals=0),
+        name="maps_backward",
+    )(place, packed, maps, *slopes, *mixes, *segs, *tokens, taps)
+
+
+def norm_kernel(place_ref, mid_ref, late_ref, w_in_ref, w_state_ref, w_step_ref, step_ref, out_ref):
+    rows = mid_ref.shape[1]
+    squares = jnp.zeros((rows, QUARTER), F32)
+    products = jnp.zeros((rows, QUARTER), F32)
+    for s in range(BLOCKS):
+        at = slice(s * QUARTER, (s + 1) * QUARTER)
+        out = mid_ref[s, :, :QUARTER].astype(F32)
+        gate = mid_ref[s, :, QUARTER:].astype(F32)
+        inner = late_ref[s, :, :QUARTER].astype(F32)
+        squares = squares + out * out + gate * gate + inner * inner
+        products = products + gate * w_in_ref[0, :, at].astype(F32)
+        products = products + inner * w_in_ref[1, :, at].astype(F32)
+    state = late_ref[0, :, QUARTER : QUARTER + STATE].astype(F32)
+    for s in range(1, BLOCKS):
+        state = state + late_ref[s, :, QUARTER : QUARTER + STATE].astype(F32)
+    step = step_ref[...]
+    by_row = jnp.sum(products, axis=1, keepdims=True)
+    by_row = by_row + jnp.sum(state * w_state_ref[...].astype(F32), axis=1, keepdims=True)
+    by_row = by_row + jnp.sum(step * w_step_ref[...].astype(F32), axis=1, keepdims=True)
+    square = jnp.sum(squares, axis=1, keepdims=True) + jnp.sum(state * state, axis=1, keepdims=True)
+    square = square + jnp.sum(step * step, axis=1, keepdims=True)
+    lanes = lax.broadcasted_iota(jnp.int32, (rows, 128), 1)
+    table = jnp.where(lanes == 0, by_row, jnp.where(lanes == 1, square, 0.0))
+    table = jnp.concatenate([table, jnp.zeros((128 - rows, 128), F32)], axis=0).T
+    total = jnp.sum(table[1:2], axis=1, keepdims=True)
+    at_row = lax.broadcasted_iota(jnp.int32, (8, 128), 0)
+    at_lane = lax.broadcasted_iota(jnp.int32, (8, 128), 1)
+    first = jnp.where((at_row == 0) & (at_lane == rows), total, table[0:8])
+    out_ref[...] = jnp.where(at_row == 0, first, 0.0)
+
+
+def update_kernel(
+    place_ref, factor_ref, mid_ref, late_ref, step_ref, w_in_ref, w_out_ref, w_state_ref,
+    w_step_ref, m_in_ref, m_out_ref, m_state_ref, m_step_ref,
+    new_in_ref, new_out_ref, new_state_ref, new_step_ref,
+    next_in_ref, next_out_ref, next_state_ref, next_step_ref,
+):
+    factor = factor_ref[0, 0]
+    rows = mid_ref.shape[1]
+
+    def write(new_ref, next_ref, at, moment, grad, weight):
+        new = 0.5 * moment + (0.5 * factor) * grad
+        new_ref[at] = new
+        next_ref[at] = (weight.astype(F32) - LEARN * new).astype(BF)
+
+    for s in range(BLOCKS):
+        lanes = slice(s * QUARTER, (s + 1) * QUARTER)
+        gate = (0, slice(None), lanes)
+        write(
+            new_in_ref, next_in_ref, gate, m_in_ref[gate],
+            mid_ref[s, :, QUARTER:].astype(F32), w_in_ref[gate],
+        )
+        inner = (1, slice(None), lanes)
+        write(
+            new_in_ref, next_in_ref, inner, m_in_ref[inner],
+            late_ref[s, :, :QUARTER].astype(F32), w_in_ref[inner],
+        )
+        out = mid_ref[s, :, :QUARTER].astype(F32)
+        out = jnp.concatenate([out, jnp.zeros((128 - rows, QUARTER), F32)], axis=0).T
+        write(
+            new_out_ref, next_out_ref, lanes, m_out_ref[lanes], out[:, :rows], w_out_ref[lanes]
+        )
+    state = late_ref[0, :, QUARTER : QUARTER + STATE].astype(F32)
+    for s in range(1, BLOCKS):
+        state = state + late_ref[s, :, QUARTER : QUARTER + STATE].astype(F32)
+    write(new_state_ref, next_state_ref, ..., m_state_ref[...], state, w_state_ref[...])
+    write(new_step_ref, next_step_ref, ..., m_step_ref[...], step_ref[...], w_step_ref[...])
+
+
+def owner_specs(rows, heads_local):
+    return [
+        pl.BlockSpec((2, rows, BLOCKS * QUARTER), lambda i, place: (0, place[1], 0)),
+        pl.BlockSpec((rows, STATE), lambda i, place: (place[1], place[0])),
+        pl.BlockSpec((rows, heads_local), lambda i, place: (place[1], 0)),
+    ]
+
+
+def run_owner(kernel, name, place, operands, in_specs, outs):
+    return pl.pallas_call(
+        kernel,
+        grid_spec=pltpu.PrefetchScalarGridSpec(
+            num_scalar_prefetch=1, grid=(1,), in_specs=in_specs,
+            out_specs=[spec for spec, _ in outs],
+        ),
+        out_shape=[shape for _, shape in outs],
+        compiler_params=pltpu.CompilerParams(vmem_limit_bytes=VMEM_LIMIT),
+        cost_estimate=pl.CostEstimate(flops=1024, bytes_accessed=1024, transcendentals=0),
+        name=name,
+    )(place, *operands)
+
+
+def swap_cores(block):
+    return lax.ppermute(block, "tensor", SWAP)
+
+
+def over_x(block):
+    return lax.ppermute(block, "seq", ROUTE_X)
+
+
+def over_y(block):
+    return lax.ppermute(block, "seq", ROUTE_Y)
+
+
+def exchange(blocks):
+    return lax.all_to_all(blocks, "seq", 0, 0, tiled=True)
+
+
+def gather_blocks(piece):
+    return exchange(jnp.broadcast_to(piece, (BLOCKS,) + piece.shape))
+
+
+def add_low(a, b):
+    return (a.astype(F32) + b.astype(F32)).astype(BF)
+
+
+def gather_halves(piece):
+    half = piece.shape[0] // 2
+    return [gather_blocks(piece[:half]), gather_blocks(piece[half:])]
+
+
+def scatter(blocks):
+    return jnp.sum(exchange(blocks).astype(F32), axis=0)
+
+
+def after(value, *others):
+    return lax.optimization_barrier((value, others))[0]
+
+
+def sum_cores(table):
+    return table + swap_cores(table)[::-1]
+
+
+def sum_plane(table):
+    table = table + over_x(table)
+    return table + over_y(table)
+
+
+def fast_body(
+    inputs,
+    segments,
+    cotangent,
+    prenorm,
+    inproj,
+    statproj,
+    stepproj,
+    outproj,
+    convinner,
+    convstate,
+    headparam,
+    gatenorm,
+    prenorm_moment,
+    inproj_moment,
+    statproj_moment,
+    stepproj_moment,
+    outproj_moment,
+    convinner_moment,
+    convstate_moment,
+    headparam_moment,
+    gatenorm_moment,
+):
+    core = lax.axis_index("tensor")
+    chip = lax.axis_index("seq")
+    data_at = lax.axis_index("dp")
+    dp_count = lax.axis_size("dp")
+    heads_local = headparam.shape[1]
+    rows_local = inproj.shape[1]
+    shard = rows_local // BLOCKS
+    half_d = D // 2
+    place = jnp.stack([core, chip]).astype(jnp.int32)
+
+    def by_core(first, second):
+        return jnp.where(core == 0, first, second)
+
+    def quarter(array, axis, width):
+        return lax.dynamic_slice_in_dim(array, chip * width, width, axis)
+
+    def all_rows(block):
+        return lax.all_gather(block, "dp", axis=0, tiled=True)
+
+    w_first = all_rows(
+        jnp.concatenate(
+            [
+                quarter(inproj[1], 1, QUARTER),
+                statproj,
+                jnp.pad(quarter(stepproj, 1, QHEADS), ((0, 0), (0, 128 - QHEADS))),
+            ],
+            axis=1,
+        )
+    )
+    w_gate = all_rows(quarter(inproj[0], 1, QUARTER))
+    w_out = all_rows(quarter(outproj, 0, QUARTER).T)
+
+    def whole_rows(array):
+        mine = lax.dynamic_index_in_dim(array, core, 1, keepdims=False)
+        theirs = lax.dynamic_index_in_dim(array, 1 - core, 1, keepdims=False)
+        got = swap_cores(theirs)
+        return by_core(
+            jnp.concatenate([mine, got], axis=2), jnp.concatenate([got, mine], axis=2)
+        )
+
+    rows_whole = whole_rows(inputs)
+    normed_own = rms_scale(rows_whole.astype(F32), prenorm).astype(BF)
+    cot_own = whole_rows(cotangent)
+    own_0 = gather_blocks(normed_own[0])
+    segments, convinner, convstate, headparam, gatenorm = after(
+        (segments, convinner, convstate, headparam, gatenorm), normed_own
+    )
+
+    seg_mine = jnp.concatenate(
+        [
+            lax.dynamic_index_in_dim(segments, core, 1),
+            lax.dynamic_index_in_dim(segments, 1 - core, 1),
+        ],
+        axis=1,
+    )
+    seg_pad = jnp.pad(
+        seg_mine.astype(F32), ((0, 0), (0, 0), (128, 128)), constant_values=-1.0
+    )
+    segs = jnp.broadcast_to(seg_pad[:, :, None], seg_pad.shape[:2] + (8, seg_pad.shape[2]))
+
+    taps_inner = quarter(convinner, 1, QUARTER)
+    taps = jnp.pad(jnp.concatenate([taps_inner, convstate], axis=1), ((0, 3), (0, 0)))
+    head_own = quarter(headparam, 1, QHEADS)
+    head = jnp.pad(
+        jnp.stack([head_own[0], jnp.exp(head_own[1]), head_own[2]]),
+        ((0, 5), (0, 128 - QHEADS)),
+    )
+    gain = quarter(gatenorm, 0, QUARTER)
+    chan = jnp.pad(jnp.stack([gain, jnp.repeat(head_own[2], HEADDIM)]), ((0, 6), (0, 0)))
+
+    def rows_dot_t(left, right):
+        return lax.dot_general(left, right, (((3,), (1,)), ((), ())), preferred_element_type=F32)
+
+    def core_sums(mine, theirs):
+        return add_low(mine, swap_cores(theirs))
+
+    def core_halves(mine, theirs):
+        got = swap_cores(theirs)
+        return [add_low(mine[:, q], got[:, q]) for q in range(2)]
+
+    def over_dp(parts):
+        return lax.psum_scatter(parts, "dp", scatter_dimension=0, tiled=True)[0]
+
+    def by_place(columns):
+        blocks = columns.T.reshape(BLOCKS, shard, -1)
+        return lax.all_to_all(blocks, "seq", 0, 0, tiled=True)
+
+    def forward(m, place, tokens):
+        return run_fwd(place, tokens, w_first, segs[m], taps, head, chan)
+
+    def gate_forward(m, place):
+        return run_gate(place, normed[m], cots[m], kept[m][3], w_gate, w_out, chan)
+
+    def gate_backward(m, place, gate, d_gated, sums, seed):
+        return run_gate_back(
+            place, normed[m], cots[m], kept[m][3], gate, d_gated, sums, chan, seed, dp_count
+        )
+
+    def backward(m, place, dy, d_gate, seed):
+        return run_bwd(
+            place, normed[m], kept[m], dy, d_gate, segs[m], taps, head, chan,
+            (w_first, w_gate), seed, dp_count,
+        )
+
+    def token_scale(sums):
+        own = lax.dynamic_index_in_dim(sums, chip, 1, keepdims=False)
+        return lax.rsqrt(own[:, 0] / INNER + EPS)[..., None]
+
+    def with_other(own):
+        return own, swap_cores(own)
+
+    own_1 = gather_blocks(after(normed_own[1], own_0))
+    normed = [with_other(own_0)]
+    (own_0, other_0), place = after((normed[0], place), w_first)
+    kept = [forward(0, place, (own_0, other_0))]
+
+    own_1, w_gate, piece, place = after((own_1, w_gate, cot_own[0], place), kept[0][1])
+    normed.append(with_other(own_1))
+    cot_0 = gather_blocks(piece)
+    kept.append(forward(1, place, normed[1]))
+
+    cot_0, w_out, piece, place = after((cot_0, w_out, cot_own[1], place), kept[1][1])
+    cot_0 = with_other(cot_0)
+    cots = [[cot_0[0], cot_0[0], cot_0[1], cot_0[1]]]
+    half = SPAN // 2
+    cot_a = gather_blocks(piece[:half])
+    gate_0, d_gated_0, mine_0, theirs_0, stat_0 = gate_forward(0, place)
+
+    cot_a, stat_0, piece, place = after((cot_a, stat_0, piece, place))
+    stat_0 = sum_cores(stat_0)
+    theirs_0 = after(theirs_0, stat_0)
+    sums_0 = sum_plane(stat_0)
+    cot_b = gather_blocks(after(piece, sums_0)[half:])
+    cot_a = [cot_a, swap_cores(cot_a)]
+    branch_0 = core_halves(mine_0, theirs_0)
+    dy_0, d_gate_0, g_gain_0, g_mid_0 = gate_backward(0, place, gate_0, d_gated_0, sums_0, None)
+
+    cot_a, cot_b, place, branch_0 = after((cot_a, cot_b, place, branch_0), dy_0)
+    cots.append([cot_a[0], cot_b, cot_a[1], swap_cores(cot_b)])
+    layer_0 = [exchange(branch_0[0])]
+    gate_1, d_gated_1, mine_1, theirs_1, stat_1 = gate_forward(1, place)
+
+    layer_0, stat_1, place = after((layer_0, stat_1, place))
+    stat_1 = sum_cores(stat_1)
+    theirs_1 = after(theirs_1, stat_1)
+    sums_1 = sum_plane(stat_1)
+    layer_0.append(exchange(after(branch_0[1], sums_1)))
+    branch_1 = core_sums(mine_1, theirs_1)
+    dy_1, d_gate_1, g_gain_1, mid_parts = gate_backward(1, place, gate_1, d_gated_1, sums_1, g_mid_0)
+
+    layer_0, branch_1, place, mid_parts = after((layer_0, branch_1, place, mid_parts), dy_1)
+    layer_1 = exchange(branch_1)
+    mid_rows = over_dp(mid_parts)
+    g_late_0, slope_0, g_taps_0, g_head_0, mine, theirs = backward(
+        0, place, dy_0, d_gate_0, None
+    )
+
+    layer_1, mid_rows, theirs, place = after((layer_1, mid_rows, theirs, place), g_taps_0)
+    back_0 = core_sums(mine, theirs)
+    back_0, place = after((back_0, place))
+    token_0 = exchange(back_0)
+    late_parts, keep_1, give_1, slope_1, g_taps_1, g_head_1, mine, theirs = backward(
+        1, place, dy_1, d_gate_1, g_late_0
+    )
+
+    token_0, late_parts, theirs, give_1, layer_0, layer_1, mid_rows = after(
+        (token_0, late_parts, theirs, give_1, layer_0, layer_1, mid_rows)
+    )
+    late_rows = over_dp(late_parts)
+    maps = core_sums(keep_1, give_1)
+    back_1 = core_sums(mine, after(theirs, maps))
+    maps = exchange(maps)
+    maps, back_1 = after((maps, back_1))
+    token_1 = exchange(back_1)
+    taps_state = lax.dynamic_slice_in_dim(convstate, core * STATE, STATE, 1)
+    d_maps, g_maps, g_state_taps = run_maps(
+        place, token_0[:, :, SPAN:], maps, (slope_0, slope_1), (kept[0][0], kept[1][0]),
+        segs, (*normed[0], *normed[1]), jnp.pad(taps_state, ((0, 3), (0, 0))), dp_count,
+    )
+
+    def for_dp(hop):
+        at = lax.rem(data_at + hop, dp_count)
+        return lax.dynamic_index_in_dim(g_maps, at, 0, keepdims=False)
+
+    state_rows = for_dp(0).astype(F32)
+    for hop in range(1, dp_count):
+        route = [(i, (i + hop) % dp_count) for i in range(dp_count)]
+        state_rows = state_rows + lax.ppermute(for_dp(hop), "dp", route).astype(F32)
+    state_rows = state_rows.astype(BF)
+    token_1, late_rows, mid_rows, state_rows = after((token_1, late_rows, mid_rows, state_rows))
+
+    def summed(blocks):
+        return jnp.sum(blocks.astype(F32), axis=0)
+
+    layer_out = [
+        jnp.stack([summed(part) for part in layer_0]) * token_scale(sums_0),
+        summed(layer_1) * token_scale(sums_1),
+    ]
+    d_tokens = [summed(token_0[:, :, :SPAN]), summed(token_1)]
+    smalls = (g_taps_0 + g_taps_1, g_head_0 + g_head_1)
+    w_state = w_first[:, QUARTER : QUARTER + 2 * STATE]
+
+    state_other = swap_cores(d_maps)[:, ::-1]
+    state_mine = d_maps
+    d_state_both = by_core(
+        jnp.concatenate([state_mine, state_other], axis=3),
+        jnp.concatenate([state_other, state_mine], axis=3),
+    )
+    from_state = rows_dot_t(
+        d_state_both, lax.dynamic_slice_in_dim(w_state, core * half_d, half_d, 0)
+    )
+
+    def in_order(block):
+        return by_core(block, block[:, ::-1])
+
+    layer_out = in_order(jnp.stack(layer_out))
+    outputs = (inputs.astype(F32) + layer_out).astype(BF)
+    d_normed = in_order(jnp.stack(d_tokens) + from_state)
+    rows_own = inputs.astype(F32)
+    gain_own = lax.dynamic_slice_in_dim(prenorm, core * half_d, half_d, 0)
+    weighted = d_normed * gain_own
+    pair_sums = jnp.stack(
+        [jnp.sum(rows_own * rows_own, axis=-1), jnp.sum(weighted * rows_own, axis=-1)]
+    )
+    pair_sums = pair_sums + swap_cores(pair_sums)
+    root = lax.rsqrt(pair_sums[0] / D + EPS)[..., None]
+    input_grads = (
+        cotangent.astype(F32)
+        + weighted * root
+        - rows_own * root * root * root * (pair_sums[1] / D)[..., None]
+    ).astype(BF)
+
+    mid_share = by_place(mid_rows)
+    late_share = by_place(
+        jnp.concatenate([late_rows[:QUARTER], state_rows, late_rows[QUARTER:]], axis=0)
+    )
+    step_share = late_share[:, :, QUARTER + STATE : QUARTER + STATE + QHEADS].astype(F32)
+    step_share = jnp.moveaxis(step_share, 0, 1).reshape(shard, heads_local)
+    row_start = chip * shard
+    in_spec, state_spec, step_spec = owner_specs(shard, heads_local)
+
+    def whole(array):
+        return pl.BlockSpec(array.shape, lambda i, place: (0,) * array.ndim)
+
+    def whole_out(shape, kind):
+        spec = pl.BlockSpec(shape, lambda i, place: (0,) * len(shape))
+        return spec, jax.ShapeDtypeStruct(shape, kind)
+
+    owner_sums = run_owner(
+        norm_kernel,
+        "owner_norm",
+        place,
+        (mid_share, late_share, inproj, statproj, stepproj, step_share),
+        [whole(mid_share), whole(late_share), in_spec, state_spec, step_spec, whole(step_share)],
+        [whole_out((8, 128), F32)],
+    )[0]
+    owner_sums = owner_sums + swap_cores(owner_sums)
+
+    g_taps, g_head = smalls
+    g_heads = jnp.concatenate(
+        [g_head[:2, :QHEADS], jnp.sum(g_head[2].reshape(1, QHEADS, HEADDIM), axis=2)], axis=0
+    )
+
+    inner_local = BLOCKS * QUARTER
+
+    def put(values, width, total):
+        base = jnp.zeros(values.shape[:-1] + (total,), F32)
+        return lax.dynamic_update_slice_in_dim(base, values, chip * width, values.ndim - 1)
+
+    small_parts = [
+        put(g_taps[: CONV + 1], QUARTER, inner_local),
+        put(g_gain_0[0] + g_gain_1[0], QUARTER, inner_local),
+        put(g_heads, QHEADS, heads_local),
+        g_state_taps[: CONV + 1],
+    ]
+    sizes = [part.size for part in small_parts]
+    vector = jnp.concatenate([part.reshape(-1) for part in small_parts])
+    vector = jnp.pad(vector, (0, -vector.size % 1024)).reshape(-1, 128)
+
+    def sum_all(value):
+        value = value + over_x(value)
+        value = value + over_y(value)
+        hop = 1
+        while hop < dp_count:
+            value = value + lax.ppermute(value, "dp", [(i, i ^ hop) for i in range(dp_count)])
+            hop *= 2
+        return value
+
+    vector = sum_all(vector).reshape(-1)
+    small_sums = []
+    start = 0
+    for part, size in zip(small_parts, sizes):
+        small_sums.append(vector[start : start + size].reshape(part.shape))
+        start += size
+    s_taps, s_gain, s_head, s_state_taps = small_sums
+
+    small_sq = sum(jnp.sum(term * term) for term in small_sums)
+    small_sq = small_sq + swap_cores(small_sq)
+    owners = dp_count * BLOCKS
+    owner = data_at * BLOCKS + chip
+    gain_rows = lax.dynamic_slice_in_dim(prenorm, owner * shard, shard, 0)
+    lanes = jnp.arange(128)
+    g_prenorm = owner_sums[0] / jnp.pad(gain_rows, (0, 128 - shard), constant_values=1.0)
+    g_prenorm = jnp.where(lanes < shard, g_prenorm, 0.0)
+    square = owner_sums[0, shard] + jnp.sum(g_prenorm * g_prenorm)
+    square = square + jnp.where(owner == 0, small_sq, 0.0)
+    line = jnp.where(lanes == shard, square, g_prenorm)
+    table = jnp.where(jnp.arange(owners)[:, None] == owner, line[None], 0.0)
+    table = sum_all(table)
+    grad_norm = jnp.sqrt(jnp.sum(table[:, shard]))
+    s_prenorm = lax.dynamic_slice_in_dim(
+        table[:, :shard], core * (owners // 2), owners // 2, 0
+    ).reshape(half_d)
+
+    entries = (
+        2 * D * INNER
+        + 2 * D * STATE
+        + D * (INNER // HEADDIM)
+        + INNER * D
+        + (CONV + 1) * (INNER + 2 * STATE)
+        + 3 * (INNER // HEADDIM)
+        + INNER
+        + D
+    )
+    limit = CLIP_RMS * math.sqrt(entries)
+    factor = limit / jnp.maximum(grad_norm, limit)
+
+    def moved(moment, grad):
+        return 0.5 * moment + 0.5 * factor * grad
+
+    def stepped(weight, moment):
+        return (weight.astype(F32) - LEARN * moment).astype(weight.dtype)
+
+    new_prenorm = moved(prenorm_moment, s_prenorm)
+    outproj_own = lax.dynamic_slice_in_dim(outproj, row_start, shard, 1)
+    moments = (inproj_moment, outproj_moment, statproj_moment, stepproj_moment)
+    new_in, new_out, new_state, new_step, next_in, next_out, next_state, next_step = run_owner(
+        update_kernel,
+        "owner_update",
+        place,
+        (
+            factor.reshape(1, 1), mid_share, late_share, step_share,
+            inproj, outproj_own, statproj, stepproj, *moments,
+        ),
+        [
+            pl.BlockSpec(memory_space=pltpu.SMEM),
+            whole(mid_share), whole(late_share), whole(step_share),
+            in_spec, whole(outproj_own), state_spec, step_spec,
+            *[whole(moment) for moment in moments],
+        ],
+        [whole_out(moment.shape, kind) for kind in (F32, BF) for moment in moments],
+    )
+    new_taps = moved(convinner_moment, s_taps)
+    new_state_taps = moved(convstate_moment, s_state_taps)
+    new_head = moved(headparam_moment, s_head)
+    new_gain = moved(gatenorm_moment, s_gain)
+    return (
+        outputs,
+        input_grads,
+        grad_norm,
+        new_prenorm,
+        new_in,
+        new_state,
+        new_step,
+        new_out,
+        new_taps,
+        new_state_taps,
+        new_head,
+        new_gain,
+        next_in,
+        next_state,
+        next_step,
+        next_out,
+        stepped(convinner, new_taps),
+        stepped(lax.dynamic_slice_in_dim(convstate, core * STATE, STATE, 1), new_state_taps),
+    )
+
+
 def solution(mesh):
+    fast = mesh.shape["seq"] == BLOCKS and mesh.shape["tensor"] == 2
     return jax.shard_map(
-        body,
+        fast_body if fast else general_body,
         mesh=mesh,
         in_specs=(
             P(None, "dp", "seq", "tensor"),

time: 1610 us -> 594 us (0.37)
  waiting for transfers between devices: 801 us -> 65.2 us
  matrix products: 313 us -> 4.11 us
  Pallas kernels: 0 us -> 255 us
  blocking collectives: 192 us -> 41.9 us
  other arithmetic: 195 us -> 66.4 us
  starting transfers between devices: 11.5 us -> 81.6 us
    reduce_scatter x5 -> x2, waiting for transfers between devices: 498 us -> 0.02 us  [over_dp(): return lax.psum_scatter(parts, 'dp', scatter_dimension=0, tiled=True)[0]]
    dot_general x54 -> x1, matrix products: 313 us -> 4.11 us  [rows_dot_t(): lax.dot_general(left, right, (((3,), (1,)), ((), ())), preferred_element_...]
    pallas_call x0 -> x11, Pallas kernels: none -> 255 us  [the longest x8 240 us: call_blocks(): pl.pallas_call(kernel, grid_spec=pltpu.PrefetchScalarGridSpec(num_scalar_...]
    all_gather x8 -> x3, waiting for transfers between devices: 254 us -> 4.41 us  [all_rows(): return lax.all_gather(block, 'dp', axis=0, tiled=True)]
    psum x4 -> x0, blocking collectives: 124 us -> none  [the longest x1 79.8 us: body(): lax.psum((small_terms[0], small_terms[1], small_terms[2], small_terms[3],...]
    all_gather x6 -> x0, blocking collectives: 68.1 us -> none  [the longest x1 21.8 us: body(): lax.all_gather(statproj, 'dp', axis=0, tiled=True)]
    all_to_all x0 -> x12, starting transfers between devices: none -> 52.8 us  [the longest x10 45 us: exchange(): return lax.all_to_all(blocks, 'seq', 0, 0, tiled=True)]
    ppermute x4 -> x33, waiting for transfers between devices: 5.2 us -> 49.4 us  [the longest x4 23.6 us: over_x(): return lax.ppermute(block, 'seq', ROUTE_X)]
  transfers between devices with their start and end apart: 20 -> 50, of which waited for: 12 -> 24; matrix products, arithmetic and copies ran while one was open for 27% -> 16% of each run, Pallas kernels for 0% -> 42%
where the time goes in v2:
time: 594 us; the launch traced here: 583 us
  Pallas kernels  255 us (43%)
  starting transfers between devices  81.6 us (14%)
  other arithmetic  66.4 us (11%)
  waiting for transfers between devices  65.2 us (11%)
  local copies, waits for them, and re-layouts  47.5 us (8%)
  blocking collectives  41.9 us (7%)
  between operations  21.5 us (4%)
    pallas_call x8, Pallas kernels, call_blocks(): pl.pallas_call(kernel, grid_spec=pltpu.PrefetchScalarGridSpec(num_scalar_...  240 us
    all_to_all x10, starting transfers between devices, exchange(): return lax.all_to_all(blocks, 'seq', 0, 0, tiled=True)  45 us
    all_to_all x1, blocking collectives, exchange(): return lax.all_to_all(blocks, 'seq', 0, 0, tiled=True)  41.9 us
    ppermute x4, waiting for transfers between devices, over_x(): return lax.ppermute(block, 'seq', ROUTE_X)  23.6 us
    convert_element_type x5, other arithmetic, add_low(): return (a.astype(F32) + b.astype(F32)).astype(BF)  20.6 us
    unnamed x86, local copies, waits for them, and re-layouts  13.4 us
    ppermute x18, waiting for transfers between devices, swap_cores(): return lax.ppermute(block, 'tensor', SWAP)  13.2 us
    reduce_sum x4, other arithmetic, summed(): return jnp.sum(blocks.astype(F32), axis=0)  12.9 us
  transfers between devices with their start and end apart: 50, of which 24 were waited for; matrix products, arithmetic and copies ran while one was open for 16% of the time, Pallas kernels for 42%

profile of v2, /device:TPU:0, one launch (start us, length us, event | category | flops | bytes accessed | tf_op | source)
XLA Modules:
  0.0 582.8 jit_solution(1862533711238472671)
XLA Ops:
  19.9 41.9 %all_to_all.65.own_ref.refs_1_.own_0 = bf16[4,256,1536]{2,1,0:T(8,128)(2,1)} all-to-all(bf16[4,256,1536]{2,1,0:T(8,128)(2,1)S(1)} %broadcast_in_dim.76), channel_id=1, replica_groups=mesh['dp'=4,'seq'=4,'tensor'=2] {'seq'}, dimensions={0} | all-to-all | bytes 6291456 | tf_op jit(solution)/shard_map/all_to_all | solution.py:1294
  63.7 4.8 all-to-all-start.1
  78.0 29.3 %mix_forward.2 = (bf16[2,4,256,640]{3,2,1,0:T(8,128)(2,1)}, f32[2,4,256,128]{3,2,1,0:T(8,128)}, f32[2,4,256,640]{3,2,1,0:T(8,128)}, f32[2,4,256,384]{3,2,1,0:T(8,128)}, bf16[2,4,768,128]{3,2,1,0:T(8,128)(2,1)}) custom-call(s32[2]{0:T(128)} %pad_add_fusion.place_ref.refs_0_, bf16[4,256,1536]{2,1,0:T(8,128)(2,1)} %all_to_all.65.own_ref.refs_1_.own_0, ...), custom_call_target="tpu_custom_call" | custom-call | flops 1024 | bytes 1024 | tf_op jit(solution)/shard_map/mix_forward/pallas_call | solution.py:915
  109.3 4.6 all-to-all-start.2
  115.7 29.1 %mix_forward.3 = (bf16[2,4,256,640]{3,2,1,0:T(8,128)(2,1)}, f32[2,4,256,128]{3,2,1,0:T(8,128)}, f32[2,4,256,640]{3,2,1,0:T(8,128)}, f32[2,4,256,384]{3,2,1,0:T(8,128)}, bf16[2,4,768,128]{3,2,1,0:T(8,128)(2,1)}) custom-call(s32[2]{0:T(128)} %pad_add_fusion.place_ref.refs_0_, bf16[4,256,1536]{2,1,0:T(8,128)(2,1)} %all-to-all-done.1.own_ref.refs_1_.own_1, ...), custom_call_target="tpu_custom_call" | custom-call | flops 1024 | bytes 1024 | tf_op jit(solution)/shard_map/mix_forward/pallas_call | solution.py:915
  144.7 4.4 all-gather.7.cloned.1.call-done.w_out_ref
  152.4 4.0 all-to-all-start.3
  157.1 17.5 %gate_forward.2 = (f32[2,4,256,384]{3,2,1,0:T(8,128)}, f32[2,4,256,384]{3,2,1,0:T(8,128)}, bf16[4,2,256,768]{3,2,1,0:T(8,128)(2,1)}, bf16[4,2,256,768]{3,2,1,0:T(8,128)(2,1)}, f32[2,4,8,256]{3,2,1,0:T(8,128)}) custom-call(s32[2]{0:T(128)} %pad_add_fusion.place_ref.refs_0_, bf16[4,256,1536]{2,1,0:T(8,128)(2,1)} %all_to_all.65.own_ref.refs_1_.own_0, ...), custom_call_target="tpu_custom_call" | custom-call | flops 1024 | bytes 1024 | tf_op jit(solution)/shard_map/gate_forward/pallas_call | solution.py:915
  190.0 4.3 all-to-all-start.4
  194.4 17.6 %gate_backward.2 = (bf16[2,4,256,384]{3,2,1,0:T(8,128)(2,1)}, bf16[2,4,256,384]{3,2,1,0:T(8,128)(2,1)}, f32[8,384]{1,0:T(8,128)}, f32[768,1536]{1,0:T(8,128)}) custom-call(s32[2]{0:T(128)} %pad_add_fusion.place_ref.refs_0_, bf16[4,256,1536]{2,1,0:T(8,128)(2,1)} %all_to_all.65.own_ref.refs_1_.own_0, ...), custom_call_target="tpu_custom_call" | custom-call | flops 1024 | bytes 1024 | tf_op jit(solution)/shard_map/gate_backward/pallas_call | solution.py:915
  212.1 4.3 fusion.13
  216.4 4.2 all-to-all-start.5
  220.6 17.5 %gate_forward.3 = (f32[2,4,256,384]{3,2,1,0:T(8,128)}, f32[2,4,256,384]{3,2,1,0:T(8,128)}, bf16[4,2,256,768]{3,2,1,0:T(8,128)(2,1)}, bf16[4,2,256,768]{3,2,1,0:T(8,128)(2,1)}, f32[2,4,8,256]{3,2,1,0:T(8,128)}) custom-call(s32[2]{0:T(128)} %pad_add_fusion.place_ref.refs_0_, bf16[4,256,1536]{2,1,0:T(8,128)(2,1)} %all-to-all-done.1.own_ref.refs_1_.own_1, ...), custom_call_target="tpu_custom_call" | custom-call | flops 1024 | bytes 1024 | tf_op jit(solution)/shard_map/gate_forward/pallas_call | solution.py:915
  252.3 4.4 all-to-all-start.6
  256.8 19.2 %gate_backward.3 = (bf16[2,4,256,384]{3,2,1,0:T(8,128)(2,1)}, bf16[2,4,256,384]{3,2,1,0:T(8,128)(2,1)}, f32[8,384]{1,0:T(8,128)}, bf16[4,768,384]{2,1,0:T(8,128)(2,1)}) custom-call(s32[2]{0:T(128)} %pad_add_fusion.place_ref.refs_0_, bf16[4,256,1536]{2,1,0:T(8,128)(2,1)} %all-to-all-done.1.own_ref.refs_1_.own_1, ...), custom_call_target="tpu_custom_call" | custom-call | flops 1024 | bytes 1024 | tf_op jit(solution)/shard_map/gate_backward/pallas_call | solution.py:915
  276.0 4.3 add_convert_fusion.2
  280.3 4.8 all-to-all-start.7
  285.2 54.8 %mix_backward.2 = (f32[400,1536]{1,0:T(8,128)}, f32[2,4,272,128]{3,2,1,0:T(8,128)}, f32[8,384]{1,0:T(8,128)}, f32[8,384]{1,0:T(8,128)}, bf16[4,2,304,768]{3,2,1,...) custom-call(s32[2]{0:T(128)} %pad_add_fusion.place_ref.refs_0_, bf16[4,256,1536]{2,1,0:T(8,128)(2,1)} %all_to_all.65.own_ref.refs_1_.own_0, ...), custom_call_target="tpu_custom_call" | custom-call | flops 1024 | bytes 1024 | tf_op jit(solution)/shard_map/mix_backward/pallas_call | solution.py:915
  340.1 6.7 %collective-permute-done.15 = bf16[4,2,304,768]{3,2,1,0:T(8,128)(2,1)S(1)} collective-permute-done((bf16[4,2,304,768]{3,2,1,0:T(8,128)(2,1)}, bf16[4,2,304,768]{3,2,1,0:T(8,128)(2,1)S(1)}, u32[]{:S(2)}, u32[]{:S(2)}) %collective-permute-start.15) | collective-permute-done | bytes 3735584 | tf_op jit(solution)/shard_map/ppermute | solution.py:1282
  346.8 4.8 add_convert_fusion
  351.5 4.8 all-to-all-start.8
  356.6 55.2 %mix_backward.3 = (bf16[4,400,384]{2,1,0:T(8,128)(2,1)}, bf16[4,2,272,128]{3,2,1,0:T(8,128)(2,1)}, bf16[4,2,272,128]{3,2,1,0:T(8,128)(2,1)}, f32[2,4,272,128]{3,...) custom-call(s32[2]{0:T(128)} %pad_add_fusion.place_ref.refs_0_, ...), custom_call_target="tpu_custom_call" | custom-call | flops 1024 | bytes 1024 | tf_op jit(solution)/shard_map/mix_backward/pallas_call | solution.py:915
  429.2 4.2 all-to-all-start.9
  433.4 5.3 add_convert_fusion.1
  443.1 4.9 all-to-all-start.10
  453.1 3.7 convert_reduce_fusion.1
  456.8 6.0 %maps_backward.1 = (bf16[2,2,256,128]{3,2,1,0:T(8,128)(2,1)}, bf16[4,128,384]{2,1,0:T(8,128)(2,1)}, f32[8,128]{1,0:T(8,128)}) custom-call(s32[2]{0:T(128)} %pad_add_fusion.place_ref.refs_0_, bf16[4,2,48,768]{3,2,1,0:T(8,128)(2,1)} %slice.151.packed_ref, bf16[4,2,272,128]{3,2,1,0:T(8,128)(2,1)} %copy-done.11, f32[2,4,272,128]{3,2,1,0:T(8,128)} %get-tuple-element.222.slope_0, ...), custom_call_target="tpu_custom_call" | custom-call | flops 1024 | bytes 1024 | tf_op jit(solution)/shard_map/maps_backward/pallas_call | solution.py:1152
  469.1 15.6 %collective-permute-done.24 = f32[80,128]{1,0:T(8,128)S(1)} collective-permute-done((f32[80,128]{1,0:T(8,128)S(1)}, f32[80,128]{1,0:T(8,128)S(1)}, u32[]{:S(2)}, u32[]{:S(2)}) %collective-permute-start.24) | collective-permute-done | bytes 40992 | tf_op jit(solution)/shard_map/ppermute | solution.py:1286
  515.7 4.3 all-to-all-start.11
  522.5 4.1 maximum_add_fusion
  550.1 7.9 %fusion.11 = (bf16[2,2,256,768]{3,2,1,0:T(8,128)(2,1)}, bf16[2,2,256,768]{3,2,1,0:T(8,128)(2,1)}) fusion(bf16[2,2,256,768]{3,2,1,0:T(8,128)(2,1)S(1)} %copy-done.3, bf16[2,2,256,768]{3,2,1,0:T(8,128)(2,1)} %param.23, f32[2,2,256,768]{3,2,1,0:T(8,128)} %maximum_add_fusion, f32[2,2,256]{2,1,0:T(2,128)S(1)} %get-tuple-element.346, ...), kind=kLoop, calls=%fused_computation.25 | loop fusion | flops 11796480 | bytes 12594177 | tf_op jit(solution)/shard_map/convert_element_type | solution.py:1580
  559.6 4.9 owner_update.1
  (303 shorter events, 157.9 us)
Async XLA Ops:
  7.2 70.1 %all-gather.5.cloned.1.call-start = ((), (), s32[]{:S(2)}) async-start(), calls=%async_computation.15 | async-start | bytes 2949120 | tf_op jit(solution)/shard_map/all_gather | solution.py:1367
  61.8 15.5 %collective-permute-start.2 = (bf16[4,256,1536]{2,1,0:T(8,128)(2,1)}, bf16[4,256,1536]{2,1,0:T(8,128)(2,1)}, u32[]{:S(2)}, u32[]{:S(2)}) collective-permute-start(bf16[4,256,1536]{2,1,0:T(8,128)(2,1)} %all_to_all.65.own_ref.refs_1_.own_0), channel_id=1, source_target_pairs={{0,1},{1,0},{2,3},{3,2},{4,5},{5,4},{6,7},{7,6},{8,9},{9,8},{10,11... | collective-permute-start | bytes 9437192 | tf_op jit(solution)/shard_map/ppermute | solution.py:1282
  63.7 43.5 %all-to-all-start.1 = ((bf16[4,256,1536]{2,1,0:T(8,128)(2,1)}), bf16[4,256,1536]{2,1,0:T(8,128)(2,1)}, u32[]{:S(2)}, u32[]{:S(2)}) async-start(bf16[4,256,1536]{2,1,0:T(8,128)(2,1)} %broadcast_in_dim.77), calls=%async_computation.1 | async-start | bytes 6291456 | tf_op jit(solution)/shard_map/all_to_all | solution.py:1294
  68.5 38.7 %all-gather.9.cloned.1.call-start = ((), (), s32[]{:S(2)}) async-start(), calls=%async_computation.19 | async-start | bytes 1474560 | tf_op jit(solution)/shard_map/all_gather | solution.py:1367
  69.6 7.2 %collective-permute-start.1 = (bf16[2,256,768]{2,1,0:T(8,128)(2,1)}, bf16[2,256,768]{2,1,0:T(8,128)(2,1)S(1)}, u32[]{:S(2)}, u32[]{:S(2)}) collective-permute-start(bf16[2,256,768]{2,1,0:T(8,128)(2,1)} %get-tuple-element.333), channel_id=1, source_target_pairs={{0,1},{1,0},{2,3},{3,2},{4,5},{5,4},{6,7},{7,6},{8,9},{9,8},{10,11... | collective-permute-start | bytes 2359304 | tf_op jit(solution)/shard_map/ppermute | solution.py:1282
  107.2 7.8 %collective-permute-start.3 = (bf16[4,256,1536]{2,1,0:T(8,128)(2,1)}, bf16[4,256,1536]{2,1,0:T(8,128)(2,1)}, u32[]{:S(2)}, u32[]{:S(2)}) collective-permute-start(bf16[4,256,1536]{2,1,0:T(8,128)(2,1)} %all-to-all-done.1.own_ref.refs_1_.own_1), channel_id=1, source_target_pairs={{0,1},{1,0},{2,3},{3,2},{4,5},{5,4},{6,7},{7,6},{8,9},{9,8},{10,11... | collective-permute-start | bytes 9437192 | tf_op jit(solution)/shard_map/ppermute | solution.py:1282
  109.3 41.8 %all-to-all-start.2 = ((bf16[4,256,1536]{2,1,0:T(8,128)(2,1)}), bf16[4,256,1536]{2,1,0:T(8,128)(2,1)}, u32[]{:S(2)}, u32[]{:S(2)}) async-start(bf16[4,256,1536]{2,1,0:T(8,128)(2,1)} %broadcast_in_dim.81), calls=%async_computation.2 | async-start | bytes 6291456 | tf_op jit(solution)/shard_map/all_to_all | solution.py:1294
  114.0 35.1 %all-gather.7.cloned.1.call-start = ((), (), s32[]{:S(2)}) async-start(), calls=%async_computation.16 | async-start | bytes 1474560 | tf_op jit(solution)/shard_map/all_gather | solution.py:1367
  152.4 24.2 %all-to-all-start.3 = ((bf16[4,128,1536]{2,1,0:T(8,128)(2,1)}), bf16[4,128,1536]{2,1,0:T(8,128)(2,1)S(1)}, u32[]{:S(2)}, u32[]{:S(2)}) async-start(bf16[4,128,1536]{2,1,0:T(8,128)(2,1)} %broadcast_in_dim.84), calls=%async_computation.3 | async-start | bytes 3145728 | tf_op jit(solution)/shard_map/all_to_all | solution.py:1294
  178.9 33.1 %collective-permute-start.9 = (bf16[4,2,256,768]{3,2,1,0:T(8,128)(2,1)}, bf16[4,2,256,768]{3,2,1,0:T(8,128)(2,1)}, u32[]{:S(2)}, u32[]{:S(2)}) collective-permute-start(bf16[4,2,256,768]{3,2,1,0:T(8,128)(2,1)} %get-tuple-element.159), channel_id=1, source_target_pairs={{0,1},{1,0},{2,3},{3,2},{4,5},{5,4},{6,7},{7,6},{8,9},{9,8},{10,11... | collective-permute-start | bytes 9437192 | tf_op jit(solution)/shard_map/ppermute | solution.py:1282
  179.1 37.2 %collective-permute-start.5 = (bf16[4,128,1536]{2,1,0:T(8,128)(2,1)S(1)}, bf16[4,128,1536]{2,1,0:T(8,128)(2,1)}, u32[]{:S(2)}, u32[]{:S(2)}) collective-permute-start(bf16[4,128,1536]{2,1,0:T(8,128)(2,1)S(1)} %all-to-all-done.3.cot_own_0.refs_3_), channel_id=1, source_target_pairs={{0,1},{1,0},{2,3},{3,2},{4,5},{5,4},{6,7},{7,6},{8,9},{9,8},{10,11... | collective-permute-start | bytes 4718600 | tf_op jit(solution)/shard_map/ppermute | solution.py:1282
  190.0 26.3 %all-to-all-start.4 = ((bf16[4,128,1536]{2,1,0:T(8,128)(2,1)}), bf16[4,128,1536]{2,1,0:T(8,128)(2,1)}, u32[]{:S(2)}, u32[]{:S(2)}) async-start(bf16[4,128,1536]{2,1,0:T(8,128)(2,1)} %broadcast_in_dim.85), calls=%async_computation.4 | async-start | bytes 3145728 | tf_op jit(solution)/shard_map/all_to_all | solution.py:1294
  216.4 24.1 %all-to-all-start.5 = ((bf16[4,256,768]{2,1,0:T(8,128)(2,1)}), bf16[4,256,768]{2,1,0:T(8,128)(2,1)S(1)}, u32[]{:S(2)}, u32[]{:S(2)}) async-start(bf16[4,256,768]{2,1,0:T(8,128)(2,1)} %get-tuple-element.163), calls=%async_computation.5 | async-start | bytes 3145728 | tf_op jit(solution)/shard_map/all_to_all | solution.py:1294
  242.8 33.2 %collective-permute-start.14 = (bf16[4,2,256,768]{3,2,1,0:T(8,128)(2,1)}, bf16[4,2,256,768]{3,2,1,0:T(8,128)(2,1)}, u32[]{:S(2)}, u32[]{:S(2)}) collective-permute-start(bf16[4,2,256,768]{3,2,1,0:T(8,128)(2,1)} %get-tuple-element.176), channel_id=1, source_target_pairs={{0,1},{1,0},{2,3},{3,2},{4,5},{5,4},{6,7},{7,6},{8,9},{9,8},{10,11... | collective-permute-start | bytes 9437192 | tf_op jit(solution)/shard_map/ppermute | solution.py:1282
  252.3 28.0 %all-to-all-start.6 = ((bf16[4,256,768]{2,1,0:T(8,128)(2,1)}), bf16[4,256,768]{2,1,0:T(8,128)(2,1)}, u32[]{:S(2)}, u32[]{:S(2)}) async-start(bf16[4,256,768]{2,1,0:T(8,128)(2,1)} %get-tuple-element.173), calls=%async_computation.6 | async-start | bytes 3145728 | tf_op jit(solution)/shard_map/all_to_all | solution.py:1294
  256.7 83.3 %reduce-scatter.3.cloned.1.call-start = ((), (), s32[]{:S(2)}) async-start(), calls=%async_computation.17 | async-start | bytes 2949120 | tf_op jit(solution)/shard_map/reduce_scatter | solution.py:1431
  280.3 59.6 %all-to-all-start.7 = ((bf16[4,2,256,768]{3,2,1,0:T(8,128)(2,1)}), bf16[4,2,256,768]{3,2,1,0:T(8,128)(2,1)}, u32[]{:S(2)}, u32[]{:S(2)}) async-start(bf16[4,2,256,768]{3,2,1,0:T(8,128)(2,1)} %add_convert_fusion.2), calls=%async_computation.7 | async-start | bytes 6291456 | tf_op jit(solution)/shard_map/all_to_all | solution.py:1294
  340.0 6.8 %collective-permute-start.15 = (bf16[4,2,304,768]{3,2,1,0:T(8,128)(2,1)}, bf16[4,2,304,768]{3,2,1,0:T(8,128)(2,1)S(1)}, u32[]{:S(2)}, u32[]{:S(2)}) collective-permute-start(bf16[4,2,304,768]{3,2,1,0:T(8,128)(2,1)} %get-tuple-element.193), channel_id=1, source_target_pairs={{0,1},{1,0},{2,3},{3,2},{4,5},{5,4},{6,7},{7,6},{8,9},{9,8},{10,11... | collective-permute-start | bytes 11206664 | tf_op jit(solution)/shard_map/ppermute | solution.py:1282
  351.5 60.3 %all-to-all-start.8 = ((bf16[4,2,304,768]{3,2,1,0:T(8,128)(2,1)}), bf16[4,2,304,768]{3,2,1,0:T(8,128)(2,1)}, u32[]{:S(2)}, u32[]{:S(2)}) async-start(bf16[4,2,304,768]{3,2,1,0:T(8,128)(2,1)} %add_convert_fusion), calls=%async_computation.9 | async-start | bytes 7471104 | tf_op jit(solution)/shard_map/all_to_all | solution.py:1294
  356.3 145.0 %reduce-scatter.5.cloned.1.call-start = ((), (), s32[]{:S(2)}) async-start(), calls=%async_computation.18 | async-start | bytes 1536000 | tf_op jit(solution)/shard_map/reduce_scatter | solution.py:1431
  416.1 17.3 %collective-permute-start.17 = (bf16[4,2,256,768]{3,2,1,0:T(8,128)(2,1)}, bf16[4,2,256,768]{3,2,1,0:T(8,128)(2,1)}, u32[]{:S(2)}, u32[]{:S(2)}) collective-permute-start(bf16[4,2,256,768]{3,2,1,0:T(8,128)(2,1)} %get-tuple-element.217), channel_id=1, source_target_pairs={{0,1},{1,0},{2,3},{3,2},{4,5},{5,4},{6,7},{7,6},{8,9},{9,8},{10,11... | collective-permute-start | bytes 9437192 | tf_op jit(solution)/shard_map/ppermute | solution.py:1282
  429.2 13.1 %all-to-all-start.9 = ((bf16[4,2,272,128]{3,2,1,0:T(8,128)(2,1)}), bf16[4,2,272,128]{3,2,1,0:T(8,128)(2,1)S(1)}, u32[]{:S(2)}, u32[]{:S(2)}) async-start(bf16[4,2,272,128]{3,2,1,0:T(8,128)(2,1)} %add_convert_fusion.5), calls=%async_computation.10 | async-start | bytes 1114112 | tf_op jit(solution)/shard_map/all_to_all | solution.py:1294
  443.1 58.2 %all-to-all-start.10 = ((bf16[4,2,256,768]{3,2,1,0:T(8,128)(2,1)}), bf16[4,2,256,768]{3,2,1,0:T(8,128)(2,1)}, u32[]{:S(2)}, u32[]{:S(2)}) async-start(bf16[4,2,256,768]{3,2,1,0:T(8,128)(2,1)} %add_convert_fusion.1), calls=%async_computation.11 | async-start | bytes 6291456 | tf_op jit(solution)/shard_map/all_to_all | solution.py:1294
  465.8 18.9 %collective-permute-start.24 = (f32[80,128]{1,0:T(8,128)S(1)}, f32[80,128]{1,0:T(8,128)S(1)}, u32[]{:S(2)}, u32[]{:S(2)}) collective-permute-start(f32[80,128]{1,0:T(8,128)S(1)} %pad_bitcast_fusion), channel_id=1, source_target_pairs={{0,2},{2,0},{4,6},{6,4},{1,3},{3,1},{5,7},{7,5},{8,10},{10,8},{12,... | collective-permute-start | bytes 122888 | tf_op jit(solution)/shard_map/ppermute | solution.py:1286
  484.7 6.2 %collective-permute-start.25 = (f32[80,128]{1,0:T(8,128)S(1)}, f32[80,128]{1,0:T(8,128)S(1)}, u32[]{:S(2)}, u32[]{:S(2)}) collective-permute-start(f32[80,128]{1,0:T(8,128)S(1)} %fusion.42), channel_id=1, source_target_pairs={{0,4},{2,6},{4,0},{6,2},{1,5},{3,7},{5,1},{7,3},{8,12},{10,14},{12... | collective-permute-start | bytes 122888 | tf_op jit(solution)/shard_map/ppermute | solution.py:1290
  486.3 11.3 %collective-permute-start.20 = (bf16[128,384]{1,0:T(8,128)(2,1)S(1)}, bf16[128,384]{1,0:T(8,128)(2,1)S(1)}, u32[]{:S(2)}, u32[]{:S(2)}) collective-permute-start(bf16[128,384]{1,0:T(8,128)(2,1)S(1)} %get-tuple-element.339), channel_id=1, source_target_pairs={{0,24},{8,0},{16,8},{24,16},{1,25},{9,1},{17,9},{25,17},{2,26},{10... | collective-permute-start | bytes 294920 | tf_op jit(solution)/shard_map/ppermute | solution.py:1537
  489.9 7.8 %collective-permute-start.19 = (bf16[128,384]{1,0:T(8,128)(2,1)S(1)}, bf16[128,384]{1,0:T(8,128)(2,1)S(1)}, u32[]{:S(2)}, u32[]{:S(2)}) collective-permute-start(bf16[128,384]{1,0:T(8,128)(2,1)S(1)} %get-tuple-element.340), channel_id=1, source_target_pairs={{0,16},{8,24},{16,0},{24,8},{1,17},{9,25},{17,1},{25,9},{2,18},{10... | collective-permute-start | bytes 294920 | tf_op jit(solution)/shard_map/ppermute | solution.py:1537
  489.9 7.8 %collective-permute-start.18 = (bf16[128,384]{1,0:T(8,128)(2,1)S(1)}, bf16[128,384]{1,0:T(8,128)(2,1)S(1)}, u32[]{:S(2)}, u32[]{:S(2)}) collective-permute-start(bf16[128,384]{1,0:T(8,128)(2,1)S(1)} %get-tuple-element.338), channel_id=1, source_target_pairs={{0,8},{8,16},{16,24},{24,0},{1,9},{9,17},{17,25},{25,1},{2,10},{10... | collective-permute-start | bytes 294920 | tf_op jit(solution)/shard_map/ppermute | solution.py:1537
  495.6 18.3 %collective-permute-start.21 = (bf16[2,2,256,128]{3,2,1,0:T(8,128)(2,1)}, bf16[2,2,256,128]{3,2,1,0:T(8,128)(2,1)S(1)}, u32[]{:S(2)}, u32[]{:S(2)}) collective-permute-start(bf16[2,2,256,128]{3,2,1,0:T(8,128)(2,1)} %get-tuple-element.226), channel_id=1, source_target_pairs={{0,1},{1,0},{2,3},{3,2},{4,5},{5,4},{6,7},{7,6},{8,9},{9,8},{10,11... | collective-permute-start | bytes 786440 | tf_op jit(solution)/shard_map/ppermute | solution.py:1282
  504.1 11.6 %all-to-all-start.12 = ((bf16[4,96,528]{2,1,0:T(8,128)(2,1)}), bf16[4,96,528]{2,1,0:T(8,128)(2,1)S(1)}, u32[]{:S(2)}, u32[]{:S(2)}) async-start(bf16[4,96,528]{2,1,0:T(8,128)(2,1)} %bitcast.40), calls=%async_computation.14 | async-start | bytes 983040 | tf_op jit(solution)/shard_map/all_to_all | solution.py:1435
  515.7 14.0 %all-to-all-start.11 = ((bf16[4,96,768]{2,1,0:T(8,128)(2,1)}), bf16[4,96,768]{2,1,0:T(8,128)(2,1)}, u32[]{:S(2)}, u32[]{:S(2)}) async-start(bf16[4,96,768]{2,1,0:T(8,128)(2,1)} %bitcast.38), calls=%async_computation.13 | async-start | bytes 1179648 | tf_op jit(solution)/shard_map/all_to_all | solution.py:1435
  548.6 9.4 %collective-permute-start.32 = (f32[16,128]{1,0:T(8,128)S(1)}, f32[16,128]{1,0:T(8,128)S(1)}, u32[]{:S(2)}, u32[]{:S(2)}) collective-permute-start(f32[16,128]{1,0:T(8,128)S(1)} %add.324), channel_id=1, source_target_pairs={{0,16},{8,24},{16,0},{24,8},{1,17},{9,25},{17,1},{25,9},{2,18},{10... | collective-permute-start | bytes 24584 | tf_op jit(solution)/shard_map/ppermute | solution.py:1634
  (57 other events, 627.9 us)
Sparse Core Ops, SparseCore 0:
  15.2 52.8 all-gather.4
  71.9 31.7 all-gather.8
  117.0 32.0 all-gather.6
  280.5 49.6 reduce-scatter.2
  425.6 31.8 reduce-scatter.4

commit v3 on v2

--- a/solution.py
+++ b/solution.py
@@ -412,8 +412,10 @@
 PART = 128
 PARTS = SPAN // PART
 PACKED = 48
+LOG2E = 1.4426950408889634
 QUARTER = 384
 QHEADS = 6
+MAPS_AT = 3 * QUARTER
 BF = jnp.bfloat16
 F32 = jnp.float32
 ROUTE_X = [(i, i ^ 1) for i in range(BLOCKS)]
@@ -442,10 +444,6 @@
 
 def sigmoid(v):
     return 1.0 / (1.0 + jnp.exp(-v))
-
-
-def pair_cols(table, k, low_half):
-    return jnp.where(low_half, table[:, 2 * k : 2 * k + 1], table[:, 2 * k + 1 : 2 * k + 2])
 
 
 def split_sum(triangle, table):
@@ -459,13 +457,33 @@
         + pltpu.roll(third.astype(F32), 16, 1)
     )
     sums = dot_nn(triangle, parts.astype(BF))
-    return sums + pltpu.roll(sums, 120, 1) + pltpu.roll(sums, 112, 1)
+    sums = sums + pltpu.roll(sums, 120, 1) + pltpu.roll(sums, 112, 1)
+    lanes = lax.broadcasted_iota(jnp.int32, sums.shape, 1)
+    return jnp.where(lanes < 8, sums, 0.0)
 
 
 def head_sums(table, gather):
     first = table.astype(BF)
     second = (table - first.astype(F32)).astype(BF)
     return dot_nn(first, gather) + dot_nn(second, gather)
+
+
+def head_spread():
+    lane = lax.broadcasted_iota(jnp.int32, (128, QUARTER), 0)
+    chan = lax.broadcasted_iota(jnp.int32, (128, QUARTER), 1)
+    base = jnp.where(lane < 8, lane, jnp.where(lane < 16, lane - 8, -1)) * HEADDIM
+    return jnp.where((chan >= base) & (chan < base + HEADDIM) & (base >= 0), 1.0, 0.0).astype(BF)
+
+
+def spread_heads(tables, spread):
+    packed = []
+    for table in tables:
+        lanes = lax.broadcasted_iota(jnp.int32, table.shape, 1)
+        table = jnp.where(lanes < 8, table, 0.0)
+        first = table.astype(BF).astype(F32)
+        packed.append((first + pltpu.roll(table - first, 8, 1)).astype(BF))
+    wide = dot_nn(jnp.concatenate(packed, axis=0), spread)
+    return [wide[PART * k : PART * (k + 1)] for k in range(len(tables))]
 
 
 def rates(raw, head):
@@ -481,21 +499,39 @@
     return jnp.where(keep(rows_at, cols_at), 1.0, 0.0).astype(BF)
 
 
-def part_terms(step, head, cols, segr):
-    cum = split_sum(triangle(lambda r, c: r >= c), -step * head[1:2])
+def part_terms(step, head, cols, segr, lower):
+    cum = split_sum(lower, -step * head[1:2]) * LOG2E
     last = cum[PART - 1 : PART]
-    enter = jnp.exp(cum) * cols[:, 4:5]
-    leave = jnp.exp(last - cum) * cols[:, 5:6]
-    passing = jnp.exp(last) * cols[PART - 1 : PART, 4:5]
+    enter = jnp.exp2(cum) * cols[:, 4:5]
+    leave = jnp.exp2(last - cum) * cols[:, 5:6]
+    passing = jnp.exp2(last) * cols[PART - 1 : PART, 4:5]
     rows_at = lax.broadcasted_iota(jnp.int32, (PART, PART), 0)
     cols_at = lax.broadcasted_iota(jnp.int32, (PART, PART), 1)
     allowed = (rows_at >= cols_at) & (cols[:, 6:7] == segr)
     return cum, enter, leave, passing, jnp.where(allowed, 0.0, -1e30)
 
 
-def segment_flags(seg_ref, block):
+def head_decay(cum, cum_t, h, block_out):
+    return jnp.exp2(cum[:, h : h + 1] - cum_t[h : h + 1] + block_out)
+
+
+def by_head(table, low_half):
+    zero = jnp.zeros_like(table)
+    return jnp.concatenate(
+        [jnp.where(low_half, table, zero), jnp.where(low_half, zero, table)], axis=0
+    )
+
+
+def pass_state(passing, state, added):
+    heads = [slice(HEADDIM * h, HEADDIM * (h + 1)) for h in range(QHEADS)]
+    return jnp.concatenate(
+        [passing[:, h : h + 1] * state[at] + added[at] for h, at in enumerate(heads)], axis=0
+    )
+
+
+def segment_flags(seg_ref, q, block):
     begin = pl.multiple_of(block * SPAN, 128)
-    around = seg_ref[0, :, pl.ds(begin, SPAN + 256)]
+    around = seg_ref[q, :, pl.ds(begin, SPAN + 256)]
     here = around[:, 128 : 128 + SPAN]
     flags = []
     for shift in (3, 2, 1, 0):
@@ -523,83 +559,84 @@
     return filled.T
 
 
-def current(own_ref, other_ref):
-    return jnp.where(pl.program_id(0) == 0, own_ref[0], other_ref[0])
-
-
-def current_halves(own_refs, other_refs):
-    halves = [current(own, other) for own, other in zip(own_refs, other_refs)]
-    return jnp.concatenate(halves, axis=0)
+def both_tokens(own_ref, other_ref):
+    return jnp.concatenate([own_ref[0], other_ref[0]], axis=0)
 
 
 def fwd_kernel(
-    place_ref, own_ref, other_ref, w_ref, seg_ref, taps_ref, head_ref, chan_ref, mixed_ref, raw_ref, pre_ref, y_ref, hin_ref, buf, state,
+    place_ref, own_ref, other_ref, w_ref, seg_ref, taps_ref, head_ref, chan_ref,
+    mixed_ref, raw_ref, pre_ref, y_ref, hin_ref, buf, state,
 ):
-    @pl.when(pl.program_id(1) == 0)
+    block = pl.program_id(0)
+
+    @pl.when(block == 0)
     def _():
-        buf[0:8] = jnp.zeros((8, buf.shape[1]), F32)
+        buf[:, 0:8] = jnp.zeros((2, 8, buf.shape[2]), F32)
         state[...] = jnp.zeros_like(state)
 
     width = QUARTER + 2 * STATE
-    projected = dot_nn(current(own_ref, other_ref), w_ref[...])
-    raw = projected[:, width:]
-    raw_ref[0, 0] = raw
-    mixed_low = projected[:, :width].astype(BF)
-    mixed_ref[0, 0] = mixed_low
-    mixed = mixed_low.astype(F32)
-    buf[8 : 8 + SPAN] = mixed
-    rows = segment_flags(seg_ref, pl.program_id(1))
-    cols_all = to_columns(rows)
+    projected = dot_nn(both_tokens(own_ref, other_ref), w_ref[...])
     taps = taps_ref[...]
     head = head_ref[...]
-    pre = jnp.broadcast_to(taps[CONV : CONV + 1], mixed.shape)
-    for j in range(CONV):
-        window = mixed if j == CONV - 1 else buf[5 + j : 5 + j + SPAN]
-        pre = pre + taps[j : j + 1] * (window * cols_all[:, j : j + 1])
-    buf[0:8] = mixed[SPAN - 8 :]
-    pre_ref[0, 0] = pre
-    act = pre * sigmoid(pre)
-    _, step_all = rates(raw, head)
     skip = chan_ref[1:2]
+    lower = triangle(lambda r, c: r >= c)
+    spread = head_spread()
     low_half = lax.broadcasted_iota(jnp.int32, (PART, 128), 1) < HEADDIM
-    zero_low = jnp.zeros((PART, 128), BF)
-    for part in range(SPAN // PART):
-        at_rows = slice(part * PART, (part + 1) * PART)
-        cols = cols_all[at_rows]
-        values = act[at_rows, :QUARTER]
-        b_low = act[at_rows, QUARTER : QUARTER + STATE].astype(BF)
-        c_low = act[at_rows, QUARTER + STATE :].astype(BF)
-        step = step_all[at_rows]
-        cum, enter, leave, passing, block_out = part_terms(step, head, cols, rows[6:7, at_rows])
+    pieces = []
+    for q in range(2):
+        rows_q = slice(q * SPAN, (q + 1) * SPAN)
+        raw = projected[rows_q, width:]
+        raw_ref[q, 0] = raw
+        mixed_low = projected[rows_q, :width].astype(BF)
+        mixed_ref[q, 0] = mixed_low
+        mixed = mixed_low.astype(F32)
+        buf[q, 8 : 8 + SPAN] = mixed
+        rows = segment_flags(seg_ref, q, block)
+        cols_all = to_columns(rows)
+        pre = jnp.broadcast_to(taps[CONV : CONV + 1], mixed.shape)
+        for j in range(CONV):
+            window = mixed if j == CONV - 1 else buf[q, 5 + j : 5 + j + SPAN]
+            pre = pre + taps[j : j + 1] * (window * cols_all[:, j : j + 1])
+        buf[q, 0:8] = mixed[SPAN - 8 :]
+        pre_ref[q, 0] = pre
+        act = pre * sigmoid(pre)
+        _, step_all = rates(raw, head)
+        for part in range(PARTS):
+            at_rows = slice(part * PART, (part + 1) * PART)
+            cols = cols_all[at_rows]
+            cum, enter, leave, passing, block_out = part_terms(
+                step_all[at_rows], head, cols, rows[6:7, at_rows], lower
+            )
+            pieces.append(
+                (q, part, act[at_rows], step_all[at_rows], cum, enter, leave, passing, block_out)
+            )
+    work = []
+    for q, part, act, step, cum, enter, leave, passing, block_out in pieces:
+        values = act[:, :QUARTER]
+        b_low = act[:, QUARTER : QUARTER + STATE].astype(BF)
+        c_low = act[:, QUARTER + STATE :].astype(BF)
+        step_w, enter_w, leave_w = spread_heads((step, enter, leave), spread)
         cum_t = cum.T
         scores = dot_nt(c_low, b_low)
-        held_f = state[...]
-        held = held_f.astype(BF)
-        hin_ref[0, 0, QUARTER * part : QUARTER * (part + 1)] = held
-        carried = dot_nt(c_low, held)
-        tails = []
+        scaled = (step_w * values).astype(BF)
+        tail = (leave_w * scaled.astype(F32)).astype(BF)
+        added = dot_tn(tail, b_low)
+        own = []
         for k in range(QHEADS // 2):
             at = slice(128 * k, 128 * (k + 1))
-            scaled = (pair_cols(step, k, low_half) * values[:, at]).astype(BF)
-            weights = []
-            for h in (2 * k, 2 * k + 1):
-                decay = jnp.exp(cum[:, h : h + 1] - cum_t[h : h + 1] + block_out)
-                weights.append((scores * decay).astype(BF))
-            both = jnp.concatenate(
-                [jnp.where(low_half, scaled, zero_low), jnp.where(low_half, zero_low, scaled)],
-                axis=0,
-            )
-            own = dot_nn(jnp.concatenate(weights, axis=1), both)
-            y_ref[0, 0, at_rows, at] = (
-                own
-                + pair_cols(enter, k, low_half) * carried[:, at]
-                + skip[:, at] * values[:, at]
-            )
-            tails.append((pair_cols(leave, k, low_half) * scaled.astype(F32)).astype(BF))
-        added = dot_tn(jnp.concatenate(tails, axis=1), b_low)
-        for h in range(QHEADS):
-            at = slice(HEADDIM * h, HEADDIM * (h + 1))
-            state[at] = passing[:, h : h + 1] * held_f[at] + added[at]
+            weights = [
+                (scores * head_decay(cum, cum_t, h, block_out)).astype(BF)
+                for h in (2 * k, 2 * k + 1)
+            ]
+            own.append(dot_nn(jnp.concatenate(weights, axis=1), by_head(scaled[:, at], low_half)))
+        own = jnp.concatenate(own, axis=1) + skip * values
+        work.append((q, part, c_low, enter_w, passing, added, own))
+    for q, part, c_low, enter_w, passing, added, own in sorted(work, key=lambda item: item[1]):
+        held_f = state[q]
+        held = held_f.astype(BF)
+        hin_ref[q, 0, QUARTER * part : QUARTER * (part + 1)] = held
+        y_ref[q, 0, part * PART : (part + 1) * PART] = own + enter_w * dot_nt(c_low, held)
+        state[q] = pass_state(passing, held_f, added)
 
 
 def core_rows(place_ref):
@@ -611,36 +648,43 @@
 
 
 def gate_kernel(
-    place_ref, own_ref, other_ref, cot_own_0, cot_own_1, cot_other_0, cot_other_1, y_ref,
-    w_gate_ref, w_out_ref, chan_ref,
+    place_ref, own_ref, other_ref, cot_own_ref, cot_other_ref, y_ref, w_gate_ref, w_out_ref,
+    chan_ref,
     gate_ref, d_gated_ref, mine_ref, theirs_ref, stat_ref,
 ):
-    gate = dot_nn(current(own_ref, other_ref), w_gate_ref[...])
-    gate_ref[0, 0] = gate
-    gated_in = y_ref[0, 0] * (gate * sigmoid(gate))
-    weighted = gated_in * chan_ref[0:1]
-    gun = weighted.astype(BF)
-    cot = current_halves((cot_own_0, cot_own_1), (cot_other_0, cot_other_1))
-    d_gated = dot_nn(cot, w_out_ref[...])
-    d_gated_ref[0, 0] = d_gated
+    gate = dot_nn(both_tokens(own_ref, other_ref), w_gate_ref[...])
+    d_gated = dot_nn(both_tokens(cot_own_ref, cot_other_ref), w_out_ref[...])
+    guns = []
+    for q in range(2):
+        at = slice(q * SPAN, (q + 1) * SPAN)
+        gate_q = gate[at]
+        gate_ref[q, 0] = gate_q
+        d_gated_ref[q, 0] = d_gated[at]
+        gated_in = y_ref[q, 0] * (gate_q * sigmoid(gate_q))
+        weighted = gated_in * chan_ref[0:1]
+        guns.append(weighted.astype(BF))
+        square = jnp.sum(gated_in * gated_in, axis=1, keepdims=True)
+        cross = jnp.sum(d_gated[at] * weighted, axis=1, keepdims=True)
+        lanes = lax.broadcasted_iota(jnp.int32, (SPAN, 128), 1)
+        table = jnp.where(lanes == 0, square, jnp.where(lanes == 1, cross, 0.0))
+        stat_ref[q, 0] = table.T[0:2]
+    gun = jnp.concatenate(guns, axis=0)
     own, other = core_rows(place_ref)
-    mine_ref[0, 0] = dot_nt(gun, w_out_ref[own]).astype(BF)
-    theirs_ref[0, 0] = dot_nt(gun, w_out_ref[other]).astype(BF)
-    square = jnp.sum(gated_in * gated_in, axis=1, keepdims=True)
-    cross = jnp.sum(d_gated * weighted, axis=1, keepdims=True)
-    lanes = lax.broadcasted_iota(jnp.int32, (SPAN, 128), 1)
-    table = jnp.where(lanes == 0, square, jnp.where(lanes == 1, cross, 0.0))
-    stat_ref[0, 0] = table.T[0:8]
+    mine = dot_nt(gun, w_out_ref[own]).astype(BF)
+    theirs = dot_nt(gun, w_out_ref[other]).astype(BF)
+    for q in range(2):
+        mine_ref[0, q] = mine[q * SPAN : (q + 1) * SPAN]
+        theirs_ref[0, 1 - q] = theirs[q * SPAN : (q + 1) * SPAN]
 
 
 def start_sums(total, seed_ref):
-    @pl.when((pl.program_id(0) == 0) & (pl.program_id(1) == 0))
+    @pl.when(pl.program_id(0) == 0)
     def _():
         total[...] = jnp.zeros_like(total) if seed_ref is None else seed_ref[...]
 
 
 def finish_sums(total, out_ref):
-    @pl.when((pl.program_id(0) == 1) & (pl.program_id(1) == BLOCKS - 1))
+    @pl.when(pl.program_id(0) == BLOCKS - 1)
     def _():
         rows_of = out_ref.shape[2]
         for z in range(out_ref.shape[0]):
@@ -648,40 +692,45 @@
 
 
 def gate_back_first(*refs):
-    gate_back_step(*refs[:12], None, *refs[12:])
+    gate_back_step(*refs[:10], None, *refs[10:])
 
 
 def gate_back_last(*refs):
-    gate_back_step(*refs[:13], *refs[13:16], refs[17])
-    finish_sums(refs[17], refs[16])
+    gate_back_step(*refs[:11], *refs[11:14], refs[15])
+    finish_sums(refs[15], refs[14])
 
 
 def gate_back_step(
-    place_ref, own_ref, other_ref, cot_own_0, cot_own_1, cot_other_0, cot_other_1, y_ref,
-    gate_ref, d_gated_ref, stat_ref, chan_ref, seed_ref,
+    place_ref, own_ref, other_ref, cot_own_ref, cot_other_ref, y_ref, gate_ref, d_gated_ref,
+    stat_ref, chan_ref, seed_ref,
     dy_ref, d_gate_ref, g_gain_ref, g_ref,
 ):
     start_sums(g_ref, seed_ref)
     start_sums(g_gain_ref, None)
-    stat = to_columns(stat_ref[0, 0])
-    scale = lax.rsqrt(stat[:, 0:1] * (1.0 / INNER) + EPS)
-    pull = stat[:, 1:2] * (1.0 / INNER) * scale * scale * scale
-    gate = gate_ref[0, 0]
-    y = y_ref[0, 0]
-    sigma = sigmoid(gate)
-    gate_act = gate * sigma
-    gated_in = y * gate_act
-    scaled_gain = chan_ref[0:1] * scale
-    d_in = d_gated_ref[0, 0] * scaled_gain - gated_in * pull
-    dy_ref[0, 0] = (d_in * gate_act).astype(BF)
-    d_gate = (d_in * y * (sigma + gate_act * (1.0 - sigma))).astype(BF)
-    d_gate_ref[0, 0] = d_gate
-    gated = (gated_in * scaled_gain).astype(BF)
-    by_gain = d_gated_ref[0, 0] * gated_in * scale
-    g_gain_ref[0:1] += jnp.sum(by_gain, axis=0, keepdims=True)
-    cot = current_halves((cot_own_0, cot_own_1), (cot_other_0, cot_other_1))
-    g_ref[:QUARTER] += dot_tn(gated, cot)
-    g_ref[QUARTER:] += dot_tn(d_gate, current(own_ref, other_ref))
+    gateds = []
+    d_gates = []
+    for q in range(2):
+        stat = to_columns(stat_ref[q, 0])
+        scale = lax.rsqrt(stat[:, 0:1] * (1.0 / INNER) + EPS)
+        pull = stat[:, 1:2] * (1.0 / INNER) * scale * scale * scale
+        gate = gate_ref[q, 0]
+        y = y_ref[q, 0]
+        d_gated = d_gated_ref[q, 0]
+        sigma = sigmoid(gate)
+        gate_act = gate * sigma
+        gated_in = y * gate_act
+        scaled_gain = chan_ref[0:1] * scale
+        d_in = d_gated * scaled_gain - gated_in * pull
+        dy_ref[q, 0] = (d_in * gate_act).astype(BF)
+        d_gate = (d_in * y * (sigma + gate_act * (1.0 - sigma))).astype(BF)
+        d_gate_ref[q, 0] = d_gate
+        d_gates.append(d_gate)
+        gateds.append((gated_in * scaled_gain).astype(BF))
+        g_gain_ref[0:1] += jnp.sum(d_gated * gated_in * scale, axis=0, keepdims=True)
+    gated = jnp.concatenate(gateds, axis=0)
+    d_gate = jnp.concatenate(d_gates, axis=0)
+    g_ref[:QUARTER] += dot_tn(gated, both_tokens(cot_own_ref, cot_other_ref))
+    g_ref[QUARTER:] += dot_tn(d_gate, both_tokens(own_ref, other_ref))
 
 
 def bwd_first(*refs):
@@ -702,176 +751,178 @@
     buf, d_state, bc_edge, slope_edge, d_late,
 ):
     start_sums(g_ref, seed_ref)
-
-    @pl.when(pl.program_id(1) == 0)
+    block = BLOCKS - 1 - pl.program_id(0)
+
+    @pl.when(pl.program_id(0) == 0)
     def _():
-        buf[SPAN:] = jnp.zeros((8, QUARTER), F32)
+        buf[:, SPAN:] = jnp.zeros((2, 8, QUARTER), F32)
         d_state[...] = jnp.zeros_like(d_state)
         bc_edge[...] = jnp.zeros_like(bc_edge)
         slope_edge[...] = jnp.zeros_like(slope_edge)
-
-    @pl.when((pl.program_id(0) == 0) & (pl.program_id(1) == 0))
-    def _():
         gtap_ref[...] = jnp.zeros_like(gtap_ref)
         ghead_ref[...] = jnp.zeros_like(ghead_ref)
 
-    rows = segment_flags(seg_ref, BLOCKS - 1 - pl.program_id(1))
-    cols_all = to_columns(rows)
     head = head_ref[...]
     taps = taps_ref[...]
-    pre = pre_ref[0, 0]
-    sigma = sigmoid(pre)
-    act = pre * sigma
-    slope = sigma * (1.0 + pre * (1.0 - sigma))
+    skip = chan_ref[1:2]
     first_core = place_ref[0] == 0
-
-    def store(ref, first_row, rows):
+    low_half = lax.broadcasted_iota(jnp.int32, (PART, 128), 1) < HEADDIM
+    chan_at = lax.broadcasted_iota(jnp.int32, (QUARTER, 128), 0)
+    head_at = lax.broadcasted_iota(jnp.int32, (QUARTER, 128), 1)
+    gather = jnp.where(
+        (chan_at >= head_at * HEADDIM) & (chan_at < (head_at + 1) * HEADDIM), 1.0, 0.0
+    )
+    gather_low = gather.astype(BF)
+    lower = triangle(lambda r, c: r >= c)
+    upper = triangle(lambda r, c: r <= c)
+    spread = head_spread()
+
+    def store(ref, q, first_row, rows):
         if keep_ref is not None:
-            ref[0, 0, first_row : first_row + rows.shape[0]] = rows
+            ref[0, q, first_row : first_row + rows.shape[0]] = rows
             return
         for at in range(first_row, first_row + rows.shape[0], 16):
             group = at // PACKED
             row = SPAN + at % PACKED
-            ref[0, 0, row : row + 16, 128 * group : 128 * (group + 1)] = rows[
+            ref[0, q, row : row + 16, 128 * group : 128 * (group + 1)] = rows[
                 at - first_row : at - first_row + 16
             ]
 
     keep_at = mine_ref if keep_ref is None else keep_ref
     give_at = theirs_ref if give_ref is None else give_ref
-    slope_half = jnp.where(
-        first_core, slope[:, QUARTER : QUARTER + STATE], slope[:, QUARTER + STATE :]
-    )
-    slope_ref[0, 0, 0:SPAN] = slope_half
-    slope_ref[0, 0, SPAN : SPAN + 16] = slope_edge[...]
-    slope_edge[...] = slope_half[0:16]
-    if keep_ref is None:
-        for ref in (mine_ref, theirs_ref):
-            ref[0, 0, SPAN + 32 :, 640:] = jnp.zeros((16, 128), BF)
-    store(keep_at, SPAN, bc_edge[:, :STATE].astype(BF))
-    store(give_at, SPAN, bc_edge[:, STATE:].astype(BF))
-    shifted_all, step_all = rates(raw_ref[0, 0], head)
-    skip = chan_ref[1:2]
-    low_half = lax.broadcasted_iota(jnp.int32, (PART, 128), 1) < HEADDIM
-    zero_low = jnp.zeros((PART, 128), BF)
-    chan_at = lax.broadcasted_iota(jnp.int32, (QUARTER, 128), 0)
-    head_at = lax.broadcasted_iota(jnp.int32, (QUARTER, 128), 1)
-    gather = jnp.where(
-        (chan_at >= head_at * HEADDIM) & (chan_at < (head_at + 1) * HEADDIM), 1.0, 0.0
-    )
-    gather_low = gather.astype(BF)
-    upper = triangle(lambda r, c: r <= c)
-    for part in reversed(range(SPAN // PART)):
-        at_rows = slice(part * PART, (part + 1) * PART)
-        cols = cols_all[at_rows]
-        values = act[at_rows, :QUARTER]
-        b_low = act[at_rows, QUARTER : QUARTER + STATE].astype(BF)
-        c_low = act[at_rows, QUARTER + STATE :].astype(BF)
-        step = step_all[at_rows]
-        cum, enter, leave, passing, block_out = part_terms(step, head, cols, rows[6:7, at_rows])
+    pieces = []
+    columns = []
+    slopes = []
+    for q in range(2):
+        rows = segment_flags(seg_ref, q, block)
+        cols_all = to_columns(rows)
+        columns.append(cols_all)
+        pre = pre_ref[q, 0]
+        sigma = sigmoid(pre)
+        act = pre * sigma
+        slope = sigma * (1.0 + pre * (1.0 - sigma))
+        slopes.append(slope)
+        slope_half = jnp.where(
+            first_core, slope[:, QUARTER : QUARTER + STATE], slope[:, QUARTER + STATE :]
+        )
+        slope_ref[q, 0, 0:SPAN] = slope_half
+        slope_ref[q, 0, SPAN : SPAN + 16] = slope_edge[q]
+        slope_edge[q] = slope_half[0:16]
+        if keep_ref is None:
+            for ref in (mine_ref, theirs_ref):
+                ref[0, q, SPAN + 32 :, 640:] = jnp.zeros((16, 128), BF)
+        store(keep_at, q, SPAN, bc_edge[q, :, :STATE].astype(BF))
+        store(give_at, 1 - q, SPAN, bc_edge[q, :, STATE:].astype(BF))
+        shifted_all, step_all = rates(raw_ref[q, 0], head)
+        for part in range(PARTS):
+            at_rows = slice(part * PART, (part + 1) * PART)
+            terms = part_terms(
+                step_all[at_rows], head, cols_all[at_rows], rows[6:7, at_rows], lower
+            )
+            pieces.append((q, part, act[at_rows], shifted_all[at_rows], step_all[at_rows], terms))
+    work = []
+    for q, part, act, shifted_raw, step, terms in pieces:
+        cum, enter, leave, passing, block_out = terms
+        values = act[:, :QUARTER]
+        b_low = act[:, QUARTER : QUARTER + STATE].astype(BF)
+        c_low = act[:, QUARTER + STATE :].astype(BF)
+        step_w, enter_w, leave_w = spread_heads((step, enter, leave), spread)
         cum_t = cum.T
         scores = dot_nt(c_low, b_low)
-        held = hin_ref[0, 0, QUARTER * part : QUARTER * (part + 1)]
-        dy_low = dy_ref[0, 0, at_rows]
-        dy = dy_low.astype(F32)
-        d_after = d_state[...]
-        d_after_low = d_after.astype(BF)
-        from_after = dot_nt(b_low, d_after_low)
+        dy_low = dy_ref[q, 0, part * PART : (part + 1) * PART]
+        scaled = (step_w * values).astype(BF)
+        tail = (leave_w * scaled.astype(F32)).astype(BF)
+        enter_dy = (enter_w * dy_low.astype(F32)).astype(BF)
         d_scores = jnp.zeros((PART, PART), F32)
-        d_scaled_all = []
-        scaled_all = []
-        tail_terms = []
-        tails = []
-        entering = []
+        own = []
         for k in range(QHEADS // 2):
             at = slice(128 * k, 128 * (k + 1))
-            step_k = pair_cols(step, k, low_half)
-            scaled = (step_k * values[:, at]).astype(BF)
-            scaled_f = scaled.astype(F32)
-            dy_k = dy_low[:, at]
-            dy_both = jnp.concatenate(
-                [jnp.where(low_half, dy_k, zero_low), jnp.where(low_half, zero_low, dy_k)],
-                axis=0,
-            )
-            d_weights = dot_nt(dy_both, scaled)
+            dy_both = by_head(dy_low[:, at], low_half)
+            d_weights = dot_nt(dy_both, scaled[:, at])
             weights = []
-            for at_h, h in enumerate((2 * k, 2 * k + 1)):
-                decay = jnp.exp(cum[:, h : h + 1] - cum_t[h : h + 1] + block_out)
+            for half, h in enumerate((2 * k, 2 * k + 1)):
+                decay = head_decay(cum, cum_t, h, block_out)
                 weights.append((scores * decay).astype(BF))
-                d_scores = d_scores + d_weights[at_h * PART : (at_h + 1) * PART] * decay
-            leave_k = pair_cols(leave, k, low_half)
-            tail_part = leave_k * from_after[:, at]
-            d_scaled = dot_tn(jnp.concatenate(weights, axis=0), dy_both) + tail_part
-            d_scaled_all.append(d_scaled)
-            scaled_all.append(scaled_f)
-            tail_terms.append(jnp.sum(scaled_f * tail_part, axis=0, keepdims=True))
-            tails.append((leave_k * scaled_f).astype(BF))
-            entering.append((pair_cols(enter, k, low_half) * dy[:, at]).astype(BF))
-            d_values = step_k * d_scaled + skip[:, at] * dy[:, at]
-            buf[at_rows, at] = d_values * slope[at_rows, at]
-        d_scaled = jnp.concatenate(d_scaled_all, axis=1)
-        scaled = jnp.concatenate(scaled_all, axis=1)
-        enter_dy = jnp.concatenate(entering, axis=1)
-        d_scores_low = d_scores.astype(BF)
-        d_c = dot_nn(d_scores_low, b_low) + dot_nn(enter_dy, held)
-        d_b = dot_tn(d_scores_low, c_low) + dot_nn(jnp.concatenate(tails, axis=1), d_after_low)
+                d_scores = d_scores + d_weights[half * PART : (half + 1) * PART] * decay
+            own.append(dot_tn(jnp.concatenate(weights, axis=0), dy_both))
+        own = jnp.concatenate(own, axis=1)
+        d_scores = d_scores.astype(BF)
+        new_state = dot_tn(enter_dy, c_low)
+        d_c = dot_nn(d_scores, b_low)
+        d_b = dot_tn(d_scores, c_low)
+        work.append(
+            (q, part, values, b_low, shifted_raw, step, step_w, leave_w, passing, dy_low, scaled,
+             tail, enter_dy, own, new_state, d_b, d_c)
+        )
+    for item in sorted(work, key=lambda item: -item[1]):
+        (q, part, values, b_low, shifted_raw, step, step_w, leave_w, passing, dy_low, scaled,
+         tail, enter_dy, own, new_state, d_b, d_c) = item
+        at_rows = slice(part * PART, (part + 1) * PART)
+        held = hin_ref[q, 0, QUARTER * part : QUARTER * (part + 1)]
+        dy = dy_low.astype(F32)
+        scaled_f = scaled.astype(F32)
+        d_after = d_state[q]
+        d_after_low = d_after.astype(BF)
+        tail_part = leave_w * dot_nt(b_low, d_after_low)
+        d_scaled = own + tail_part
+        d_c = d_c + dot_nn(enter_dy, held)
+        d_b = d_b + dot_nn(tail, d_after_low)
+        d_state[q] = pass_state(passing, d_after, new_state)
         kept_half = jnp.where(first_core, d_b, d_c)
         given_half = jnp.where(first_core, d_c, d_b)
-        store(keep_at, part * PART, kept_half.astype(BF))
-        store(give_at, part * PART, given_half.astype(BF))
+        store(keep_at, q, part * PART, kept_half.astype(BF))
+        store(give_at, 1 - q, part * PART, given_half.astype(BF))
         if part == 0:
-            bc_edge[:, :STATE] = kept_half[0:16]
-            bc_edge[:, STATE:] = given_half[0:16]
-        by_values = head_sums(values * d_scaled, gather_low)
-        y_part = y_ref[0, 0, at_rows] - skip * values
-        d_cum = head_sums(dy * y_part - scaled * d_scaled, gather_low)
-        tail_row = jnp.concatenate(tail_terms, axis=1)
+            bc_edge[q, :, :STATE] = kept_half[0:16]
+            bc_edge[q, :, STATE:] = given_half[0:16]
+        d_values = step_w * d_scaled + skip * dy
+        buf[q, at_rows] = d_values * slopes[q][at_rows, :QUARTER]
+        by_values = dot_nn((values * d_scaled).astype(BF), gather_low)
+        y_part = y_ref[q, 0, at_rows] - skip * values
+        d_cum = head_sums(dy * y_part - scaled_f * d_scaled, gather_low)
+        tail_row = jnp.sum(scaled_f * tail_part, axis=0, keepdims=True)
         tail_sum = dot_exact(jnp.broadcast_to(tail_row, (8, QUARTER)), gather)[0:1]
         state_dot = jnp.sum(d_after * held.astype(F32), axis=1, keepdims=True)
         state_terms = jnp.sum(state_dot * gather, axis=0, keepdims=True)
-        at_last = tail_sum + passing * state_terms
-        d_rate = split_sum(upper, d_cum) + at_last
-        d_step = by_values - head[1:2] * d_rate
-        d_raw = d_step * sigmoid(shifted_all[at_rows])
+        d_rate = split_sum(upper, d_cum) + tail_sum + passing * state_terms
+        d_raw = (by_values - head[1:2] * d_rate) * sigmoid(shifted_raw)
         ghead_ref[0:1, :128] += jnp.sum(d_raw, axis=0, keepdims=True)
         ghead_ref[1:2, :128] += jnp.sum(-step * head[1:2] * d_rate, axis=0, keepdims=True)
         ghead_ref[2:3] += jnp.sum(values * dy, axis=0, keepdims=True)
-        d_late[at_rows, QUARTER:] = d_raw.astype(BF)
-        new_state = dot_tn(enter_dy, c_low)
-        for h in range(QHEADS):
-            at = slice(HEADDIM * h, HEADDIM * (h + 1))
-            d_state[at] = passing[:, h : h + 1] * d_after[at] + new_state[at]
-    mixed = mixed_ref[0, 0, :, :QUARTER].astype(F32)
-    d_mixed = jnp.zeros((SPAN, QUARTER), F32)
-    for j in range(CONV):
-        ahead = CONV - 1 - j
-        window = buf[ahead : ahead + SPAN] * cols_all[:, 8 + j : 9 + j]
-        d_mixed = d_mixed + taps[j : j + 1, :QUARTER] * window
-        gtap_ref[j : j + 1] += jnp.sum(mixed * window, axis=0, keepdims=True)
-    gtap_ref[CONV : CONV + 1] += jnp.sum(buf[0:SPAN], axis=0, keepdims=True)
-    buf[SPAN:] = buf[0:8]
-    d_late[:, :QUARTER] = d_mixed.astype(BF)
+        d_late[q * SPAN + part * PART : q * SPAN + (part + 1) * PART, QUARTER:] = d_raw.astype(BF)
+    for q in range(2):
+        mixed = mixed_ref[q, 0, :, :QUARTER].astype(F32)
+        d_mixed = jnp.zeros((SPAN, QUARTER), F32)
+        for j in range(CONV):
+            ahead = CONV - 1 - j
+            window = buf[q, ahead : ahead + SPAN] * columns[q][:, 8 + j : 9 + j]
+            d_mixed = d_mixed + taps[j : j + 1, :QUARTER] * window
+            gtap_ref[j : j + 1] += jnp.sum(mixed * window, axis=0, keepdims=True)
+        gtap_ref[CONV : CONV + 1] += jnp.sum(buf[q, 0:SPAN], axis=0, keepdims=True)
+        buf[q, SPAN:] = buf[q, 0:8]
+        d_late[q * SPAN : (q + 1) * SPAN, :QUARTER] = d_mixed.astype(BF)
     late = d_late[...]
-    g_ref[...] += dot_tn(late, current(own_ref, other_ref))[: QUARTER + 16]
-    d_gate = d_gate_ref[0, 0]
+    g_ref[...] += dot_tn(late, both_tokens(own_ref, other_ref))[: QUARTER + 16]
+    d_gate = jnp.concatenate([d_gate_ref[0, 0], d_gate_ref[1, 0]], axis=0)
+    grads = jnp.concatenate([late, d_gate], axis=1)
     width = QUARTER + 2 * STATE
-    for rows_at, out_ref in zip(core_rows(place_ref), (mine_ref, theirs_ref)):
-        total = dot_nt(late[:, :QUARTER], w_ref[rows_at, :QUARTER])
-        total = total + dot_nt(late[:, QUARTER:], w_ref[rows_at, width:])
-        out_ref[0, 0, :SPAN] = (total + dot_nt(d_gate, w_gate_ref[rows_at])).astype(BF)
+    for rows_at, out_ref, flip in zip(core_rows(place_ref), (mine_ref, theirs_ref), (0, 1)):
+        weights = [w_ref[rows_at, :QUARTER], w_ref[rows_at, width:], w_gate_ref[rows_at]]
+        total = dot_nt(grads, jnp.concatenate(weights, axis=1)).astype(BF)
+        for q in range(2):
+            out_ref[0, q ^ flip, :SPAN] = total[q * SPAN : (q + 1) * SPAN]
 
 
 def slot_spec(rows, width, order):
-    return pl.BlockSpec((1, 1, rows, width), lambda q, j, place: (q, order(j), 0, 0))
+    return pl.BlockSpec((2, 1, rows, width), lambda j, place: (0, order(j), 0, 0))
 
 
 def segment_spec():
-    return pl.BlockSpec(
-        (1, 8, BLOCKS * SPAN + 256), lambda q, j, place: (q, 0, 0)
-    )
+    return pl.BlockSpec((2, 8, BLOCKS * SPAN + 256), lambda j, place: (0, 0, 0))
 
 
 def fixed_spec(rows, width):
-    return pl.BlockSpec((rows, width), lambda q, j, place: (0, 0))
+    return pl.BlockSpec((rows, width), lambda j, place: (0, 0))
 
 
 def out_shape(rows, cols_of, kind):
@@ -886,29 +937,8 @@
     return BLOCKS - 1 - j
 
 
-def own_spec(order, rows=SPAN, at=0):
-    def index(q, j, place):
-        return (jnp.where(q == 0, order(j), order(BLOCKS - 1)), at, 0)
-
-    return pl.BlockSpec((1, rows, D), index)
-
-
-def other_spec(order, rows=SPAN, at=0):
-    def index(q, j, place):
-        return (jnp.where(q == 0, order(0), order(j)), at, 0)
-
-    return pl.BlockSpec((1, rows, D), index)
-
-
-def cot_specs(cots):
-    half = SPAN // 2
-    second = 0 if cots[0].shape[1] == half else 1
-    return [
-        own_spec(upward, half),
-        own_spec(upward, half, second),
-        other_spec(upward, half),
-        other_spec(upward, half, second),
-    ]
+def token_specs(order):
+    return [pl.BlockSpec((1, SPAN, D), lambda j, place: (order(j), 0, 0))] * 2
 
 
 def call_blocks(kernel, name, place, operands, in_specs, outs, scratch=()):
@@ -916,7 +946,7 @@
         kernel,
         grid_spec=pltpu.PrefetchScalarGridSpec(
             num_scalar_prefetch=1,
-            grid=(2, BLOCKS),
+            grid=(BLOCKS,),
             in_specs=in_specs,
             out_specs=[spec for spec, _ in outs],
             scratch_shapes=list(scratch),
@@ -932,12 +962,9 @@
     return slot_spec(rows, width, order), out_shape(rows, width, kind)
 
 
-def lead_out(rows, width, order, flipped):
-    def index(q, j, place):
-        return (order(j), 1 - q if flipped else q, 0, 0)
-
+def lead_out(rows, width, order):
     shape = jax.ShapeDtypeStruct((BLOCKS, 2, rows, width), BF)
-    return pl.BlockSpec((1, 1, rows, width), index), shape
+    return pl.BlockSpec((1, 2, rows, width), lambda j, place: (order(j), 0, 0, 0)), shape
 
 
 def fixed_out(rows, width):
@@ -952,8 +979,7 @@
         place,
         (*tokens, w_first, rows, taps, head, chan),
         [
-            own_spec(upward),
-            other_spec(upward),
+            *token_specs(upward),
             fixed_spec(D, width + 128),
             segment_spec(),
             fixed_spec(8, width),
@@ -967,7 +993,7 @@
             slot_out(SPAN, QUARTER, F32, upward),
             slot_out(PARTS * QUARTER, STATE, BF, upward),
         ],
-        [pltpu.VMEM((SPAN + 8, width), F32), pltpu.VMEM((QUARTER, STATE), F32)],
+        [pltpu.VMEM((2, SPAN + 8, width), F32), pltpu.VMEM((2, QUARTER, STATE), F32)],
     )
 
 
@@ -979,9 +1005,8 @@
         place,
         (*tokens, *cots, y, w_gate, w_out, chan),
         [
-            own_spec(upward),
-            other_spec(upward),
-            *cot_specs(cots),
+            *token_specs(upward),
+            *token_specs(upward),
             slot_spec(SPAN, QUARTER, upward),
             fixed_spec(D, QUARTER),
             fixed_spec(D, QUARTER),
@@ -990,9 +1015,9 @@
         [
             slot_out(SPAN, QUARTER, F32, upward),
             slot_out(SPAN, QUARTER, F32, upward),
-            lead_out(SPAN, half, upward, False),
-            lead_out(SPAN, half, upward, True),
-            slot_out(8, SPAN, F32, upward),
+            lead_out(SPAN, half, upward),
+            lead_out(SPAN, half, upward),
+            slot_out(2, SPAN, F32, upward),
         ],
     )
 
@@ -1001,7 +1026,7 @@
     if not last:
         return fixed_out(rows, D), []
     share = D // dp_count
-    spec = pl.BlockSpec((dp_count, rows, share), lambda q, j, place: (0, 0, 0))
+    spec = pl.BlockSpec((dp_count, rows, share), lambda j, place: (0, 0, 0))
     out = spec, jax.ShapeDtypeStruct((dp_count, rows, share), BF)
     return out, [pltpu.VMEM((rows, D), F32)]
 
@@ -1015,13 +1040,12 @@
         place,
         (*tokens, *cots, y, gate, d_gated, stat, chan) + ((seed,) if last else ()),
         [
-            own_spec(upward),
-            other_spec(upward),
-            *cot_specs(cots),
+            *token_specs(upward),
+            *token_specs(upward),
             slot_spec(SPAN, QUARTER, upward),
             slot_spec(SPAN, QUARTER, upward),
             slot_spec(SPAN, QUARTER, upward),
-            slot_spec(8, SPAN, upward),
+            slot_spec(2, SPAN, upward),
             fixed_spec(8, QUARTER),
         ]
         + ([fixed_spec(2 * QUARTER, D)] if last else []),
@@ -1043,7 +1067,7 @@
     last = seed is not None
     total, scratch = sums_out(QUARTER + 16, dp_count, last)
     rows_out = SPAN if last else SPAN + PACKED
-    maps_out = [lead_out(SPAN + 16, STATE, downward, flip) for flip in (False, True)] if last else []
+    maps_out = [lead_out(SPAN + 16, STATE, downward)] * 2 if last else []
     return call_blocks(
         bwd_last if last else bwd_first,
         "mix_backward",
@@ -1051,8 +1075,7 @@
         (*tokens, mixed, pre, raw, y, hin, dy, d_gate, rows, taps, head, chan, *weights)
         + ((seed,) if last else ()),
         [
-            own_spec(downward),
-            other_spec(downward),
+            *token_specs(downward),
             slot_spec(SPAN, width, downward),
             slot_spec(SPAN, width, downward),
             slot_spec(SPAN, 128, downward),
@@ -1074,15 +1097,15 @@
             slot_out(SPAN + 16, STATE, F32, downward),
             fixed_out(8, QUARTER),
             fixed_out(8, QUARTER),
-            lead_out(rows_out, half, downward, False),
-            lead_out(rows_out, half, downward, True),
+            lead_out(rows_out, half, downward),
+            lead_out(rows_out, half, downward),
         ],
         [
-            pltpu.VMEM((SPAN + 8, QUARTER), F32),
-            pltpu.VMEM((QUARTER, STATE), F32),
-            pltpu.VMEM((16, states), F32),
-            pltpu.VMEM((16, STATE), F32),
-            pltpu.VMEM((SPAN, QUARTER + 128), BF),
+            pltpu.VMEM((2, SPAN + 8, QUARTER), F32),
+            pltpu.VMEM((2, QUARTER, STATE), F32),
+            pltpu.VMEM((2, 16, states), F32),
+            pltpu.VMEM((2, 16, STATE), F32),
+            pltpu.VMEM((2 * SPAN, QUARTER + 128), BF),
         ]
         + scratch,
     )
@@ -1114,7 +1137,7 @@
                     d_conv = d_conv + maps_ref[src, q].astype(F32)
             d_pre = d_conv * slopes[m][q, 0]
             buf[0 : SPAN + 16] = d_pre
-            cols = to_columns(segment_flags(segs[m].at[q : q + 1], chip))
+            cols = to_columns(segment_flags(segs[m], q, chip))
             mixed = mixes[m][q, 0].astype(F32)
             d_mixed = jnp.zeros((SPAN, STATE), F32)
             for j in range(CONV):
@@ -1187,45 +1210,45 @@
     )(place, packed, maps, *slopes, *mixes, *segs, *tokens, taps)
 
 
-def norm_kernel(place_ref, mid_ref, late_ref, w_in_ref, w_state_ref, w_step_ref, step_ref, out_ref):
-    rows = mid_ref.shape[1]
+def norm_kernel(place_ref, share_ref, w_in_ref, w_state_ref, w_step_ref, step_ref, out_ref):
+    rows = share_ref.shape[1]
     squares = jnp.zeros((rows, QUARTER), F32)
     products = jnp.zeros((rows, QUARTER), F32)
     for s in range(BLOCKS):
         at = slice(s * QUARTER, (s + 1) * QUARTER)
-        out = mid_ref[s, :, :QUARTER].astype(F32)
-        gate = mid_ref[s, :, QUARTER:].astype(F32)
-        inner = late_ref[s, :, :QUARTER].astype(F32)
+        out = share_ref[s, :, :QUARTER].astype(F32)
+        gate = share_ref[s, :, QUARTER : 2 * QUARTER].astype(F32)
+        inner = share_ref[s, :, 2 * QUARTER : 3 * QUARTER].astype(F32)
         squares = squares + out * out + gate * gate + inner * inner
         products = products + gate * w_in_ref[0, :, at].astype(F32)
         products = products + inner * w_in_ref[1, :, at].astype(F32)
-    state = late_ref[0, :, QUARTER : QUARTER + STATE].astype(F32)
+    state = share_ref[0, :, MAPS_AT : MAPS_AT + STATE].astype(F32)
     for s in range(1, BLOCKS):
-        state = state + late_ref[s, :, QUARTER : QUARTER + STATE].astype(F32)
+        state = state + share_ref[s, :, MAPS_AT : MAPS_AT + STATE].astype(F32)
     step = step_ref[...]
     by_row = jnp.sum(products, axis=1, keepdims=True)
     by_row = by_row + jnp.sum(state * w_state_ref[...].astype(F32), axis=1, keepdims=True)
-    by_row = by_row + jnp.sum(step * w_step_ref[...].astype(F32), axis=1, keepdims=True)
     square = jnp.sum(squares, axis=1, keepdims=True) + jnp.sum(state * state, axis=1, keepdims=True)
-    square = square + jnp.sum(step * step, axis=1, keepdims=True)
     lanes = lax.broadcasted_iota(jnp.int32, (rows, 128), 1)
     table = jnp.where(lanes == 0, by_row, jnp.where(lanes == 1, square, 0.0))
     table = jnp.concatenate([table, jnp.zeros((128 - rows, 128), F32)], axis=0).T
     total = jnp.sum(table[1:2], axis=1, keepdims=True)
+    total = total + jnp.sum(jnp.sum(step * step, axis=0, keepdims=True), axis=1, keepdims=True)
+    by_step = jnp.sum(step * w_step_ref[...].astype(F32), axis=0, keepdims=True)
+    by_step = jnp.concatenate([by_step, jnp.zeros((1, 128 - rows), F32)], axis=1)
     at_row = lax.broadcasted_iota(jnp.int32, (8, 128), 0)
     at_lane = lax.broadcasted_iota(jnp.int32, (8, 128), 1)
-    first = jnp.where((at_row == 0) & (at_lane == rows), total, table[0:8])
+    first = jnp.where((at_row == 0) & (at_lane == rows), total, table[0:8] + by_step)
     out_ref[...] = jnp.where(at_row == 0, first, 0.0)
 
 
 def update_kernel(
-    place_ref, factor_ref, mid_ref, late_ref, step_ref, w_in_ref, w_out_ref, w_state_ref,
+    place_ref, factor_ref, share_ref, step_ref, w_in_ref, w_out_ref, w_state_ref,
     w_step_ref, m_in_ref, m_out_ref, m_state_ref, m_step_ref,
     new_in_ref, new_out_ref, new_state_ref, new_step_ref,
     next_in_ref, next_out_ref, next_state_ref, next_step_ref,
 ):
     factor = factor_ref[0, 0]
-    rows = mid_ref.shape[1]
 
     def write(new_ref, next_ref, at, moment, grad, weight):
         new = 0.5 * moment + (0.5 * factor) * grad
@@ -1237,30 +1260,29 @@
         gate = (0, slice(None), lanes)
         write(
             new_in_ref, next_in_ref, gate, m_in_ref[gate],
-            mid_ref[s, :, QUARTER:].astype(F32), w_in_ref[gate],
+            share_ref[s, :, QUARTER : 2 * QUARTER].astype(F32), w_in_ref[gate],
         )
         inner = (1, slice(None), lanes)
         write(
             new_in_ref, next_in_ref, inner, m_in_ref[inner],
-            late_ref[s, :, :QUARTER].astype(F32), w_in_ref[inner],
-        )
-        out = mid_ref[s, :, :QUARTER].astype(F32)
-        out = jnp.concatenate([out, jnp.zeros((128 - rows, QUARTER), F32)], axis=0).T
+            share_ref[s, :, 2 * QUARTER : 3 * QUARTER].astype(F32), w_in_ref[inner],
+        )
+        out = (slice(None), lanes)
         write(
-            new_out_ref, next_out_ref, lanes, m_out_ref[lanes], out[:, :rows], w_out_ref[lanes]
-        )
-    state = late_ref[0, :, QUARTER : QUARTER + STATE].astype(F32)
+            new_out_ref, next_out_ref, out, m_out_ref[out],
+            share_ref[s, :, :QUARTER].astype(F32), w_out_ref[out],
+        )
+    state = share_ref[0, :, MAPS_AT : MAPS_AT + STATE].astype(F32)
     for s in range(1, BLOCKS):
-        state = state + late_ref[s, :, QUARTER : QUARTER + STATE].astype(F32)
+        state = state + share_ref[s, :, MAPS_AT : MAPS_AT + STATE].astype(F32)
     write(new_state_ref, next_state_ref, ..., m_state_ref[...], state, w_state_ref[...])
     write(new_step_ref, next_step_ref, ..., m_step_ref[...], step_ref[...], w_step_ref[...])
 
 
-def owner_specs(rows, heads_local):
+def owner_specs(rows):
     return [
         pl.BlockSpec((2, rows, BLOCKS * QUARTER), lambda i, place: (0, place[1], 0)),
         pl.BlockSpec((rows, STATE), lambda i, place: (place[1], place[0])),
-        pl.BlockSpec((rows, heads_local), lambda i, place: (place[1], 0)),
     ]
 
 
@@ -1294,34 +1316,20 @@
     return lax.all_to_all(blocks, "seq", 0, 0, tiled=True)
 
 
-def gather_blocks(piece):
-    return exchange(jnp.broadcast_to(piece, (BLOCKS,) + piece.shape))
+def copies(piece):
+    return jnp.broadcast_to(piece, (BLOCKS,) + piece.shape)
 
 
 def add_low(a, b):
     return (a.astype(F32) + b.astype(F32)).astype(BF)
 
 
-def gather_halves(piece):
-    half = piece.shape[0] // 2
-    return [gather_blocks(piece[:half]), gather_blocks(piece[half:])]
-
-
 def scatter(blocks):
     return jnp.sum(exchange(blocks).astype(F32), axis=0)
 
 
 def after(value, *others):
     return lax.optimization_barrier((value, others))[0]
-
-
-def sum_cores(table):
-    return table + swap_cores(table)[::-1]
-
-
-def sum_plane(table):
-    table = table + over_x(table)
-    return table + over_y(table)
 
 
 def fast_body(
@@ -1366,7 +1374,7 @@
     def all_rows(block):
         return lax.all_gather(block, "dp", axis=0, tiled=True)
 
-    w_first = all_rows(
+    first_block = (
         jnp.concatenate(
             [
                 quarter(inproj[1], 1, QUARTER),
@@ -1376,6 +1384,8 @@
             axis=1,
         )
     )
+    inputs, first_block = after((inputs, first_block))
+    w_first = all_rows(first_block)
     w_gate = all_rows(quarter(inproj[0], 1, QUARTER))
     w_out = all_rows(quarter(outproj, 0, QUARTER).T)
 
@@ -1390,10 +1400,8 @@
     rows_whole = whole_rows(inputs)
     normed_own = rms_scale(rows_whole.astype(F32), prenorm).astype(BF)
     cot_own = whole_rows(cotangent)
-    own_0 = gather_blocks(normed_own[0])
-    segments, convinner, convstate, headparam, gatenorm = after(
-        (segments, convinner, convstate, headparam, gatenorm), normed_own
-    )
+    first_copies, second_copies = after((copies(normed_own[0]), copies(normed_own[1])))
+    own_0 = exchange(first_copies)
 
     seg_mine = jnp.concatenate(
         [
@@ -1423,10 +1431,6 @@
     def core_sums(mine, theirs):
         return add_low(mine, swap_cores(theirs))
 
-    def core_halves(mine, theirs):
-        got = swap_cores(theirs)
-        return [add_low(mine[:, q], got[:, q]) for q in range(2)]
-
     def over_dp(parts):
         return lax.psum_scatter(parts, "dp", scatter_dimension=0, tiled=True)[0]
 
@@ -1451,75 +1455,98 @@
             (w_first, w_gate), seed, dp_count,
         )
 
+    def summed(blocks):
+        return jnp.sum(blocks.astype(F32), axis=0)
+
+    def in_order(block):
+        return by_core(block, block[:, ::-1])
+
     def token_scale(sums):
         own = lax.dynamic_index_in_dim(sums, chip, 1, keepdims=False)
         return lax.rsqrt(own[:, 0] / INNER + EPS)[..., None]
 
+    def sum_dp(value):
+        hop = 1
+        while hop < dp_count:
+            value = value + lax.ppermute(value, "dp", [(i, i ^ hop) for i in range(dp_count)])
+            hop *= 2
+        return value
+
+    def sum_seq(value):
+        value = value + over_x(value)
+        return value + over_y(value)
+
     def with_other(own):
         return own, swap_cores(own)
 
-    own_1 = gather_blocks(after(normed_own[1], own_0))
+    stepproj_own = lax.dynamic_slice_in_dim(stepproj.T, chip * shard, shard, 1)
+    outproj_own = lax.dynamic_slice_in_dim(outproj, chip * shard, shard, 1).T
+    own_0, w_first, second_copies, cot_own, segs, taps, head, chan, stepproj_own, outproj_own = (
+        after(
+            (
+                own_0, w_first, second_copies, cot_own, segs, taps, head, chan, stepproj_own,
+                outproj_own,
+            )
+        )
+    )
+    own_1 = exchange(second_copies)
     normed = [with_other(own_0)]
-    (own_0, other_0), place = after((normed[0], place), w_first)
-    kept = [forward(0, place, (own_0, other_0))]
-
-    own_1, w_gate, piece, place = after((own_1, w_gate, cot_own[0], place), kept[0][1])
+    place, cot_copies = after((place, [copies(cot) for cot in (cot_own[0], cot_own[1])]))
+    kept = [forward(0, place, normed[0])]
+
+    own_1, w_gate, piece, place = after((own_1, w_gate, cot_copies[0], place), kept[0][1])
     normed.append(with_other(own_1))
-    cot_0 = gather_blocks(piece)
+    cot_0 = exchange(piece)
     kept.append(forward(1, place, normed[1]))
 
-    cot_0, w_out, piece, place = after((cot_0, w_out, cot_own[1], place), kept[1][1])
-    cot_0 = with_other(cot_0)
-    cots = [[cot_0[0], cot_0[0], cot_0[1], cot_0[1]]]
-    half = SPAN // 2
-    cot_a = gather_blocks(piece[:half])
+    cot_0, w_out, piece, place = after((cot_0, w_out, cot_copies[1], place), kept[1][1])
+    cots = [with_other(cot_0)]
+    cot_1 = exchange(piece)
     gate_0, d_gated_0, mine_0, theirs_0, stat_0 = gate_forward(0, place)
 
-    cot_a, stat_0, piece, place = after((cot_a, stat_0, piece, place))
-    stat_0 = sum_cores(stat_0)
-    theirs_0 = after(theirs_0, stat_0)
-    sums_0 = sum_plane(stat_0)
-    cot_b = gather_blocks(after(piece, sums_0)[half:])
-    cot_a = [cot_a, swap_cores(cot_a)]
-    branch_0 = core_halves(mine_0, theirs_0)
+    cot_1, place, theirs_0 = after((cot_1, place, theirs_0), stat_0)
+    cots.append(with_other(cot_1))
+    branch_0 = core_sums(mine_0, after(theirs_0, cots[1][1]))
+    gate_1, d_gated_1, mine_1, theirs_1, stat_1 = gate_forward(1, place)
+
+    stats = jnp.stack([stat_0, after(stat_1, branch_0)])
+    stats = stats + swap_cores(stats)[:, ::-1]
+    theirs_1 = after(theirs_1, stats)
+    sums_0, sums_1 = sum_seq(stats)
+    branch_0 = after(branch_0, sums_0)
+    layer_0 = exchange(branch_0)
     dy_0, d_gate_0, g_gain_0, g_mid_0 = gate_backward(0, place, gate_0, d_gated_0, sums_0, None)
-
-    cot_a, cot_b, place, branch_0 = after((cot_a, cot_b, place, branch_0), dy_0)
-    cots.append([cot_a[0], cot_b, cot_a[1], swap_cores(cot_b)])
-    layer_0 = [exchange(branch_0[0])]
-    gate_1, d_gated_1, mine_1, theirs_1, stat_1 = gate_forward(1, place)
-
-    layer_0, stat_1, place = after((layer_0, stat_1, place))
-    stat_1 = sum_cores(stat_1)
-    theirs_1 = after(theirs_1, stat_1)
-    sums_1 = sum_plane(stat_1)
-    layer_0.append(exchange(after(branch_0[1], sums_1)))
     branch_1 = core_sums(mine_1, theirs_1)
-    dy_1, d_gate_1, g_gain_1, mid_parts = gate_backward(1, place, gate_1, d_gated_1, sums_1, g_mid_0)
+    place = after(place, dy_0)
+    dy_1, d_gate_1, g_gain_1, mid_parts = gate_backward(
+        1, place, gate_1, d_gated_1, sums_1, g_mid_0
+    )
 
     layer_0, branch_1, place, mid_parts = after((layer_0, branch_1, place, mid_parts), dy_1)
     layer_1 = exchange(branch_1)
     mid_rows = over_dp(mid_parts)
-    g_late_0, slope_0, g_taps_0, g_head_0, mine, theirs = backward(
-        0, place, dy_0, d_gate_0, None
-    )
+    g_late_0, slope_0, g_taps_0, g_head_0, mine, theirs = backward(0, place, dy_0, d_gate_0, None)
 
     layer_1, mid_rows, theirs, place = after((layer_1, mid_rows, theirs, place), g_taps_0)
     back_0 = core_sums(mine, theirs)
-    back_0, place = after((back_0, place))
+    layer_out = [
+        summed(layer_0) * token_scale(sums_0), summed(layer_1) * token_scale(sums_1)
+    ]
+    layer_out = (inputs.astype(F32) + in_order(jnp.stack(layer_out))).astype(BF)
+    back_0, place, layer_out = after((back_0, place, layer_out))
     token_0 = exchange(back_0)
     late_parts, keep_1, give_1, slope_1, g_taps_1, g_head_1, mine, theirs = backward(
         1, place, dy_1, d_gate_1, g_late_0
     )
 
-    token_0, late_parts, theirs, give_1, layer_0, layer_1, mid_rows = after(
-        (token_0, late_parts, theirs, give_1, layer_0, layer_1, mid_rows)
-    )
+    token_0, late_parts, theirs, give_1 = after((token_0, late_parts, theirs, give_1))
     late_rows = over_dp(late_parts)
     maps = core_sums(keep_1, give_1)
     back_1 = core_sums(mine, after(theirs, maps))
     maps = exchange(maps)
-    maps, back_1 = after((maps, back_1))
+    maps, back_1, token_0, mid_rows, g_taps_1 = after(
+        (maps, back_1, token_0, mid_rows, g_taps_1)
+    )
     token_1 = exchange(back_1)
     taps_state = lax.dynamic_slice_in_dim(convstate, core * STATE, STATE, 1)
     d_maps, g_maps, g_state_taps = run_maps(
@@ -1536,17 +1563,35 @@
         route = [(i, (i + hop) % dp_count) for i in range(dp_count)]
         state_rows = state_rows + lax.ppermute(for_dp(hop), "dp", route).astype(F32)
     state_rows = state_rows.astype(BF)
-    token_1, late_rows, mid_rows, state_rows = after((token_1, late_rows, mid_rows, state_rows))
-
-    def summed(blocks):
-        return jnp.sum(blocks.astype(F32), axis=0)
-
-    layer_out = [
-        jnp.stack([summed(part) for part in layer_0]) * token_scale(sums_0),
-        summed(layer_1) * token_scale(sums_1),
+
+    inner_local = BLOCKS * QUARTER
+
+    def put(values, width, total):
+        base = jnp.zeros(values.shape[:-1] + (total,), F32)
+        return lax.dynamic_update_slice_in_dim(base, values, chip * width, values.ndim - 1)
+
+    g_taps, g_head = g_taps_0 + g_taps_1, g_head_0 + g_head_1
+    g_heads = jnp.concatenate(
+        [g_head[:2, :QHEADS], jnp.sum(g_head[2].reshape(1, QHEADS, HEADDIM), axis=2)], axis=0
+    )
+    small_parts = [
+        put(g_taps[: CONV + 1], QUARTER, inner_local),
+        put(g_gain_0[0] + g_gain_1[0], QUARTER, inner_local),
+        put(g_heads, QHEADS, heads_local),
+        g_state_taps[: CONV + 1],
     ]
+    small_shapes = [small.shape for small in small_parts]
+    vector = jnp.concatenate([small.reshape(-1) for small in small_parts])
+    vector = jnp.pad(vector, (0, -vector.size % 1024)).reshape(-1, 128)
+
+    token_1, mid_rows, late_rows, state_rows = after(
+        (token_1, mid_rows, late_rows, state_rows), vector
+    )
+    shares = jnp.concatenate(
+        [mid_rows, late_rows[:QUARTER], state_rows, late_rows[QUARTER:]], axis=0
+    )
+    share = by_place(shares)
     d_tokens = [summed(token_0[:, :, :SPAN]), summed(token_1)]
-    smalls = (g_taps_0 + g_taps_1, g_head_0 + g_head_1)
     w_state = w_first[:, QUARTER : QUARTER + 2 * STATE]
 
     state_other = swap_cores(d_maps)[:, ::-1]
@@ -1559,11 +1604,7 @@
         d_state_both, lax.dynamic_slice_in_dim(w_state, core * half_d, half_d, 0)
     )
 
-    def in_order(block):
-        return by_core(block, block[:, ::-1])
-
-    layer_out = in_order(jnp.stack(layer_out))
-    outputs = (inputs.astype(F32) + layer_out).astype(BF)
+    outputs = layer_out
     d_normed = in_order(jnp.stack(d_tokens) + from_state)
     rows_own = inputs.astype(F32)
     gain_own = lax.dynamic_slice_in_dim(prenorm, core * half_d, half_d, 0)
@@ -1579,14 +1620,10 @@
         - rows_own * root * root * root * (pair_sums[1] / D)[..., None]
     ).astype(BF)
 
-    mid_share = by_place(mid_rows)
-    late_share = by_place(
-        jnp.concatenate([late_rows[:QUARTER], state_rows, late_rows[QUARTER:]], axis=0)
-    )
-    step_share = late_share[:, :, QUARTER + STATE : QUARTER + STATE + QHEADS].astype(F32)
-    step_share = jnp.moveaxis(step_share, 0, 1).reshape(shard, heads_local)
-    row_start = chip * shard
-    in_spec, state_spec, step_spec = owner_specs(shard, heads_local)
+    step_at = MAPS_AT + STATE
+    step_share = share[:, :, step_at : step_at + QHEADS].astype(F32)
+    step_share = jnp.moveaxis(step_share, 1, 2).reshape(heads_local, shard)
+    in_spec, state_spec = owner_specs(shard)
 
     def whole(array):
         return pl.BlockSpec(array.shape, lambda i, place: (0,) * array.ndim)
@@ -1599,52 +1636,12 @@
         norm_kernel,
         "owner_norm",
         place,
-        (mid_share, late_share, inproj, statproj, stepproj, step_share),
-        [whole(mid_share), whole(late_share), in_spec, state_spec, step_spec, whole(step_share)],
+        (share, inproj, statproj, stepproj_own, step_share),
+        [whole(share), in_spec, state_spec, whole(stepproj_own), whole(step_share)],
         [whole_out((8, 128), F32)],
     )[0]
     owner_sums = owner_sums + swap_cores(owner_sums)
 
-    g_taps, g_head = smalls
-    g_heads = jnp.concatenate(
-        [g_head[:2, :QHEADS], jnp.sum(g_head[2].reshape(1, QHEADS, HEADDIM), axis=2)], axis=0
-    )
-
-    inner_local = BLOCKS * QUARTER
-
-    def put(values, width, total):
-        base = jnp.zeros(values.shape[:-1] + (total,), F32)
-        return lax.dynamic_update_slice_in_dim(base, values, chip * width, values.ndim - 1)
-
-    small_parts = [
-        put(g_taps[: CONV + 1], QUARTER, inner_local),
-        put(g_gain_0[0] + g_gain_1[0], QUARTER, inner_local),
-        put(g_heads, QHEADS, heads_local),
-        g_state_taps[: CONV + 1],
-    ]
-    sizes = [part.size for part in small_parts]
-    vector = jnp.concatenate([part.reshape(-1) for part in small_parts])
-    vector = jnp.pad(vector, (0, -vector.size % 1024)).reshape(-1, 128)
-
-    def sum_all(value):
-        value = value + over_x(value)
-        value = value + over_y(value)
-        hop = 1
-        while hop < dp_count:
-            value = value + lax.ppermute(value, "dp", [(i, i ^ hop) for i in range(dp_count)])
-            hop *= 2
-        return value
-
-    vector = sum_all(vector).reshape(-1)
-    small_sums = []
-    start = 0
-    for part, size in zip(small_parts, sizes):
-        small_sums.append(vector[start : start + size].reshape(part.shape))
-        start += size
-    s_taps, s_gain, s_head, s_state_taps = small_sums
-
-    small_sq = sum(jnp.sum(term * term) for term in small_sums)
-    small_sq = small_sq + swap_cores(small_sq)
     owners = dp_count * BLOCKS
     owner = data_at * BLOCKS + chip
     gain_rows = lax.dynamic_slice_in_dim(prenorm, owner * shard, shard, 0)
@@ -1652,13 +1649,23 @@
     g_prenorm = owner_sums[0] / jnp.pad(gain_rows, (0, 128 - shard), constant_values=1.0)
     g_prenorm = jnp.where(lanes < shard, g_prenorm, 0.0)
     square = owner_sums[0, shard] + jnp.sum(g_prenorm * g_prenorm)
-    square = square + jnp.where(owner == 0, small_sq, 0.0)
     line = jnp.where(lanes == shard, square, g_prenorm)
     table = jnp.where(jnp.arange(owners)[:, None] == owner, line[None], 0.0)
-    table = sum_all(table)
-    grad_norm = jnp.sqrt(jnp.sum(table[:, shard]))
+    table = sum_seq(sum_dp(jnp.concatenate([table, vector], axis=0)))
+    small_sums = []
+    start = 0
+    vector = table[owners:].reshape(-1)
+    for shape in small_shapes:
+        size = math.prod(shape)
+        small_sums.append(vector[start : start + size].reshape(shape))
+        start += size
+    s_taps, s_gain, s_head, s_state_taps = small_sums
+
+    small_sq = sum(jnp.sum(term * term) for term in small_sums)
+    small_sq = small_sq + swap_cores(small_sq)
+    grad_norm = jnp.sqrt(jnp.sum(table[:owners, shard]) + small_sq)
     s_prenorm = lax.dynamic_slice_in_dim(
-        table[:, :shard], core * (owners // 2), owners // 2, 0
+        table[:owners, :shard], core * (owners // 2), owners // 2, 0
     ).reshape(half_d)
 
     entries = (
@@ -1681,20 +1688,19 @@
         return (weight.astype(F32) - LEARN * moment).astype(weight.dtype)
 
     new_prenorm = moved(prenorm_moment, s_prenorm)
-    outproj_own = lax.dynamic_slice_in_dim(outproj, row_start, shard, 1)
-    moments = (inproj_moment, outproj_moment, statproj_moment, stepproj_moment)
+    moments = (inproj_moment, outproj_moment.T, statproj_moment, stepproj_moment.T)
     new_in, new_out, new_state, new_step, next_in, next_out, next_state, next_step = run_owner(
         update_kernel,
         "owner_update",
         place,
         (
-            factor.reshape(1, 1), mid_share, late_share, step_share,
-            inproj, outproj_own, statproj, stepproj, *moments,
+            factor.reshape(1, 1), share, step_share,
+            inproj, outproj_own, statproj, stepproj_own, *moments,
         ),
         [
             pl.BlockSpec(memory_space=pltpu.SMEM),
-            whole(mid_share), whole(late_share), whole(step_share),
-            in_spec, whole(outproj_own), state_spec, step_spec,
+            whole(share), whole(step_share),
+            in_spec, whole(outproj_own), state_spec, whole(stepproj_own),
             *[whole(moment) for moment in moments],
         ],
         [whole_out(moment.shape, kind) for kind in (F32, BF) for moment in moments],
@@ -1710,16 +1716,16 @@
         new_prenorm,
         new_in,
         new_state,
-        new_step,
-        new_out,
+        new_step.T,
+        new_out.T,
         new_taps,
         new_state_taps,
         new_head,
         new_gain,
         next_in,
         next_state,
-        next_step,
-        next_out,
+        next_step.T,
+        next_out.T,
         stepped(convinner, new_taps),
         stepped(lax.dynamic_slice_in_dim(convstate, core * STATE, STATE, 1), new_state_taps),
     )

time: 594 us -> 535 us (0.901)
  waiting for transfers between devices: 65.2 us -> 118 us
  blocking collectives: 41.9 us -> 0 us
  Pallas kernels: 255 us -> 216 us
  starting transfers between devices: 81.6 us -> 67.4 us
  other arithmetic: 66.4 us -> 56.7 us
    all_to_all x10 -> x9, waiting for transfers between devices: 9.94 us -> 65.4 us  [exchange(): return lax.all_to_all(blocks, 'seq', 0, 0, tiled=True)]
    all_to_all x1 -> x0, blocking collectives: 41.9 us -> none  [exchange(): return lax.all_to_all(blocks, 'seq', 0, 0, tiled=True)]
    pallas_call x8, Pallas kernels: 240 us -> 202 us  [call_blocks(): pl.pallas_call(kernel, grid_spec=pltpu.PrefetchScalarGridSpec(num_scalar_...]
    ppermute x4 -> x2, waiting for transfers between devices: 23.6 us -> 5.15 us  [over_x(): return lax.ppermute(block, 'seq', ROUTE_X)]
    ppermute x3, waiting for transfers between devices: 0.12 us -> 7.01 us  [fast_body(): state_rows = state_rows + lax.ppermute(for_dp(hop), 'dp', route).astype(F32)]
    unnamed x86 -> x67, local copies, waits for them, and re-layouts: 13.4 us -> 6.67 us
    ppermute x4 -> x2, starting transfers between devices: 8.14 us -> 1.62 us  [sum_dp(): lax.ppermute(value, 'dp', [(i, i ^ hop) for i in range(dp_count)])]
    all_gather x3, waiting for transfers between devices: 4.41 us -> 10.4 us  [all_rows(): return lax.all_gather(block, 'dp', axis=0, tiled=True)]
  transfers between devices with their start and end apart: 50 -> 40, of which waited for: 24 -> 26; matrix products, arithmetic and copies ran while one was open for 16% -> 13% of each run, Pallas kernels for 42% -> 40%
where the time goes in v3:
time: 535 us; the launch traced here: 525 us
  Pallas kernels  216 us (40%)
  waiting for transfers between devices  118 us (22%)
  starting transfers between devices  67.4 us (13%)
  other arithmetic  56.7 us (11%)
  local copies, waits for them, and re-layouts  43.3 us (8%)
  between operations  21.4 us (4%)
    pallas_call x8, Pallas kernels, call_blocks(): pl.pallas_call(kernel, grid_spec=pltpu.PrefetchScalarGridSpec(num_scalar_...  202 us
    all_to_all x9, waiting for transfers between devices, exchange(): return lax.all_to_all(blocks, 'seq', 0, 0, tiled=True)  65.4 us
    all_to_all x9, starting transfers between devices, exchange(): return lax.all_to_all(blocks, 'seq', 0, 0, tiled=True)  48 us
    convert_element_type x5, other arithmetic, add_low(): return (a.astype(F32) + b.astype(F32)).astype(BF)  20.9 us
    ppermute x16, waiting for transfers between devices, swap_cores(): return lax.ppermute(block, 'tensor', SWAP)  15.2 us
  transfers between devices with their start and end apart: 40, of which 26 were waited for; matrix products, arithmetic and copies ran while one was open for 13% of the time, Pallas kernels for 40%

profile of v3, /device:TPU:0, one launch (start us, length us, event | category | flops | bytes accessed | tf_op | source)
XLA Modules:
  0.0 525.4 jit_solution(1575605313783429349)
XLA Ops:
  23.8 5.2 all-to-all-start
  40.9 25.6 %all-to-all-done.own_ref.refs_1_.own_0 = bf16[4,256,1536]{2,1,0:T(8,128)(2,1)} async-done(((bf16[4,256,1536]{2,1,0:T(8,128)(2,1)}), bf16[4,256,1536]{2,1,0:T(8,128)(2,1)}, u32[]{:S(2)}, u32[]{:S(2)}) %all-to-all-start) | async-done | bytes 3145760 | tf_op jit(solution)/shard_map/all_to_all | solution.py:1316
  68.8 4.7 all-to-all-start.1
  80.6 25.2 %mix_forward.2 = (bf16[2,4,256,640]{3,2,1,0:T(8,128)(2,1)}, f32[2,4,256,128]{3,2,1,0:T(8,128)}, f32[2,4,256,640]{3,2,1,0:T(8,128)}, f32[2,4,256,384]{3,2,1,0:T(8,128)}, bf16[2,4,768,128]{3,2,1,0:T(8,128)(2,1)}) custom-call(s32[2]{0:T(128)} %pad_add_fusion.place_ref.refs_0_, bf16[4,256,1536]{2,1,0:T(8,128)(2,1)} %all-to-all-done.own_ref.refs_1_.own_0, ...), custom_call_target="tpu_custom_call" | custom-call | flops 1024 | bytes 1024 | tf_op jit(solution)/shard_map/mix_forward/pallas_call | solution.py:945
  110.6 4.6 all-to-all-start.2
  116.6 25.1 %mix_forward.3 = (bf16[2,4,256,640]{3,2,1,0:T(8,128)(2,1)}, f32[2,4,256,128]{3,2,1,0:T(8,128)}, f32[2,4,256,640]{3,2,1,0:T(8,128)}, f32[2,4,256,384]{3,2,1,0:T(8,128)}, bf16[2,4,768,128]{3,2,1,0:T(8,128)(2,1)}) custom-call(s32[2]{0:T(128)} %pad_add_fusion.place_ref.refs_0_, bf16[4,256,1536]{2,1,0:T(8,128)(2,1)} %all-to-all-done.1.own_ref.refs_1_.own_1, ...), custom_call_target="tpu_custom_call" | custom-call | flops 1024 | bytes 1024 | tf_op jit(solution)/shard_map/mix_forward/pallas_call | solution.py:945
  141.7 7.3 %all-gather.7.cloned.1.call-done.w_out_ref = bf16[1536,384]{1,0:T(8,128)(2,1)} async-done(((bf16[384,384]{1,0:T(8,128)(2,1)}), bf16[1536,384]{1,0:T(8,128)(2,1)}) %all-gather.7.cloned.1.call-update) | async-done | bytes 1179664 | tf_op jit(solution)/shard_map/all_gather | solution.py:1375
  152.3 3.7 all-to-all-start.3
  158.3 16.6 %gate_forward.2 = (f32[2,4,256,384]{3,2,1,0:T(8,128)}, f32[2,4,256,384]{3,2,1,0:T(8,128)}, bf16[4,2,256,768]{3,2,1,0:T(8,128)(2,1)}, bf16[4,2,256,768]{3,2,1,0:T(8,128)(2,1)}, f32[2,4,2,256]{3,2,1,0:T(2,128)}) custom-call(s32[2]{0:T(128)} %pad_add_fusion.place_ref.refs_0_, bf16[4,256,1536]{2,1,0:T(8,128)(2,1)} %all-to-all-done.own_ref.refs_1_.own_0, ...), custom_call_target="tpu_custom_call" | custom-call | flops 1024 | bytes 1024 | tf_op jit(solution)/shard_map/gate_forward/pallas_call | solution.py:945
  174.9 18.2 %all-to-all-done.3.cot_own_ref.refs_3_ = bf16[4,256,1536]{2,1,0:T(8,128)(2,1)S(1)} async-done(((bf16[4,256,1536]{2,1,0:T(8,128)(2,1)}), bf16[4,256,1536]{2,1,0:T(8,128)(2,1)S(1)}, u32[]{:S(2)}, u32[]{:S(2)}) %all-to-all-start.3) | async-done | bytes 3145760 | tf_op jit(solution)/shard_map/all_to_all | solution.py:1316
  193.1 5.7 %collective-permute-done.5.cot_other_ref.refs_4_ = bf16[4,256,1536]{2,1,0:T(8,128)(2,1)S(1)} collective-permute-done((bf16[4,256,1536]{2,1,0:T(8,128)(2,1)S(1)}, bf16[4,256,1536]{2,1,0:T(8,128)(2,1)S(1)}, u32[]{:S(2)}, u32[]{:S(2)}) %collective-permute-start.5) | collective-permute-done | bytes 3145760 | tf_op jit(solution)/shard_map/ppermute | solution.py:1304
  200.5 16.5 %gate_forward.3 = (f32[2,4,256,384]{3,2,1,0:T(8,128)}, f32[2,4,256,384]{3,2,1,0:T(8,128)}, bf16[4,2,256,768]{3,2,1,0:T(8,128)(2,1)}, bf16[4,2,256,768]{3,2,1,0:T(8,128)(2,1)}, f32[2,4,2,256]{3,2,1,0:T(2,128)}) custom-call(s32[2]{0:T(128)} %pad_add_fusion.place_ref.refs_0_, bf16[4,256,1536]{2,1,0:T(8,128)(2,1)} %all-to-all-done.1.own_ref.refs_1_.own_1, ...), custom_call_target="tpu_custom_call" | custom-call | flops 1024 | bytes 1024 | tf_op jit(solution)/shard_map/gate_forward/pallas_call | solution.py:945
  217.0 5.3 %add_convert_fusion.3 = bf16[4,2,256,768]{3,2,1,0:T(8,128)(2,1)} fusion(bf16[4,2,256,768]{3,2,1,0:T(8,128)(2,1)} %collective-permute-done.6, bf16[4,2,256,768]{3,2,1,0:T(8,128)(2,1)} %get-tuple-element.154), kind=kLoop, calls=%fused_computation.7 | loop fusion | flops 6291456 | bytes 9437184 | tf_op jit(solution)/shard_map/convert_element_type | solution.py:1324
  232.4 3.7 all-to-all-start.4
  236.2 15.4 %gate_backward.2 = (bf16[2,4,256,384]{3,2,1,0:T(8,128)(2,1)}, bf16[2,4,256,384]{3,2,1,0:T(8,128)(2,1)}, f32[8,384]{1,0:T(8,128)}, f32[768,1536]{1,0:T(8,128)}) custom-call(s32[2]{0:T(128)} %pad_add_fusion.place_ref.refs_0_, bf16[4,256,1536]{2,1,0:T(8,128)(2,1)} %all-to-all-done.own_ref.refs_1_.own_0, ...), custom_call_target="tpu_custom_call" | custom-call | flops 1024 | bytes 1024 | tf_op jit(solution)/shard_map/gate_backward/pallas_call | solution.py:945
  251.6 16.6 %gate_backward.3 = (bf16[2,4,256,384]{3,2,1,0:T(8,128)(2,1)}, bf16[2,4,256,384]{3,2,1,0:T(8,128)(2,1)}, f32[8,384]{1,0:T(8,128)}, bf16[4,768,384]{2,1,0:T(8,128)(2,1)}) custom-call(s32[2]{0:T(128)} %pad_add_fusion.place_ref.refs_0_, bf16[4,256,1536]{2,1,0:T(8,128)(2,1)} %all-to-all-done.1.own_ref.refs_1_.own_1, ...), custom_call_target="tpu_custom_call" | custom-call | flops 1024 | bytes 1024 | tf_op jit(solution)/shard_map/gate_backward/pallas_call | solution.py:945
  268.3 4.3 add_convert_fusion.2
  272.6 13.0 %all-to-all-start.5 = ((bf16[4,2,256,768]{3,2,1,0:T(8,128)(2,1)}), bf16[4,2,256,768]{3,2,1,0:T(8,128)(2,1)}, u32[]{:S(2)}, u32[]{:S(2)}) async-start(bf16[4,2,256,768]{3,2,1,0:T(8,128)(2,1)} %add_convert_fusion.2), calls=%async_computation.5 | async-start | bytes 6291456 | tf_op jit(solution)/shard_map/all_to_all | solution.py:1316
  285.6 43.2 %mix_backward.2 = (f32[400,1536]{1,0:T(8,128)}, f32[2,4,272,128]{3,2,1,0:T(8,128)}, f32[8,384]{1,0:T(8,128)}, f32[8,384]{1,0:T(8,128)}, bf16[4,2,304,768]{3,2,1,...) custom-call(s32[2]{0:T(128)} %pad_add_fusion.place_ref.refs_0_, bf16[4,256,1536]{2,1,0:T(8,128)(2,1)} %all-to-all-done.own_ref.refs_1_.own_0, ...), custom_call_target="tpu_custom_call" | custom-call | flops 1024 | bytes 1024 | tf_op jit(solution)/shard_map/mix_backward/pallas_call | solution.py:945
  336.4 4.9 add_convert_fusion
  341.2 4.8 all-to-all-start.6
  346.3 43.8 %mix_backward.3 = (bf16[4,400,384]{2,1,0:T(8,128)(2,1)}, bf16[4,2,272,128]{3,2,1,0:T(8,128)(2,1)}, bf16[4,2,272,128]{3,2,1,0:T(8,128)(2,1)}, f32[2,4,272,128]{3,...) custom-call(s32[2]{0:T(128)} %pad_add_fusion.place_ref.refs_0_, ...), custom_call_target="tpu_custom_call" | custom-call | flops 1024 | bytes 1024 | tf_op jit(solution)/shard_map/mix_backward/pallas_call | solution.py:945
  394.8 4.2 all-to-all-start.7
  400.5 4.5 add_convert_fusion.1
  408.3 4.1 all-to-all-start.8
  416.6 6.1 %maps_backward.1 = (bf16[2,2,256,128]{3,2,1,0:T(8,128)(2,1)}, bf16[4,128,384]{2,1,0:T(8,128)(2,1)}, f32[8,128]{1,0:T(8,128)}) custom-call(s32[2]{0:T(128)} %pad_add_fusion.place_ref.refs_0_, bf16[4,2,48,768]{3,2,1,0:T(8,128)(2,1)} %slice.129.packed_ref, bf16[4,2,272,128]{3,2,1,0:T(8,128)(2,1)} %all-to-all-done.7.maps_ref, ...), custom_call_target="tpu_custom_call" | custom-call | flops 1024 | bytes 1024 | tf_op jit(solution)/shard_map/maps_backward/pallas_call | solution.py:1175
  430.3 5.3 %collective-permute-done.15 = bf16[128,384]{1,0:T(8,128)(2,1)S(1)} collective-permute-done((bf16[128,384]{1,0:T(8,128)(2,1)}, bf16[128,384]{1,0:T(8,128)(2,1)S(1)}, u32[]{:S(2)}, u32[]{:S(2)}) %collective-permute-start.15) | collective-permute-done | bytes 98336 | tf_op jit(solution)/shard_map/ppermute | solution.py:1564
  436.7 11.8 %all-to-all-done.8 = bf16[4,2,256,768]{3,2,1,0:T(8,128)(2,1)S(1)} async-done(((bf16[4,2,256,768]{3,2,1,0:T(8,128)(2,1)}), bf16[4,2,256,768]{3,2,1,0:T(8,128)(2,1)S(1)}, u32[]{:S(2)}, u32[]{:S(2)}) %all-to-all-start.8) | async-done | bytes 3145760 | tf_op jit(solution)/shard_map/all_to_all | solution.py:1316
  454.8 4.2 all-to-all-start.9
  467.5 5.1 all-to-all-done.9.share_ref
  487.8 4.0 collective-permute-done.21
  512.9 4.4 owner_update.1
  (258 shorter events, 137.1 us)
Async XLA Ops:
  7.2 60.8 %all-gather.5.cloned.1.call-start = ((), (), s32[]{:S(2)}) async-start(), calls=%async_computation.12 | async-start | bytes 2949120 | tf_op jit(solution)/shard_map/all_gather | solution.py:1375
  23.8 42.7 %all-to-all-start = ((bf16[4,256,1536]{2,1,0:T(8,128)(2,1)}), bf16[4,256,1536]{2,1,0:T(8,128)(2,1)}, u32[]{:S(2)}, u32[]{:S(2)}) async-start(bf16[4,256,1536]{2,1,0:T(8,128)(2,1)} %broadcast_in_dim.67), calls=%async_computation | async-start | bytes 6291456 | tf_op jit(solution)/shard_map/all_to_all | solution.py:1316
  30.0 8.2 %collective-permute-start.1 = (bf16[2,256,768]{2,1,0:T(8,128)(2,1)}, bf16[2,256,768]{2,1,0:T(8,128)(2,1)S(1)}, u32[]{:S(2)}, u32[]{:S(2)}) collective-permute-start(bf16[2,256,768]{2,1,0:T(8,128)(2,1)} %get-tuple-element.253), channel_id=1, source_target_pairs={{0,1},{1,0},{2,3},{3,2},{4,5},{5,4},{6,7},{7,6},{8,9},{9,8},{10,11... | collective-permute-start | bytes 2359304 | tf_op jit(solution)/shard_map/ppermute | solution.py:1304
  68.7 11.9 %collective-permute-start.2 = (bf16[4,256,1536]{2,1,0:T(8,128)(2,1)}, bf16[4,256,1536]{2,1,0:T(8,128)(2,1)}, u32[]{:S(2)}, u32[]{:S(2)}) collective-permute-start(bf16[4,256,1536]{2,1,0:T(8,128)(2,1)} %all-to-all-done.own_ref.refs_1_.own_0), channel_id=1, source_target_pairs={{0,1},{1,0},{2,3},{3,2},{4,5},{5,4},{6,7},{7,6},{8,9},{9,8},{10,11... | collective-permute-start | bytes 9437192 | tf_op jit(solution)/shard_map/ppermute | solution.py:1304
  68.8 41.8 %all-to-all-start.1 = ((bf16[4,256,1536]{2,1,0:T(8,128)(2,1)}), bf16[4,256,1536]{2,1,0:T(8,128)(2,1)}, u32[]{:S(2)}, u32[]{:S(2)}) async-start(bf16[4,256,1536]{2,1,0:T(8,128)(2,1)} %broadcast_in_dim.68), calls=%async_computation.1 | async-start | bytes 6291456 | tf_op jit(solution)/shard_map/all_to_all | solution.py:1316
  73.5 33.9 %all-gather.9.cloned.1.call-start = ((), (), s32[]{:S(2)}) async-start(), calls=%async_computation.16 | async-start | bytes 1474560 | tf_op jit(solution)/shard_map/all_gather | solution.py:1375
  110.6 6.0 %collective-permute-start.3 = (bf16[4,256,1536]{2,1,0:T(8,128)(2,1)}, bf16[4,256,1536]{2,1,0:T(8,128)(2,1)}, u32[]{:S(2)}, u32[]{:S(2)}) collective-permute-start(bf16[4,256,1536]{2,1,0:T(8,128)(2,1)} %all-to-all-done.1.own_ref.refs_1_.own_1), channel_id=1, source_target_pairs={{0,1},{1,0},{2,3},{3,2},{4,5},{5,4},{6,7},{7,6},{8,9},{9,8},{10,11... | collective-permute-start | bytes 9437192 | tf_op jit(solution)/shard_map/ppermute | solution.py:1304
  110.6 41.7 %all-to-all-start.2 = ((bf16[4,256,1536]{2,1,0:T(8,128)(2,1)}), bf16[4,256,1536]{2,1,0:T(8,128)(2,1)}, u32[]{:S(2)}, u32[]{:S(2)}) async-start(bf16[4,256,1536]{2,1,0:T(8,128)(2,1)} %broadcast_in_dim.71), calls=%async_computation.2 | async-start | bytes 6291456 | tf_op jit(solution)/shard_map/all_to_all | solution.py:1316
  115.2 33.8 %all-gather.7.cloned.1.call-start = ((), (), s32[]{:S(2)}) async-start(), calls=%async_computation.13 | async-start | bytes 1474560 | tf_op jit(solution)/shard_map/all_gather | solution.py:1375
  152.3 6.0 %collective-permute-start.4 = (bf16[4,256,1536]{2,1,0:T(8,128)(2,1)}, bf16[4,256,1536]{2,1,0:T(8,128)(2,1)}, u32[]{:S(2)}, u32[]{:S(2)}) collective-permute-start(bf16[4,256,1536]{2,1,0:T(8,128)(2,1)} %all-to-all-done.2.cot_own_ref.refs_3_), channel_id=1, source_target_pairs={{0,1},{1,0},{2,3},{3,2},{4,5},{5,4},{6,7},{7,6},{8,9},{9,8},{10,11... | collective-permute-start | bytes 9437192 | tf_op jit(solution)/shard_map/ppermute | solution.py:1304
  152.3 40.7 %all-to-all-start.3 = ((bf16[4,256,1536]{2,1,0:T(8,128)(2,1)}), bf16[4,256,1536]{2,1,0:T(8,128)(2,1)S(1)}, u32[]{:S(2)}, u32[]{:S(2)}) async-start(bf16[4,256,1536]{2,1,0:T(8,128)(2,1)} %broadcast_in_dim.72), calls=%async_computation.3 | async-start | bytes 6291456 | tf_op jit(solution)/shard_map/all_to_all | solution.py:1316
  193.1 5.7 %collective-permute-start.5 = (bf16[4,256,1536]{2,1,0:T(8,128)(2,1)S(1)}, bf16[4,256,1536]{2,1,0:T(8,128)(2,1)S(1)}, u32[]{:S(2)}, u32[]{:S(2)}) collective-permute-start(bf16[4,256,1536]{2,1,0:T(8,128)(2,1)S(1)} %all-to-all-done.3.cot_own_ref.refs_3_), channel_id=1, source_target_pairs={{0,1},{1,0},{2,3},{3,2},{4,5},{5,4},{6,7},{7,6},{8,9},{9,8},{10,11... | collective-permute-start | bytes 9437192 | tf_op jit(solution)/shard_map/ppermute | solution.py:1304
  198.7 18.3 %collective-permute-start.6 = (bf16[4,2,256,768]{3,2,1,0:T(8,128)(2,1)}, bf16[4,2,256,768]{3,2,1,0:T(8,128)(2,1)}, u32[]{:S(2)}, u32[]{:S(2)}) collective-permute-start(bf16[4,2,256,768]{3,2,1,0:T(8,128)(2,1)} %get-tuple-element.160), channel_id=1, source_target_pairs={{0,1},{1,0},{2,3},{3,2},{4,5},{5,4},{6,7},{7,6},{8,9},{9,8},{10,11... | collective-permute-start | bytes 9437192 | tf_op jit(solution)/shard_map/ppermute | solution.py:1304
  223.6 44.7 %collective-permute-start.10 = (bf16[4,2,256,768]{3,2,1,0:T(8,128)(2,1)}, bf16[4,2,256,768]{3,2,1,0:T(8,128)(2,1)}, u32[]{:S(2)}, u32[]{:S(2)}) collective-permute-start(bf16[4,2,256,768]{3,2,1,0:T(8,128)(2,1)} %get-tuple-element.168), channel_id=1, source_target_pairs={{0,1},{1,0},{2,3},{3,2},{4,5},{5,4},{6,7},{7,6},{8,9},{9,8},{10,11... | collective-permute-start | bytes 9437192 | tf_op jit(solution)/shard_map/ppermute | solution.py:1304
  232.4 40.2 %all-to-all-start.4 = ((bf16[4,2,256,768]{3,2,1,0:T(8,128)(2,1)}), bf16[4,2,256,768]{3,2,1,0:T(8,128)(2,1)S(1)}, u32[]{:S(2)}, u32[]{:S(2)}) async-start(bf16[4,2,256,768]{3,2,1,0:T(8,128)(2,1)} %add_convert_fusion.3), calls=%async_computation.4 | async-start | bytes 6291456 | tf_op jit(solution)/shard_map/all_to_all | solution.py:1316
  236.1 92.7 %reduce-scatter.3.cloned.1.call-start = ((), (), s32[]{:S(2)}) async-start(), calls=%async_computation.14 | async-start | bytes 2949120 | tf_op jit(solution)/shard_map/reduce_scatter | solution.py:1435
  272.6 56.2 %all-to-all-start.5 = ((bf16[4,2,256,768]{3,2,1,0:T(8,128)(2,1)}), bf16[4,2,256,768]{3,2,1,0:T(8,128)(2,1)}, u32[]{:S(2)}, u32[]{:S(2)}) async-start(bf16[4,2,256,768]{3,2,1,0:T(8,128)(2,1)} %add_convert_fusion.2), calls=%async_computation.5 | async-start | bytes 6291456 | tf_op jit(solution)/shard_map/all_to_all | solution.py:1316
  328.9 6.9 %collective-permute-start.11 = (bf16[4,2,304,768]{3,2,1,0:T(8,128)(2,1)}, bf16[4,2,304,768]{3,2,1,0:T(8,128)(2,1)}, u32[]{:S(2)}, u32[]{:S(2)}) collective-permute-start(bf16[4,2,304,768]{3,2,1,0:T(8,128)(2,1)} %get-tuple-element.188), channel_id=1, source_target_pairs={{0,1},{1,0},{2,3},{3,2},{4,5},{5,4},{6,7},{7,6},{8,9},{9,8},{10,11... | collective-permute-start | bytes 11206664 | tf_op jit(solution)/shard_map/ppermute | solution.py:1304
  341.2 48.9 %all-to-all-start.6 = ((bf16[4,2,304,768]{3,2,1,0:T(8,128)(2,1)}), bf16[4,2,304,768]{3,2,1,0:T(8,128)(2,1)}, u32[]{:S(2)}, u32[]{:S(2)}) async-start(bf16[4,2,304,768]{3,2,1,0:T(8,128)(2,1)} %add_convert_fusion), calls=%async_computation.7 | async-start | bytes 7471104 | tf_op jit(solution)/shard_map/all_to_all | solution.py:1316
  346.0 90.6 %reduce-scatter.5.cloned.1.call-start = ((), (), s32[]{:S(2)}) async-start(), calls=%async_computation.15 | async-start | bytes 1536000 | tf_op jit(solution)/shard_map/reduce_scatter | solution.py:1435
  394.4 6.0 %collective-permute-start.13 = (bf16[4,2,256,768]{3,2,1,0:T(8,128)(2,1)}, bf16[4,2,256,768]{3,2,1,0:T(8,128)(2,1)}, u32[]{:S(2)}, u32[]{:S(2)}) collective-permute-start(bf16[4,2,256,768]{3,2,1,0:T(8,128)(2,1)} %get-tuple-element.207), channel_id=1, source_target_pairs={{0,1},{1,0},{2,3},{3,2},{4,5},{5,4},{6,7},{7,6},{8,9},{9,8},{10,11... | collective-permute-start | bytes 9437192 | tf_op jit(solution)/shard_map/ppermute | solution.py:1304
  394.8 13.4 %all-to-all-start.7 = ((bf16[4,2,272,128]{3,2,1,0:T(8,128)(2,1)}), bf16[4,2,272,128]{3,2,1,0:T(8,128)(2,1)}, u32[]{:S(2)}, u32[]{:S(2)}) async-start(bf16[4,2,272,128]{3,2,1,0:T(8,128)(2,1)} %add_convert_fusion.4), calls=%async_computation.8 | async-start | bytes 1114112 | tf_op jit(solution)/shard_map/all_to_all | solution.py:1316
  408.3 40.2 %all-to-all-start.8 = ((bf16[4,2,256,768]{3,2,1,0:T(8,128)(2,1)}), bf16[4,2,256,768]{3,2,1,0:T(8,128)(2,1)S(1)}, u32[]{:S(2)}, u32[]{:S(2)}) async-start(bf16[4,2,256,768]{3,2,1,0:T(8,128)(2,1)} %add_convert_fusion.1), calls=%async_computation.9 | async-start | bytes 6291456 | tf_op jit(solution)/shard_map/all_to_all | solution.py:1316
  424.4 5.9 %collective-permute-start.16 = (bf16[128,384]{1,0:T(8,128)(2,1)}, bf16[128,384]{1,0:T(8,128)(2,1)S(1)}, u32[]{:S(2)}, u32[]{:S(2)}) collective-permute-start(bf16[128,384]{1,0:T(8,128)(2,1)} %get-tuple-element.259), channel_id=1, source_target_pairs={{0,24},{8,0},{16,8},{24,16},{1,25},{9,1},{17,9},{25,17},{2,26},{10... | collective-permute-start | bytes 294920 | tf_op jit(solution)/shard_map/ppermute | solution.py:1564
  426.8 8.9 %collective-permute-start.15 = (bf16[128,384]{1,0:T(8,128)(2,1)}, bf16[128,384]{1,0:T(8,128)(2,1)S(1)}, u32[]{:S(2)}, u32[]{:S(2)}) collective-permute-start(bf16[128,384]{1,0:T(8,128)(2,1)} %get-tuple-element.260), channel_id=1, source_target_pairs={{0,16},{8,24},{16,0},{24,8},{1,17},{9,25},{17,1},{25,9},{2,18},{10... | collective-permute-start | bytes 294920 | tf_op jit(solution)/shard_map/ppermute | solution.py:1564
  426.8 8.9 %collective-permute-start.14 = (bf16[128,384]{1,0:T(8,128)(2,1)}, bf16[128,384]{1,0:T(8,128)(2,1)}, u32[]{:S(2)}, u32[]{:S(2)}) collective-permute-start(bf16[128,384]{1,0:T(8,128)(2,1)} %get-tuple-element.258), channel_id=1, source_target_pairs={{0,8},{8,16},{16,24},{24,0},{1,9},{9,17},{17,25},{25,1},{2,10},{10... | collective-permute-start | bytes 294920 | tf_op jit(solution)/shard_map/ppermute | solution.py:1564
  427.8 33.8 %collective-permute-start.17 = (bf16[2,2,256,128]{3,2,1,0:T(8,128)(2,1)}, bf16[2,2,256,128]{3,2,1,0:T(8,128)(2,1)}, u32[]{:S(2)}, u32[]{:S(2)}) collective-permute-start(bf16[2,2,256,128]{3,2,1,0:T(8,128)(2,1)} %get-tuple-element.226), channel_id=1, source_target_pairs={{0,1},{1,0},{2,3},{3,2},{4,5},{5,4},{6,7},{7,6},{8,9},{9,8},{10,11... | collective-permute-start | bytes 786440 | tf_op jit(solution)/shard_map/ppermute | solution.py:1304
  454.8 17.8 %all-to-all-start.9 = ((bf16[4,96,1296]{2,1,0:T(8,128)(2,1)}), bf16[4,96,1296]{2,1,0:T(8,128)(2,1)}, u32[]{:S(2)}, u32[]{:S(2)}) async-start(bf16[4,96,1296]{2,1,0:T(8,128)(2,1)} %bitcast.111), calls=%async_computation.11 | async-start | bytes 2162688 | tf_op jit(solution)/shard_map/all_to_all | solution.py:1439
  482.2 4.2 collective-permute-start.20
  482.5 5.2 collective-permute-start.18
  486.4 5.3 %collective-permute-start.21 = (f32[96,128]{1,0:T(8,128)S(1)}, f32[96,128]{1,0:T(8,128)S(1)}, u32[]{:S(2)}, u32[]{:S(2)}) collective-permute-start(f32[96,128]{1,0:T(8,128)S(1)} %fusion.40), channel_id=1, source_target_pairs={{0,16},{8,24},{16,0},{24,8},{1,17},{9,25},{17,1},{25,9},{2,18},{10... | collective-permute-start | bytes 147464 | tf_op jit(solution)/shard_map/ppermute | solution.py:1471
  495.9 5.2 collective-permute-start.23
  (40 other events, 276.8 us)
Sparse Core Ops, SparseCore 0:
  15.1 52.8 all-gather.4
  76.5 30.8 all-gather.8
  118.2 30.8 all-gather.6
  272.7 48.4 reduce-scatter.2
  395.0 30.4 reduce-scatter.4

commit v4 on v3

--- a/solution.py
+++ b/solution.py
@@ -1,3 +1,4 @@
+import functools
 import math
 
 import jax
@@ -563,10 +564,23 @@
     return jnp.concatenate([own_ref[0], other_ref[0]], axis=0)
 
 
-def fwd_kernel(
-    place_ref, own_ref, other_ref, w_ref, seg_ref, taps_ref, head_ref, chan_ref,
-    mixed_ref, raw_ref, pre_ref, y_ref, hin_ref, buf, state,
+def fwd_pieces(place_ref, *refs):
+    own_out, other_out, held, sems = refs[20:24]
+    tokens = block_rows(refs[:10], place_ref, held, sems)
+    own_out[0] = tokens[:SPAN]
+    other_out[0] = tokens[SPAN:]
+    fwd_step(tokens, *refs[10:20], *refs[24:])
+
+
+def fwd_blocks(place_ref, own_ref, other_ref, *refs):
+    fwd_step(both_tokens(own_ref, other_ref), *refs)
+
+
+def fwd_step(
+    tokens, w_ref, seg_ref, taps_ref, head_ref, chan_ref,
+    mixed_ref, raw_ref, pre_ref, y_ref, hin_ref, *more,
 ):
+    buf, state = more[-2:]
     block = pl.program_id(0)
 
     @pl.when(block == 0)
@@ -575,7 +589,7 @@
         state[...] = jnp.zeros_like(state)
 
     width = QUARTER + 2 * STATE
-    projected = dot_nn(both_tokens(own_ref, other_ref), w_ref[...])
+    projected = dot_nn(tokens, w_ref[...])
     taps = taps_ref[...]
     head = head_ref[...]
     skip = chan_ref[1:2]
@@ -639,6 +653,56 @@
         state[q] = pass_state(passing, held_f, added)
 
 
+def piece_copies(refs, m, slot, held, sems):
+    half = SPAN // 2
+    for q in range(2):
+        own, by_x, by_y, far_a, far_b = refs[5 * q : 5 * (q + 1)]
+        if slot < 3:
+            at = pl.ds(q * SPAN, SPAN)
+            source = (own, by_x, by_y)[slot]
+            source = source if m is None else source.at[m]
+            yield pltpu.make_async_copy(source, held.at[slot, at], sems.at[slot, q, 0])
+        else:
+            for part, source in enumerate((far_a, far_b)):
+                at = pl.ds(q * SPAN + part * half, half)
+                yield pltpu.make_async_copy(source, held.at[slot, at], sems.at[slot, q, part])
+
+
+def start_pieces(refs, m, held, sems):
+    @pl.when(pl.program_id(0) == 0)
+    def _():
+        for slot in range(BLOCKS):
+            for copy in piece_copies(refs, m, slot, held, sems):
+                copy.start()
+
+
+def slot_rows(refs, m, held, sems):
+    start_pieces(refs, m, held, sems)
+    for slot in range(BLOCKS):
+        @pl.when(pl.program_id(0) == slot)
+        def _():
+            for copy in piece_copies(refs, m, slot, held, sems):
+                copy.wait()
+
+    return held[pl.program_id(0)]
+
+
+def block_rows(refs, place_ref, held, sems):
+    start_pieces(refs, None, held, sems)
+
+    @pl.when(pl.program_id(0) == 0)
+    def _():
+        for slot in range(BLOCKS):
+            for copy in piece_copies(refs, None, slot, held, sems):
+                copy.wait()
+
+    return held[pl.program_id(0) ^ place_ref[1]]
+
+
+def cot_scratch():
+    return [pltpu.VMEM((BLOCKS, 2 * SPAN, D), BF), pltpu.SemaphoreType.DMA((BLOCKS, 2, 2))]
+
+
 def core_rows(place_ref):
     half = D // 2
     core = place_ref[0]
@@ -647,13 +711,12 @@
     return pl.ds(own, half), pl.ds(other, half)
 
 
-def gate_kernel(
-    place_ref, own_ref, other_ref, cot_own_ref, cot_other_ref, y_ref, w_gate_ref, w_out_ref,
-    chan_ref,
-    gate_ref, d_gated_ref, mine_ref, theirs_ref, stat_ref,
-):
+def gate_kernel(m, place_ref, own_ref, other_ref, *refs):
+    cots = refs[:10]
+    (y_ref, w_gate_ref, w_out_ref, chan_ref, gate_ref, d_gated_ref, mine_ref, theirs_ref,
+     stat_ref, held, sems) = refs[10:]
     gate = dot_nn(both_tokens(own_ref, other_ref), w_gate_ref[...])
-    d_gated = dot_nn(both_tokens(cot_own_ref, cot_other_ref), w_out_ref[...])
+    d_gated = dot_nn(slot_rows(cots, m, held, sems), w_out_ref[...])
     guns = []
     for q in range(2):
         at = slice(q * SPAN, (q + 1) * SPAN)
@@ -692,21 +755,22 @@
 
 
 def gate_back_first(*refs):
-    gate_back_step(*refs[:10], None, *refs[10:])
+    gate_back_step(0, refs, None, *refs[18:])
 
 
 def gate_back_last(*refs):
-    gate_back_step(*refs[:11], *refs[11:14], refs[15])
-    finish_sums(refs[15], refs[14])
-
-
-def gate_back_step(
-    place_ref, own_ref, other_ref, cot_own_ref, cot_other_ref, y_ref, gate_ref, d_gated_ref,
-    stat_ref, chan_ref, seed_ref,
-    dy_ref, d_gate_ref, g_gain_ref, g_ref,
-):
+    dy_ref, d_gate_ref, g_gain_ref, parts_ref, held, sems, total = refs[19:]
+    gate_back_step(1, refs, refs[18], dy_ref, d_gate_ref, g_gain_ref, total, held, sems)
+    finish_sums(total, parts_ref)
+
+
+def gate_back_step(m, refs, seed_ref, dy_ref, d_gate_ref, g_gain_ref, g_ref, held, sems):
+    own_ref, other_ref = refs[1:3]
+    cots = refs[3:13]
+    y_ref, gate_ref, d_gated_ref, stat_ref, chan_ref = refs[13:18]
     start_sums(g_ref, seed_ref)
     start_sums(g_gain_ref, None)
+    cot = slot_rows(cots, m, held, sems)
     gateds = []
     d_gates = []
     for q in range(2):
@@ -729,7 +793,7 @@
         g_gain_ref[0:1] += jnp.sum(d_gated * gated_in * scale, axis=0, keepdims=True)
     gated = jnp.concatenate(gateds, axis=0)
     d_gate = jnp.concatenate(d_gates, axis=0)
-    g_ref[:QUARTER] += dot_tn(gated, both_tokens(cot_own_ref, cot_other_ref))
+    g_ref[:QUARTER] += dot_tn(gated, cot)
     g_ref[QUARTER:] += dot_tn(d_gate, both_tokens(own_ref, other_ref))
 
 
@@ -971,54 +1035,78 @@
     return fixed_spec(rows, width), jax.ShapeDtypeStruct((rows, width), F32)
 
 
-def run_fwd(place, tokens, w_first, rows, taps, head, chan):
+def run_fwd(place, tokens, w_first, segs, taps, head, chan):
     width = QUARTER + 2 * STATE
+    pieces = len(tokens) > 2
+    outs = [
+        slot_out(SPAN, width, BF, upward),
+        slot_out(SPAN, 128, F32, upward),
+        slot_out(SPAN, width, F32, upward),
+        slot_out(SPAN, QUARTER, F32, upward),
+        slot_out(PARTS * QUARTER, STATE, BF, upward),
+    ]
+    if pieces:
+        shape = jax.ShapeDtypeStruct((BLOCKS, SPAN, D), BF)
+        outs += [(spec, shape) for spec in token_specs(upward)]
     return call_blocks(
-        fwd_kernel,
+        fwd_pieces if pieces else fwd_blocks,
         "mix_forward",
         place,
-        (*tokens, w_first, rows, taps, head, chan),
+        (*tokens, w_first, segs, taps, head, chan),
         [
-            *token_specs(upward),
+            *(cot_specs() if pieces else token_specs(upward)),
             fixed_spec(D, width + 128),
             segment_spec(),
             fixed_spec(8, width),
             fixed_spec(8, 128),
             fixed_spec(8, QUARTER),
         ],
-        [
-            slot_out(SPAN, width, BF, upward),
-            slot_out(SPAN, 128, F32, upward),
-            slot_out(SPAN, width, F32, upward),
-            slot_out(SPAN, QUARTER, F32, upward),
-            slot_out(PARTS * QUARTER, STATE, BF, upward),
-        ],
-        [pltpu.VMEM((2, SPAN + 8, width), F32), pltpu.VMEM((2, QUARTER, STATE), F32)],
-    )
-
-
-def run_gate(place, tokens, cots, y, w_gate, w_out, chan):
+        outs,
+        (cot_scratch() if pieces else [])
+        + [pltpu.VMEM((2, SPAN + 8, width), F32), pltpu.VMEM((2, QUARTER, STATE), F32)],
+    )
+
+
+def by_slot(spec):
+    def index(j, place):
+        return spec.index_map(j ^ place[1], place)
+
+    return pl.BlockSpec(spec.block_shape, index)
+
+
+def cot_specs():
+    return [pl.BlockSpec(memory_space=pl.ANY)] * 10
+
+
+def by_slot_outs(outs):
+    return [(by_slot(spec), shape) for spec, shape in outs]
+
+
+def run_gate(m, place, tokens, cots, y, w_gate, w_out, chan):
     half = D // 2
     return call_blocks(
-        gate_kernel,
+        functools.partial(gate_kernel, m),
         "gate_forward",
         place,
         (*tokens, *cots, y, w_gate, w_out, chan),
         [
-            *token_specs(upward),
-            *token_specs(upward),
-            slot_spec(SPAN, QUARTER, upward),
+            *[by_slot(spec) for spec in token_specs(upward)],
+            *cot_specs(),
+            by_slot(slot_spec(SPAN, QUARTER, upward)),
             fixed_spec(D, QUARTER),
             fixed_spec(D, QUARTER),
             fixed_spec(8, QUARTER),
         ],
-        [
-            slot_out(SPAN, QUARTER, F32, upward),
-            slot_out(SPAN, QUARTER, F32, upward),
-            lead_out(SPAN, half, upward),
-            lead_out(SPAN, half, upward),
-            slot_out(2, SPAN, F32, upward),
-        ],
+        by_slot_outs(
+            [
+                slot_out(SPAN, QUARTER, F32, upward),
+                slot_out(SPAN, QUARTER, F32, upward),
+                lead_out(SPAN, half, upward),
+                lead_out(SPAN, half, upward),
+                slot_out(2, SPAN, F32, upward),
+            ]
+        ),
+        cot_scratch(),
     )
 
 
@@ -1040,22 +1128,16 @@
         place,
         (*tokens, *cots, y, gate, d_gated, stat, chan) + ((seed,) if last else ()),
         [
-            *token_specs(upward),
-            *token_specs(upward),
-            slot_spec(SPAN, QUARTER, upward),
-            slot_spec(SPAN, QUARTER, upward),
-            slot_spec(SPAN, QUARTER, upward),
-            slot_spec(2, SPAN, upward),
+            *[by_slot(spec) for spec in token_specs(upward)],
+            *cot_specs(),
+            *[by_slot(slot_spec(SPAN, QUARTER, upward))] * 3,
+            by_slot(slot_spec(2, SPAN, upward)),
             fixed_spec(8, QUARTER),
         ]
         + ([fixed_spec(2 * QUARTER, D)] if last else []),
-        [
-            slot_out(SPAN, QUARTER, BF, upward),
-            slot_out(SPAN, QUARTER, BF, upward),
-            fixed_out(8, QUARTER),
-            total,
-        ],
-        scratch,
+        by_slot_outs([slot_out(SPAN, QUARTER, BF, upward), slot_out(SPAN, QUARTER, BF, upward)])
+        + [fixed_out(8, QUARTER), total],
+        cot_scratch() + scratch,
     )
 
 
@@ -1400,8 +1482,10 @@
     rows_whole = whole_rows(inputs)
     normed_own = rms_scale(rows_whole.astype(F32), prenorm).astype(BF)
     cot_own = whole_rows(cotangent)
-    first_copies, second_copies = after((copies(normed_own[0]), copies(normed_own[1])))
-    own_0 = exchange(first_copies)
+    half = SPAN // 2
+    mine_0, second_copies = after((normed_own[0], copies(normed_own[1])))
+    near_0 = (mine_0, over_x(mine_0), over_y(mine_0))
+    own_swapped = swap_cores(mine_0)
 
     seg_mine = jnp.concatenate(
         [
@@ -1435,14 +1519,13 @@
         return lax.psum_scatter(parts, "dp", scatter_dimension=0, tiled=True)[0]
 
     def by_place(columns):
-        blocks = columns.T.reshape(BLOCKS, shard, -1)
-        return lax.all_to_all(blocks, "seq", 0, 0, tiled=True)
+        return columns.T.reshape(BLOCKS, shard, -1)
 
     def forward(m, place, tokens):
         return run_fwd(place, tokens, w_first, segs[m], taps, head, chan)
 
     def gate_forward(m, place):
-        return run_gate(place, normed[m], cots[m], kept[m][3], w_gate, w_out, chan)
+        return run_gate(m, place, normed[m], cots[m], kept[m][3], w_gate, w_out, chan)
 
     def gate_backward(m, place, gate, d_gated, sums, seed):
         return run_gate_back(
@@ -1481,32 +1564,43 @@
 
     stepproj_own = lax.dynamic_slice_in_dim(stepproj.T, chip * shard, shard, 1)
     outproj_own = lax.dynamic_slice_in_dim(outproj, chip * shard, shard, 1).T
-    own_0, w_first, second_copies, cot_own, segs, taps, head, chan, stepproj_own, outproj_own = (
-        after(
-            (
-                own_0, w_first, second_copies, cot_own, segs, taps, head, chan, stepproj_own,
-                outproj_own,
-            )
-        )
-    )
+    near_0, own_swapped, cot_own, segs, taps, head, chan, stepproj_own, outproj_own = after(
+        (near_0, own_swapped, cot_own, segs, taps, head, chan, stepproj_own, outproj_own)
+    )
+    far = over_x(near_0[2][:half]), over_y(near_0[1][half:])
+    near_swapped = [swap_cores(piece) for piece in near_0[1:]]
+    far, near_swapped, second_copies = after((far, near_swapped, second_copies))
     own_1 = exchange(second_copies)
-    normed = [with_other(own_0)]
-    place, cot_copies = after((place, [copies(cot) for cot in (cot_own[0], cot_own[1])]))
-    kept = [forward(0, place, normed[0])]
-
-    own_1, w_gate, piece, place = after((own_1, w_gate, cot_copies[0], place), kept[0][1])
+    far, w_first = after((far, w_first))
+    cot_other = swap_cores(cot_own)
+    first_pieces = (
+        *near_0, *far, own_swapped, *near_swapped, *[swap_cores(piece) for piece in far]
+    )
+    *kept_0, own_0, other_0 = forward(0, place, first_pieces)
+    kept = [kept_0]
+    normed = [(own_0, other_0)]
+    cot_own, cot_other, place = after((cot_own, cot_other, place), kept[0][1])
+    by_x, by_y = over_x(cot_own), over_y(cot_own)
+    own_1, w_gate, place = after((own_1, w_gate, place))
     normed.append(with_other(own_1))
-    cot_0 = exchange(piece)
     kept.append(forward(1, place, normed[1]))
 
-    cot_0, w_out, piece, place = after((cot_0, w_out, cot_copies[1], place), kept[1][1])
-    cots = [with_other(cot_0)]
-    cot_1 = exchange(piece)
+    by_x, by_y, w_out, place = after((by_x, by_y, w_out, place), kept[1][1])
+    def far_pieces(m, by_x, by_y):
+        return over_x(by_y[m, :half]), over_y(by_x[m, half:])
+
+    def cot_pieces(far):
+        return (cot_own, by_x, by_y, *far, *near_other, *[swap_cores(piece) for piece in far])
+
+    far_0 = far_pieces(0, by_x, by_y)
+    near_other = (cot_other, swap_cores(by_x), swap_cores(by_y))
+    far_0, near_other, far_from, place = after((far_0, near_other, (by_x, by_y), place))
+    cots = [cot_pieces(far_0)]
+    far_1 = far_pieces(1, *far_from)
     gate_0, d_gated_0, mine_0, theirs_0, stat_0 = gate_forward(0, place)
-
-    cot_1, place, theirs_0 = after((cot_1, place, theirs_0), stat_0)
-    cots.append(with_other(cot_1))
-    branch_0 = core_sums(mine_0, after(theirs_0, cots[1][1]))
+    place, theirs_0, far_1 = after((place, theirs_0, far_1), stat_0)
+    cots.append(cot_pieces(far_1))
+    branch_0 = core_sums(mine_0, after(theirs_0, cots[1][8:]))
     gate_1, d_gated_1, mine_1, theirs_1, stat_1 = gate_forward(1, place)
 
     stats = jnp.stack([stat_0, after(stat_1, branch_0)])
@@ -1584,13 +1678,15 @@
     vector = jnp.concatenate([small.reshape(-1) for small in small_parts])
     vector = jnp.pad(vector, (0, -vector.size % 1024)).reshape(-1, 128)
 
-    token_1, mid_rows, late_rows, state_rows = after(
-        (token_1, mid_rows, late_rows, state_rows), vector
-    )
+    late_rows, mid_rows, state_rows = after((late_rows, mid_rows, state_rows))
     shares = jnp.concatenate(
         [mid_rows, late_rows[:QUARTER], state_rows, late_rows[QUARTER:]], axis=0
     )
-    share = by_place(shares)
+    other_vector = swap_cores(vector)
+    token_1, shares, vector, other_vector = after(
+        (token_1, by_place(shares), vector, other_vector)
+    )
+    share = exchange(shares)
     d_tokens = [summed(token_0[:, :, :SPAN]), summed(token_1)]
     w_state = w_first[:, QUARTER : QUARTER + 2 * STATE]
 
@@ -1651,19 +1747,19 @@
     square = owner_sums[0, shard] + jnp.sum(g_prenorm * g_prenorm)
     line = jnp.where(lanes == shard, square, g_prenorm)
     table = jnp.where(jnp.arange(owners)[:, None] == owner, line[None], 0.0)
-    table = sum_seq(sum_dp(jnp.concatenate([table, vector], axis=0)))
+    table = sum_seq(sum_dp(jnp.concatenate([table, vector, other_vector], axis=0)))
     small_sums = []
     start = 0
-    vector = table[owners:].reshape(-1)
+    both_vectors = table[owners:].reshape(2, -1)
+    vector = both_vectors[0]
     for shape in small_shapes:
         size = math.prod(shape)
         small_sums.append(vector[start : start + size].reshape(shape))
         start += size
     s_taps, s_gain, s_head, s_state_taps = small_sums
 
-    small_sq = sum(jnp.sum(term * term) for term in small_sums)
-    small_sq = small_sq + swap_cores(small_sq)
-    grad_norm = jnp.sqrt(jnp.sum(table[:owners, shard]) + small_sq)
+    small_sq = jnp.sum(both_vectors * both_vectors, axis=1)
+    grad_norm = jnp.sqrt(jnp.sum(table[:owners, shard]) + (small_sq[0] + small_sq[1]))
     s_prenorm = lax.dynamic_slice_in_dim(
         table[:owners, :shard], core * (owners // 2), owners // 2, 0
     ).reshape(half_d)

time: 535 us -> 501 us (0.936)
  waiting for transfers between devices: 118 us -> 87.3 us
  Pallas kernels: 216 us -> 226 us
    all_to_all x9 -> x7, waiting for transfers between devices: 65.4 us -> 12 us  [exchange(): return lax.all_to_all(blocks, 'seq', 0, 0, tiled=True)]
    ppermute x2 -> x7, waiting for transfers between devices: 5.15 us -> 40 us  [over_x(): return lax.ppermute(block, 'seq', ROUTE_X)]
    all_to_all x9 -> x7, starting transfers between devices: 48 us -> 30.4 us  [exchange(): return lax.all_to_all(blocks, 'seq', 0, 0, tiled=True)]
    pallas_call x8, Pallas kernels: 202 us -> 212 us  [call_blocks(): pl.pallas_call(kernel, grid_spec=pltpu.PrefetchScalarGridSpec(num_scalar_...]
    all_gather x3, waiting for transfers between devices: 10.4 us -> 3.02 us  [all_rows(): return lax.all_gather(block, 'dp', axis=0, tiled=True)]
    ppermute x2 -> x7, starting transfers between devices: 3.08 us -> 10.1 us  [over_y(): return lax.ppermute(block, 'seq', ROUTE_Y)]
    ppermute x2 -> x7, starting transfers between devices: 2.9 us -> 9.03 us  [over_x(): return lax.ppermute(block, 'seq', ROUTE_X)]
    ppermute x16 -> x25, waiting for transfers between devices: 15.2 us -> 9.06 us  [swap_cores(): return lax.ppermute(block, 'tensor', SWAP)]
  transfers between devices with their start and end apart: 40 -> 56, of which waited for: 26 -> 30; matrix products, arithmetic and copies ran while one was open for 13% -> 14% of each run, Pallas kernels for 40% -> 44%
where the time goes in v4:
time: 501 us; the launch traced here: 495 us
  Pallas kernels  226 us (45%)
  waiting for transfers between devices  87.3 us (17%)
  starting transfers between devices  63.4 us (13%)
  other arithmetic  52.7 us (11%)
  local copies, waits for them, and re-layouts  44.5 us (9%)
  between operations  19.5 us (4%)
    pallas_call x8, Pallas kernels, call_blocks(): pl.pallas_call(kernel, grid_spec=pltpu.PrefetchScalarGridSpec(num_scalar_...  212 us
    ppermute x7, waiting for transfers between devices, over_x(): return lax.ppermute(block, 'seq', ROUTE_X)  40 us
    all_to_all x7, starting transfers between devices, exchange(): return lax.all_to_all(blocks, 'seq', 0, 0, tiled=True)  30.4 us
    convert_element_type x5, other arithmetic, add_low(): return (a.astype(F32) + b.astype(F32)).astype(BF)  18 us
    all_to_all x7, waiting for transfers between devices, exchange(): return lax.all_to_all(blocks, 'seq', 0, 0, tiled=True)  12 us
    ppermute x7, starting transfers between devices, over_y(): return lax.ppermute(block, 'seq', ROUTE_Y)  10.1 us
  transfers between devices with their start and end apart: 56, of which 30 were waited for; matrix products, arithmetic and copies ran while one was open for 14% of the time, Pallas kernels for 44%

profile of v4, /device:TPU:0, one launch (start us, length us, event | category | flops | bytes accessed | tf_op | source)
XLA Modules:
  0.0 495.2 jit_solution(13908789242514623880)
XLA Ops:
  35.4 11.0 %collective-permute-done.1.refs_1_ = bf16[256,1536]{1,0:T(8,128)(2,1)S(1)} collective-permute-done((bf16[256,1536]{1,0:T(8,128)(2,1)S(1)}, bf16[256,1536]{1,0:T(8,128)(2,1)S(1)}, u32[]{:S(2)}, u32[]{:S(2)}) %collective-permute-start.1) | collective-permute-done | bytes 786464 | tf_op jit(solution)/shard_map/ppermute | solution.py:1390
  51.3 9.0 %collective-permute-done.6.refs_3_ = bf16[128,1536]{1,0:T(8,128)(2,1)S(1)} collective-permute-done((bf16[128,1536]{1,0:T(8,128)(2,1)S(1)}, bf16[128,1536]{1,0:T(8,128)(2,1)S(1)}, u32[]{:S(2)}, u32[]{:S(2)}) %collective-permute-start.6) | collective-permute-done | bytes 393248 | tf_op jit(solution)/shard_map/ppermute | solution.py:1390
  61.2 4.7 all-to-all-start
  73.8 29.1 %mix_forward.2 = (bf16[2,4,256,640]{3,2,1,0:T(8,128)(2,1)}, f32[2,4,256,128]{3,2,1,0:T(8,128)}, f32[2,4,256,640]{3,2,1,0:T(8,128)}, f32[2,4,256,384]{3,2,1,0:T(8...) custom-call(s32[2]{0:T(128)} %pad_add_fusion.place_ref.refs_0_, ...), custom_call_target="tpu_custom_call" | custom-call | flops 1024 | bytes 1024 | tf_op jit(solution)/shard_map/mix_forward/pallas_call | solution.py:1009
  109.0 25.5 %mix_forward.3 = (bf16[2,4,256,640]{3,2,1,0:T(8,128)(2,1)}, f32[2,4,256,128]{3,2,1,0:T(8,128)}, f32[2,4,256,640]{3,2,1,0:T(8,128)}, f32[2,4,256,384]{3,2,1,0:T(8,128)}, bf16[2,4,768,128]{3,2,1,0:T(8,128)(2,1)}) custom-call(s32[2]{0:T(128)} %pad_add_fusion.place_ref.refs_0_, bf16[4,256,1536]{2,1,0:T(8,128)(2,1)} %all-to-all-done.own_ref.refs_1_.own_1, ...), custom_call_target="tpu_custom_call" | custom-call | flops 1024 | bytes 1024 | tf_op jit(solution)/shard_map/mix_forward/pallas_call | solution.py:1009
  136.6 4.6 collective-permute-done.12.refs_1_.refs_4_
  147.3 9.0 %collective-permute-done.15.refs_3_.refs_6_ = bf16[128,1536]{1,0:T(8,128)(2,1)S(1)} collective-permute-done((bf16[128,1536]{1,0:T(8,128)(2,1)S(1)}, bf16[128,1536]{1,0:T(8,128)(2,1)S(1)}, u32[]{:S(2)}, u32[]{:S(2)}) %collective-permute-start.15) | collective-permute-done | bytes 393248 | tf_op jit(solution)/shard_map/ppermute | solution.py:1390
  163.4 18.1 %gate_forward.2 = (f32[2,4,256,384]{3,2,1,0:T(8,128)}, f32[2,4,256,384]{3,2,1,0:T(8,128)}, bf16[4,2,256,768]{3,2,1,0:T(8,128)(2,1)}, bf16[4,2,256,768]{3,2,1,0:T(8,128)(2,1)}, f32[2,4,2,256]{3,2,1,0:T(2,128)}) custom-call(s32[2]{0:T(128)} %pad_add_fusion.place_ref.refs_0_, bf16[4,256,1536]{2,1,0:T(8,128)(2,1)} %get-tuple-element.183.own_ref.refs_1_.own_0, ...), custom_call_target="tpu_custom_call" | custom-call | flops 1024 | bytes 1024 | tf_op jit(solution)/shard_map/gate_forward/pallas_call | solution.py:1009
  184.7 18.3 %gate_forward.3 = (f32[2,4,256,384]{3,2,1,0:T(8,128)}, f32[2,4,256,384]{3,2,1,0:T(8,128)}, bf16[4,2,256,768]{3,2,1,0:T(8,128)(2,1)}, bf16[4,2,256,768]{3,2,1,0:T(8,128)(2,1)}, f32[2,4,2,256]{3,2,1,0:T(2,128)}) custom-call(s32[2]{0:T(128)} %pad_add_fusion.place_ref.refs_0_, bf16[4,256,1536]{2,1,0:T(8,128)(2,1)} %all-to-all-done.own_ref.refs_1_.own_1, ...), custom_call_target="tpu_custom_call" | custom-call | flops 1024 | bytes 1024 | tf_op jit(solution)/shard_map/gate_forward/pallas_call | solution.py:1009
  207.5 3.4 collective-permute-done.27
  215.6 3.7 all-to-all-start.1
  219.4 16.2 %gate_backward.2 = (bf16[2,4,256,384]{3,2,1,0:T(8,128)(2,1)}, bf16[2,4,256,384]{3,2,1,0:T(8,128)(2,1)}, f32[8,384]{1,0:T(8,128)}, f32[768,1536]{1,0:T(8,128)}) custom-call(s32[2]{0:T(128)} %pad_add_fusion.place_ref.refs_0_, bf16[4,256,1536]{2,1,0:T(8,128)(2,1)} %get-tuple-element.183.own_ref.refs_1_.own_0, ...), custom_call_target="tpu_custom_call" | custom-call | flops 1024 | bytes 1024 | tf_op jit(solution)/shard_map/gate_backward/pallas_call | solution.py:1009
  235.5 17.3 %gate_backward.3 = (bf16[2,4,256,384]{3,2,1,0:T(8,128)(2,1)}, bf16[2,4,256,384]{3,2,1,0:T(8,128)(2,1)}, f32[8,384]{1,0:T(8,128)}, bf16[4,768,384]{2,1,0:T(8,128)(2,1)}) custom-call(s32[2]{0:T(128)} %pad_add_fusion.place_ref.refs_0_, bf16[4,256,1536]{2,1,0:T(8,128)(2,1)} %all-to-all-done.own_ref.refs_1_.own_1, ...), custom_call_target="tpu_custom_call" | custom-call | flops 1024 | bytes 1024 | tf_op jit(solution)/shard_map/gate_backward/pallas_call | solution.py:1009
  252.9 4.3 add_convert_fusion.2
  257.1 4.9 all-to-all-start.2
  262.1 43.5 %mix_backward.2 = (f32[400,1536]{1,0:T(8,128)}, f32[2,4,272,128]{3,2,1,0:T(8,128)}, f32[8,384]{1,0:T(8,128)}, f32[8,384]{1,0:T(8,128)}, bf16[4,2,304,768]{3,2,1,...) custom-call(s32[2]{0:T(128)} %pad_add_fusion.place_ref.refs_0_, ...), custom_call_target="tpu_custom_call" | custom-call | flops 1024 | bytes 1024 | tf_op jit(solution)/shard_map/mix_backward/pallas_call | solution.py:1009
  314.6 4.8 add_convert_fusion
  319.4 4.8 all-to-all-start.3
  324.7 43.9 %mix_backward.3 = (bf16[4,400,384]{2,1,0:T(8,128)(2,1)}, bf16[4,2,272,128]{3,2,1,0:T(8,128)(2,1)}, bf16[4,2,272,128]{3,2,1,0:T(8,128)(2,1)}, f32[2,4,272,128]{3,...) custom-call(s32[2]{0:T(128)} %pad_add_fusion.place_ref.refs_0_, ...), custom_call_target="tpu_custom_call" | custom-call | flops 1024 | bytes 1024 | tf_op jit(solution)/shard_map/mix_backward/pallas_call | solution.py:1009
  373.3 4.2 all-to-all-start.4
  378.9 4.5 add_convert_fusion.1
  386.6 4.0 all-to-all-start.5
  395.4 6.1 %maps_backward.1 = (bf16[2,2,256,128]{3,2,1,0:T(8,128)(2,1)}, bf16[4,128,384]{2,1,0:T(8,128)(2,1)}, f32[8,128]{1,0:T(8,128)}) custom-call(s32[2]{0:T(128)} %pad_add_fusion.place_ref.refs_0_, bf16[4,2,48,768]{3,2,1,0:T(8,128)(2,1)} %slice.156.packed_ref, bf16[4,2,272,128]{3,2,1,0:T(8,128)(2,1)} %all-to-all-done.4.maps_ref, ...), custom_call_target="tpu_custom_call" | custom-call | flops 1024 | bytes 1024 | tf_op jit(solution)/shard_map/maps_backward/pallas_call | solution.py:1257
  409.3 5.0 %collective-permute-done.34 = bf16[128,384]{1,0:T(8,128)(2,1)S(1)} collective-permute-done((bf16[128,384]{1,0:T(8,128)(2,1)}, bf16[128,384]{1,0:T(8,128)(2,1)S(1)}, u32[]{:S(2)}, u32[]{:S(2)}) %collective-permute-start.34) | collective-permute-done | bytes 98336 | tf_op jit(solution)/shard_map/ppermute | solution.py:1658
  421.5 5.0 %all-to-all-done.5 = bf16[4,2,256,768]{3,2,1,0:T(8,128)(2,1)S(1)} async-done(((bf16[4,2,256,768]{3,2,1,0:T(8,128)(2,1)}), bf16[4,2,256,768]{3,2,1,0:T(8,128)(2,1)S(1)}, u32[]{:S(2)}, u32[]{:S(2)}) %all-to-all-start.5) | async-done | bytes 3145760 | tf_op jit(solution)/shard_map/all_to_all | solution.py:1398
  426.5 4.3 all-to-all-start.6
  430.8 3.6 convert_reduce_fusion.1
  440.4 3.9 all-to-all-done.6.share_ref
  454.9 4.1 collective-permute-done.40
  461.0 5.1 %collective-permute-done.41 = f32[176,128]{1,0:T(8,128)S(1)} collective-permute-done((f32[176,128]{1,0:T(8,128)S(1)}, f32[176,128]{1,0:T(8,128)S(1)}, u32[]{:S(2)}, u32[]{:S(2)}) %collective-permute-start.41) | collective-permute-done | bytes 90144 | tf_op jit(solution)/shard_map/ppermute | solution.py:1554
  472.3 3.6 fusion.11
  482.9 4.4 owner_update.1
  (348 shorter events, 142.0 us)
Async XLA Ops:
  7.2 62.7 %all-gather.5.cloned.1.call-start = ((), (), s32[]{:S(2)}) async-start(), calls=%async_computation.9 | async-start | bytes 2949120 | tf_op jit(solution)/shard_map/all_gather | solution.py:1457
  16.4 17.2 %collective-permute-start.4 = (bf16[2,256,768]{2,1,0:T(8,128)(2,1)}, bf16[2,256,768]{2,1,0:T(8,128)(2,1)}, u32[]{:S(2)}, u32[]{:S(2)}) collective-permute-start(bf16[2,256,768]{2,1,0:T(8,128)(2,1)} %get-tuple-element.295), channel_id=1, source_target_pairs={{0,1},{1,0},{2,3},{3,2},{4,5},{5,4},{6,7},{7,6},{8,9},{9,8},{10,11... | collective-permute-start | bytes 2359304 | tf_op jit(solution)/shard_map/ppermute | solution.py:1386
  25.7 20.7 %collective-permute-start.1 = (bf16[256,1536]{1,0:T(8,128)(2,1)S(1)}, bf16[256,1536]{1,0:T(8,128)(2,1)S(1)}, u32[]{:S(2)}, u32[]{:S(2)}) collective-permute-start(bf16[256,1536]{1,0:T(8,128)(2,1)S(1)} %get-tuple-element.154.refs_0_), channel_id=1, source_target_pairs={{0,2},{2,0},{4,6},{6,4},{1,3},{3,1},{5,7},{7,5},{8,10},{10,8},{12,... | collective-permute-start | bytes 2359304 | tf_op jit(solution)/shard_map/ppermute | solution.py:1390
  28.2 19.7 %collective-permute-start.2 = (bf16[256,1536]{1,0:T(8,128)(2,1)S(1)}, bf16[256,1536]{1,0:T(8,128)(2,1)S(1)}, u32[]{:S(2)}, u32[]{:S(2)}) collective-permute-start(bf16[256,1536]{1,0:T(8,128)(2,1)S(1)} %get-tuple-element.154.refs_0_), channel_id=1, source_target_pairs={{0,4},{2,6},{4,0},{6,2},{1,5},{3,7},{5,1},{7,3},{8,12},{10,14},{12... | collective-permute-start | bytes 2359304 | tf_op jit(solution)/shard_map/ppermute | solution.py:1394
  29.7 18.2 %collective-permute-start.3 = (bf16[256,1536]{1,0:T(8,128)(2,1)S(1)}, bf16[256,1536]{1,0:T(8,128)(2,1)S(1)}, u32[]{:S(2)}, u32[]{:S(2)}) collective-permute-start(bf16[256,1536]{1,0:T(8,128)(2,1)S(1)} %get-tuple-element.154.refs_0_), channel_id=1, source_target_pairs={{0,1},{1,0},{2,3},{3,2},{4,5},{5,4},{6,7},{7,6},{8,9},{9,8},{10,11... | collective-permute-start | bytes 2359304 | tf_op jit(solution)/shard_map/ppermute | solution.py:1386
  48.6 11.8 %collective-permute-start.8 = (bf16[256,1536]{1,0:T(8,128)(2,1)S(1)}, bf16[256,1536]{1,0:T(8,128)(2,1)S(1)}, u32[]{:S(2)}, u32[]{:S(2)}) collective-permute-start(bf16[256,1536]{1,0:T(8,128)(2,1)S(1)} %collective-permute-done.1.refs_1_), channel_id=1, source_target_pairs={{0,1},{1,0},{2,3},{3,2},{4,5},{5,4},{6,7},{7,6},{8,9},{9,8},{10,11... | collective-permute-start | bytes 2359304 | tf_op jit(solution)/shard_map/ppermute | solution.py:1386
  48.6 12.5 %collective-permute-start.9 = (bf16[256,1536]{1,0:T(8,128)(2,1)S(1)}, bf16[256,1536]{1,0:T(8,128)(2,1)}, u32[]{:S(2)}, u32[]{:S(2)}) collective-permute-start(bf16[256,1536]{1,0:T(8,128)(2,1)S(1)} %collective-permute-done.2.refs_2_), channel_id=1, source_target_pairs={{0,1},{1,0},{2,3},{3,2},{4,5},{5,4},{6,7},{7,6},{8,9},{9,8},{10,11... | collective-permute-start | bytes 2359304 | tf_op jit(solution)/shard_map/ppermute | solution.py:1386
  49.2 11.1 %collective-permute-start.6 = (bf16[128,1536]{1,0:T(8,128)(2,1)S(1)}, bf16[128,1536]{1,0:T(8,128)(2,1)S(1)}, u32[]{:S(2)}, u32[]{:S(2)}) collective-permute-start(bf16[128,1536]{1,0:T(8,128)(2,1)S(1)} %slice.144), channel_id=1, source_target_pairs={{0,2},{2,0},{4,6},{6,4},{1,3},{3,1},{5,7},{7,5},{8,10},{10,8},{12,... | collective-permute-start | bytes 1179656 | tf_op jit(solution)/shard_map/ppermute | solution.py:1390
  49.6 10.8 %collective-permute-start.7 = (bf16[128,1536]{1,0:T(8,128)(2,1)S(1)}, bf16[128,1536]{1,0:T(8,128)(2,1)S(1)}, u32[]{:S(2)}, u32[]{:S(2)}) collective-permute-start(bf16[128,1536]{1,0:T(8,128)(2,1)S(1)} %slice.145), channel_id=1, source_target_pairs={{0,4},{2,6},{4,0},{6,2},{1,5},{3,7},{5,1},{7,3},{8,12},{10,14},{12... | collective-permute-start | bytes 1179656 | tf_op jit(solution)/shard_map/ppermute | solution.py:1394
  61.2 41.8 %all-to-all-start = ((bf16[4,256,1536]{2,1,0:T(8,128)(2,1)}), bf16[4,256,1536]{2,1,0:T(8,128)(2,1)}, u32[]{:S(2)}, u32[]{:S(2)}) async-start(bf16[4,256,1536]{2,1,0:T(8,128)(2,1)} %broadcast_in_dim.58), calls=%async_computation | async-start | bytes 6291456 | tf_op jit(solution)/shard_map/all_to_all | solution.py:1398
  65.9 37.1 %all-gather.9.cloned.1.call-start = ((), (), s32[]{:S(2)}) async-start(), calls=%async_computation.13 | async-start | bytes 1474560 | tf_op jit(solution)/shard_map/all_gather | solution.py:1457
  67.7 68.9 %all-gather.7.cloned.1.call-start = ((), (), s32[]{:S(2)}) async-start(), calls=%async_computation.10 | async-start | bytes 1474560 | tf_op jit(solution)/shard_map/all_gather | solution.py:1457
  68.2 34.7 %collective-permute-start.5 = (bf16[2,256,1536]{2,1,0:T(8,128)(2,1)S(1)}, bf16[2,256,1536]{2,1,0:T(8,128)(2,1)}, u32[]{:S(2)}, u32[]{:S(2)}) collective-permute-start(bf16[2,256,1536]{2,1,0:T(8,128)(2,1)S(1)} %maximum_select_fusion.1.refs_0_.refs_3_), channel_id=1, source_target_pairs={{0,1},{1,0},{2,3},{3,2},{4,5},{5,4},{6,7},{7,6},{8,9},{9,8},{10,11... | collective-permute-start | bytes 4718600 | tf_op jit(solution)/shard_map/ppermute | solution.py:1386
  104.1 37.0 %collective-permute-start.12 = (bf16[2,256,1536]{2,1,0:T(8,128)(2,1)S(1)}, bf16[2,256,1536]{2,1,0:T(8,128)(2,1)}, u32[]{:S(2)}, u32[]{:S(2)}) collective-permute-start(bf16[2,256,1536]{2,1,0:T(8,128)(2,1)S(1)} %maximum_select_fusion.1.refs_0_.refs_3_), channel_id=1, source_target_pairs={{0,2},{2,0},{4,6},{6,4},{1,3},{3,1},{5,7},{7,5},{8,10},{10,8},{12,... | collective-permute-start | bytes 4718600 | tf_op jit(solution)/shard_map/ppermute | solution.py:1390
  106.1 36.5 %collective-permute-start.13 = (bf16[2,256,1536]{2,1,0:T(8,128)(2,1)S(1)}, bf16[2,256,1536]{2,1,0:T(8,128)(2,1)}, u32[]{:S(2)}, u32[]{:S(2)}) collective-permute-start(bf16[2,256,1536]{2,1,0:T(8,128)(2,1)S(1)} %maximum_select_fusion.1.refs_0_.refs_3_), channel_id=1, source_target_pairs={{0,4},{2,6},{4,0},{6,2},{1,5},{3,7},{5,1},{7,3},{8,12},{10,14},{12... | collective-permute-start | bytes 4718600 | tf_op jit(solution)/shard_map/ppermute | solution.py:1394
  142.6 13.7 %collective-permute-start.17 = (bf16[2,256,1536]{2,1,0:T(8,128)(2,1)}, bf16[2,256,1536]{2,1,0:T(8,128)(2,1)S(1)}, u32[]{:S(2)}, u32[]{:S(2)}) collective-permute-start(bf16[2,256,1536]{2,1,0:T(8,128)(2,1)} %collective-permute-done.12.refs_1_.refs_4_), channel_id=1, source_target_pairs={{0,1},{1,0},{2,3},{3,2},{4,5},{5,4},{6,7},{7,6},{8,9},{9,8},{10,11... | collective-permute-start | bytes 4718600 | tf_op jit(solution)/shard_map/ppermute | solution.py:1386
  142.6 13.7 %collective-permute-start.18 = (bf16[2,256,1536]{2,1,0:T(8,128)(2,1)}, bf16[2,256,1536]{2,1,0:T(8,128)(2,1)S(1)}, u32[]{:S(2)}, u32[]{:S(2)}) collective-permute-start(bf16[2,256,1536]{2,1,0:T(8,128)(2,1)} %collective-permute-done.13.refs_2_.refs_5_), channel_id=1, source_target_pairs={{0,1},{1,0},{2,3},{3,2},{4,5},{5,4},{6,7},{7,6},{8,9},{9,8},{10,11... | collective-permute-start | bytes 4718600 | tf_op jit(solution)/shard_map/ppermute | solution.py:1386
  145.2 11.1 %collective-permute-start.15 = (bf16[128,1536]{1,0:T(8,128)(2,1)S(1)}, bf16[128,1536]{1,0:T(8,128)(2,1)S(1)}, u32[]{:S(2)}, u32[]{:S(2)}) collective-permute-start(bf16[128,1536]{1,0:T(8,128)(2,1)S(1)} %slice_bitcast_fusion.5), channel_id=1, source_target_pairs={{0,2},{2,0},{4,6},{6,4},{1,3},{3,1},{5,7},{7,5},{8,10},{10,8},{12,... | collective-permute-start | bytes 1179656 | tf_op jit(solution)/shard_map/ppermute | solution.py:1390
  158.3 23.3 %collective-permute-start.21 = (bf16[128,1536]{1,0:T(8,128)(2,1)S(1)}, bf16[128,1536]{1,0:T(8,128)(2,1)S(1)}, u32[]{:S(2)}, u32[]{:S(2)}) collective-permute-start(bf16[128,1536]{1,0:T(8,128)(2,1)S(1)} %slice_bitcast_fusion.3), channel_id=1, source_target_pairs={{0,2},{2,0},{4,6},{6,4},{1,3},{3,1},{5,7},{7,5},{8,10},{10,8},{12,... | collective-permute-start | bytes 1179656 | tf_op jit(solution)/shard_map/ppermute | solution.py:1390
  161.0 20.6 %collective-permute-start.22 = (bf16[128,1536]{1,0:T(8,128)(2,1)S(1)}, bf16[128,1536]{1,0:T(8,128)(2,1)S(1)}, u32[]{:S(2)}, u32[]{:S(2)}) collective-permute-start(bf16[128,1536]{1,0:T(8,128)(2,1)S(1)} %slice_bitcast_fusion.2), channel_id=1, source_target_pairs={{0,4},{2,6},{4,0},{6,2},{1,5},{3,7},{5,1},{7,3},{8,12},{10,14},{12... | collective-permute-start | bytes 1179656 | tf_op jit(solution)/shard_map/ppermute | solution.py:1394
  184.0 19.0 %collective-permute-start.25 = (bf16[4,2,256,768]{3,2,1,0:T(8,128)(2,1)}, bf16[4,2,256,768]{3,2,1,0:T(8,128)(2,1)S(1)}, u32[]{:S(2)}, u32[]{:S(2)}) collective-permute-start(bf16[4,2,256,768]{3,2,1,0:T(8,128)(2,1)} %get-tuple-element.201), channel_id=1, source_target_pairs={{0,1},{1,0},{2,3},{3,2},{4,5},{5,4},{6,7},{7,6},{8,9},{9,8},{10,11... | collective-permute-start | bytes 9437192 | tf_op jit(solution)/shard_map/ppermute | solution.py:1386
  206.8 46.0 %collective-permute-start.29 = (bf16[4,2,256,768]{3,2,1,0:T(8,128)(2,1)}, bf16[4,2,256,768]{3,2,1,0:T(8,128)(2,1)}, u32[]{:S(2)}, u32[]{:S(2)}) collective-permute-start(bf16[4,2,256,768]{3,2,1,0:T(8,128)(2,1)} %get-tuple-element.209), channel_id=1, source_target_pairs={{0,1},{1,0},{2,3},{3,2},{4,5},{5,4},{6,7},{7,6},{8,9},{9,8},{10,11... | collective-permute-start | bytes 9437192 | tf_op jit(solution)/shard_map/ppermute | solution.py:1386
  215.6 41.5 %all-to-all-start.1 = ((bf16[4,2,256,768]{3,2,1,0:T(8,128)(2,1)}), bf16[4,2,256,768]{3,2,1,0:T(8,128)(2,1)S(1)}, u32[]{:S(2)}, u32[]{:S(2)}) async-start(bf16[4,2,256,768]{3,2,1,0:T(8,128)(2,1)} %add_convert_fusion.3), calls=%async_computation.1 | async-start | bytes 6291456 | tf_op jit(solution)/shard_map/all_to_all | solution.py:1398
  219.3 87.9 %reduce-scatter.3.cloned.1.call-start = ((), (), s32[]{:S(2)}) async-start(), calls=%async_computation.11 | async-start | bytes 2949120 | tf_op jit(solution)/shard_map/reduce_scatter | solution.py:1519
  257.1 48.5 %all-to-all-start.2 = ((bf16[4,2,256,768]{3,2,1,0:T(8,128)(2,1)}), bf16[4,2,256,768]{3,2,1,0:T(8,128)(2,1)}, u32[]{:S(2)}, u32[]{:S(2)}) async-start(bf16[4,2,256,768]{3,2,1,0:T(8,128)(2,1)} %add_convert_fusion.2), calls=%async_computation.2 | async-start | bytes 6291456 | tf_op jit(solution)/shard_map/all_to_all | solution.py:1398
  319.4 49.1 %all-to-all-start.3 = ((bf16[4,2,304,768]{3,2,1,0:T(8,128)(2,1)}), bf16[4,2,304,768]{3,2,1,0:T(8,128)(2,1)}, u32[]{:S(2)}, u32[]{:S(2)}) async-start(bf16[4,2,304,768]{3,2,1,0:T(8,128)(2,1)} %add_convert_fusion), calls=%async_computation.4 | async-start | bytes 7471104 | tf_op jit(solution)/shard_map/all_to_all | solution.py:1398
  324.2 91.1 %reduce-scatter.5.cloned.1.call-start = ((), (), s32[]{:S(2)}) async-start(), calls=%async_computation.12 | async-start | bytes 1536000 | tf_op jit(solution)/shard_map/reduce_scatter | solution.py:1519
  373.3 13.2 %all-to-all-start.4 = ((bf16[4,2,272,128]{3,2,1,0:T(8,128)(2,1)}), bf16[4,2,272,128]{3,2,1,0:T(8,128)(2,1)}, u32[]{:S(2)}, u32[]{:S(2)}) async-start(bf16[4,2,272,128]{3,2,1,0:T(8,128)(2,1)} %add_convert_fusion.4), calls=%async_computation.5 | async-start | bytes 1114112 | tf_op jit(solution)/shard_map/all_to_all | solution.py:1398
  386.6 39.9 %all-to-all-start.5 = ((bf16[4,2,256,768]{3,2,1,0:T(8,128)(2,1)}), bf16[4,2,256,768]{3,2,1,0:T(8,128)(2,1)S(1)}, u32[]{:S(2)}, u32[]{:S(2)}) async-start(bf16[4,2,256,768]{3,2,1,0:T(8,128)(2,1)} %add_convert_fusion.1), calls=%async_computation.6 | async-start | bytes 6291456 | tf_op jit(solution)/shard_map/all_to_all | solution.py:1398
  407.9 13.5 %collective-permute-start.36 = (f32[80,128]{1,0:T(8,128)S(1)}, f32[80,128]{1,0:T(8,128)S(1)}, u32[]{:S(2)}, u32[]{:S(2)}) collective-permute-start(f32[80,128]{1,0:T(8,128)S(1)} %pad_bitcast_fusion), channel_id=1, source_target_pairs={{0,1},{1,0},{2,3},{3,2},{4,5},{5,4},{6,7},{7,6},{8,9},{9,8},{10,11... | collective-permute-start | bytes 122888 | tf_op jit(solution)/shard_map/ppermute | solution.py:1386
  408.0 26.5 %collective-permute-start.37 = (bf16[2,2,256,128]{3,2,1,0:T(8,128)(2,1)}, bf16[2,2,256,128]{3,2,1,0:T(8,128)(2,1)}, u32[]{:S(2)}, u32[]{:S(2)}) collective-permute-start(bf16[2,2,256,128]{3,2,1,0:T(8,128)(2,1)} %get-tuple-element.270), channel_id=1, source_target_pairs={{0,1},{1,0},{2,3},{3,2},{4,5},{5,4},{6,7},{7,6},{8,9},{9,8},{10,11... | collective-permute-start | bytes 786440 | tf_op jit(solution)/shard_map/ppermute | solution.py:1386
  426.5 17.8 %all-to-all-start.6 = ((bf16[4,96,1296]{2,1,0:T(8,128)(2,1)}), bf16[4,96,1296]{2,1,0:T(8,128)(2,1)}, u32[]{:S(2)}, u32[]{:S(2)}) async-start(bf16[4,96,1296]{2,1,0:T(8,128)(2,1)} %bitcast.120), calls=%async_computation.8 | async-start | bytes 2162688 | tf_op jit(solution)/shard_map/all_to_all | solution.py:1398
  (84 other events, 552.8 us)
Sparse Core Ops, SparseCore 0:
  17.0 52.8 all-gather.4
  72.1 29.2 all-gather.8
  104.2 32.2 all-gather.6
  257.3 49.8 reduce-scatter.2
  373.5 30.5 reduce-scatter.4

commit v5 on v4

--- a/solution.py
+++ b/solution.py
@@ -656,11 +656,11 @@
 def piece_copies(refs, m, slot, held, sems):
     half = SPAN // 2
     for q in range(2):
-        own, by_x, by_y, far_a, far_b = refs[5 * q : 5 * (q + 1)]
+        pieces = refs[5 * q : 5 * (q + 1)]
+        own, by_x, by_y, far_a, far_b = pieces if m is None else [ref.at[m] for ref in pieces]
         if slot < 3:
             at = pl.ds(q * SPAN, SPAN)
             source = (own, by_x, by_y)[slot]
-            source = source if m is None else source.at[m]
             yield pltpu.make_async_copy(source, held.at[slot, at], sems.at[slot, q, 0])
         else:
             for part, source in enumerate((far_a, far_b)):
@@ -676,15 +676,12 @@
                 copy.start()
 
 
-def slot_rows(refs, m, held, sems):
-    start_pieces(refs, m, held, sems)
+def wait_slot(refs, m, held, sems, first_step):
     for slot in range(BLOCKS):
-        @pl.when(pl.program_id(0) == slot)
+        @pl.when(pl.program_id(0) == first_step + slot)
         def _():
             for copy in piece_copies(refs, m, slot, held, sems):
                 copy.wait()
-
-    return held[pl.program_id(0)]
 
 
 def block_rows(refs, place_ref, held, sems):
@@ -711,33 +708,66 @@
     return pl.ds(own, half), pl.ds(other, half)
 
 
-def gate_kernel(m, place_ref, own_ref, other_ref, *refs):
-    cots = refs[:10]
-    (y_ref, w_gate_ref, w_out_ref, chan_ref, gate_ref, d_gated_ref, mine_ref, theirs_ref,
-     stat_ref, held, sems) = refs[10:]
-    gate = dot_nn(both_tokens(own_ref, other_ref), w_gate_ref[...])
-    d_gated = dot_nn(slot_rows(cots, m, held, sems), w_out_ref[...])
-    guns = []
-    for q in range(2):
-        at = slice(q * SPAN, (q + 1) * SPAN)
-        gate_q = gate[at]
-        gate_ref[q, 0] = gate_q
-        d_gated_ref[q, 0] = d_gated[at]
-        gated_in = y_ref[q, 0] * (gate_q * sigmoid(gate_q))
-        weighted = gated_in * chan_ref[0:1]
-        guns.append(weighted.astype(BF))
-        square = jnp.sum(gated_in * gated_in, axis=1, keepdims=True)
-        cross = jnp.sum(d_gated[at] * weighted, axis=1, keepdims=True)
-        lanes = lax.broadcasted_iota(jnp.int32, (SPAN, 128), 1)
-        table = jnp.where(lanes == 0, square, jnp.where(lanes == 1, cross, 0.0))
-        stat_ref[q, 0] = table.T[0:2]
-    gun = jnp.concatenate(guns, axis=0)
-    own, other = core_rows(place_ref)
-    mine = dot_nt(gun, w_out_ref[own]).astype(BF)
-    theirs = dot_nt(gun, w_out_ref[other]).astype(BF)
-    for q in range(2):
-        mine_ref[0, q] = mine[q * SPAN : (q + 1) * SPAN]
-        theirs_ref[0, 1 - q] = theirs[q * SPAN : (q + 1) * SPAN]
+def stat_rows(row, column):
+    lanes = lax.broadcasted_iota(jnp.int32, (SPAN, 128), 1)
+    return jnp.where(lanes == row, column, 0.0).T[0:2]
+
+
+def gate_kernel(place_ref, *refs):
+    tokens, y_refs, (w_gate_ref, w_out_ref, chan_ref) = (refs[0:2], refs[2:4]), refs[4:6], refs[6:9]
+    gate_refs, gun_refs, mine_refs, theirs_refs, stat_refs = [
+        refs[at : at + 2] for at in range(9, 19, 2)
+    ]
+    step = pl.program_id(0)
+
+    def one_block(m):
+        gate = dot_nn(both_tokens(*tokens[m]), w_gate_ref[...])
+        guns = []
+        for q in range(2):
+            gate_q = gate[q * SPAN : (q + 1) * SPAN]
+            gate_refs[m][q, 0] = gate_q
+            gated_in = y_refs[m][q, 0] * (gate_q * sigmoid(gate_q))
+            gun = (gated_in * chan_ref[0:1]).astype(BF)
+            gun_refs[m][q, 0] = gun
+            guns.append(gun)
+            square = jnp.sum(gated_in * gated_in, axis=1, keepdims=True)
+            stat_refs[m][q, 0] = stat_rows(0, square)
+        gun = jnp.concatenate(guns, axis=0)
+        own, other = core_rows(place_ref)
+        mine = dot_nt(gun, w_out_ref[own]).astype(BF)
+        theirs = dot_nt(gun, w_out_ref[other]).astype(BF)
+        for q in range(2):
+            mine_refs[m][0, q] = mine[q * SPAN : (q + 1) * SPAN]
+            theirs_refs[m][0, 1 - q] = theirs[q * SPAN : (q + 1) * SPAN]
+
+    for m in range(2):
+        @pl.when((step >= m * BLOCKS) & (step < (m + 1) * BLOCKS))
+        def _():
+            one_block(m)
+
+
+def cross_kernel(place_ref, *refs):
+    cots, refs = (refs[0:10], refs[0:10]), refs[10:]
+    gun_refs, w_out_ref, d_gated_refs, stat_refs = refs[0:2], refs[2], refs[3:5], refs[5:7]
+    held_0, sems_0, held_1, sems_1 = refs[7:]
+    step = pl.program_id(0)
+    start_pieces(cots[0], 0, held_0, sems_0)
+    start_pieces(cots[1], 1, held_1, sems_1)
+
+    def one_block(m, held):
+        d_gated = dot_nn(held[step - m * BLOCKS], w_out_ref[...])
+        for q in range(2):
+            d_gated_q = d_gated[q * SPAN : (q + 1) * SPAN]
+            d_gated_refs[m][q, 0] = d_gated_q
+            cross = d_gated_q * gun_refs[m][q, 0].astype(F32)
+            stat_refs[m][q, 0] = stat_rows(1, jnp.sum(cross, axis=1, keepdims=True))
+
+    for m, held, sems in ((0, held_0, sems_0), (1, held_1, sems_1)):
+        wait_slot(cots[m], m, held, sems, m * BLOCKS)
+
+        @pl.when((step >= m * BLOCKS) & (step < (m + 1) * BLOCKS))
+        def _():
+            one_block(m, held)
 
 
 def start_sums(total, seed_ref):
@@ -754,47 +784,60 @@
             out_ref[z] = total[:, z * rows_of : (z + 1) * rows_of].astype(BF)
 
 
-def gate_back_first(*refs):
-    gate_back_step(0, refs, None, *refs[18:])
-
-
-def gate_back_last(*refs):
-    dy_ref, d_gate_ref, g_gain_ref, parts_ref, held, sems, total = refs[19:]
-    gate_back_step(1, refs, refs[18], dy_ref, d_gate_ref, g_gain_ref, total, held, sems)
-    finish_sums(total, parts_ref)
-
-
-def gate_back_step(m, refs, seed_ref, dy_ref, d_gate_ref, g_gain_ref, g_ref, held, sems):
-    own_ref, other_ref = refs[1:3]
-    cots = refs[3:13]
-    y_ref, gate_ref, d_gated_ref, stat_ref, chan_ref = refs[13:18]
-    start_sums(g_ref, seed_ref)
-    start_sums(g_gain_ref, None)
-    cot = slot_rows(cots, m, held, sems)
-    gateds = []
-    d_gates = []
-    for q in range(2):
-        stat = to_columns(stat_ref[q, 0])
-        scale = lax.rsqrt(stat[:, 0:1] * (1.0 / INNER) + EPS)
-        pull = stat[:, 1:2] * (1.0 / INNER) * scale * scale * scale
-        gate = gate_ref[q, 0]
-        y = y_ref[q, 0]
-        d_gated = d_gated_ref[q, 0]
-        sigma = sigmoid(gate)
-        gate_act = gate * sigma
-        gated_in = y * gate_act
-        scaled_gain = chan_ref[0:1] * scale
-        d_in = d_gated * scaled_gain - gated_in * pull
-        dy_ref[q, 0] = (d_in * gate_act).astype(BF)
-        d_gate = (d_in * y * (sigma + gate_act * (1.0 - sigma))).astype(BF)
-        d_gate_ref[q, 0] = d_gate
-        d_gates.append(d_gate)
-        gateds.append((gated_in * scaled_gain).astype(BF))
-        g_gain_ref[0:1] += jnp.sum(d_gated * gated_in * scale, axis=0, keepdims=True)
-    gated = jnp.concatenate(gateds, axis=0)
-    d_gate = jnp.concatenate(d_gates, axis=0)
-    g_ref[:QUARTER] += dot_tn(gated, cot)
-    g_ref[QUARTER:] += dot_tn(d_gate, both_tokens(own_ref, other_ref))
+def gate_back_kernel(place_ref, *refs):
+    tokens, refs = (refs[0:2], refs[2:4]), refs[4:]
+    cots, refs = (refs[0:10], refs[0:10]), refs[10:]
+    y_refs, gate_refs, d_gated_refs, stat_refs = refs[0:2], refs[2:4], refs[4:6], refs[6:8]
+    chan_ref, dy_refs, d_gate_refs = refs[8], refs[9:11], refs[11:13]
+    g_gain_ref, parts_ref, held_0, sems_0, held_1, sems_1, total = refs[13:]
+    step = pl.program_id(0)
+
+    @pl.when(step == 0)
+    def _():
+        total[...] = jnp.zeros_like(total)
+        g_gain_ref[...] = jnp.zeros_like(g_gain_ref)
+
+    start_pieces(cots[0], 0, held_0, sems_0)
+    start_pieces(cots[1], 1, held_1, sems_1)
+
+    def one_block(m, held):
+        gateds = []
+        d_gates = []
+        for q in range(2):
+            stat = to_columns(stat_refs[m][q, 0])
+            scale = lax.rsqrt(stat[:, 0:1] * (1.0 / INNER) + EPS)
+            pull = stat[:, 1:2] * (1.0 / INNER) * scale * scale * scale
+            gate = gate_refs[m][q, 0]
+            y = y_refs[m][q, 0]
+            d_gated = d_gated_refs[m][q, 0]
+            sigma = sigmoid(gate)
+            gate_act = gate * sigma
+            gated_in = y * gate_act
+            scaled_gain = chan_ref[0:1] * scale
+            d_in = d_gated * scaled_gain - gated_in * pull
+            dy_refs[m][q, 0] = (d_in * gate_act).astype(BF)
+            d_gate = (d_in * y * (sigma + gate_act * (1.0 - sigma))).astype(BF)
+            d_gate_refs[m][q, 0] = d_gate
+            d_gates.append(d_gate)
+            gateds.append((gated_in * scaled_gain).astype(BF))
+            g_gain_ref[0:1] += jnp.sum(d_gated * gated_in * scale, axis=0, keepdims=True)
+        gated = jnp.concatenate(gateds, axis=0)
+        d_gate = jnp.concatenate(d_gates, axis=0)
+        total[:QUARTER] += dot_tn(gated, held[step - m * BLOCKS])
+        total[QUARTER:] += dot_tn(d_gate, both_tokens(*tokens[m]))
+
+    for m, held, sems in ((0, held_0, sems_0), (1, held_1, sems_1)):
+        wait_slot(cots[m], m, held, sems, m * BLOCKS)
+
+        @pl.when((step >= m * BLOCKS) & (step < (m + 1) * BLOCKS))
+        def _():
+            one_block(m, held)
+
+    @pl.when(step == 2 * BLOCKS - 1)
+    def _():
+        rows_of = parts_ref.shape[2]
+        for z in range(parts_ref.shape[0]):
+            parts_ref[z] = total[:, z * rows_of : (z + 1) * rows_of].astype(BF)
 
 
 def bwd_first(*refs):
@@ -1005,12 +1048,12 @@
     return [pl.BlockSpec((1, SPAN, D), lambda j, place: (order(j), 0, 0))] * 2
 
 
-def call_blocks(kernel, name, place, operands, in_specs, outs, scratch=()):
+def call_blocks(kernel, name, place, operands, in_specs, outs, scratch=(), steps=BLOCKS):
     return pl.pallas_call(
         kernel,
         grid_spec=pltpu.PrefetchScalarGridSpec(
             num_scalar_prefetch=1,
-            grid=(BLOCKS,),
+            grid=(steps,),
             in_specs=in_specs,
             out_specs=[spec for spec, _ in outs],
             scratch_shapes=list(scratch),
@@ -1067,46 +1110,53 @@
     )
 
 
-def by_slot(spec):
-    def index(j, place):
-        return spec.index_map(j ^ place[1], place)
-
-    return pl.BlockSpec(spec.block_shape, index)
-
-
 def cot_specs():
     return [pl.BlockSpec(memory_space=pl.ANY)] * 10
 
 
-def by_slot_outs(outs):
-    return [(by_slot(spec), shape) for spec, shape in outs]
-
-
-def run_gate(m, place, tokens, cots, y, w_gate, w_out, chan):
-    half = D // 2
+def run_gate(place, tokens, y, w_gate, w_out, chan):
+    both = range(2)
+    wide = slot_spec(SPAN, QUARTER, upward)
+    lead, lead_shape = lead_out(SPAN, D // 2, upward)
+    rows = slot_spec(2, SPAN, upward)
+    kinds = (
+        (wide, out_shape(SPAN, QUARTER, F32)),
+        (wide, out_shape(SPAN, QUARTER, BF)),
+        (lead, lead_shape),
+        (lead, lead_shape),
+        (rows, out_shape(2, SPAN, F32)),
+    )
     return call_blocks(
-        functools.partial(gate_kernel, m),
+        gate_kernel,
         "gate_forward",
         place,
-        (*tokens, *cots, y, w_gate, w_out, chan),
+        (*tokens[0], *tokens[1], *y, w_gate, w_out, chan),
         [
-            *[by_slot(spec) for spec in token_specs(upward)],
-            *cot_specs(),
-            by_slot(slot_spec(SPAN, QUARTER, upward)),
+            *[in_half(spec, m) for m in both for spec in token_specs(upward)],
+            *[in_half(wide, m) for m in both],
             fixed_spec(D, QUARTER),
             fixed_spec(D, QUARTER),
             fixed_spec(8, QUARTER),
         ],
-        by_slot_outs(
-            [
-                slot_out(SPAN, QUARTER, F32, upward),
-                slot_out(SPAN, QUARTER, F32, upward),
-                lead_out(SPAN, half, upward),
-                lead_out(SPAN, half, upward),
-                slot_out(2, SPAN, F32, upward),
-            ]
-        ),
-        cot_scratch(),
+        [(in_half(spec, m), shape) for spec, shape in kinds for m in both],
+        steps=2 * BLOCKS,
+    )
+
+
+def run_cross(place, cots, gun, w_out):
+    both = range(2)
+    wide = slot_spec(SPAN, QUARTER, upward)
+    rows = slot_spec(2, SPAN, upward)
+    return call_blocks(
+        cross_kernel,
+        "cross_forward",
+        place,
+        (*cots, *gun, w_out),
+        [*cot_specs(), *[in_half(wide, m) for m in both], fixed_spec(D, QUARTER)],
+        [(in_half(wide, m), out_shape(SPAN, QUARTER, F32)) for m in both]
+        + [(in_half(rows, m), out_shape(2, SPAN, F32)) for m in both],
+        cot_scratch() + cot_scratch(),
+        steps=2 * BLOCKS,
     )
 
 
@@ -1119,25 +1169,36 @@
     return out, [pltpu.VMEM((rows, D), F32)]
 
 
-def run_gate_back(place, tokens, cots, y, gate, d_gated, stat, chan, seed, dp_count):
-    last = seed is not None
-    total, scratch = sums_out(2 * QUARTER, dp_count, last)
+def in_half(spec, m):
+    def index(j, place):
+        slot = jnp.minimum(j, BLOCKS - 1) if m == 0 else jnp.maximum(j - BLOCKS, 0)
+        return spec.index_map(slot ^ place[1], place)
+
+    return pl.BlockSpec(spec.block_shape, index)
+
+
+def run_gate_back(place, tokens, cots, y, gate, d_gated, stat, chan, dp_count):
+    (parts_spec, parts_shape), total = sums_out(2 * QUARTER, dp_count, True)
+    both = range(2)
+    wide = slot_spec(SPAN, QUARTER, upward)
+    outs = [
+        (in_half(wide, m), out_shape(SPAN, QUARTER, BF)) for _ in range(2) for m in both
+    ]
     return call_blocks(
-        gate_back_last if last else gate_back_first,
+        gate_back_kernel,
         "gate_backward",
         place,
-        (*tokens, *cots, y, gate, d_gated, stat, chan) + ((seed,) if last else ()),
+        (*tokens[0], *tokens[1], *cots, *y, *gate, *d_gated, *stat, chan),
         [
-            *[by_slot(spec) for spec in token_specs(upward)],
+            *[in_half(spec, m) for m in both for spec in token_specs(upward)],
             *cot_specs(),
-            *[by_slot(slot_spec(SPAN, QUARTER, upward))] * 3,
-            by_slot(slot_spec(2, SPAN, upward)),
+            *[in_half(wide, m) for _ in range(3) for m in both],
+            *[in_half(slot_spec(2, SPAN, upward), m) for m in both],
             fixed_spec(8, QUARTER),
-        ]
-        + ([fixed_spec(2 * QUARTER, D)] if last else []),
-        by_slot_outs([slot_out(SPAN, QUARTER, BF, upward), slot_out(SPAN, QUARTER, BF, upward)])
-        + [fixed_out(8, QUARTER), total],
-        cot_scratch() + scratch,
+        ],
+        outs + [fixed_out(8, QUARTER), (parts_spec, parts_shape)],
+        cot_scratch() + cot_scratch() + total,
+        steps=2 * BLOCKS,
     )
 
 
@@ -1468,8 +1529,8 @@
     )
     inputs, first_block = after((inputs, first_block))
     w_first = all_rows(first_block)
-    w_gate = all_rows(quarter(inproj[0], 1, QUARTER))
-    w_out = all_rows(quarter(outproj, 0, QUARTER).T)
+    gate_block = quarter(inproj[0], 1, QUARTER)
+    out_block = quarter(outproj, 0, QUARTER).T
 
     def whole_rows(array):
         mine = lax.dynamic_index_in_dim(array, core, 1, keepdims=False)
@@ -1524,14 +1585,6 @@
     def forward(m, place, tokens):
         return run_fwd(place, tokens, w_first, segs[m], taps, head, chan)
 
-    def gate_forward(m, place):
-        return run_gate(m, place, normed[m], cots[m], kept[m][3], w_gate, w_out, chan)
-
-    def gate_backward(m, place, gate, d_gated, sums, seed):
-        return run_gate_back(
-            place, normed[m], cots[m], kept[m][3], gate, d_gated, sums, chan, seed, dp_count
-        )
-
     def backward(m, place, dy, d_gate, seed):
         return run_bwd(
             place, normed[m], kept[m], dy, d_gate, segs[m], taps, head, chan,
@@ -1564,9 +1617,17 @@
 
     stepproj_own = lax.dynamic_slice_in_dim(stepproj.T, chip * shard, shard, 1)
     outproj_own = lax.dynamic_slice_in_dim(outproj, chip * shard, shard, 1).T
-    near_0, own_swapped, cot_own, segs, taps, head, chan, stepproj_own, outproj_own = after(
-        (near_0, own_swapped, cot_own, segs, taps, head, chan, stepproj_own, outproj_own)
-    )
+    (
+        near_0, own_swapped, cot_own, segs, taps, head, chan, stepproj_own, outproj_own, place,
+        gate_block, out_block,
+    ) = after(
+        (
+            near_0, own_swapped, cot_own, segs, taps, head, chan, stepproj_own, outproj_own, place,
+            gate_block, out_block,
+        )
+    )
+    w_gate = all_rows(gate_block)
+    w_out = all_rows(out_block)
     far = over_x(near_0[2][:half]), over_y(near_0[1][half:])
     near_swapped = [swap_cores(piece) for piece in near_0[1:]]
     far, near_swapped, second_copies = after((far, near_swapped, second_copies))
@@ -1586,34 +1647,29 @@
     kept.append(forward(1, place, normed[1]))
 
     by_x, by_y, w_out, place = after((by_x, by_y, w_out, place), kept[1][1])
-    def far_pieces(m, by_x, by_y):
-        return over_x(by_y[m, :half]), over_y(by_x[m, half:])
-
-    def cot_pieces(far):
-        return (cot_own, by_x, by_y, *far, *near_other, *[swap_cores(piece) for piece in far])
-
-    far_0 = far_pieces(0, by_x, by_y)
+    far = over_x(by_y[:, :half]), over_y(by_x[:, half:])
     near_other = (cot_other, swap_cores(by_x), swap_cores(by_y))
-    far_0, near_other, far_from, place = after((far_0, near_other, (by_x, by_y), place))
-    cots = [cot_pieces(far_0)]
-    far_1 = far_pieces(1, *far_from)
-    gate_0, d_gated_0, mine_0, theirs_0, stat_0 = gate_forward(0, place)
-    place, theirs_0, far_1 = after((place, theirs_0, far_1), stat_0)
-    cots.append(cot_pieces(far_1))
-    branch_0 = core_sums(mine_0, after(theirs_0, cots[1][8:]))
-    gate_1, d_gated_1, mine_1, theirs_1, stat_1 = gate_forward(1, place)
-
-    stats = jnp.stack([stat_0, after(stat_1, branch_0)])
+    gate_0, gate_1, gun_0, gun_1, mine_0, mine_1, theirs_0, theirs_1, stat_0, stat_1 = run_gate(
+        place, normed, (kept[0][3], kept[1][3]), w_gate, w_out, chan
+    )
+    far, near_other, place = after((far, near_other, place), stat_0)
+    far_other = [swap_cores(piece) for piece in far]
+    far_other, place, theirs_0, theirs_1 = after((far_other, place, theirs_0, theirs_1))
+    cots = (cot_own, by_x, by_y, *far, *near_other, *far_other)
+    d_gated_0, d_gated_1, cross_0, cross_1 = run_cross(place, cots, (gun_0, gun_1), w_out)
+    branch_0 = core_sums(mine_0, theirs_0)
+
+    stats = jnp.stack([stat_0 + cross_0, stat_1 + cross_1])
+    stats = after(stats, branch_0)
     stats = stats + swap_cores(stats)[:, ::-1]
     theirs_1 = after(theirs_1, stats)
     sums_0, sums_1 = sum_seq(stats)
     branch_0 = after(branch_0, sums_0)
     layer_0 = exchange(branch_0)
-    dy_0, d_gate_0, g_gain_0, g_mid_0 = gate_backward(0, place, gate_0, d_gated_0, sums_0, None)
     branch_1 = core_sums(mine_1, theirs_1)
-    place = after(place, dy_0)
-    dy_1, d_gate_1, g_gain_1, mid_parts = gate_backward(
-        1, place, gate_1, d_gated_1, sums_1, g_mid_0
+    dy_0, dy_1, d_gate_0, d_gate_1, g_gain, mid_parts = run_gate_back(
+        place, normed, cots, (kept[0][3], kept[1][3]), (gate_0, gate_1), (d_gated_0, d_gated_1),
+        (sums_0, sums_1), chan, dp_count,
     )
 
     layer_0, branch_1, place, mid_parts = after((layer_0, branch_1, place, mid_parts), dy_1)
@@ -1670,7 +1726,7 @@
     )
     small_parts = [
         put(g_taps[: CONV + 1], QUARTER, inner_local),
-        put(g_gain_0[0] + g_gain_1[0], QUARTER, inner_local),
+        put(g_gain[0], QUARTER, inner_local),
         put(g_heads, QHEADS, heads_local),
         g_state_taps[: CONV + 1],
     ]
@@ -1682,6 +1738,7 @@
     shares = jnp.concatenate(
         [mid_rows, late_rows[:QUARTER], state_rows, late_rows[QUARTER:]], axis=0
     )
+    vector = sum_dp(after(vector, state_rows))
     other_vector = swap_cores(vector)
     token_1, shares, vector, other_vector = after(
         (token_1, by_place(shares), vector, other_vector)
@@ -1747,7 +1804,7 @@
     square = owner_sums[0, shard] + jnp.sum(g_prenorm * g_prenorm)
     line = jnp.where(lanes == shard, square, g_prenorm)
     table = jnp.where(jnp.arange(owners)[:, None] == owner, line[None], 0.0)
-    table = sum_seq(sum_dp(jnp.concatenate([table, vector, other_vector], axis=0)))
+    table = sum_seq(jnp.concatenate([sum_dp(table), vector, other_vector], axis=0))
     small_sums = []
     start = 0
     both_vectors = table[owners:].reshape(2, -1)

time: 501 us -> 489 us (0.976)
  waiting for transfers between devices: 87.3 us -> 69.2 us
  other arithmetic: 52.7 us -> 57.8 us
    ppermute x7 -> x6, waiting for transfers between devices: 40 us -> 21.6 us  [over_x(): return lax.ppermute(block, 'seq', ROUTE_X)]
    ppermute x7 -> x6, starting transfers between devices: 10.1 us -> 8.26 us  [over_y(): return lax.ppermute(block, 'seq', ROUTE_Y)]
    ppermute x25 -> x23, waiting for transfers between devices: 9.06 us -> 10.3 us  [swap_cores(): return lax.ppermute(block, 'tensor', SWAP)]
    ppermute x2 -> x4, waiting for transfers between devices: 9.26 us -> 10.1 us  [sum_dp(): lax.ppermute(value, 'dp', [(i, i ^ hop) for i in range(dp_count)])]
    pallas_call x8 -> x7, Pallas kernels: 212 us -> 211 us  [call_blocks(): pl.pallas_call(kernel, grid_spec=pltpu.PrefetchScalarGridSpec(num_scalar_...]
  transfers between devices with their start and end apart: 56 -> 54, of which waited for: 30 -> 29; matrix products, arithmetic and copies ran while one was open for 14% -> 16% of each run, Pallas kernels for 44% -> 45%
where the time goes in v5:
time: 489 us; the launch traced here: 483 us
  Pallas kernels  225 us (46%)
  waiting for transfers between devices  69.2 us (14%)
  starting transfers between devices  61.8 us (13%)
  other arithmetic  57.8 us (12%)
  local copies, waits for them, and re-layouts  46.6 us (10%)
  between operations  19.3 us (4%)
    pallas_call x7, Pallas kernels, call_blocks(): pl.pallas_call(kernel, grid_spec=pltpu.PrefetchScalarGridSpec(num_scalar_...  211 us
    all_to_all x7, starting transfers between devices, exchange(): return lax.all_to_all(blocks, 'seq', 0, 0, tiled=True)  29.6 us
    ppermute x6, waiting for transfers between devices, over_x(): return lax.ppermute(block, 'seq', ROUTE_X)  21.6 us
    convert_element_type x5, other arithmetic, add_low(): return (a.astype(F32) + b.astype(F32)).astype(BF)  20.8 us
    ppermute x23, waiting for transfers between devices, swap_cores(): return lax.ppermute(block, 'tensor', SWAP)  10.3 us
    ppermute x4, waiting for transfers between devices, sum_dp(): lax.ppermute(value, 'dp', [(i, i ^ hop) for i in range(dp_count)])  10.1 us
  transfers between devices with their start and end apart: 54, of which 29 were waited for; matrix products, arithmetic and copies ran while one was open for 16% of the time, Pallas kernels for 45%

profile of v5, /device:TPU:0, one launch (start us, length us, event | category | flops | bytes accessed | tf_op | source)
XLA Modules:
  0.0 483.1 jit_solution(8424247374336998461)
XLA Ops:
  8.3 3.3 fusion.48
  51.7 9.0 %collective-permute-done.6.refs_3_ = bf16[128,1536]{1,0:T(8,128)(2,1)S(1)} collective-permute-done((bf16[128,1536]{1,0:T(8,128)(2,1)S(1)}, bf16[128,1536]{1,0:T(8,128)(2,1)S(1)}, u32[]{:S(2)}, u32[]{:S(2)}) %collective-permute-start.6) | collective-permute-done | bytes 393248 | tf_op jit(solution)/shard_map/ppermute | solution.py:1451
  62.4 3.8 all-to-all-start
  73.1 29.1 %mix_forward.2 = (bf16[2,4,256,640]{3,2,1,0:T(8,128)(2,1)}, f32[2,4,256,128]{3,2,1,0:T(8,128)}, f32[2,4,256,640]{3,2,1,0:T(8,128)}, f32[2,4,256,384]{3,2,1,0:T(8...) custom-call(s32[2]{0:T(128)} %pad_add_fusion.place_ref.refs_0_, ...), custom_call_target="tpu_custom_call" | custom-call | flops 1024 | bytes 1024 | tf_op jit(solution)/shard_map/mix_forward/pallas_call | solution.py:1052
  108.1 25.6 %mix_forward.3 = (bf16[2,4,256,640]{3,2,1,0:T(8,128)(2,1)}, f32[2,4,256,128]{3,2,1,0:T(8,128)}, f32[2,4,256,640]{3,2,1,0:T(8,128)}, f32[2,4,256,384]{3,2,1,0:T(8,128)}, bf16[2,4,768,128]{3,2,1,0:T(8,128)(2,1)}) custom-call(s32[2]{0:T(128)} %pad_add_fusion.place_ref.refs_0_, bf16[4,256,1536]{2,1,0:T(8,128)(2,1)} %copy-done.2, ...), custom_call_target="tpu_custom_call" | custom-call | flops 1024 | bytes 1024 | tf_op jit(solution)/shard_map/mix_forward/pallas_call | solution.py:1052
  134.9 5.0 %collective-permute-done.12.refs_1_.refs_5_ = bf16[2,256,1536]{2,1,0:T(8,128)(2,1)} collective-permute-done((bf16[2,256,1536]{2,1,0:T(8,128)(2,1)}, bf16[2,256,1536]{2,1,0:T(8,128)(2,1)}, u32[]{:S(2)}, u32[]{:S(2)}) %collective-permute-start.12) | collective-permute-done | bytes 1572896 | tf_op jit(solution)/shard_map/ppermute | solution.py:1451
  146.3 24.4 %gate_forward.1 = (f32[2,4,256,384]{3,2,1,0:T(8,128)}, f32[2,4,256,384]{3,2,1,0:T(8,128)}, bf16[2,4,256,384]{3,2,1,0:T(8,128)(2,1)}, bf16[2,4,256,384]{3,2,1,0:T...) custom-call(s32[2]{0:T(128)} %pad_add_fusion.place_ref.refs_0_, ...), custom_call_target="tpu_custom_call" | custom-call | flops 1024 | bytes 1024 | tf_op jit(solution)/shard_map/gate_forward/pallas_call | solution.py:1052
  175.1 16.5 %cross_forward.1 = (f32[2,4,256,384]{3,2,1,0:T(8,128)}, f32[2,4,256,384]{3,2,1,0:T(8,128)}, f32[2,4,2,256]{3,2,1,0:T(2,128)}, f32[2,4,2,256]{3,2,1,0:T(2,128)}) custom-call(s32[2]{0:T(128)} %pad_add_fusion.place_ref.refs_0_, bf16[2,256,1536]{2,1,0:T(8,128)(2,1)} %maximum_select_fusion.1.refs_0_.refs_4_, ...), custom_call_target="tpu_custom_call" | custom-call | flops 1024 | bytes 1024 | tf_op jit(solution)/shard_map/cross_forward/pallas_call | solution.py:1052
  192.4 5.3 %add_convert_fusion.3 = bf16[4,2,256,768]{3,2,1,0:T(8,128)(2,1)} fusion(bf16[4,2,256,768]{3,2,1,0:T(8,128)(2,1)} %collective-permute-done.21, bf16[4,2,256,768]{3,2,1,0:T(8,128)(2,1)} %get-tuple-element.191), kind=kLoop, calls=%fused_computation.7 | loop fusion | flops 6291456 | bytes 9437184 | tf_op jit(solution)/shard_map/convert_element_type | solution.py:1467
  203.5 3.6 collective-permute-done.24
  207.7 3.7 all-to-all-start.1
  211.5 28.2 %gate_backward.1 = (bf16[2,4,256,384]{3,2,1,0:T(8,128)(2,1)}, bf16[2,4,256,384]{3,2,1,0:T(8,128)(2,1)}, bf16[2,4,256,384]{3,2,1,0:T(8,128)(2,1)}, bf16[2,4,256,3...) custom-call(s32[2]{0:T(128)} %pad_add_fusion.place_ref.refs_0_, ...), custom_call_target="tpu_custom_call" | custom-call | flops 1024 | bytes 1024 | tf_op jit(solution)/shard_map/gate_backward/pallas_call | solution.py:1052
  239.7 4.3 add_convert_fusion.2
  246.0 4.9 %all-to-all-start.2 = ((bf16[4,2,256,768]{3,2,1,0:T(8,128)(2,1)}), bf16[4,2,256,768]{3,2,1,0:T(8,128)(2,1)}, u32[]{:S(2)}, u32[]{:S(2)}) async-start(bf16[4,2,256,768]{3,2,1,0:T(8,128)(2,1)} %add_convert_fusion.2), calls=%async_computation.2 | async-start | bytes 6291456 | tf_op jit(solution)/shard_map/all_to_all | solution.py:1459
  250.9 43.5 %mix_backward.2 = (f32[400,1536]{1,0:T(8,128)}, f32[2,4,272,128]{3,2,1,0:T(8,128)}, f32[8,384]{1,0:T(8,128)}, f32[8,384]{1,0:T(8,128)}, bf16[4,2,304,768]{3,2,1,...) custom-call(s32[2]{0:T(128)} %pad_add_fusion.place_ref.refs_0_, ...), custom_call_target="tpu_custom_call" | custom-call | flops 1024 | bytes 1024 | tf_op jit(solution)/shard_map/mix_backward/pallas_call | solution.py:1052
  302.0 4.8 add_convert_fusion
  306.7 4.8 all-to-all-start.3
  311.6 44.2 %mix_backward.3 = (bf16[4,400,384]{2,1,0:T(8,128)(2,1)}, bf16[4,2,272,128]{3,2,1,0:T(8,128)(2,1)}, bf16[4,2,272,128]{3,2,1,0:T(8,128)(2,1)}, f32[2,4,272,128]{3,...) custom-call(s32[2]{0:T(128)} %pad_add_fusion.place_ref.refs_0_, ...), custom_call_target="tpu_custom_call" | custom-call | flops 1024 | bytes 1024 | tf_op jit(solution)/shard_map/mix_backward/pallas_call | solution.py:1052
  360.6 4.2 all-to-all-start.4
  366.2 4.4 add_convert_fusion.1
  370.6 3.4 all-to-all-done.4.maps_ref
  374.0 4.0 all-to-all-start.5
  382.1 6.1 %maps_backward.1 = (bf16[2,2,256,128]{3,2,1,0:T(8,128)(2,1)}, bf16[4,128,384]{2,1,0:T(8,128)(2,1)}, f32[8,128]{1,0:T(8,128)}) custom-call(s32[2]{0:T(128)} %pad_add_fusion.place_ref.refs_0_, bf16[4,2,48,768]{3,2,1,0:T(8,128)(2,1)} %slice.145.packed_ref, bf16[4,2,272,128]{3,2,1,0:T(8,128)(2,1)} %all-to-all-done.4.maps_ref, ...), custom_call_target="tpu_custom_call" | custom-call | flops 1024 | bytes 1024 | tf_op jit(solution)/shard_map/maps_backward/pallas_call | solution.py:1318
  389.9 3.5 collective-permute-start.31
  396.9 5.0 %collective-permute-done.30 = bf16[128,384]{1,0:T(8,128)(2,1)S(1)} collective-permute-done((bf16[128,384]{1,0:T(8,128)(2,1)}, bf16[128,384]{1,0:T(8,128)(2,1)S(1)}, u32[]{:S(2)}, u32[]{:S(2)}) %collective-permute-start.30) | collective-permute-done | bytes 98336 | tf_op jit(solution)/shard_map/ppermute | solution.py:1714
  403.5 3.5 collective-permute-done.32
  416.8 4.3 all-to-all-start.6
  421.1 3.6 convert_reduce_fusion.1
  428.4 3.4 maximum_add_fusion
  431.8 4.4 all-to-all-done.6.share_ref
  460.3 3.6 fusion.11
  470.9 4.4 owner_update.1
  (317 shorter events, 142.3 us)
Async XLA Ops:
  7.2 62.5 %all-gather.4.cloned.1.call-start = ((), (), s32[]{:S(2)}) async-start(), calls=%async_computation.9 | async-start | bytes 2949120 | tf_op jit(solution)/shard_map/all_gather | solution.py:1518
  16.2 25.6 %collective-permute-start.4 = (bf16[2,256,768]{2,1,0:T(8,128)(2,1)}, bf16[2,256,768]{2,1,0:T(8,128)(2,1)}, u32[]{:S(2)}, u32[]{:S(2)}) collective-permute-start(bf16[2,256,768]{2,1,0:T(8,128)(2,1)} %get-tuple-element.301), channel_id=1, source_target_pairs={{0,1},{1,0},{2,3},{3,2},{4,5},{5,4},{6,7},{7,6},{8,9},{9,8},{10,11... | collective-permute-start | bytes 2359304 | tf_op jit(solution)/shard_map/ppermute | solution.py:1447
  26.1 20.7 %collective-permute-start.1 = (bf16[256,1536]{1,0:T(8,128)(2,1)S(1)}, bf16[256,1536]{1,0:T(8,128)(2,1)S(1)}, u32[]{:S(2)}, u32[]{:S(2)}) collective-permute-start(bf16[256,1536]{1,0:T(8,128)(2,1)S(1)} %get-tuple-element.158.refs_0_), channel_id=1, source_target_pairs={{0,2},{2,0},{4,6},{6,4},{1,3},{3,1},{5,7},{7,5},{8,10},{10,8},{12,... | collective-permute-start | bytes 2359304 | tf_op jit(solution)/shard_map/ppermute | solution.py:1451
  28.6 19.7 %collective-permute-start.2 = (bf16[256,1536]{1,0:T(8,128)(2,1)S(1)}, bf16[256,1536]{1,0:T(8,128)(2,1)S(1)}, u32[]{:S(2)}, u32[]{:S(2)}) collective-permute-start(bf16[256,1536]{1,0:T(8,128)(2,1)S(1)} %get-tuple-element.158.refs_0_), channel_id=1, source_target_pairs={{0,4},{2,6},{4,0},{6,2},{1,5},{3,7},{5,1},{7,3},{8,12},{10,14},{12... | collective-permute-start | bytes 2359304 | tf_op jit(solution)/shard_map/ppermute | solution.py:1455
  30.1 18.2 %collective-permute-start.3 = (bf16[256,1536]{1,0:T(8,128)(2,1)S(1)}, bf16[256,1536]{1,0:T(8,128)(2,1)}, u32[]{:S(2)}, u32[]{:S(2)}) collective-permute-start(bf16[256,1536]{1,0:T(8,128)(2,1)S(1)} %get-tuple-element.158.refs_0_), channel_id=1, source_target_pairs={{0,1},{1,0},{2,3},{3,2},{4,5},{5,4},{6,7},{7,6},{8,9},{9,8},{10,11... | collective-permute-start | bytes 2359304 | tf_op jit(solution)/shard_map/ppermute | solution.py:1447
  49.0 11.7 %collective-permute-start.8 = (bf16[256,1536]{1,0:T(8,128)(2,1)S(1)}, bf16[256,1536]{1,0:T(8,128)(2,1)S(1)}, u32[]{:S(2)}, u32[]{:S(2)}) collective-permute-start(bf16[256,1536]{1,0:T(8,128)(2,1)S(1)} %collective-permute-done.1.refs_1_), channel_id=1, source_target_pairs={{0,1},{1,0},{2,3},{3,2},{4,5},{5,4},{6,7},{7,6},{8,9},{9,8},{10,11... | collective-permute-start | bytes 2359304 | tf_op jit(solution)/shard_map/ppermute | solution.py:1447
  49.0 12.6 %collective-permute-start.9 = (bf16[256,1536]{1,0:T(8,128)(2,1)S(1)}, bf16[256,1536]{1,0:T(8,128)(2,1)}, u32[]{:S(2)}, u32[]{:S(2)}) collective-permute-start(bf16[256,1536]{1,0:T(8,128)(2,1)S(1)} %collective-permute-done.2.refs_2_), channel_id=1, source_target_pairs={{0,1},{1,0},{2,3},{3,2},{4,5},{5,4},{6,7},{7,6},{8,9},{9,8},{10,11... | collective-permute-start | bytes 2359304 | tf_op jit(solution)/shard_map/ppermute | solution.py:1447
  49.6 11.1 %collective-permute-start.6 = (bf16[128,1536]{1,0:T(8,128)(2,1)S(1)}, bf16[128,1536]{1,0:T(8,128)(2,1)S(1)}, u32[]{:S(2)}, u32[]{:S(2)}) collective-permute-start(bf16[128,1536]{1,0:T(8,128)(2,1)S(1)} %slice.136), channel_id=1, source_target_pairs={{0,2},{2,0},{4,6},{6,4},{1,3},{3,1},{5,7},{7,5},{8,10},{10,8},{12,... | collective-permute-start | bytes 1179656 | tf_op jit(solution)/shard_map/ppermute | solution.py:1451
  50.0 10.8 %collective-permute-start.7 = (bf16[128,1536]{1,0:T(8,128)(2,1)S(1)}, bf16[128,1536]{1,0:T(8,128)(2,1)S(1)}, u32[]{:S(2)}, u32[]{:S(2)}) collective-permute-start(bf16[128,1536]{1,0:T(8,128)(2,1)S(1)} %slice.137), channel_id=1, source_target_pairs={{0,4},{2,6},{4,0},{6,2},{1,5},{3,7},{5,1},{7,3},{8,12},{10,14},{12... | collective-permute-start | bytes 1179656 | tf_op jit(solution)/shard_map/ppermute | solution.py:1455
  62.4 39.8 %all-to-all-start = ((bf16[4,256,1536]{2,1,0:T(8,128)(2,1)}), bf16[4,256,1536]{2,1,0:T(8,128)(2,1)S(1)}, u32[]{:S(2)}, u32[]{:S(2)}) async-start(bf16[4,256,1536]{2,1,0:T(8,128)(2,1)} %broadcast_in_dim.58), calls=%async_computation | async-start | bytes 6291456 | tf_op jit(solution)/shard_map/all_to_all | solution.py:1459
  66.2 36.0 %all-gather.8.cloned.1.call-start = ((), (), s32[]{:S(2)}) async-start(), calls=%async_computation.11 | async-start | bytes 1474560 | tf_op jit(solution)/shard_map/all_gather | solution.py:1518
  67.0 67.9 %all-gather.6.cloned.1.call-start = ((), (), s32[]{:S(2)}) async-start(), calls=%async_computation.10 | async-start | bytes 1474560 | tf_op jit(solution)/shard_map/all_gather | solution.py:1518
  67.5 34.6 %collective-permute-start.5 = (bf16[2,256,1536]{2,1,0:T(8,128)(2,1)}, bf16[2,256,1536]{2,1,0:T(8,128)(2,1)}, u32[]{:S(2)}, u32[]{:S(2)}) collective-permute-start(bf16[2,256,1536]{2,1,0:T(8,128)(2,1)} %maximum_select_fusion.1.refs_0_.refs_4_), channel_id=1, source_target_pairs={{0,1},{1,0},{2,3},{3,2},{4,5},{5,4},{6,7},{7,6},{8,9},{9,8},{10,11... | collective-permute-start | bytes 4718600 | tf_op jit(solution)/shard_map/ppermute | solution.py:1447
  102.4 37.4 %collective-permute-start.12 = (bf16[2,256,1536]{2,1,0:T(8,128)(2,1)}, bf16[2,256,1536]{2,1,0:T(8,128)(2,1)}, u32[]{:S(2)}, u32[]{:S(2)}) collective-permute-start(bf16[2,256,1536]{2,1,0:T(8,128)(2,1)} %maximum_select_fusion.1.refs_0_.refs_4_), channel_id=1, source_target_pairs={{0,2},{2,0},{4,6},{6,4},{1,3},{3,1},{5,7},{7,5},{8,10},{10,8},{12,... | collective-permute-start | bytes 4718600 | tf_op jit(solution)/shard_map/ppermute | solution.py:1451
  104.6 36.7 %collective-permute-start.13 = (bf16[2,256,1536]{2,1,0:T(8,128)(2,1)}, bf16[2,256,1536]{2,1,0:T(8,128)(2,1)}, u32[]{:S(2)}, u32[]{:S(2)}) collective-permute-start(bf16[2,256,1536]{2,1,0:T(8,128)(2,1)} %maximum_select_fusion.1.refs_0_.refs_4_), channel_id=1, source_target_pairs={{0,4},{2,6},{4,0},{6,2},{1,5},{3,7},{5,1},{7,3},{8,12},{10,14},{12... | collective-permute-start | bytes 4718600 | tf_op jit(solution)/shard_map/ppermute | solution.py:1455
  141.3 29.4 %collective-permute-start.17 = (bf16[2,256,1536]{2,1,0:T(8,128)(2,1)}, bf16[2,256,1536]{2,1,0:T(8,128)(2,1)S(1)}, u32[]{:S(2)}, u32[]{:S(2)}) collective-permute-start(bf16[2,256,1536]{2,1,0:T(8,128)(2,1)} %collective-permute-done.12.refs_1_.refs_5_), channel_id=1, source_target_pairs={{0,1},{1,0},{2,3},{3,2},{4,5},{5,4},{6,7},{7,6},{8,9},{9,8},{10,11... | collective-permute-start | bytes 4718600 | tf_op jit(solution)/shard_map/ppermute | solution.py:1447
  141.3 29.4 %collective-permute-start.18 = (bf16[2,256,1536]{2,1,0:T(8,128)(2,1)}, bf16[2,256,1536]{2,1,0:T(8,128)(2,1)S(1)}, u32[]{:S(2)}, u32[]{:S(2)}) collective-permute-start(bf16[2,256,1536]{2,1,0:T(8,128)(2,1)} %collective-permute-done.13.refs_2_.refs_6_), channel_id=1, source_target_pairs={{0,1},{1,0},{2,3},{3,2},{4,5},{5,4},{6,7},{7,6},{8,9},{9,8},{10,11... | collective-permute-start | bytes 4718600 | tf_op jit(solution)/shard_map/ppermute | solution.py:1447
  144.2 26.5 %collective-permute-start.15 = (bf16[2,128,1536]{2,1,0:T(8,128)(2,1)S(1)}, bf16[2,128,1536]{2,1,0:T(8,128)(2,1)S(1)}, u32[]{:S(2)}, u32[]{:S(2)}) collective-permute-start(bf16[2,128,1536]{2,1,0:T(8,128)(2,1)S(1)} %slice.140), channel_id=1, source_target_pairs={{0,2},{2,0},{4,6},{6,4},{1,3},{3,1},{5,7},{7,5},{8,10},{10,8},{12,... | collective-permute-start | bytes 2359304 | tf_op jit(solution)/shard_map/ppermute | solution.py:1451
  144.6 26.1 %collective-permute-start.16 = (bf16[2,128,1536]{2,1,0:T(8,128)(2,1)S(1)}, bf16[2,128,1536]{2,1,0:T(8,128)(2,1)S(1)}, u32[]{:S(2)}, u32[]{:S(2)}) collective-permute-start(bf16[2,128,1536]{2,1,0:T(8,128)(2,1)S(1)} %slice.141), channel_id=1, source_target_pairs={{0,4},{2,6},{4,0},{6,2},{1,5},{3,7},{5,1},{7,3},{8,12},{10,14},{12... | collective-permute-start | bytes 2359304 | tf_op jit(solution)/shard_map/ppermute | solution.py:1455
  174.2 18.2 %collective-permute-start.21 = (bf16[4,2,256,768]{3,2,1,0:T(8,128)(2,1)}, bf16[4,2,256,768]{3,2,1,0:T(8,128)(2,1)}, u32[]{:S(2)}, u32[]{:S(2)}) collective-permute-start(bf16[4,2,256,768]{3,2,1,0:T(8,128)(2,1)} %get-tuple-element.201), channel_id=1, source_target_pairs={{0,1},{1,0},{2,3},{3,2},{4,5},{5,4},{6,7},{7,6},{8,9},{9,8},{10,11... | collective-permute-start | bytes 9437192 | tf_op jit(solution)/shard_map/ppermute | solution.py:1447
  198.9 40.8 %collective-permute-start.25 = (bf16[4,2,256,768]{3,2,1,0:T(8,128)(2,1)}, bf16[4,2,256,768]{3,2,1,0:T(8,128)(2,1)}, u32[]{:S(2)}, u32[]{:S(2)}) collective-permute-start(bf16[4,2,256,768]{3,2,1,0:T(8,128)(2,1)} %get-tuple-element.217), channel_id=1, source_target_pairs={{0,1},{1,0},{2,3},{3,2},{4,5},{5,4},{6,7},{7,6},{8,9},{9,8},{10,11... | collective-permute-start | bytes 9437192 | tf_op jit(solution)/shard_map/ppermute | solution.py:1447
  207.7 38.3 %all-to-all-start.1 = ((bf16[4,2,256,768]{3,2,1,0:T(8,128)(2,1)}), bf16[4,2,256,768]{3,2,1,0:T(8,128)(2,1)S(1)}, u32[]{:S(2)}, u32[]{:S(2)}) async-start(bf16[4,2,256,768]{3,2,1,0:T(8,128)(2,1)} %add_convert_fusion.3), calls=%async_computation.1 | async-start | bytes 6291456 | tf_op jit(solution)/shard_map/all_to_all | solution.py:1459
  211.4 83.1 %reduce-scatter.3.cloned.1.call-start = ((), (), s32[]{:S(2)}) async-start(), calls=%async_computation.12 | async-start | bytes 2949120 | tf_op jit(solution)/shard_map/reduce_scatter | solution.py:1580
  246.0 48.4 %all-to-all-start.2 = ((bf16[4,2,256,768]{3,2,1,0:T(8,128)(2,1)}), bf16[4,2,256,768]{3,2,1,0:T(8,128)(2,1)}, u32[]{:S(2)}, u32[]{:S(2)}) async-start(bf16[4,2,256,768]{3,2,1,0:T(8,128)(2,1)} %add_convert_fusion.2), calls=%async_computation.2 | async-start | bytes 6291456 | tf_op jit(solution)/shard_map/all_to_all | solution.py:1459
  306.7 49.1 %all-to-all-start.3 = ((bf16[4,2,304,768]{3,2,1,0:T(8,128)(2,1)}), bf16[4,2,304,768]{3,2,1,0:T(8,128)(2,1)}, u32[]{:S(2)}, u32[]{:S(2)}) async-start(bf16[4,2,304,768]{3,2,1,0:T(8,128)(2,1)} %add_convert_fusion), calls=%async_computation.4 | async-start | bytes 7471104 | tf_op jit(solution)/shard_map/all_to_all | solution.py:1459
  311.5 91.5 %reduce-scatter.5.cloned.1.call-start = ((), (), s32[]{:S(2)}) async-start(), calls=%async_computation.13 | async-start | bytes 1536000 | tf_op jit(solution)/shard_map/reduce_scatter | solution.py:1580
  360.6 13.4 %all-to-all-start.4 = ((bf16[4,2,272,128]{3,2,1,0:T(8,128)(2,1)}), bf16[4,2,272,128]{3,2,1,0:T(8,128)(2,1)}, u32[]{:S(2)}, u32[]{:S(2)}) async-start(bf16[4,2,272,128]{3,2,1,0:T(8,128)(2,1)} %add_convert_fusion.4), calls=%async_computation.5 | async-start | bytes 1114112 | tf_op jit(solution)/shard_map/all_to_all | solution.py:1459
  374.0 42.9 %all-to-all-start.5 = ((bf16[4,2,256,768]{3,2,1,0:T(8,128)(2,1)}), bf16[4,2,256,768]{3,2,1,0:T(8,128)(2,1)S(1)}, u32[]{:S(2)}, u32[]{:S(2)}) async-start(bf16[4,2,256,768]{3,2,1,0:T(8,128)(2,1)} %add_convert_fusion.1), calls=%async_computation.6 | async-start | bytes 6291456 | tf_op jit(solution)/shard_map/all_to_all | solution.py:1459
  393.4 8.6 %collective-permute-start.30 = (bf16[128,384]{1,0:T(8,128)(2,1)}, bf16[128,384]{1,0:T(8,128)(2,1)S(1)}, u32[]{:S(2)}, u32[]{:S(2)}) collective-permute-start(bf16[128,384]{1,0:T(8,128)(2,1)} %get-tuple-element.308), channel_id=1, source_target_pairs={{0,16},{8,24},{16,0},{24,8},{1,17},{9,25},{17,1},{25,9},{2,18},{10... | collective-permute-start | bytes 294920 | tf_op jit(solution)/shard_map/ppermute | solution.py:1714
  393.4 8.6 %collective-permute-start.29 = (bf16[128,384]{1,0:T(8,128)(2,1)}, bf16[128,384]{1,0:T(8,128)(2,1)}, u32[]{:S(2)}, u32[]{:S(2)}) collective-permute-start(bf16[128,384]{1,0:T(8,128)(2,1)} %get-tuple-element.306), channel_id=1, source_target_pairs={{0,8},{8,16},{16,24},{24,0},{1,9},{9,17},{17,25},{25,1},{2,10},{10... | collective-permute-start | bytes 294920 | tf_op jit(solution)/shard_map/ppermute | solution.py:1714
  409.6 15.1 %collective-permute-start.35 = (bf16[2,2,256,128]{3,2,1,0:T(8,128)(2,1)}, bf16[2,2,256,128]{3,2,1,0:T(8,128)(2,1)}, u32[]{:S(2)}, u32[]{:S(2)}) collective-permute-start(bf16[2,2,256,128]{3,2,1,0:T(8,128)(2,1)} %get-tuple-element.276), channel_id=1, source_target_pairs={{0,1},{1,0},{2,3},{3,2},{4,5},{5,4},{6,7},{7,6},{8,9},{9,8},{10,11... | collective-permute-start | bytes 786440 | tf_op jit(solution)/shard_map/ppermute | solution.py:1447
  416.8 19.3 %all-to-all-start.6 = ((bf16[4,96,1296]{2,1,0:T(8,128)(2,1)}), bf16[4,96,1296]{2,1,0:T(8,128)(2,1)}, u32[]{:S(2)}, u32[]{:S(2)}) async-start(bf16[4,96,1296]{2,1,0:T(8,128)(2,1)} %bitcast.111), calls=%async_computation.8 | async-start | bytes 2162688 | tf_op jit(solution)/shard_map/all_to_all | solution.py:1459
  (68 other events, 447.5 us)
Sparse Core Ops, SparseCore 0:
  16.8 52.8 all-gather.3
  71.8 29.5 all-gather.7
  103.0 31.8 all-gather.5
  246.1 48.3 reduce-scatter.2
  360.7 31.5 reduce-scatter.4

commit v6 on v5

--- a/solution.py
+++ b/solution.py
@@ -1657,10 +1657,11 @@
     far_other, place, theirs_0, theirs_1 = after((far_other, place, theirs_0, theirs_1))
     cots = (cot_own, by_x, by_y, *far, *near_other, *far_other)
     d_gated_0, d_gated_1, cross_0, cross_1 = run_cross(place, cots, (gun_0, gun_1), w_out)
-    branch_0 = core_sums(mine_0, theirs_0)
+    got_0 = swap_cores(theirs_0)
 
     stats = jnp.stack([stat_0 + cross_0, stat_1 + cross_1])
-    stats = after(stats, branch_0)
+    got_0, stats = after((got_0, stats))
+    branch_0 = add_low(mine_0, got_0)
     stats = stats + swap_cores(stats)[:, ::-1]
     theirs_1 = after(theirs_1, stats)
     sums_0, sums_1 = sum_seq(stats)

time: 489 us -> 487 us (level)
  transfers between devices with their start and end apart: 54 -> 54, of which waited for: 29 -> 28; matrix products, arithmetic and copies ran while one was open for 16% -> 17% of each run, Pallas kernels for 45% -> 45%
where the time goes in v6:
time: 487 us; the launch traced here: 480 us
  Pallas kernels  225 us (46%)
  waiting for transfers between devices  66.4 us (14%)
  starting transfers between devices  61.9 us (13%)
  other arithmetic  57.8 us (12%)
  local copies, waits for them, and re-layouts  46.7 us (10%)
  between operations  19.3 us (4%)
    pallas_call x7, Pallas kernels, call_blocks(): pl.pallas_call(kernel, grid_spec=pltpu.PrefetchScalarGridSpec(num_scalar_...  211 us
    all_to_all x7, starting transfers between devices, exchange(): return lax.all_to_all(blocks, 'seq', 0, 0, tiled=True)  29.7 us
    ppermute x6, waiting for transfers between devices, over_x(): return lax.ppermute(block, 'seq', ROUTE_X)  21.5 us
    convert_element_type x5, other arithmetic, add_low(): return (a.astype(F32) + b.astype(F32)).astype(BF)  20.6 us
    all_to_all x7, waiting for transfers between devices, exchange(): return lax.all_to_all(blocks, 'seq', 0, 0, tiled=True)  10.7 us
    ppermute x23, waiting for transfers between devices, swap_cores(): return lax.ppermute(block, 'tensor', SWAP)  10.3 us
    ppermute x4, waiting for transfers between devices, sum_dp(): lax.ppermute(value, 'dp', [(i, i ^ hop) for i in range(dp_count)])  10.1 us
  transfers between devices with their start and end apart: 54, of which 28 were waited for; matrix products, arithmetic and copies ran while one was open for 17% of the time, Pallas kernels for 45%

profile of v6, /device:TPU:0, one launch (start us, length us, event | category | flops | bytes accessed | tf_op | source)
XLA Modules:
  0.0 480.5 jit_solution(2838361783826191269)
XLA Ops:
  8.3 3.3 fusion.48
  51.6 9.0 %collective-permute-done.6.refs_3_ = bf16[128,1536]{1,0:T(8,128)(2,1)S(1)} collective-permute-done((bf16[128,1536]{1,0:T(8,128)(2,1)S(1)}, bf16[128,1536]{1,0:T(8,128)(2,1)S(1)}, u32[]{:S(2)}, u32[]{:S(2)}) %collective-permute-start.6) | collective-permute-done | bytes 393248 | tf_op jit(solution)/shard_map/ppermute | solution.py:1451
  62.4 3.8 all-to-all-start
  73.1 29.2 %mix_forward.2 = (bf16[2,4,256,640]{3,2,1,0:T(8,128)(2,1)}, f32[2,4,256,128]{3,2,1,0:T(8,128)}, f32[2,4,256,640]{3,2,1,0:T(8,128)}, f32[2,4,256,384]{3,2,1,0:T(8...) custom-call(s32[2]{0:T(128)} %pad_add_fusion.place_ref.refs_0_, ...), custom_call_target="tpu_custom_call" | custom-call | flops 1024 | bytes 1024 | tf_op jit(solution)/shard_map/mix_forward/pallas_call | solution.py:1052
  108.2 25.5 %mix_forward.3 = (bf16[2,4,256,640]{3,2,1,0:T(8,128)(2,1)}, f32[2,4,256,128]{3,2,1,0:T(8,128)}, f32[2,4,256,640]{3,2,1,0:T(8,128)}, f32[2,4,256,384]{3,2,1,0:T(8,128)}, bf16[2,4,768,128]{3,2,1,0:T(8,128)(2,1)}) custom-call(s32[2]{0:T(128)} %pad_add_fusion.place_ref.refs_0_, bf16[4,256,1536]{2,1,0:T(8,128)(2,1)} %copy-done.2, ...), custom_call_target="tpu_custom_call" | custom-call | flops 1024 | bytes 1024 | tf_op jit(solution)/shard_map/mix_forward/pallas_call | solution.py:1052
  134.9 5.0 %collective-permute-done.12.refs_1_.refs_5_ = bf16[2,256,1536]{2,1,0:T(8,128)(2,1)} collective-permute-done((bf16[2,256,1536]{2,1,0:T(8,128)(2,1)}, bf16[2,256,1536]{2,1,0:T(8,128)(2,1)}, u32[]{:S(2)}, u32[]{:S(2)}) %collective-permute-start.12) | collective-permute-done | bytes 1572896 | tf_op jit(solution)/shard_map/ppermute | solution.py:1451
  146.3 24.4 %gate_forward.1 = (f32[2,4,256,384]{3,2,1,0:T(8,128)}, f32[2,4,256,384]{3,2,1,0:T(8,128)}, bf16[2,4,256,384]{3,2,1,0:T(8,128)(2,1)}, bf16[2,4,256,384]{3,2,1,0:T...) custom-call(s32[2]{0:T(128)} %pad_add_fusion.place_ref.refs_0_, ...), custom_call_target="tpu_custom_call" | custom-call | flops 1024 | bytes 1024 | tf_op jit(solution)/shard_map/gate_forward/pallas_call | solution.py:1052
  175.2 16.5 %cross_forward.1 = (f32[2,4,256,384]{3,2,1,0:T(8,128)}, f32[2,4,256,384]{3,2,1,0:T(8,128)}, f32[2,4,2,256]{3,2,1,0:T(2,128)}, f32[2,4,2,256]{3,2,1,0:T(2,128)}) custom-call(s32[2]{0:T(128)} %pad_add_fusion.place_ref.refs_0_, bf16[2,256,1536]{2,1,0:T(8,128)(2,1)} %maximum_select_fusion.1.refs_0_.refs_4_, ...), custom_call_target="tpu_custom_call" | custom-call | flops 1024 | bytes 1024 | tf_op jit(solution)/shard_map/cross_forward/pallas_call | solution.py:1052
  198.3 5.3 %add_convert_fusion.3 = bf16[4,2,256,768]{3,2,1,0:T(8,128)(2,1)} fusion(bf16[4,2,256,768]{3,2,1,0:T(8,128)(2,1)} %collective-permute-done.21, bf16[4,2,256,768]{3,2,1,0:T(8,128)(2,1)} %get-tuple-element.192), kind=kLoop, calls=%fused_computation.7 | loop fusion | flops 6291456 | bytes 9437184 | tf_op jit(solution)/shard_map/convert_element_type | solution.py:1467
  204.3 3.8 all-to-all-start.1
  208.0 28.2 %gate_backward.1 = (bf16[2,4,256,384]{3,2,1,0:T(8,128)(2,1)}, bf16[2,4,256,384]{3,2,1,0:T(8,128)(2,1)}, bf16[2,4,256,384]{3,2,1,0:T(8,128)(2,1)}, bf16[2,4,256,3...) custom-call(s32[2]{0:T(128)} %pad_add_fusion.place_ref.refs_0_, ...), custom_call_target="tpu_custom_call" | custom-call | flops 1024 | bytes 1024 | tf_op jit(solution)/shard_map/gate_backward/pallas_call | solution.py:1052
  236.3 4.3 add_convert_fusion.2
  243.4 4.9 %all-to-all-start.2 = ((bf16[4,2,256,768]{3,2,1,0:T(8,128)(2,1)}), bf16[4,2,256,768]{3,2,1,0:T(8,128)(2,1)}, u32[]{:S(2)}, u32[]{:S(2)}) async-start(bf16[4,2,256,768]{3,2,1,0:T(8,128)(2,1)} %add_convert_fusion.2), calls=%async_computation.2 | async-start | bytes 6291456 | tf_op jit(solution)/shard_map/all_to_all | solution.py:1459
  248.4 43.5 %mix_backward.2 = (f32[400,1536]{1,0:T(8,128)}, f32[2,4,272,128]{3,2,1,0:T(8,128)}, f32[8,384]{1,0:T(8,128)}, f32[8,384]{1,0:T(8,128)}, bf16[4,2,304,768]{3,2,1,...) custom-call(s32[2]{0:T(128)} %pad_add_fusion.place_ref.refs_0_, ...), custom_call_target="tpu_custom_call" | custom-call | flops 1024 | bytes 1024 | tf_op jit(solution)/shard_map/mix_backward/pallas_call | solution.py:1052
  299.4 4.8 add_convert_fusion
  304.2 4.7 all-to-all-start.3
  309.0 44.2 %mix_backward.3 = (bf16[4,400,384]{2,1,0:T(8,128)(2,1)}, bf16[4,2,272,128]{3,2,1,0:T(8,128)(2,1)}, bf16[4,2,272,128]{3,2,1,0:T(8,128)(2,1)}, f32[2,4,272,128]{3,...) custom-call(s32[2]{0:T(128)} %pad_add_fusion.place_ref.refs_0_, ...), custom_call_target="tpu_custom_call" | custom-call | flops 1024 | bytes 1024 | tf_op jit(solution)/shard_map/mix_backward/pallas_call | solution.py:1052
  358.0 4.2 all-to-all-start.4
  363.6 4.3 add_convert_fusion.1
  367.9 3.5 all-to-all-done.4.maps_ref
  371.3 4.0 all-to-all-start.5
  379.4 6.1 %maps_backward.1 = (bf16[2,2,256,128]{3,2,1,0:T(8,128)(2,1)}, bf16[4,128,384]{2,1,0:T(8,128)(2,1)}, f32[8,128]{1,0:T(8,128)}) custom-call(s32[2]{0:T(128)} %pad_add_fusion.place_ref.refs_0_, bf16[4,2,48,768]{3,2,1,0:T(8,128)(2,1)} %slice.145.packed_ref, bf16[4,2,272,128]{3,2,1,0:T(8,128)(2,1)} %all-to-all-done.4.maps_ref, ...), custom_call_target="tpu_custom_call" | custom-call | flops 1024 | bytes 1024 | tf_op jit(solution)/shard_map/maps_backward/pallas_call | solution.py:1318
  387.3 3.5 collective-permute-start.31
  394.3 5.0 %collective-permute-done.30 = bf16[128,384]{1,0:T(8,128)(2,1)S(1)} collective-permute-done((bf16[128,384]{1,0:T(8,128)(2,1)}, bf16[128,384]{1,0:T(8,128)(2,1)S(1)}, u32[]{:S(2)}, u32[]{:S(2)}) %collective-permute-start.30) | collective-permute-done | bytes 98336 | tf_op jit(solution)/shard_map/ppermute | solution.py:1715
  400.9 3.5 collective-permute-done.32
  414.2 4.3 all-to-all-start.6
  418.5 3.6 convert_reduce_fusion.1
  425.8 3.3 maximum_add_fusion
  429.1 4.4 all-to-all-done.6.share_ref
  435.1 3.1 owner_norm.1
  457.6 3.6 fusion.11
  468.2 4.4 owner_update.1
  (317 shorter events, 140.0 us)
Async XLA Ops:
  7.2 62.4 %all-gather.4.cloned.1.call-start = ((), (), s32[]{:S(2)}) async-start(), calls=%async_computation.9 | async-start | bytes 2949120 | tf_op jit(solution)/shard_map/all_gather | solution.py:1518
  16.2 25.6 %collective-permute-start.4 = (bf16[2,256,768]{2,1,0:T(8,128)(2,1)}, bf16[2,256,768]{2,1,0:T(8,128)(2,1)}, u32[]{:S(2)}, u32[]{:S(2)}) collective-permute-start(bf16[2,256,768]{2,1,0:T(8,128)(2,1)} %get-tuple-element.303), channel_id=1, source_target_pairs={{0,1},{1,0},{2,3},{3,2},{4,5},{5,4},{6,7},{7,6},{8,9},{9,8},{10,11... | collective-permute-start | bytes 2359304 | tf_op jit(solution)/shard_map/ppermute | solution.py:1447
  26.0 20.7 %collective-permute-start.1 = (bf16[256,1536]{1,0:T(8,128)(2,1)S(1)}, bf16[256,1536]{1,0:T(8,128)(2,1)S(1)}, u32[]{:S(2)}, u32[]{:S(2)}) collective-permute-start(bf16[256,1536]{1,0:T(8,128)(2,1)S(1)} %get-tuple-element.159.refs_0_), channel_id=1, source_target_pairs={{0,2},{2,0},{4,6},{6,4},{1,3},{3,1},{5,7},{7,5},{8,10},{10,8},{12,... | collective-permute-start | bytes 2359304 | tf_op jit(solution)/shard_map/ppermute | solution.py:1451
  28.5 19.7 %collective-permute-start.2 = (bf16[256,1536]{1,0:T(8,128)(2,1)S(1)}, bf16[256,1536]{1,0:T(8,128)(2,1)S(1)}, u32[]{:S(2)}, u32[]{:S(2)}) collective-permute-start(bf16[256,1536]{1,0:T(8,128)(2,1)S(1)} %get-tuple-element.159.refs_0_), channel_id=1, source_target_pairs={{0,4},{2,6},{4,0},{6,2},{1,5},{3,7},{5,1},{7,3},{8,12},{10,14},{12... | collective-permute-start | bytes 2359304 | tf_op jit(solution)/shard_map/ppermute | solution.py:1455
  30.0 18.2 %collective-permute-start.3 = (bf16[256,1536]{1,0:T(8,128)(2,1)S(1)}, bf16[256,1536]{1,0:T(8,128)(2,1)}, u32[]{:S(2)}, u32[]{:S(2)}) collective-permute-start(bf16[256,1536]{1,0:T(8,128)(2,1)S(1)} %get-tuple-element.159.refs_0_), channel_id=1, source_target_pairs={{0,1},{1,0},{2,3},{3,2},{4,5},{5,4},{6,7},{7,6},{8,9},{9,8},{10,11... | collective-permute-start | bytes 2359304 | tf_op jit(solution)/shard_map/ppermute | solution.py:1447
  48.9 11.7 %collective-permute-start.8 = (bf16[256,1536]{1,0:T(8,128)(2,1)S(1)}, bf16[256,1536]{1,0:T(8,128)(2,1)S(1)}, u32[]{:S(2)}, u32[]{:S(2)}) collective-permute-start(bf16[256,1536]{1,0:T(8,128)(2,1)S(1)} %collective-permute-done.1.refs_1_), channel_id=1, source_target_pairs={{0,1},{1,0},{2,3},{3,2},{4,5},{5,4},{6,7},{7,6},{8,9},{9,8},{10,11... | collective-permute-start | bytes 2359304 | tf_op jit(solution)/shard_map/ppermute | solution.py:1447
  48.9 12.6 %collective-permute-start.9 = (bf16[256,1536]{1,0:T(8,128)(2,1)S(1)}, bf16[256,1536]{1,0:T(8,128)(2,1)}, u32[]{:S(2)}, u32[]{:S(2)}) collective-permute-start(bf16[256,1536]{1,0:T(8,128)(2,1)S(1)} %collective-permute-done.2.refs_2_), channel_id=1, source_target_pairs={{0,1},{1,0},{2,3},{3,2},{4,5},{5,4},{6,7},{7,6},{8,9},{9,8},{10,11... | collective-permute-start | bytes 2359304 | tf_op jit(solution)/shard_map/ppermute | solution.py:1447
  49.5 11.1 %collective-permute-start.6 = (bf16[128,1536]{1,0:T(8,128)(2,1)S(1)}, bf16[128,1536]{1,0:T(8,128)(2,1)S(1)}, u32[]{:S(2)}, u32[]{:S(2)}) collective-permute-start(bf16[128,1536]{1,0:T(8,128)(2,1)S(1)} %slice.136), channel_id=1, source_target_pairs={{0,2},{2,0},{4,6},{6,4},{1,3},{3,1},{5,7},{7,5},{8,10},{10,8},{12,... | collective-permute-start | bytes 1179656 | tf_op jit(solution)/shard_map/ppermute | solution.py:1451
  49.9 10.8 %collective-permute-start.7 = (bf16[128,1536]{1,0:T(8,128)(2,1)S(1)}, bf16[128,1536]{1,0:T(8,128)(2,1)S(1)}, u32[]{:S(2)}, u32[]{:S(2)}) collective-permute-start(bf16[128,1536]{1,0:T(8,128)(2,1)S(1)} %slice.137), channel_id=1, source_target_pairs={{0,4},{2,6},{4,0},{6,2},{1,5},{3,7},{5,1},{7,3},{8,12},{10,14},{12... | collective-permute-start | bytes 1179656 | tf_op jit(solution)/shard_map/ppermute | solution.py:1455
  62.4 39.9 %all-to-all-start = ((bf16[4,256,1536]{2,1,0:T(8,128)(2,1)}), bf16[4,256,1536]{2,1,0:T(8,128)(2,1)S(1)}, u32[]{:S(2)}, u32[]{:S(2)}) async-start(bf16[4,256,1536]{2,1,0:T(8,128)(2,1)} %broadcast_in_dim.58), calls=%async_computation | async-start | bytes 6291456 | tf_op jit(solution)/shard_map/all_to_all | solution.py:1459
  66.2 36.1 %all-gather.8.cloned.1.call-start = ((), (), s32[]{:S(2)}) async-start(), calls=%async_computation.11 | async-start | bytes 1474560 | tf_op jit(solution)/shard_map/all_gather | solution.py:1518
  67.0 67.9 %all-gather.6.cloned.1.call-start = ((), (), s32[]{:S(2)}) async-start(), calls=%async_computation.10 | async-start | bytes 1474560 | tf_op jit(solution)/shard_map/all_gather | solution.py:1518
  67.5 34.7 %collective-permute-start.5 = (bf16[2,256,1536]{2,1,0:T(8,128)(2,1)}, bf16[2,256,1536]{2,1,0:T(8,128)(2,1)}, u32[]{:S(2)}, u32[]{:S(2)}) collective-permute-start(bf16[2,256,1536]{2,1,0:T(8,128)(2,1)} %maximum_select_fusion.1.refs_0_.refs_4_), channel_id=1, source_target_pairs={{0,1},{1,0},{2,3},{3,2},{4,5},{5,4},{6,7},{7,6},{8,9},{9,8},{10,11... | collective-permute-start | bytes 4718600 | tf_op jit(solution)/shard_map/ppermute | solution.py:1447
  102.5 37.4 %collective-permute-start.12 = (bf16[2,256,1536]{2,1,0:T(8,128)(2,1)}, bf16[2,256,1536]{2,1,0:T(8,128)(2,1)}, u32[]{:S(2)}, u32[]{:S(2)}) collective-permute-start(bf16[2,256,1536]{2,1,0:T(8,128)(2,1)} %maximum_select_fusion.1.refs_0_.refs_4_), channel_id=1, source_target_pairs={{0,2},{2,0},{4,6},{6,4},{1,3},{3,1},{5,7},{7,5},{8,10},{10,8},{12,... | collective-permute-start | bytes 4718600 | tf_op jit(solution)/shard_map/ppermute | solution.py:1451
  104.7 36.7 %collective-permute-start.13 = (bf16[2,256,1536]{2,1,0:T(8,128)(2,1)}, bf16[2,256,1536]{2,1,0:T(8,128)(2,1)}, u32[]{:S(2)}, u32[]{:S(2)}) collective-permute-start(bf16[2,256,1536]{2,1,0:T(8,128)(2,1)} %maximum_select_fusion.1.refs_0_.refs_4_), channel_id=1, source_target_pairs={{0,4},{2,6},{4,0},{6,2},{1,5},{3,7},{5,1},{7,3},{8,12},{10,14},{12... | collective-permute-start | bytes 4718600 | tf_op jit(solution)/shard_map/ppermute | solution.py:1455
  141.4 29.4 %collective-permute-start.17 = (bf16[2,256,1536]{2,1,0:T(8,128)(2,1)}, bf16[2,256,1536]{2,1,0:T(8,128)(2,1)S(1)}, u32[]{:S(2)}, u32[]{:S(2)}) collective-permute-start(bf16[2,256,1536]{2,1,0:T(8,128)(2,1)} %collective-permute-done.12.refs_1_.refs_5_), channel_id=1, source_target_pairs={{0,1},{1,0},{2,3},{3,2},{4,5},{5,4},{6,7},{7,6},{8,9},{9,8},{10,11... | collective-permute-start | bytes 4718600 | tf_op jit(solution)/shard_map/ppermute | solution.py:1447
  141.4 29.4 %collective-permute-start.18 = (bf16[2,256,1536]{2,1,0:T(8,128)(2,1)}, bf16[2,256,1536]{2,1,0:T(8,128)(2,1)S(1)}, u32[]{:S(2)}, u32[]{:S(2)}) collective-permute-start(bf16[2,256,1536]{2,1,0:T(8,128)(2,1)} %collective-permute-done.13.refs_2_.refs_6_), channel_id=1, source_target_pairs={{0,1},{1,0},{2,3},{3,2},{4,5},{5,4},{6,7},{7,6},{8,9},{9,8},{10,11... | collective-permute-start | bytes 4718600 | tf_op jit(solution)/shard_map/ppermute | solution.py:1447
  144.3 26.5 %collective-permute-start.15 = (bf16[2,128,1536]{2,1,0:T(8,128)(2,1)S(1)}, bf16[2,128,1536]{2,1,0:T(8,128)(2,1)S(1)}, u32[]{:S(2)}, u32[]{:S(2)}) collective-permute-start(bf16[2,128,1536]{2,1,0:T(8,128)(2,1)S(1)} %slice.140), channel_id=1, source_target_pairs={{0,2},{2,0},{4,6},{6,4},{1,3},{3,1},{5,7},{7,5},{8,10},{10,8},{12,... | collective-permute-start | bytes 2359304 | tf_op jit(solution)/shard_map/ppermute | solution.py:1451
  144.7 26.1 %collective-permute-start.16 = (bf16[2,128,1536]{2,1,0:T(8,128)(2,1)S(1)}, bf16[2,128,1536]{2,1,0:T(8,128)(2,1)S(1)}, u32[]{:S(2)}, u32[]{:S(2)}) collective-permute-start(bf16[2,128,1536]{2,1,0:T(8,128)(2,1)S(1)} %slice.141), channel_id=1, source_target_pairs={{0,4},{2,6},{4,0},{6,2},{1,5},{3,7},{5,1},{7,3},{8,12},{10,14},{12... | collective-permute-start | bytes 2359304 | tf_op jit(solution)/shard_map/ppermute | solution.py:1455
  174.3 18.2 %collective-permute-start.21 = (bf16[4,2,256,768]{3,2,1,0:T(8,128)(2,1)}, bf16[4,2,256,768]{3,2,1,0:T(8,128)(2,1)}, u32[]{:S(2)}, u32[]{:S(2)}) collective-permute-start(bf16[4,2,256,768]{3,2,1,0:T(8,128)(2,1)} %get-tuple-element.202), channel_id=1, source_target_pairs={{0,1},{1,0},{2,3},{3,2},{4,5},{5,4},{6,7},{7,6},{8,9},{9,8},{10,11... | collective-permute-start | bytes 9437192 | tf_op jit(solution)/shard_map/ppermute | solution.py:1447
  193.8 42.5 %collective-permute-start.25 = (bf16[4,2,256,768]{3,2,1,0:T(8,128)(2,1)}, bf16[4,2,256,768]{3,2,1,0:T(8,128)(2,1)}, u32[]{:S(2)}, u32[]{:S(2)}) collective-permute-start(bf16[4,2,256,768]{3,2,1,0:T(8,128)(2,1)} %get-tuple-element.219), channel_id=1, source_target_pairs={{0,1},{1,0},{2,3},{3,2},{4,5},{5,4},{6,7},{7,6},{8,9},{9,8},{10,11... | collective-permute-start | bytes 9437192 | tf_op jit(solution)/shard_map/ppermute | solution.py:1447
  204.3 39.1 %all-to-all-start.1 = ((bf16[4,2,256,768]{3,2,1,0:T(8,128)(2,1)}), bf16[4,2,256,768]{3,2,1,0:T(8,128)(2,1)S(1)}, u32[]{:S(2)}, u32[]{:S(2)}) async-start(bf16[4,2,256,768]{3,2,1,0:T(8,128)(2,1)} %add_convert_fusion.3), calls=%async_computation.1 | async-start | bytes 6291456 | tf_op jit(solution)/shard_map/all_to_all | solution.py:1459
  208.0 83.9 %reduce-scatter.3.cloned.1.call-start = ((), (), s32[]{:S(2)}) async-start(), calls=%async_computation.12 | async-start | bytes 2949120 | tf_op jit(solution)/shard_map/reduce_scatter | solution.py:1580
  243.4 48.4 %all-to-all-start.2 = ((bf16[4,2,256,768]{3,2,1,0:T(8,128)(2,1)}), bf16[4,2,256,768]{3,2,1,0:T(8,128)(2,1)}, u32[]{:S(2)}, u32[]{:S(2)}) async-start(bf16[4,2,256,768]{3,2,1,0:T(8,128)(2,1)} %add_convert_fusion.2), calls=%async_computation.2 | async-start | bytes 6291456 | tf_op jit(solution)/shard_map/all_to_all | solution.py:1459
  304.2 49.1 %all-to-all-start.3 = ((bf16[4,2,304,768]{3,2,1,0:T(8,128)(2,1)}), bf16[4,2,304,768]{3,2,1,0:T(8,128)(2,1)}, u32[]{:S(2)}, u32[]{:S(2)}) async-start(bf16[4,2,304,768]{3,2,1,0:T(8,128)(2,1)} %add_convert_fusion), calls=%async_computation.4 | async-start | bytes 7471104 | tf_op jit(solution)/shard_map/all_to_all | solution.py:1459
  308.9 91.4 %reduce-scatter.5.cloned.1.call-start = ((), (), s32[]{:S(2)}) async-start(), calls=%async_computation.13 | async-start | bytes 1536000 | tf_op jit(solution)/shard_map/reduce_scatter | solution.py:1580
  358.0 13.4 %all-to-all-start.4 = ((bf16[4,2,272,128]{3,2,1,0:T(8,128)(2,1)}), bf16[4,2,272,128]{3,2,1,0:T(8,128)(2,1)}, u32[]{:S(2)}, u32[]{:S(2)}) async-start(bf16[4,2,272,128]{3,2,1,0:T(8,128)(2,1)} %add_convert_fusion.4), calls=%async_computation.5 | async-start | bytes 1114112 | tf_op jit(solution)/shard_map/all_to_all | solution.py:1459
  371.3 42.8 %all-to-all-start.5 = ((bf16[4,2,256,768]{3,2,1,0:T(8,128)(2,1)}), bf16[4,2,256,768]{3,2,1,0:T(8,128)(2,1)S(1)}, u32[]{:S(2)}, u32[]{:S(2)}) async-start(bf16[4,2,256,768]{3,2,1,0:T(8,128)(2,1)} %add_convert_fusion.1), calls=%async_computation.6 | async-start | bytes 6291456 | tf_op jit(solution)/shard_map/all_to_all | solution.py:1459
  390.8 8.6 %collective-permute-start.30 = (bf16[128,384]{1,0:T(8,128)(2,1)}, bf16[128,384]{1,0:T(8,128)(2,1)S(1)}, u32[]{:S(2)}, u32[]{:S(2)}) collective-permute-start(bf16[128,384]{1,0:T(8,128)(2,1)} %get-tuple-element.310), channel_id=1, source_target_pairs={{0,16},{8,24},{16,0},{24,8},{1,17},{9,25},{17,1},{25,9},{2,18},{10... | collective-permute-start | bytes 294920 | tf_op jit(solution)/shard_map/ppermute | solution.py:1715
  390.8 8.6 %collective-permute-start.29 = (bf16[128,384]{1,0:T(8,128)(2,1)}, bf16[128,384]{1,0:T(8,128)(2,1)}, u32[]{:S(2)}, u32[]{:S(2)}) collective-permute-start(bf16[128,384]{1,0:T(8,128)(2,1)} %get-tuple-element.308), channel_id=1, source_target_pairs={{0,8},{8,16},{16,24},{24,0},{1,9},{9,17},{17,25},{25,1},{2,10},{10... | collective-permute-start | bytes 294920 | tf_op jit(solution)/shard_map/ppermute | solution.py:1715
  407.0 15.1 %collective-permute-start.35 = (bf16[2,2,256,128]{3,2,1,0:T(8,128)(2,1)}, bf16[2,2,256,128]{3,2,1,0:T(8,128)(2,1)}, u32[]{:S(2)}, u32[]{:S(2)}) collective-permute-start(bf16[2,2,256,128]{3,2,1,0:T(8,128)(2,1)} %get-tuple-element.278), channel_id=1, source_target_pairs={{0,1},{1,0},{2,3},{3,2},{4,5},{5,4},{6,7},{7,6},{8,9},{9,8},{10,11... | collective-permute-start | bytes 786440 | tf_op jit(solution)/shard_map/ppermute | solution.py:1447
  414.2 19.3 %all-to-all-start.6 = ((bf16[4,96,1296]{2,1,0:T(8,128)(2,1)}), bf16[4,96,1296]{2,1,0:T(8,128)(2,1)}, u32[]{:S(2)}, u32[]{:S(2)}) async-start(bf16[4,96,1296]{2,1,0:T(8,128)(2,1)} %bitcast.111), calls=%async_computation.8 | async-start | bytes 2162688 | tf_op jit(solution)/shard_map/all_to_all | solution.py:1459
  (68 other events, 449.4 us)
Sparse Core Ops, SparseCore 0:
  16.8 52.8 all-gather.3
  71.8 29.5 all-gather.7
  103.0 31.8 all-gather.5
  243.5 48.3 reduce-scatter.2
  358.1 31.6 reduce-scatter.4
